TPU v7x, 256 devices: a whole 4x4x8 slice. The times are simulated.
256 devices in a mesh: img: 4 (over x), band: 64 (over y, z, core).
Axes of the slice: x: 4, y: 4, z: 8, core: 2. Of those that a mesh axis runs over, the one named last changes fastest.
Arguments:
- features: bfloat16 [4, 512, 512, 256], P('img', 'band'), may hold values from -6 to 6
- w_rpn: bfloat16 [3, 3, 256, 256], replicated, may hold values from -0.125 to 0.125
- w_anchor: bfloat16 [256, 15], replicated, may hold values from -0.375 to 0.375
- pixel_slots: int32 [4, 64, 64, 32], P('img', None, 'band'), may hold values from 0 to 4095
- sample_slot: int32 [4, 512, 49, 4], P('img', 'band'), may hold values from 0 to 2047
- sample_weight: float32 [4, 512, 49, 4], P('img', 'band'), may hold values from 0 to 1, as said below
- roi_labels: int32 [4, 512], P('img', 'band'), may hold values from 0 to 80
- w_fc1: bfloat16 [12544, 1024], P('band'), may hold values from -0.0546875 to 0.0546875
- w_fc2: bfloat16 [1024, 1024], replicated, may hold values from -0.1875 to 0.1875
- w_class: bfloat16 [1024, 81], replicated, may hold values from -6 to 6
Outputs:
- rpn_out: bfloat16 [4, 15, 512, 512], P('img', None, 'band')
- grad_fc1: float32 [12544, 1024], P('band')
- grad_fc2: float32 [1024, 1024], replicated
- grad_class: float32 [1024, 81], replicated
Inputs may be any that keep to these rules, and one draw needn't show every extreme that they name: `pixel_slots`: a pixel of band b given as its row within the band times 512 plus its column. `sample_slot`: a slot of the proposal's head rank, band times 32 plus slot. `sample_weight`: nonnegative bilinear weights, the four of a bin summing to one.
All inputs are finite; a program needn't handle non-finite values.
Results may differ from a plain program's by a relative error of at most 0.015.
Values may be sent and summed in bfloat16 or wider, within the bound.
No kernel may reach another device: no remote copies, remote signals or barrier semaphores. Data moves between devices by JAX's collectives and lax.ppermute only.
A program may use at most 128 MiB of HBM per device.

v0:
```python
import jax
import jax.numpy as jnp
from jax import lax
from jax.sharding import PartitionSpec as P


def extended(array, sides, width):
    for axis, dim in sides:
        devices, length = (lax.axis_size(axis), array.shape[dim])
        up = [(i, (i + 1) % devices) for i in range(devices - 1)]
        down = [(j, i) for i, j in up]
        last = lax.slice_in_dim(array, length - width, length, axis=dim)
        leading = lax.slice_in_dim(array, 0, width, axis=dim)
        before = lax.ppermute(last, axis, up)
        after = lax.ppermute(leading, axis, down)
        array = jnp.concatenate([before, array, after], axis=dim)
    return array


def gelu_slope(value):
    out, pull = jax.vjp(jax.nn.gelu, value)
    return pull(jnp.ones_like(value))[0]


def side_pad(array):
    return jnp.pad(array, ((0, 0), (0, 0), (1, 1), (0, 0)))


def conv_rows(source, w_rpn, count):
    batch = source.shape[0]
    width = source.shape[2] - 2
    channels = source.shape[3]
    total = jnp.zeros((batch * count * width, w_rpn.shape[3]), jnp.float32)
    for dy in range(3):
        for dx in range(3):
            window = source[:, dy : dy + count, dx : dx + width, :].reshape(
                batch * count * width, channels
            )
            total = total + jnp.dot(window, w_rpn[dy, dx], preferred_element_type=jnp.float32)
    return total.reshape(batch, count, width, w_rpn.shape[3])


def shards(
    features,
    w_rpn,
    w_anchor,
    pixel_slots,
    sample_slot,
    sample_weight,
    roi_labels,
    w_fc1,
    w_fc2,
    w_class,
):
    rows = features.shape[1]
    width = features.shape[2]
    channels = features.shape[3]
    nband = lax.axis_size("band")
    padded = side_pad(extended(features, (("band", 1),), 1))
    conv = conv_rows(padded, w_rpn, rows)
    rpn_hidden = jnp.maximum(conv, 0.0).astype(jnp.bfloat16)
    anchors = w_anchor.shape[1]
    batch = rpn_hidden.shape[0]
    rpn_flat = jnp.dot(
        rpn_hidden.reshape(batch * rows * width, channels),
        w_anchor,
        preferred_element_type=jnp.float32,
    )
    rpn_out = jnp.transpose(rpn_flat.reshape(batch, rows, width, anchors), (0, 3, 1, 2)).astype(
        jnp.bfloat16
    )
    flat = features.reshape(rows * width, channels)
    capacity = pixel_slots.shape[3]
    wanted = pixel_slots[0, :, 0, :].reshape(nband * capacity)
    sending = flat[wanted].reshape(nband, capacity, channels)
    received = lax.all_to_all(sending, "band", split_axis=0, concat_axis=0, tiled=True)
    received = received.reshape(nband * capacity, channels).astype(jnp.float32)
    roi_count = sample_slot.shape[1]
    bins = sample_slot.shape[2]
    corner_slots = sample_slot[0].reshape(roi_count * bins, 4)
    corner_weights = sample_weight[0].reshape(roi_count * bins, 4)
    slot_ids = jnp.arange(nband * capacity, dtype=jnp.int32)[None, :]
    pooling = jnp.zeros((roi_count * bins, nband * capacity), jnp.float32)
    for corner in range(4):
        hits = (corner_slots[:, corner : corner + 1] == slot_ids).astype(jnp.float32)
        pooling = pooling + hits * corner_weights[:, corner : corner + 1]
    pooled = jnp.dot(
        pooling, received, precision=lax.Precision.HIGHEST, preferred_element_type=jnp.float32
    )
    pooled = pooled.astype(jnp.bfloat16).reshape(roi_count, bins, channels)
    x_local = jnp.transpose(pooled, (0, 2, 1)).reshape(roi_count, channels * bins)
    x_cols = lax.all_to_all(x_local, "band", split_axis=1, concat_axis=0, tiled=True)
    block = x_cols
    a1 = lax.psum_scatter(
        jnp.dot(block, w_fc1, preferred_element_type=jnp.float32),
        "band",
        scatter_dimension=0,
        tiled=True,
    )
    h1 = jax.nn.gelu(a1).astype(jnp.bfloat16)
    a2 = jnp.dot(h1, w_fc2, preferred_element_type=jnp.float32)
    h2 = jax.nn.gelu(a2).astype(jnp.bfloat16)
    logits = jnp.dot(h2, w_class, preferred_element_type=jnp.float32)
    expo = jnp.exp(logits)
    prob = expo / jnp.sum(expo, axis=1, keepdims=True)
    classes = w_class.shape[1]
    onehot = (roi_labels[0][:, None] == jnp.arange(classes, dtype=jnp.int32)[None, :]).astype(
        jnp.float32
    )
    dlogits = (prob - onehot).astype(jnp.bfloat16)
    dh2 = jnp.dot(dlogits, w_class.T, preferred_element_type=jnp.float32)
    da2 = (dh2 * gelu_slope(a2)).astype(jnp.bfloat16)
    dh1 = jnp.dot(da2, w_fc2.T, preferred_element_type=jnp.float32)
    da1 = (dh1 * gelu_slope(a1)).astype(jnp.bfloat16)
    block = x_cols
    grad_fc1 = lax.dot_general(
        block,
        lax.all_gather(da1, "band", axis=0, tiled=True),
        (((0,), (0,)), ((), ())),
        preferred_element_type=jnp.float32,
    )
    contract = (((0,), (0,)), ((), ()))
    grad_fc2 = lax.dot_general(h1, da2, contract, preferred_element_type=jnp.float32)
    grad_class = lax.dot_general(h2, dlogits, contract, preferred_element_type=jnp.float32)
    grad_fc2, grad_class = lax.psum((grad_fc2, grad_class), ("img", "band"))
    grad_fc1 = lax.psum(grad_fc1.astype(jnp.bfloat16), "img").astype(jnp.float32)
    return (rpn_out, grad_fc1, grad_fc2, grad_class)


def solution(mesh):
    return jax.shard_map(
        shards,
        mesh=mesh,
        in_specs=(
            P("img", "band", None, None),
            P(),
            P(),
            P("img", None, "band", None),
            P("img", "band", None, None),
            P("img", "band", None, None),
            P("img", "band"),
            P("band", None),
            P(),
            P(),
        ),
        out_specs=(P("img", None, "band", None), P("band", None), P(), P()),
        check_vma=False,
    )
```

profile of v0, /device:TPU:1, one launch (start us, length us, event | category | flops | bytes accessed | tf_op | source)
XLA Modules:
  0.0 636.8 jit_solution(18278802109133222292)
XLA Ops:
  8.2 10.4 %gather_fusion = bf16[2048,256]{1,0:T(8,128)(2,1)} fusion(bf16[4096,256]{1,0:T(8,128)(2,1)} %bitcast.95, s32[2048]{0:T(1024)S(1)} %broadcast_clamp_fusion), kind=kCustom, calls=%fused_computation | custom fusion | bytes 2105344 | tf_op jit(solution)/shard_map/gather | solution.py:75
  18.6 13.3 %all-to-all-start = ((bf16[64,32,256]{2,1,0:T(8,128)(2,1)}), bf16[64,32,256]{2,1,0:T(8,128)(2,1)S(1)}, u32[]{:S(2)}, u32[]{:S(2)}) async-start(bf16[64,32,256]{2,1,0:T(8,128)(2,1)} %bitcast.31), calls=%async_computation | async-start | bytes 2097152 | tf_op jit(solution)/shard_map/all_to_all | solution.py:76
  32.2 28.3 %all-to-all-done = bf16[64,32,256]{2,1,0:T(8,128)(2,1)S(1)} async-done(((bf16[64,32,256]{2,1,0:T(8,128)(2,1)}), bf16[64,32,256]{2,1,0:T(8,128)(2,1)S(1)}, u32[]{:S(2)}, u32[]{:S(2)}) %all-to-all-start) | async-done | bytes 1048608 | tf_op jit(solution)/shard_map/all_to_all | solution.py:76
  60.5 3.1 fusion.26
  64.4 18.0 %all_to_all.24 = bf16[8,64,196]{2,0,1:T(8,128)(2,1)S(1)} all-to-all(bf16[8,64,196]{2,0,1:T(8,128)(2,1)S(1)} %copy.25), channel_id=1, replica_groups=mesh['img'=4,'band'=64] {'band'}, dimensions={1} | all-to-all | bytes 401408 | tf_op jit(solution)/shard_map/all_to_all | solution.py:92
  82.4 1.8 fusion.33
  85.4 2.4 collective-permute-start.1
  87.7 3.2 collective-permute-start
  90.9 2.2 collective-permute-done.1
  94.9 2.2 fusion.16
  97.2 4.9 fusion.72
  102.1 114.6 %reduce-scatter.2.cloned.1.call-done = f32[8,1024]{1,0:T(8,128)} async-done(((f32[512,1024]{1,0:T(8,128)}), f32[8,1024]{1,0:T(8,128)}) %reduce-scatter.2.cloned.1.call-update) | async-done | bytes 32784 | tf_op jit(solution)/shard_map/reduce_scatter | solution.py:94
  216.7 1.2 fusion.71
  218.7 1.3 fusion.31
  220.3 4.0 pad_maximum_fusion
  228.1 2.8 convolution_add_fusion.4
  231.0 69.6 %all-gather.2.cloned.1.call-done = bf16[512,1024]{1,0:T(8,128)(2,1)} async-done(((bf16[8,1024]{1,0:T(8,128)(2,1)}), bf16[512,1024]{1,0:T(8,128)(2,1)}) %all-gather.2.cloned.1.call-update) | async-done | bytes 1048592 | tf_op jit(solution)/shard_map/all_gather | solution.py:118
  300.6 2.4 convolution_convert_fusion
  304.2 2.8 fusion.70
  307.0 2.4 fusion.35
  317.4 28.9 %all-reduce.5.cloned.1.call-done = bf16[196,1024]{1,0:T(8,128)(2,1)} async-done(((bf16[196,1024]{1,0:T(8,128)(2,1)}), bf16[196,1024]{1,0:T(8,128)(2,1)}) %all-reduce.5.cloned.1.call-update) | async-done | bytes 401424 | tf_op jit(solution)/shard_map/psum | solution.py:126
  346.3 2.0 convert_element_type.61
  348.2 276.3 %all-reduce.7.cloned.1.call-done = (f32[1024,1024]{1,0:T(8,128)}, f32[1024,81]{0,1:T(8,128)}) async-done(((f32[1024,1024]{1,0:T(8,128)}, f32[1024,81]{0,1:T(8,128)}), (f32[1024,1024]{1,0:T(8,128)}, f32[1024,81]{0,1:T(8,128)})) %all-reduce.7.cloned.1.call-update) | async-done | bytes 4526096 | tf_op jit(solution)/shard_map/psum | solution.py:125
  624.6 4.9 copy.30
  (93 shorter events, 19.7 us)
Async XLA Ops:
  7.2 209.5 %copy-start = (bf16[1024,1024]{1,0:T(8,128)(2,1)S(1)}, bf16[1024,1024]{1,0:T(8,128)(2,1)}, u32[]{:S(2)}) copy-start(bf16[1024,1024]{1,0:T(8,128)(2,1)} %param.18) | copy-start | bytes 6291460
  18.6 13.3 %copy-start.21 = (f32[1,8,49,4]{2,3,1,0:T(4,128)S(1)}, f32[1,8,49,4]{2,3,1,0:T(4,128)}, u32[]{:S(2)}) copy-start(f32[1,8,49,4]{2,3,1,0:T(4,128)} %param.15) | copy-start | bytes 18820
  18.6 13.5 %copy-start.22 = (s32[1,8,49,4]{2,3,1,0:T(4,128)S(1)}, s32[1,8,49,4]{2,3,1,0:T(4,128)}, u32[]{:S(2)}) copy-start(s32[1,8,49,4]{2,3,1,0:T(4,128)} %param.14) | copy-start | bytes 18820
  18.6 41.9 %all-to-all-start = ((bf16[64,32,256]{2,1,0:T(8,128)(2,1)}), bf16[64,32,256]{2,1,0:T(8,128)(2,1)S(1)}, u32[]{:S(2)}, u32[]{:S(2)}) async-start(bf16[64,32,256]{2,1,0:T(8,128)(2,1)} %bitcast.31), calls=%async_computation | async-start | bytes 2097152 | tf_op jit(solution)/shard_map/all_to_all | solution.py:76
  31.9 184.8 %reduce-scatter.2.cloned.1.call-start = ((), (), s32[]{:S(2)}) async-start(), calls=%async_computation.3 | async-start | bytes 2129920 | tf_op jit(solution)/shard_map/reduce_scatter | solution.py:94
  63.5 18.9 %copy-start.12 = (bf16[196,1024]{1,0:T(8,128)(2,1)S(1)}, bf16[196,1024]{1,0:T(8,128)(2,1)}, u32[]{:S(2)}) copy-start(bf16[196,1024]{1,0:T(8,128)(2,1)} %param.17) | copy-start | bytes 1204228
  84.2 216.4 %all-gather.2.cloned.1.call-start = ((), (), s32[]{:S(2)}) async-start(), calls=%async_computation.4 | async-start | bytes 1064960 | tf_op jit(solution)/shard_map/all_gather | solution.py:118
  85.4 7.8 %collective-permute-start.1 = (bf16[1,1,512,256]{3,2,1,0:T(8,128)(2,1)S(1)}, bf16[1,1,512,256]{3,2,1,0:T(8,128)(2,1)}, u32[]{:S(2)}, u32[]{:S(2)}) collective-permute-start(bf16[1,1,512,256]{3,2,1,0:T(8,128)(2,1)S(1)} %get-tuple-element.27), channel_id=1, source_target_pairs={{1,0},{2,1},{3,2},{4,3},{5,4},{6,5},{7,6},{8,7},{9,8},{10,9},{11,1... | collective-permute-start | bytes 786440 | tf_op jit(solution)/shard_map/ppermute | solution.py:15
  87.7 6.5 %collective-permute-start = (bf16[1,1,512,256]{3,2,1,0:T(8,128)(2,1)S(1)}, bf16[1,1,512,256]{3,2,1,0:T(8,128)(2,1)S(1)}, u32[]{:S(2)}, u32[]{:S(2)}) collective-permute-start(bf16[1,1,512,256]{3,2,1,0:T(8,128)(2,1)S(1)} %get-tuple-element.26), channel_id=1, source_target_pairs={{0,1},{1,2},{2,3},{3,4},{4,5},{5,6},{6,7},{7,8},{8,9},{9,10},{10,1... | collective-permute-start | bytes 786440 | tf_op jit(solution)/shard_map/ppermute | solution.py:14
  102.1 115.8 %copy-start.18 = (bf16[1024,81]{0,1:T(8,128)(2,1)S(1)}, bf16[1024,81]{0,1:T(8,128)(2,1)}, u32[]{:S(2)}) copy-start(bf16[1024,81]{0,1:T(8,128)(2,1)} %param.19) | copy-start | bytes 497668
  102.1 116.4 %copy-start.26 = (s32[1,8]{1,0:T(1,128)S(1)}, s32[1,8]{1,0:T(1,128)}, u32[]{:S(2)}) copy-start(s32[1,8]{1,0:T(1,128)} %param.16) | copy-start | bytes 100
  220.0 4.2 copy-start.4
  220.0 4.2 copy-start.10
  220.1 126.2 %all-reduce.5.cloned.1.call-start = ((), (), s32[]{:S(2)}) async-start(), calls=%async_computation.5 | async-start | bytes 819200 | tf_op jit(solution)/shard_map/psum | solution.py:126
  231.0 72.1 %copy-start.17 = (f32[8,1024]{1,0:T(8,128)S(1)}, f32[8,1024]{1,0:T(8,128)}, u32[]{:S(2)}) copy-start(f32[8,1024]{1,0:T(8,128)} %copy-done.16) | copy-start | bytes 98308
  231.0 72.1 %copy-start.20 = (f32[8,81]{1,0:T(8,128)S(1)}, f32[8,81]{1,0:T(8,128)}, u32[]{:S(2)}) copy-start(f32[8,81]{1,0:T(8,128)} %copy-done.19) | copy-start | bytes 7780
  231.0 72.1 %copy-start.25 = (f32[8]{0:T(128)S(1)}, f32[8]{0:T(128)}, u32[]{:S(2)}) copy-start(f32[8]{0:T(128)} %copy-done.24) | copy-start | bytes 100
  231.0 72.1 %copy-start.27 = (s32[1,8]{1,0:T(1,128)S(1)}, s32[1,8]{1,0:T(1,128)}, u32[]{:S(2)}) copy-start(s32[1,8]{1,0:T(1,128)} %param.16) | copy-start | bytes 100
  231.0 73.2 %copy-start.15 = (f32[8,1024]{1,0:T(8,128)S(1)}, f32[8,1024]{1,0:T(8,128)}, u32[]{:S(2)}) copy-start(f32[8,1024]{1,0:T(8,128)} %reduce-scatter.2.cloned.1.call-done) | copy-start | bytes 98308
  303.0 321.5 %all-reduce.7.cloned.1.call-start = ((), (), s32[]{:S(2)}) async-start(), calls=%async_computation.6 | async-start | bytes 9109504 | tf_op jit(solution)/shard_map/psum | solution.py:125
  307.0 2.5 copy-start.2
  307.0 3.4 copy-start.3
  624.5 4.9 copy-start.13
  624.6 5.7 copy-start.1
  (11 other events, 15.7 us)
Sparse Core Ops, SparseCore 0:
  84.4 132.2 reduce-scatter.1
  220.4 80.1 all-gather.1
  303.7 42.5 all-reduce.4
  352.2 272.2 all-reduce.6
where the time goes:
time: 639 us; the launch traced here: 637 us
  waiting for transfers between devices  521 us (82%)
  local copies, waits for them, and re-layouts  31.3 us (5%)
  matrix products  25 us (4%)
  starting transfers between devices  19.2 us (3%)
  blocking collectives  18 us (3%)
  between operations  14.1 us (2%)
  other arithmetic  8.18 us (1%)
    psum x1, waiting for transfers between devices, shards(): grad_fc2, grad_class = lax.psum((grad_fc2, grad_class), ('img', 'band'))  276 us
    reduce_scatter x1, waiting for transfers between devices, shards(): lax.psum_scatter(jnp.dot(block, w_fc1, preferred_element_type=jnp.float32...  115 us
    all_gather x1, waiting for transfers between devices, shards(): lax.all_gather(da1, 'band', axis=0, tiled=True)  69.6 us
    psum x1, waiting for transfers between devices, shards(): lax.psum(grad_fc1.astype(jnp.bfloat16), 'img').astype(jnp.float32)  28.9 us
    all_to_all x1, waiting for transfers between devices, shards(): lax.all_to_all(sending, 'band', split_axis=0, concat_axis=0, tiled=True)  28.3 us
    all_to_all x1, blocking collectives, shards(): lax.all_to_all(x_local, 'band', split_axis=1, concat_axis=0, tiled=True)  18 us
    unnamed x62, local copies, waits for them, and re-layouts  13.8 us
    all_to_all x1, starting transfers between devices, shards(): lax.all_to_all(sending, 'band', split_axis=0, concat_axis=0, tiled=True)  13.3 us
  transfers between devices with their start and end apart: 7, of which 7 were waited for; matrix products, arithmetic and copies ran while one was open for 5% of the time, Pallas kernels for 0%

commit v1 on v0

v1 whole, which is shorter than its diff:
```python
import jax
import jax.numpy as jnp
from jax import lax
from jax.sharding import PartitionSpec as P

NY, NZ, NC = 4, 8, 2
BAND = NY * NZ * NC
F32, BF16 = jnp.float32, jnp.bfloat16
CORE_SWAP = [(b, b ^ 1) for b in range(BAND)]
Z_GROUPS = [[(y * NZ + z) * NC + c for z in range(NZ)] for y in range(NY) for c in range(NC)]
Y_GROUPS = [[(y * NZ + z) * NC + c for y in range(NY)] for z in range(NZ) for c in range(NC)]


def halo(array):
    devices = lax.axis_size("band")
    up = [(i, i + 1) for i in range(devices - 1)]
    down = [(j, i) for i, j in up]
    before = lax.ppermute(array[:, -1:], "band", up)
    after = lax.ppermute(array[:, :1], "band", down)
    return jnp.concatenate([before, array, after], axis=1)


def side_pad(array):
    return jnp.pad(array, ((0, 0), (0, 0), (1, 1), (0, 0)))


def conv_rows(source, w_rpn, count):
    batch = source.shape[0]
    width = source.shape[2] - 2
    channels = source.shape[3]
    total = jnp.zeros((batch * count * width, w_rpn.shape[3]), F32)
    for dy in range(3):
        for dx in range(3):
            window = source[:, dy : dy + count, dx : dx + width, :].reshape(
                batch * count * width, channels
            )
            total = total + jnp.dot(window, w_rpn[dy, dx], preferred_element_type=F32)
    return total


def rpn(features, w_rpn, w_anchor):
    batch, rows, width, channels = features.shape
    conv = conv_rows(side_pad(halo(features)), w_rpn, rows)
    hidden = jnp.maximum(conv, 0.0).astype(BF16)
    anchors = w_anchor.shape[1]
    flat = jnp.dot(hidden, w_anchor, preferred_element_type=F32)
    return jnp.transpose(flat.reshape(batch, rows, width, anchors), (0, 3, 1, 2)).astype(BF16)


def gelu_and_slope(value):
    out, pull = jax.vjp(jax.nn.gelu, value)
    return out.astype(BF16), pull(jnp.ones_like(value))[0]


def exchange(array, groups):
    return lax.all_to_all(
        array, "band", split_axis=0, concat_axis=0, tiled=True, axis_index_groups=groups
    )


def dot(left, right, contract):
    return lax.dot_general(left, right, ((contract[:1], contract[1:]), ((), ())), preferred_element_type=F32)


def shift_img(array, step):
    size = lax.axis_size("img")
    return lax.ppermute(array, "img", [(i, (i + step) % size) for i in range(size)])


def sum_chunks(chunks, image):
    size = chunks.shape[0]
    sent = chunks.astype(BF16)
    got = [
        shift_img(lax.dynamic_index_in_dim(sent, (image + step) % size, 0, False), step)
        for step in range(1, size)
    ]
    total = lax.dynamic_index_in_dim(chunks, image, 0, False)
    for part in got:
        total = total + part.astype(F32)
    return total


def spread_chunks(chunk, image):
    size = lax.axis_size("img")
    parts = [chunk] + [shift_img(chunk, step) for step in range(1, size)]
    stacked = jnp.stack(parts)
    order = (image - jnp.arange(size, dtype=jnp.int32)) % size
    return [lax.dynamic_index_in_dim(stacked, order[k], 0, False) for k in range(size)]


def shards(
    features,
    w_rpn,
    w_anchor,
    pixel_slots,
    sample_slot,
    sample_weight,
    roi_labels,
    w_fc1,
    w_fc2,
    w_class,
):
    rows, width, channels = features.shape[1:]
    nband = lax.axis_size("band")
    band, image = lax.axis_index("band"), lax.axis_index("img")
    core = band % NC
    hid = w_fc2.shape[0]
    half = hid // NC
    labels = lax.all_gather(roi_labels[0], "band", axis=0, tiled=True)

    flat = features.reshape(rows * width, channels)
    capacity = pixel_slots.shape[3]
    wanted = pixel_slots[0, :, 0, :].reshape(nband * capacity)
    sending = flat[wanted].reshape(nband, capacity, channels)
    received = lax.all_to_all(sending, "band", split_axis=0, concat_axis=0, tiled=True)

    rpn_out = rpn(features, w_rpn, w_anchor)
    w_mine = lax.dynamic_slice_in_dim(w_fc1, core * half, half, 1)
    w_theirs = lax.dynamic_slice_in_dim(w_fc1, (1 - core) * half, half, 1)
    w_other = lax.ppermute(w_theirs, "band", CORE_SWAP)
    received, rpn_out, w_other = lax.optimization_barrier((received, rpn_out, w_other))

    received = received.reshape(nband * capacity, channels).astype(F32)
    roi_count, bins = sample_slot.shape[1:3]
    corner_slots = sample_slot[0].reshape(roi_count * bins, 4)
    corner_weights = sample_weight[0].reshape(roi_count * bins, 4)
    slot_ids = jnp.arange(nband * capacity, dtype=jnp.int32)[None, :]
    pooling = jnp.zeros((roi_count * bins, nband * capacity), F32)
    for corner in range(4):
        hits = (corner_slots[:, corner : corner + 1] == slot_ids).astype(F32)
        pooling = pooling + hits * corner_weights[:, corner : corner + 1]
    pooled = jnp.dot(pooling, received, precision=lax.Precision.HIGHEST, preferred_element_type=F32)
    pooled = pooled.astype(BF16).reshape(roi_count, bins, channels)
    x_local = jnp.transpose(pooled, (0, 2, 1)).reshape(roi_count, channels * bins)
    x_cols = lax.all_to_all(x_local, "band", split_axis=1, concat_axis=0, tiled=True)

    x_other = lax.ppermute(x_cols, "band", CORE_SWAP)
    partial = dot(x_cols, w_mine, (1, 0)) + dot(x_other, w_other, (1, 0))
    count = x_cols.shape[0]
    by_y = exchange(partial.astype(BF16).reshape(NY, count // NY, half), Y_GROUPS)
    by_y = jnp.sum(by_y.astype(F32), axis=0).astype(BF16)
    by_z = exchange(by_y.reshape(NZ, count // NY // NZ, half), Z_GROUPS)
    a1_own = jnp.sum(by_z.astype(F32), axis=0).astype(BF16)
    a1_z = exchange(jnp.broadcast_to(a1_own[None], (NZ,) + a1_own.shape), Z_GROUPS)
    a1_z = a1_z.reshape(1, count // NY, half)
    a1_mine = exchange(jnp.broadcast_to(a1_z, (NY,) + a1_z.shape[1:]), Y_GROUPS).reshape(count, half)
    a1_other = lax.ppermute(a1_mine, "band", CORE_SWAP)
    first = core == 0
    a1 = jnp.concatenate(
        [jnp.where(first, a1_mine, a1_other), jnp.where(first, a1_other, a1_mine)], axis=1
    ).astype(F32)

    h1, slope1 = gelu_and_slope(a1)
    a2 = dot(h1, w_fc2, (1, 0))
    h2, slope2 = gelu_and_slope(a2)
    logits = dot(h2, w_class, (1, 0))
    expo = jnp.exp(logits)
    prob = expo / jnp.sum(expo, axis=1, keepdims=True)
    classes = w_class.shape[1]
    onehot = (labels[:, None] == jnp.arange(classes, dtype=jnp.int32)[None, :]).astype(F32)
    dlogits = (prob - onehot).astype(BF16)
    da2 = (dot(dlogits, w_class, (1, 1)) * slope2).astype(BF16)

    nimg = lax.axis_size("img")
    wide = hid // nimg
    h1_mine = lax.dynamic_slice_in_dim(h1, core * half, half, 1)
    h2_mine = lax.dynamic_slice_in_dim(h2, core * half, half, 1)
    part_fc2 = dot(h1_mine, da2, (0, 0)).reshape(half, nimg, wide).transpose(1, 0, 2)
    part_class = jnp.pad(dot(h2_mine, dlogits, (0, 0)), ((0, 0), (0, 128 - classes)))
    part_class = part_class.reshape(nimg, NC, half // nimg // NC, 128).transpose(0, 2, 1, 3)
    part_class = part_class.reshape(nimg, half // nimg // NC, wide)
    total_head = sum_chunks(jnp.concatenate([part_fc2, part_class], axis=1), image)

    da1 = (dot(da2, w_fc2, (1, 1)) * slope1).astype(BF16)
    part_fc1 = dot(x_cols, da1, (0, 0))
    part_fc1 = part_fc1.reshape(-1, nimg, wide).transpose(1, 0, 2)
    total_fc1 = sum_chunks(part_fc1, image)

    heads = spread_chunks(total_head.astype(BF16), image)
    grad_fc1 = jnp.concatenate(spread_chunks(total_fc1.astype(BF16), image), axis=1).astype(F32)
    fc2_mine = jnp.concatenate([chunk[:half] for chunk in heads], axis=1)
    class_mine = jnp.stack([chunk[half:] for chunk in heads])
    class_mine = class_mine.reshape(nimg, half // nimg // NC, NC, 128).transpose(0, 2, 1, 3)
    class_mine = class_mine.reshape(half, 128)
    mine = jnp.concatenate([fc2_mine, class_mine], axis=1)
    other = lax.ppermute(mine, "band", CORE_SWAP)
    whole = jnp.concatenate(
        [jnp.where(first, mine, other), jnp.where(first, other, mine)], axis=0
    ).astype(F32)
    return (rpn_out, grad_fc1, whole[:, :hid], whole[:, hid : hid + classes])


def solution(mesh):
    return jax.shard_map(
        shards,
        mesh=mesh,
        in_specs=(
            P("img", "band", None, None),
            P(),
            P(),
            P("img", None, "band", None),
            P("img", "band", None, None),
            P("img", "band", None, None),
            P("img", "band"),
            P("band", None),
            P(),
            P(),
        ),
        out_specs=(P("img", None, "band", None), P("band", None), P(), P()),
        check_vma=False,
    )
```

time: 639 us -> 263 us (0.41)
  waiting for transfers between devices: 521 us -> 30.6 us
  blocking collectives: 18 us -> 54.9 us
  starting transfers between devices: 19.2 us -> 53.4 us
  local copies, waits for them, and re-layouts: 31.3 us -> 58.4 us
  matrix products: 25 us -> 36.5 us
  other arithmetic: 8.18 us -> 15.8 us
    psum x2 -> x0, waiting for transfers between devices: 305 us -> none  [the longest x1 276 us: shards(): grad_fc2, grad_class = lax.psum((grad_fc2, grad_class), ('img', 'band'))]
    reduce_scatter x1 -> x0, waiting for transfers between devices: 115 us -> none  [shards(): lax.psum_scatter(jnp.dot(block, w_fc1, preferred_element_type=jnp.float32...]
    all_gather x1 -> x0, waiting for transfers between devices: 69.6 us -> none  [shards(): lax.all_gather(da1, 'band', axis=0, tiled=True)]
    ppermute x2 -> x18, starting transfers between devices: 5.56 us -> 33.1 us  [the longest x12 16.2 us: shift_img(): lax.ppermute(array, 'img', [(i, (i + step) % size) for i in range(size)])]
    all_to_all x1 -> x4, blocking collectives: 18 us -> 42.8 us  [exchange(): lax.all_to_all(array, 'band', split_axis=0, concat_axis=0, tiled=True, ax...]
    all_to_all x1, waiting for transfers between devices: 28.3 us -> 3.52 us  [shards(): lax.all_to_all(sending, 'band', split_axis=0, concat_axis=0, tiled=True)]
    unnamed x0 -> x1, blocking collectives: none -> 12 us
    all_to_all x0 -> x1, waiting for transfers between devices: none -> 12 us  [shards(): lax.all_to_all(x_local, 'band', split_axis=1, concat_axis=0, tiled=True)]
  transfers between devices with their start and end apart: 7 -> 20, of which waited for: 7 -> 10; matrix products, arithmetic and copies ran while one was open for 5% -> 20% of each run, Pallas kernels for 0% -> 0%
where the time goes in v1:
time: 263 us; the launch traced here: 259 us
  local copies, waits for them, and re-layouts  58.4 us (22%)
  blocking collectives  54.9 us (21%)
  starting transfers between devices  53.4 us (20%)
  matrix products  36.5 us (14%)
  waiting for transfers between devices  30.6 us (12%)
  other arithmetic  15.8 us (6%)
  between operations  9.5 us (4%)
    all_to_all x4, blocking collectives, exchange(): lax.all_to_all(array, 'band', split_axis=0, concat_axis=0, tiled=True, ax...  42.8 us
    dot_general x8, matrix products, dot(): lax.dot_general(left, right, ((contract[:1], contract[1:]), ((), ())), pr...  16.7 us
    ppermute x12, starting transfers between devices, shift_img(): lax.ppermute(array, 'img', [(i, (i + step) % size) for i in range(size)])  16.2 us
    ppermute x12, waiting for transfers between devices, shift_img(): lax.ppermute(array, 'img', [(i, (i + step) % size) for i in range(size)])  14.2 us
    unnamed x66, local copies, waits for them, and re-layouts  13.8 us
    all_to_all x1, starting transfers between devices, shards(): lax.all_to_all(sending, 'band', split_axis=0, concat_axis=0, tiled=True)  13 us
    unnamed x1, blocking collectives  12 us
    all_to_all x1, waiting for transfers between devices, shards(): lax.all_to_all(x_local, 'band', split_axis=1, concat_axis=0, tiled=True)  12 us
  transfers between devices with their start and end apart: 20, of which 10 were waited for; matrix products, arithmetic and copies ran while one was open for 20% of the time, Pallas kernels for 0%

profile of v1, /device:TPU:1, one launch (start us, length us, event | category | flops | bytes accessed | tf_op | source)
XLA Modules:
  0.0 259.1 jit_solution(15194524743520544349)
XLA Ops:
  2.4 3.2 %collective-permute-start.2 = (bf16[196,512]{1,0:T(8,128)(2,1)}, bf16[196,512]{1,0:T(8,128)(2,1)}, u32[]{:S(2)}, u32[]{:S(2)}) collective-permute-start(bf16[196,512]{1,0:T(8,128)(2,1)} %constant_dynamic-slice_fusion.7), channel_id=1, source_target_pairs={{0,1},{1,0},{2,3},{3,2},{4,5},{5,4},{6,7},{7,6},{8,9},{9,8},{10,11... | collective-permute-start | bytes 602120 | tf_op jit(solution)/shard_map/ppermute | solution.py:120
  12.0 10.4 %gather_fusion = bf16[2048,256]{1,0:T(8,128)(2,1)} fusion(bf16[4096,256]{1,0:T(8,128)(2,1)} %bitcast.188, s32[2048]{0:T(1024)S(1)} %broadcast_clamp_fusion), kind=kCustom, calls=%fused_computation | custom fusion | bytes 2105344 | tf_op jit(solution)/shard_map/gather | solution.py:114
  22.4 13.0 %all-to-all-start = ((bf16[64,32,256]{2,1,0:T(8,128)(2,1)}), bf16[64,32,256]{2,1,0:T(8,128)(2,1)}, u32[]{:S(2)}, u32[]{:S(2)}) async-start(bf16[64,32,256]{2,1,0:T(8,128)(2,1)} %bitcast.2), calls=%async_computation | async-start | bytes 2097152 | tf_op jit(solution)/shard_map/all_to_all | solution.py:115
  47.9 2.7 %fusion.69 = f32[4096,256]{1,0:T(8,128)} fusion(bf16[4096,256]{1,0:T(8,128)(2,1)S(1)} %bitcast.192, bf16[3,3,256,256]{3,2,1,0:T(8,128)(2,1)S(1)} %copy-done.8), kind=kOutput, calls=%fused_computation.116 | convolution fusion | flops 536870912 | bytes 6422528 | tf_op jit(solution)/shard_map/dot_general | solution.py:37
  54.0 5.4 %convolution_convert_fusion = bf16[4096,15]{0,1:T(8,128)(2,1)S(1)} fusion(bf16[256,15]{0,1:T(8,128)(2,1)S(1)} %copy-done.20, f32[4096,256]{1,0:T(8,128)} %fusion.69, f32[4096,256]{1,0:T(8,128)} %convolution_add_fusion.1, bf16[4096,256]{1,0:T(8,128)(2,1)} %bitcast.198, bf16[3,3,256,256]{3,2,1,0:T(8,128)(2,1)S(1)} %copy-done.8), kind=kOutput, calls=%fused_computation.14 | convolution fusion | flops 572583936 | bytes 10747904 | tf_op jit(solution)/shard_map/dot_general | solution.py:46
  60.2 3.5 %all-to-all-done = bf16[64,32,256]{2,1,0:T(8,128)(2,1)} async-done(((bf16[64,32,256]{2,1,0:T(8,128)(2,1)}), bf16[64,32,256]{2,1,0:T(8,128)(2,1)}, u32[]{:S(2)}, u32[]{:S(2)}) %all-to-all-start) | async-done | bytes 1048608 | tf_op jit(solution)/shard_map/all_to_all | solution.py:115
  63.7 4.3 %fusion.47 = bf16[392,256]{1,0:T(8,128)(2,1)S(1)} fusion(bf16[2048,256]{1,0:T(8,128)(2,1)} %bitcast.29, f32[392]{0:T(512)S(1)} %bitcast.231, s32[392]{0:T(512)S(1)} %bitcast.227, f32[392]{0:T(512)S(1)} %bitcast.232, s32[392]{0:T(512)S(1)} %bitcast.228, f32[392]{0:T(512)S(1)} %bitcast.233, s32[392]{0:T(512)S(1)} %bitcast.229, f32[392]{0:T(512)S(1)} %bitcast.230, ...), kind=kOutput, calls=%fused_computation.78 | convolution fusion | flops 2475182080 | bytes 1261824 | tf_op jit(solution)/shard_map/dot_general | solution.py:132
  69.6 7.2 %all-to-all-start.1 = ((bf16[8,64,196]{2,0,1:T(8,128)(2,1)}), bf16[8,64,196]{2,0,1:T(8,128)(2,1)S(1)}, u32[]{:S(2)}, u32[]{:S(2)}) async-start(bf16[8,64,196]{2,0,1:T(8,128)(2,1)} %copy.85), calls=%async_computation.1 | async-start | bytes 524288 | tf_op jit(solution)/shard_map/all_to_all | solution.py:135
  76.8 12.0 %all-to-all-done.1 = bf16[8,64,196]{2,0,1:T(8,128)(2,1)S(1)} async-done(((bf16[8,64,196]{2,0,1:T(8,128)(2,1)}), bf16[8,64,196]{2,0,1:T(8,128)(2,1)S(1)}, u32[]{:S(2)}, u32[]{:S(2)}) %all-to-all-start.1) | async-done | bytes 200736 | tf_op jit(solution)/shard_map/all_to_all | solution.py:135
  91.7 12.1 %all_to_all.44 = bf16[4,128,512]{2,1,0:T(8,128)(2,1)S(1)} all-to-all(bf16[4,128,512]{2,1,0:T(8,128)(2,1)S(1)} %bitcast.203), channel_id=1, replica_groups={{0,16,32,48},{1,17,33,49},{2,18,34,50},{3,19,35,51},{4,20,36,52},{5,21,..., dimensions={0} | all-to-all | bytes 1048576 | tf_op jit(solution)/shard_map/all_to_all | solution.py:56
  103.9 11.1 %all_to_all.45 = bf16[8,16,512]{2,1,0:T(8,128)(2,1)S(1)} all-to-all(bf16[8,16,512]{2,1,0:T(8,128)(2,1)S(1)} %bitcast.210), channel_id=1, replica_groups={{0,2,4,6,8,10,12,14},{1,3,5,7,9,11,13,15},{16,18,20,22,24,26,28,30},{17..., dimensions={0} | all-to-all | bytes 262144 | tf_op jit(solution)/shard_map/all_to_all | solution.py:56
  115.0 10.3 %all_to_all.46 = bf16[8,16,512]{2,1,0:T(8,128)(2,1)S(1)} all-to-all(bf16[8,16,512]{2,1,0:T(8,128)(2,1)S(1)} %broadcast_in_dim.6), channel_id=1, replica_groups={{0,2,4,6,8,10,12,14},{1,3,5,7,9,11,13,15},{16,18,20,22,24,26,28,30},{17..., dimensions={0} | all-to-all | bytes 262144 | tf_op jit(solution)/shard_map/all_to_all | solution.py:56
  125.4 9.3 %all_to_all.47 = bf16[4,128,512]{2,1,0:T(8,128)(2,1)S(1)} all-to-all(bf16[4,128,512]{2,1,0:T(8,128)(2,1)S(1)} %broadcast_in_dim.8), channel_id=1, replica_groups={{0,16,32,48},{1,17,33,49},{2,18,34,50},{3,19,35,51},{4,20,36,52},{5,21,..., dimensions={0} | all-to-all | bytes 1048576 | tf_op jit(solution)/shard_map/all_to_all | solution.py:56
  134.7 4.9 %collective-permute-start.4 = (bf16[512,512]{1,0:T(8,128)(2,1)S(1)}, bf16[512,512]{1,0:T(8,128)(2,1)S(1)}, u32[]{:S(2)}, u32[]{:S(2)}) collective-permute-start(bf16[512,512]{1,0:T(8,128)(2,1)S(1)} %bitcast.202), channel_id=1, source_target_pairs={{0,1},{1,0},{2,3},{3,2},{4,5},{5,4},{6,7},{7,6},{8,9},{9,8},{10,11... | collective-permute-start | bytes 1572872 | tf_op jit(solution)/shard_map/ppermute | solution.py:147
  141.0 12.0 %all-reduce.2 = s32[512]{0:T(512)S(1)} all-reduce(s32[512]{0:T(512)S(1)} %bitcast_dynamic-update-slice_fusion), channel_id=2, replica_groups=mesh['img'=4,'band'=64] {'band'}, use_global_device_ids=true, to_apply=%add.2 | all-reduce | flops 512 | bytes 4096
  153.9 3.1 %multiply_convert_fusion = (bf16[512,1024]{1,0:T(8,128)(2,1)S(1)}, f32[512,1024]{1,0:T(8,128)}) fusion(bf16[1024,1024]{1,0:T(8,128)(2,1)S(1)} %copy-done, bf16[512,512]{1,0:T(8,128)(2,1)S(1)} %get-tuple-element.50, bf16[512,512]{1,0:T(8,128)(2,1)S(1)} %get-tuple-element.49), kind=kOutput, calls=%fused_computation.64 | convolution fusion | flops 1085276160 | bytes 6291456 | tf_op jit(solution)/shard_map/dot_general | solution.py:62
  160.7 3.3 %fusion.26 = bf16[512,1024]{1,0:T(8,128)(2,1)S(1)} fusion(f32[512,1024]{1,0:T(8,128)} %get-tuple-element.71, bf16[1024,81]{0,1:T(8,128)(2,1)} %param.19, f32[512,81]{0,1:T(8,128)} %copy-done.17, s32[512]{0:T(512)S(1)} %all-reduce.2, f32[512]{0:T(512)S(1)} %get-tuple-element.72), kind=kOutput, calls=%fused_computation.52 | convolution fusion | flops 95103488 | bytes 3481600 | tf_op jit(solution)/shard_map/dot_general | solution.py:62
  167.1 3.2 %reshape.148 = f32[512,4,256]{2,1,0:T(4,128)} reshape(f32[512,1024]{1,0:T(8,128)} %fusion.56) | data formatting | bytes 4194304 | tf_op jit(solution)/shard_map/reshape | solution.py:168
  201.1 4.8 %fusion.45 = bf16[1024,512]{0,1:T(8,128)(2,1)} fusion(bf16[512,1024]{1,0:T(8,128)(2,1)} %copy-done.9, bf16[1024,1024]{1,0:T(8,128)(2,1)S(1)} %copy-done, bf16[512,512]{1,0:T(8,128)(2,1)} %copy-done.5, bf16[512,512]{1,0:T(8,128)(2,1)} %copy-done.4), kind=kOutput, calls=%fused_computation.74 | convolution fusion | flops 1085800448 | bytes 5242880 | tf_op jit(solution)/shard_map/dot_general | solution.py:62
  208.9 3.6 %collective-permute-done.16 = bf16[576,256]{0,1:T(8,128)(2,1)S(1)} collective-permute-done((bf16[576,256]{0,1:T(8,128)(2,1)S(1)}, bf16[576,256]{0,1:T(8,128)(2,1)S(1)}, u32[]{:S(2)}, u32[]{:S(2)}) %collective-permute-start.16) | collective-permute-done | bytes 294944 | tf_op jit(solution)/shard_map/ppermute | solution.py:67
  225.6 4.0 %collective-permute-start.17 = (bf16[512,1152]{0,1:T(8,128)(2,1)}, bf16[512,1152]{0,1:T(8,128)(2,1)S(1)}, u32[]{:S(2)}, u32[]{:S(2)}) collective-permute-start(bf16[512,1152]{0,1:T(8,128)(2,1)} %constant_dynamic-update-slice_fusion), channel_id=1, source_target_pairs={{0,1},{1,0},{2,3},{3,2},{4,5},{5,4},{6,7},{7,6},{8,9},{9,8},{10,11... | collective-permute-start | bytes 3538952 | tf_op jit(solution)/shard_map/ppermute | solution.py:186
  236.9 3.0 %collective-permute-done.6 = bf16[196,256]{1,0:T(8,128)(2,1)S(1)} collective-permute-done((bf16[196,256]{1,0:T(8,128)(2,1)S(1)}, bf16[196,256]{1,0:T(8,128)(2,1)S(1)}, u32[]{:S(2)}, u32[]{:S(2)}) %collective-permute-start.6) | collective-permute-done | bytes 100384 | tf_op jit(solution)/shard_map/ppermute | solution.py:67
  244.8 3.6 %collective-permute-done.9 = bf16[196,256]{1,0:T(8,128)(2,1)S(1)} collective-permute-done((bf16[196,256]{1,0:T(8,128)(2,1)S(1)}, bf16[196,256]{1,0:T(8,128)(2,1)S(1)}, u32[]{:S(2)}, u32[]{:S(2)}) %collective-permute-start.9) | collective-permute-done | bytes 100384 | tf_op jit(solution)/shard_map/ppermute | solution.py:67
  253.5 5.3 %copy.101 = f32[1024,1024]{1,0:T(8,128)} copy(f32[1024,1024]{0,1:T(8,128)} %slice.210) | data formatting | bytes 8388608
  (164 shorter events, 94.1 us)
Async XLA Ops:
  0.6 153.3 %copy-start = (bf16[1024,1024]{1,0:T(8,128)(2,1)S(1)}, bf16[1024,1024]{1,0:T(8,128)(2,1)}, u32[]{:S(2)}) copy-start(bf16[1024,1024]{1,0:T(8,128)(2,1)} %param.18) | copy-start | bytes 6291460
  2.4 57.8 %collective-permute-start.2 = (bf16[196,512]{1,0:T(8,128)(2,1)}, bf16[196,512]{1,0:T(8,128)(2,1)}, u32[]{:S(2)}, u32[]{:S(2)}) collective-permute-start(bf16[196,512]{1,0:T(8,128)(2,1)} %constant_dynamic-slice_fusion.7), channel_id=1, source_target_pairs={{0,1},{1,0},{2,3},{3,2},{4,5},{5,4},{6,7},{7,6},{8,9},{9,8},{10,11... | collective-permute-start | bytes 602120 | tf_op jit(solution)/shard_map/ppermute | solution.py:120
  6.7 29.5 %collective-permute-start = (bf16[1,1,512,256]{3,2,1,0:T(8,128)(2,1)S(1)}, bf16[1,1,512,256]{3,2,1,0:T(8,128)(2,1)S(1)}, u32[]{:S(2)}, u32[]{:S(2)}) collective-permute-start(bf16[1,1,512,256]{3,2,1,0:T(8,128)(2,1)S(1)} %get-tuple-element.40), channel_id=1, source_target_pairs={{0,1},{1,2},{2,3},{3,4},{4,5},{5,6},{6,7},{7,8},{8,9},{9,10},{10,1... | collective-permute-start | bytes 786440 | tf_op jit(solution)/shard_map/ppermute | solution.py:18
  8.7 27.6 %collective-permute-start.1 = (bf16[1,1,512,256]{3,2,1,0:T(8,128)(2,1)S(1)}, bf16[1,1,512,256]{3,2,1,0:T(8,128)(2,1)S(1)}, u32[]{:S(2)}, u32[]{:S(2)}) collective-permute-start(bf16[1,1,512,256]{3,2,1,0:T(8,128)(2,1)S(1)} %get-tuple-element.41), channel_id=1, source_target_pairs={{1,0},{2,1},{3,2},{4,3},{5,4},{6,5},{7,6},{8,7},{9,8},{10,9},{11,1... | collective-permute-start | bytes 786440 | tf_op jit(solution)/shard_map/ppermute | solution.py:19
  22.4 41.3 %all-to-all-start = ((bf16[64,32,256]{2,1,0:T(8,128)(2,1)}), bf16[64,32,256]{2,1,0:T(8,128)(2,1)}, u32[]{:S(2)}, u32[]{:S(2)}) async-start(bf16[64,32,256]{2,1,0:T(8,128)(2,1)} %bitcast.2), calls=%async_computation | async-start | bytes 2097152 | tf_op jit(solution)/shard_map/all_to_all | solution.py:115
  68.0 21.3 %copy-start.12 = (bf16[196,1024]{1,0:T(8,128)(2,1)S(1)}, bf16[196,1024]{1,0:T(8,128)(2,1)}, u32[]{:S(2)}) copy-start(bf16[196,1024]{1,0:T(8,128)(2,1)} %param.17) | copy-start | bytes 1204228
  69.6 19.3 %all-to-all-start.1 = ((bf16[8,64,196]{2,0,1:T(8,128)(2,1)}), bf16[8,64,196]{2,0,1:T(8,128)(2,1)S(1)}, u32[]{:S(2)}, u32[]{:S(2)}) async-start(bf16[8,64,196]{2,0,1:T(8,128)(2,1)} %copy.85), calls=%async_computation.1 | async-start | bytes 524288 | tf_op jit(solution)/shard_map/all_to_all | solution.py:135
  88.8 1.6 collective-permute-start.3
  91.7 48.0 %copy-start.26 = (u32[256]{0:T(256)S(1)}, u32[256]{0:T(256)}, u32[]{:S(2)}) copy-start(u32[256]{0:T(256)} %constant.144) | copy-start | bytes 3076
  91.7 49.2 %copy-start.25 = (s32[1,8]{1,0:T(1,128)S(1)}, s32[1,8]{1,0:T(1,128)}, u32[]{:S(2)}) copy-start(s32[1,8]{1,0:T(1,128)} %param.16) | copy-start | bytes 100
  134.7 18.3 %collective-permute-start.4 = (bf16[512,512]{1,0:T(8,128)(2,1)S(1)}, bf16[512,512]{1,0:T(8,128)(2,1)S(1)}, u32[]{:S(2)}, u32[]{:S(2)}) collective-permute-start(bf16[512,512]{1,0:T(8,128)(2,1)S(1)} %bitcast.202), channel_id=1, source_target_pairs={{0,1},{1,0},{2,3},{3,2},{4,5},{5,4},{6,7},{7,6},{8,9},{9,8},{10,11... | collective-permute-start | bytes 1572872 | tf_op jit(solution)/shard_map/ppermute | solution.py:147
  177.1 18.9 %collective-permute-start.11 = (bf16[576,256]{0,1:T(8,128)(2,1)}, bf16[576,256]{0,1:T(8,128)(2,1)}, u32[]{:S(2)}, u32[]{:S(2)}) collective-permute-start(bf16[576,256]{0,1:T(8,128)(2,1)} %bitcast.213), channel_id=1, source_target_pairs={{0,64},{64,128},{128,192},{192,0},{1,65},{65,129},{129,193},{193,1... | collective-permute-start | bytes 884744 | tf_op jit(solution)/shard_map/ppermute | solution.py:67
  179.7 16.2 %collective-permute-start.12 = (bf16[576,256]{0,1:T(8,128)(2,1)}, bf16[576,256]{0,1:T(8,128)(2,1)}, u32[]{:S(2)}, u32[]{:S(2)}) collective-permute-start(bf16[576,256]{0,1:T(8,128)(2,1)} %bitcast.214), channel_id=1, source_target_pairs={{0,128},{64,192},{128,0},{192,64},{1,129},{65,193},{129,1},{193,65... | collective-permute-start | bytes 884744 | tf_op jit(solution)/shard_map/ppermute | solution.py:67
  183.6 12.4 %collective-permute-start.13 = (bf16[576,256]{0,1:T(8,128)(2,1)}, bf16[576,256]{0,1:T(8,128)(2,1)}, u32[]{:S(2)}, u32[]{:S(2)}) collective-permute-start(bf16[576,256]{0,1:T(8,128)(2,1)} %bitcast.65), channel_id=1, source_target_pairs={{0,192},{64,0},{128,64},{192,128},{1,193},{65,1},{129,65},{193,129... | collective-permute-start | bytes 884744 | tf_op jit(solution)/shard_map/ppermute | solution.py:67
  197.3 11.5 %collective-permute-start.14 = (bf16[576,256]{0,1:T(8,128)(2,1)S(1)}, bf16[576,256]{0,1:T(8,128)(2,1)S(1)}, u32[]{:S(2)}, u32[]{:S(2)}) collective-permute-start(bf16[576,256]{0,1:T(8,128)(2,1)S(1)} %fusion.52), channel_id=1, source_target_pairs={{0,64},{64,128},{128,192},{192,0},{1,65},{65,129},{129,193},{193,1... | collective-permute-start | bytes 884744 | tf_op jit(solution)/shard_map/ppermute | solution.py:67
  198.6 10.2 %collective-permute-start.15 = (bf16[576,256]{0,1:T(8,128)(2,1)S(1)}, bf16[576,256]{0,1:T(8,128)(2,1)S(1)}, u32[]{:S(2)}, u32[]{:S(2)}) collective-permute-start(bf16[576,256]{0,1:T(8,128)(2,1)S(1)} %fusion.52), channel_id=1, source_target_pairs={{0,128},{64,192},{128,0},{192,64},{1,129},{65,193},{129,1},{193,65... | collective-permute-start | bytes 884744 | tf_op jit(solution)/shard_map/ppermute | solution.py:67
  198.6 13.8 %collective-permute-start.16 = (bf16[576,256]{0,1:T(8,128)(2,1)S(1)}, bf16[576,256]{0,1:T(8,128)(2,1)S(1)}, u32[]{:S(2)}, u32[]{:S(2)}) collective-permute-start(bf16[576,256]{0,1:T(8,128)(2,1)S(1)} %fusion.52), channel_id=1, source_target_pairs={{0,192},{64,0},{128,64},{192,128},{1,193},{65,1},{129,65},{193,129... | collective-permute-start | bytes 884744 | tf_op jit(solution)/shard_map/ppermute | solution.py:67
  225.6 24.1 %collective-permute-start.17 = (bf16[512,1152]{0,1:T(8,128)(2,1)}, bf16[512,1152]{0,1:T(8,128)(2,1)S(1)}, u32[]{:S(2)}, u32[]{:S(2)}) collective-permute-start(bf16[512,1152]{0,1:T(8,128)(2,1)} %constant_dynamic-update-slice_fusion), channel_id=1, source_target_pairs={{0,1},{1,0},{2,3},{3,2},{4,5},{5,4},{6,7},{7,6},{8,9},{9,8},{10,11... | collective-permute-start | bytes 3538952 | tf_op jit(solution)/shard_map/ppermute | solution.py:186
  231.1 5.8 %collective-permute-start.5 = (bf16[196,256]{1,0:T(8,128)(2,1)S(1)}, bf16[196,256]{1,0:T(8,128)(2,1)S(1)}, u32[]{:S(2)}, u32[]{:S(2)}) collective-permute-start(bf16[196,256]{1,0:T(8,128)(2,1)S(1)} %get-tuple-element.55), channel_id=1, source_target_pairs={{0,64},{64,128},{128,192},{192,0},{1,65},{65,129},{129,193},{193,1... | collective-permute-start | bytes 301064 | tf_op jit(solution)/shard_map/ppermute | solution.py:67
  232.1 7.8 %collective-permute-start.6 = (bf16[196,256]{1,0:T(8,128)(2,1)S(1)}, bf16[196,256]{1,0:T(8,128)(2,1)S(1)}, u32[]{:S(2)}, u32[]{:S(2)}) collective-permute-start(bf16[196,256]{1,0:T(8,128)(2,1)S(1)} %get-tuple-element.57), channel_id=1, source_target_pairs={{0,128},{64,192},{128,0},{192,64},{1,129},{65,193},{129,1},{193,65... | collective-permute-start | bytes 301064 | tf_op jit(solution)/shard_map/ppermute | solution.py:67
  234.7 5.2 %collective-permute-start.7 = (bf16[196,256]{1,0:T(8,128)(2,1)S(1)}, bf16[196,256]{1,0:T(8,128)(2,1)S(1)}, u32[]{:S(2)}, u32[]{:S(2)}) collective-permute-start(bf16[196,256]{1,0:T(8,128)(2,1)S(1)} %get-tuple-element.56), channel_id=1, source_target_pairs={{0,192},{64,0},{128,64},{192,128},{1,193},{65,1},{129,65},{193,129... | collective-permute-start | bytes 301064 | tf_op jit(solution)/shard_map/ppermute | solution.py:67
  240.0 4.8 %collective-permute-start.8 = (bf16[196,256]{1,0:T(8,128)(2,1)S(1)}, bf16[196,256]{1,0:T(8,128)(2,1)S(1)}, u32[]{:S(2)}, u32[]{:S(2)}) collective-permute-start(bf16[196,256]{1,0:T(8,128)(2,1)S(1)} %fusion.66), channel_id=1, source_target_pairs={{0,64},{64,128},{128,192},{192,0},{1,65},{65,129},{129,193},{193,1... | collective-permute-start | bytes 301064 | tf_op jit(solution)/shard_map/ppermute | solution.py:67
  241.1 7.2 %collective-permute-start.9 = (bf16[196,256]{1,0:T(8,128)(2,1)S(1)}, bf16[196,256]{1,0:T(8,128)(2,1)S(1)}, u32[]{:S(2)}, u32[]{:S(2)}) collective-permute-start(bf16[196,256]{1,0:T(8,128)(2,1)S(1)} %fusion.66), channel_id=1, source_target_pairs={{0,128},{64,192},{128,0},{192,64},{1,129},{65,193},{129,1},{193,65... | collective-permute-start | bytes 301064 | tf_op jit(solution)/shard_map/ppermute | solution.py:67
  243.7 4.9 %collective-permute-start.10 = (bf16[196,256]{1,0:T(8,128)(2,1)S(1)}, bf16[196,256]{1,0:T(8,128)(2,1)S(1)}, u32[]{:S(2)}, u32[]{:S(2)}) collective-permute-start(bf16[196,256]{1,0:T(8,128)(2,1)S(1)} %fusion.66), channel_id=1, source_target_pairs={{0,192},{64,0},{128,64},{192,128},{1,193},{65,1},{129,65},{193,129... | collective-permute-start | bytes 301064 | tf_op jit(solution)/shard_map/ppermute | solution.py:67
  (23 other events, 143.7 us)

commit v2 on v1

--- a/solution.py
+++ b/solution.py
@@ -1,6 +1,10 @@
+import functools
+
 import jax
 import jax.numpy as jnp
 from jax import lax
+from jax.experimental import pallas as pl
+from jax.experimental.pallas import tpu as pltpu
 from jax.sharding import PartitionSpec as P
 
 NY, NZ, NC = 4, 8, 2
@@ -47,11 +51,6 @@
     return jnp.transpose(flat.reshape(batch, rows, width, anchors), (0, 3, 1, 2)).astype(BF16)
 
 
-def gelu_and_slope(value):
-    out, pull = jax.vjp(jax.nn.gelu, value)
-    return out.astype(BF16), pull(jnp.ones_like(value))[0]
-
-
 def exchange(array, groups):
     return lax.all_to_all(
         array, "band", split_axis=0, concat_axis=0, tiled=True, axis_index_groups=groups
@@ -67,25 +66,175 @@
     return lax.ppermute(array, "img", [(i, (i + step) % size) for i in range(size)])
 
 
-def sum_chunks(chunks, image):
-    size = chunks.shape[0]
-    sent = chunks.astype(BF16)
-    got = [
-        shift_img(lax.dynamic_index_in_dim(sent, (image + step) % size, 0, False), step)
-        for step in range(1, size)
-    ]
-    total = lax.dynamic_index_in_dim(chunks, image, 0, False)
-    for part in got:
-        total = total + part.astype(F32)
-    return total
-
-
-def spread_chunks(chunk, image):
-    size = lax.axis_size("img")
-    parts = [chunk] + [shift_img(chunk, step) for step in range(1, size)]
-    stacked = jnp.stack(parts)
-    order = (image - jnp.arange(size, dtype=jnp.int32)) % size
-    return [lax.dynamic_index_in_dim(stacked, order[k], 0, False) for k in range(size)]
+def gelu_parts(value):
+    cubic = 0.044715 * (value * value * value)
+    tanh = jnp.tanh(0.7978845608028654 * (value + cubic))
+    return tanh
+
+
+def gelu_of(value):
+    return 0.5 * value * (1.0 + gelu_parts(value))
+
+
+def slope_of(value):
+    tanh = gelu_parts(value)
+    inner = 0.7978845608028654 * (1.0 + 3.0 * 0.044715 * (value * value))
+    return 0.5 * (1.0 + tanh) + 0.5 * value * (1.0 - tanh * tanh) * inner
+
+
+ROW_BLOCK = 128
+
+
+def join_halves(core, mine_ref, other_ref, whole_ref):
+    half = mine_ref.shape[1]
+    whole_ref[:, pl.ds(pl.multiple_of(core * half, half), half)] = mine_ref[...]
+    whole_ref[:, pl.ds(pl.multiple_of((1 - core) * half, half), half)] = other_ref[...]
+
+
+def head_kernel(classes, place, mine_ref, other_ref, labels_ref, fc2_ref, class_ref,
+                da2_ref, own_ref, s1_ref, s2_ref, s3_ref, a1, h1, h2, dlog):
+    core, image = place[0], place[1]
+    join_halves(core, mine_ref, other_ref, a1)
+    count, hid = a1.shape
+    lanes = class_ref.shape[1]
+
+    def block(step, carry):
+        rows = pl.ds(pl.multiple_of(step * ROW_BLOCK, ROW_BLOCK), ROW_BLOCK)
+        hidden = gelu_of(a1[rows, :].astype(F32)).astype(BF16)
+        h1[rows, :] = hidden
+        a2 = dot(hidden, fc2_ref[...], (1, 0))
+        second = gelu_of(a2).astype(BF16)
+        h2[rows, :] = second
+        logits = dot(second, class_ref[...], (1, 0))
+        column = lax.broadcasted_iota(jnp.int32, (ROW_BLOCK, lanes), 1)
+        expo = jnp.where(column < classes, jnp.exp(logits), 0.0)
+        prob = expo / jnp.sum(expo, axis=1, keepdims=True)
+        onehot = (labels_ref[rows, :] == column).astype(F32)
+        dlogits = (prob - onehot).astype(BF16)
+        dlog[rows, :] = dlogits
+        dh2 = dot(dlogits, class_ref[...], (1, 1))
+        da2_ref[rows, :] = (dh2 * slope_of(a2)).astype(BF16)
+        return carry
+
+    lax.fori_loop(0, count // ROW_BLOCK, block, 0)
+    images = 4
+    wide = hid // NC // images
+    for step, out in enumerate((own_ref, s1_ref, s2_ref, s3_ref)):
+        chunk = lax.rem(image + step, images)
+        cols = pl.ds(pl.multiple_of(core * (hid // NC) + chunk * wide, wide), wide)
+        out[:, :hid] = dot(h1[:, cols], da2_ref[...], (0, 0)).astype(out.dtype)
+        out[:, hid:] = dot(dlog[...], h2[:, cols], (0, 0)).astype(out.dtype)
+
+
+def vmem_spec(count):
+    return [pl.BlockSpec(memory_space=pltpu.VMEM)] * count
+
+
+SMEM_SPEC = pl.BlockSpec(memory_space=pltpu.SMEM)
+
+
+def head(place, mine, other, labels, w_fc2, w_class, classes):
+    count, half = mine.shape
+    hid = w_fc2.shape[0]
+    lanes = w_class.shape[1]
+    wide = half // 4
+    struct = jax.ShapeDtypeStruct
+    return pl.pallas_call(
+        functools.partial(head_kernel, classes),
+        out_shape=[struct((count, hid), BF16), struct((wide, hid + lanes), F32)]
+        + [struct((wide, hid + lanes), BF16)] * 3,
+        in_specs=[SMEM_SPEC] + vmem_spec(5),
+        out_specs=vmem_spec(5),
+        scratch_shapes=[
+            pltpu.VMEM((count, hid), BF16),
+            pltpu.VMEM((count, hid), BF16),
+            pltpu.VMEM((count, hid), BF16),
+            pltpu.VMEM((count, lanes), BF16),
+        ],
+        compiler_params=pltpu.CompilerParams(vmem_limit_bytes=40 * 2**20),
+        name="head",
+    )(place, mine, other, labels, w_fc2, w_class)
+
+
+def first_kernel(place, mine_ref, other_ref, da2_ref, fc2_ref, x_ref,
+                 own_ref, s1_ref, s2_ref, s3_ref, a1, da1):
+    core, image = place[0], place[1]
+    join_halves(core, mine_ref, other_ref, a1)
+    count, hid = a1.shape
+
+    def block(step, carry):
+        rows = pl.ds(pl.multiple_of(step * ROW_BLOCK, ROW_BLOCK), ROW_BLOCK)
+        dh1 = dot(da2_ref[rows, :], fc2_ref[...], (1, 1))
+        da1[rows, :] = (dh1 * slope_of(a1[rows, :].astype(F32))).astype(BF16)
+        return carry
+
+    lax.fori_loop(0, count // ROW_BLOCK, block, 0)
+    images = 4
+    wide = hid // images
+    for step, out in enumerate((own_ref, s1_ref, s2_ref, s3_ref)):
+        chunk = lax.rem(image + step, images)
+        cols = pl.ds(pl.multiple_of(chunk * wide, wide), wide)
+        out[...] = dot(x_ref[...], da1[:, cols], (0, 0)).astype(out.dtype)
+
+
+def first_layer(place, mine, other, da2, w_fc2, x_cols):
+    count, hid = da2.shape
+    depth = x_cols.shape[1]
+    wide = hid // 4
+    struct = jax.ShapeDtypeStruct
+    return pl.pallas_call(
+        first_kernel,
+        out_shape=[struct((depth, wide), F32)] + [struct((depth, wide), BF16)] * 3,
+        in_specs=[SMEM_SPEC] + vmem_spec(5),
+        out_specs=vmem_spec(4),
+        scratch_shapes=[pltpu.VMEM((count, hid), BF16), pltpu.VMEM((count, hid), BF16)],
+        compiler_params=pltpu.CompilerParams(vmem_limit_bytes=40 * 2**20),
+        name="first_layer",
+    )(place, mine, other, da2, w_fc2, x_cols)
+
+
+def assemble_kernel(depth, place, *refs):
+    core, image = place[0], place[1]
+    mine, other, first = refs[:4], refs[4:8], refs[8:12]
+    fc1_ref, fc2_ref, class_ref = refs[12:]
+    hid = fc2_ref.shape[1]
+    images = 4
+    classes = class_ref.shape[0]
+    tall = mine[0].shape[0]
+    for step in range(images):
+        chunk = lax.rem(image + images - step, images)
+        for side, ref in ((core, mine[step]), (1 - core, other[step])):
+            at = pl.ds(pl.multiple_of(side * (hid // NC) + chunk * tall, tall), tall)
+            fc2_ref[at, :] = ref[:, :hid].astype(F32)
+            class_ref[:, at] = ref[:classes, hid:].astype(F32)
+        wide = hid // images
+        cols = pl.ds(pl.multiple_of(chunk * wide, wide), wide)
+        fc1_ref[:, cols] = first[step][...].astype(F32)
+
+
+def assemble(place, mine, other, first, classes):
+    hid = mine[0].shape[1] - 128
+    depth = first[0].shape[0]
+    struct = jax.ShapeDtypeStruct
+    return pl.pallas_call(
+        functools.partial(assemble_kernel, depth),
+        out_shape=[struct((depth, hid), F32), struct((hid, hid), F32), struct((classes, hid), F32)],
+        in_specs=[SMEM_SPEC] + vmem_spec(12),
+        out_specs=vmem_spec(3),
+        compiler_params=pltpu.CompilerParams(vmem_limit_bytes=40 * 2**20),
+        name="assemble",
+    )(place, *mine, *other, *first)
+
+
+def sum_img(own, sent):
+    total = own
+    for step, part in enumerate(sent, 1):
+        total = total + shift_img(part, step).astype(F32)
+    return total.astype(BF16)
+
+
+def spread_img(chunk):
+    return [chunk] + [shift_img(chunk, step) for step in range(1, lax.axis_size("img"))]
 
 
 def shards(
@@ -106,7 +255,7 @@
     core = band % NC
     hid = w_fc2.shape[0]
     half = hid // NC
-    labels = lax.all_gather(roi_labels[0], "band", axis=0, tiled=True)
+    place = jnp.stack([core, image]).astype(jnp.int32)
 
     flat = features.reshape(rows * width, channels)
     capacity = pixel_slots.shape[3]
@@ -131,8 +280,13 @@
         pooling = pooling + hits * corner_weights[:, corner : corner + 1]
     pooled = jnp.dot(pooling, received, precision=lax.Precision.HIGHEST, preferred_element_type=F32)
     pooled = pooled.astype(BF16).reshape(roi_count, bins, channels)
-    x_local = jnp.transpose(pooled, (0, 2, 1)).reshape(roi_count, channels * bins)
+    depth = w_fc1.shape[0]
+    x_local = jnp.transpose(pooled, (0, 2, 1)).reshape(roi_count, nband, depth)
+    label_column = jnp.broadcast_to(roi_labels[0].astype(BF16)[:, None, None], (roi_count, nband, 1))
+    x_local = jnp.concatenate([x_local, label_column], axis=2).reshape(roi_count, nband * (depth + 1))
     x_cols = lax.all_to_all(x_local, "band", split_axis=1, concat_axis=0, tiled=True)
+    labels = x_cols[:, depth:].astype(jnp.int32)
+    x_cols = x_cols[:, :depth]
 
     x_other = lax.ppermute(x_cols, "band", CORE_SWAP)
     partial = dot(x_cols, w_mine, (1, 0)) + dot(x_other, w_other, (1, 0))
@@ -145,49 +299,17 @@
     a1_z = a1_z.reshape(1, count // NY, half)
     a1_mine = exchange(jnp.broadcast_to(a1_z, (NY,) + a1_z.shape[1:]), Y_GROUPS).reshape(count, half)
     a1_other = lax.ppermute(a1_mine, "band", CORE_SWAP)
-    first = core == 0
-    a1 = jnp.concatenate(
-        [jnp.where(first, a1_mine, a1_other), jnp.where(first, a1_other, a1_mine)], axis=1
-    ).astype(F32)
-
-    h1, slope1 = gelu_and_slope(a1)
-    a2 = dot(h1, w_fc2, (1, 0))
-    h2, slope2 = gelu_and_slope(a2)
-    logits = dot(h2, w_class, (1, 0))
-    expo = jnp.exp(logits)
-    prob = expo / jnp.sum(expo, axis=1, keepdims=True)
     classes = w_class.shape[1]
-    onehot = (labels[:, None] == jnp.arange(classes, dtype=jnp.int32)[None, :]).astype(F32)
-    dlogits = (prob - onehot).astype(BF16)
-    da2 = (dot(dlogits, w_class, (1, 1)) * slope2).astype(BF16)
-
-    nimg = lax.axis_size("img")
-    wide = hid // nimg
-    h1_mine = lax.dynamic_slice_in_dim(h1, core * half, half, 1)
-    h2_mine = lax.dynamic_slice_in_dim(h2, core * half, half, 1)
-    part_fc2 = dot(h1_mine, da2, (0, 0)).reshape(half, nimg, wide).transpose(1, 0, 2)
-    part_class = jnp.pad(dot(h2_mine, dlogits, (0, 0)), ((0, 0), (0, 128 - classes)))
-    part_class = part_class.reshape(nimg, NC, half // nimg // NC, 128).transpose(0, 2, 1, 3)
-    part_class = part_class.reshape(nimg, half // nimg // NC, wide)
-    total_head = sum_chunks(jnp.concatenate([part_fc2, part_class], axis=1), image)
-
-    da1 = (dot(da2, w_fc2, (1, 1)) * slope1).astype(BF16)
-    part_fc1 = dot(x_cols, da1, (0, 0))
-    part_fc1 = part_fc1.reshape(-1, nimg, wide).transpose(1, 0, 2)
-    total_fc1 = sum_chunks(part_fc1, image)
-
-    heads = spread_chunks(total_head.astype(BF16), image)
-    grad_fc1 = jnp.concatenate(spread_chunks(total_fc1.astype(BF16), image), axis=1).astype(F32)
-    fc2_mine = jnp.concatenate([chunk[:half] for chunk in heads], axis=1)
-    class_mine = jnp.stack([chunk[half:] for chunk in heads])
-    class_mine = class_mine.reshape(nimg, half // nimg // NC, NC, 128).transpose(0, 2, 1, 3)
-    class_mine = class_mine.reshape(half, 128)
-    mine = jnp.concatenate([fc2_mine, class_mine], axis=1)
-    other = lax.ppermute(mine, "band", CORE_SWAP)
-    whole = jnp.concatenate(
-        [jnp.where(first, mine, other), jnp.where(first, other, mine)], axis=0
-    ).astype(F32)
-    return (rpn_out, grad_fc1, whole[:, :hid], whole[:, hid : hid + classes])
+    class_wide = jnp.pad(w_class, ((0, 0), (0, 128 - classes)))
+    da2, *parts = head(place, a1_mine, a1_other, labels, w_fc2, class_wide, classes)
+    total_head = sum_img(parts[0], parts[1:])
+    parts = first_layer(place, a1_mine, a1_other, da2, w_fc2, x_cols)
+    total_fc1 = sum_img(parts[0], parts[1:])
+    mine = spread_img(total_head)
+    other = [lax.ppermute(part, "band", CORE_SWAP) for part in mine]
+    fc1 = spread_img(total_fc1)
+    grad_fc1, grad_fc2, grad_class = assemble(place, mine, other, fc1, classes)
+    return (rpn_out, grad_fc1, grad_fc2, grad_class.T)
 
 
 def solution(mesh):

time: 263 us -> 208 us (0.79)
  local copies, waits for them, and re-layouts: 58.4 us -> 30 us
  matrix products: 36.5 us -> 20.8 us
  Pallas kernels: 0 us -> 15 us
  blocking collectives: 54.9 us -> 43.2 us
  other arithmetic: 15.8 us -> 6.52 us
  between operations: 9.5 us -> 0.99 us
  starting transfers between devices: 53.4 us -> 58.8 us
    dot_general x8 -> x2, matrix products: 16.7 us -> 1.5 us  [dot(): lax.dot_general(left, right, ((contract[:1], contract[1:]), ((), ())), pr...]
    pallas_call x0 -> x3, Pallas kernels: none -> 15 us  [the longest x1 6.22 us: head(): pl.pallas_call(functools.partial(head_kernel, classes), out_shape=[struct...]
    unnamed x1 -> x0, blocking collectives: 12 us -> none
    dynamic_slice x5 -> x0, local copies, waits for them, and re-layouts: 8.25 us -> none  [the longest x4 7.47 us: sum_chunks(): lax.dynamic_index_in_dim(sent, (image + step) % size, 0, False)]
    unnamed x66 -> x17, local copies, waits for them, and re-layouts: 13.8 us -> 6.5 us
    reshape x4 -> x1, local copies, waits for them, and re-layouts: 6.28 us -> 0.3 us  [shards(): x_local = jnp.transpose(pooled, (0, 2, 1)).reshape(roi_count, nband, depth)]
    ppermute x1 -> x4, starting transfers between devices: 3.96 us -> 8.57 us  [shards(): other = [lax.ppermute(part, 'band', CORE_SWAP) for part in mine]]
    convert_element_type x6 -> x4, other arithmetic: 5.96 us -> 1.55 us  [the longest x1 1.23 us: shards(): roi_labels[0].astype(BF16)[:, None, None]]
  transfers between devices with their start and end apart: 20 -> 23, of which waited for: 10 -> 8; matrix products, arithmetic and copies ran while one was open for 20% -> 24% of each run, Pallas kernels for 0% -> 3%
where the time goes in v2:
time: 208 us; the launch traced here: 206 us
  starting transfers between devices  58.8 us (28%)
  blocking collectives  43.2 us (21%)
  waiting for transfers between devices  31 us (15%)
  local copies, waits for them, and re-layouts  30 us (14%)
  matrix products  20.8 us (10%)
  Pallas kernels  15 us (7%)
  other arithmetic  6.52 us (3%)
    all_to_all x4, blocking collectives, exchange(): lax.all_to_all(array, 'band', split_axis=0, concat_axis=0, tiled=True, ax...  43.2 us
    ppermute x12, waiting for transfers between devices, shift_img(): lax.ppermute(array, 'img', [(i, (i + step) % size) for i in range(size)])  17.8 us
    ppermute x12, starting transfers between devices, shift_img(): lax.ppermute(array, 'img', [(i, (i + step) % size) for i in range(size)])  14.4 us
    all_to_all x1, waiting for transfers between devices, shards(): lax.all_to_all(x_local, 'band', split_axis=1, concat_axis=0, tiled=True)  12 us
    all_to_all x1, starting transfers between devices, shards(): lax.all_to_all(sending, 'band', split_axis=0, concat_axis=0, tiled=True)  11.8 us
    all_to_all x1, starting transfers between devices, shards(): lax.all_to_all(x_local, 'band', split_axis=1, concat_axis=0, tiled=True)  10.5 us
    gather x1, local copies, waits for them, and re-layouts, shards(): sending = flat[wanted].reshape(nband, capacity, channels)  10.3 us
    dot_general x8, matrix products, conv_rows(): total = total + jnp.dot(window, w_rpn[dy, dx], preferred_element_type=F32)  9.95 us
  transfers between devices with their start and end apart: 23, of which 8 were waited for; matrix products, arithmetic and copies ran while one was open for 24% of the time, Pallas kernels for 3%

profile of v2, /device:TPU:1, one launch (start us, length us, event | category | flops | bytes accessed | tf_op | source)
XLA Modules:
  0.0 206.1 jit_solution(16816609020471167277)
XLA Ops:
  2.3 3.2 %collective-permute-start.2 = (bf16[196,512]{1,0:T(8,128)(2,1)}, bf16[196,512]{1,0:T(8,128)(2,1)}, u32[]{:S(2)}, u32[]{:S(2)}) collective-permute-start(bf16[196,512]{1,0:T(8,128)(2,1)} %constant_dynamic-slice_fusion), channel_id=1, source_target_pairs={{0,1},{1,0},{2,3},{3,2},{4,5},{5,4},{6,7},{7,6},{8,9},{9,8},{10,11... | collective-permute-start | bytes 602120 | tf_op jit(solution)/shard_map/ppermute | solution.py:269
  9.3 3.1 %collective-permute-start.1 = (bf16[1,1,512,256]{3,2,1,0:T(8,128)(2,1)}, bf16[1,1,512,256]{3,2,1,0:T(8,128)(2,1)}, u32[]{:S(2)}, u32[]{:S(2)}) collective-permute-start(bf16[1,1,512,256]{3,2,1,0:T(8,128)(2,1)} %get-tuple-element.43), channel_id=1, source_target_pairs={{1,0},{2,1},{3,2},{4,3},{5,4},{6,5},{7,6},{8,7},{9,8},{10,9},{11,1... | collective-permute-start | bytes 786440 | tf_op jit(solution)/shard_map/ppermute | solution.py:23
  13.4 10.3 %gather_fusion = bf16[2048,256]{1,0:T(8,128)(2,1)} fusion(bf16[4096,256]{1,0:T(8,128)(2,1)} %bitcast.103, s32[2048]{0:T(1024)S(1)} %broadcast_clamp_fusion), kind=kCustom, calls=%fused_computation | custom fusion | bytes 2105344 | tf_op jit(solution)/shard_map/gather | solution.py:263
  23.7 11.8 %all-to-all-start = ((bf16[64,32,256]{2,1,0:T(8,128)(2,1)}), bf16[64,32,256]{2,1,0:T(8,128)(2,1)S(1)}, u32[]{:S(2)}, u32[]{:S(2)}) async-start(bf16[64,32,256]{2,1,0:T(8,128)(2,1)} %bitcast.2), calls=%async_computation | async-start | bytes 2097152 | tf_op jit(solution)/shard_map/all_to_all | solution.py:264
  50.2 2.8 %pad_maximum_fusion = (bf16[1,8,512,256]{3,2,1,0:T(8,128)(2,1)}, bf16[1,8,512,256]{3,2,1,0:T(8,128)(2,1)S(1)}) fusion(bf16[1,1,512,256]{3,2,1,0:T(8,128)(2,1)} %collective-permute-done.1, bf16[1,8,512,256]{3,2,1,0:T(8,128)(2,1)S(1)} %copy-done.2, bf16[1,1,512,256]{3,2,1,0:T(8,128)(2,1)} %collective-permute-done), kind=kLoop, calls=%fused_computation.32 | loop fusion | flops 2097152 | bytes 6815744 | tf_op jit(solution)/shard_map/concatenate | solution.py:24
  59.5 2.7 %convolution_add_fusion.1 = f32[4096,256]{1,0:T(8,128)} fusion(f32[4096,256]{1,0:T(8,128)S(1)} %convolution_add_fusion.2, bf16[4096,256]{1,0:T(8,128)(2,1)S(1)} %bitcast.107, bf16[3,3,256,256]{3,2,1,0:T(8,128)(2,1)S(1)} %copy-done.4), kind=kOutput, calls=%fused_computation.6 | convolution fusion | flops 537919488 | bytes 10616832 | tf_op jit(solution)/shard_map/dot_general | solution.py:41
  62.3 5.5 %convolution_convert_fusion = bf16[4096,15]{0,1:T(8,128)(2,1)} fusion(bf16[256,15]{0,1:T(8,128)(2,1)} %param.12, f32[4096,256]{1,0:T(8,128)} %fusion.32, f32[4096,256]{1,0:T(8,128)} %convolution_add_fusion.1, bf16[4096,256]{1,0:T(8,128)(2,1)S(1)} %bitcast.111, bf16[3,3,256,256]{3,2,1,0:T(8,128)(2,1)} %param.11), kind=kOutput, calls=%fused_computation.14 | convolution fusion | flops 572583936 | bytes 10747904 | tf_op jit(solution)/shard_map/dot_general | solution.py:50
  69.4 3.8 %fusion.27 = bf16[392,256]{1,0:T(8,128)(2,1)S(1)} fusion(bf16[2048,256]{1,0:T(8,128)(2,1)S(1)} %bitcast.114, f32[392]{0:T(512)} %bitcast.126, s32[392]{0:T(512)} %bitcast.122, f32[392]{0:T(512)} %bitcast.127, s32[392]{0:T(512)} %bitcast.123, f32[392]{0:T(512)} %bitcast.128, s32[392]{0:T(512)} %bitcast.124, f32[392]{0:T(512)} %bitcast.125, s32[392]{0:T(512)} %bitcast.121), kind=kOutput, calls=%fused_computation.45 | convolution fusion | flops 2475182080 | bytes 1261824 | tf_op jit(solution)/shard_map/dot_general | solution.py:281
  75.0 10.5 %all-to-all-start.1 = ((bf16[8,64,197]{2,0,1:T(8,128)(2,1)}), bf16[8,64,197]{2,0,1:T(8,128)(2,1)S(1)}, u32[]{:S(2)}, u32[]{:S(2)}) async-start(bf16[8,64,197]{2,0,1:T(8,128)(2,1)} %copy.31), calls=%async_computation.1 | async-start | bytes 524288 | tf_op jit(solution)/shard_map/all_to_all | solution.py:287
  85.5 12.0 %all-to-all-done.1 = bf16[8,64,197]{2,0,1:T(8,128)(2,1)S(1)} async-done(((bf16[8,64,197]{2,0,1:T(8,128)(2,1)}), bf16[8,64,197]{2,0,1:T(8,128)(2,1)S(1)}, u32[]{:S(2)}, u32[]{:S(2)}) %all-to-all-start.1) | async-done | bytes 201760 | tf_op jit(solution)/shard_map/all_to_all | solution.py:287
  100.3 12.1 %all_to_all.41 = bf16[4,128,512]{2,1,0:T(8,128)(2,1)S(1)} all-to-all(bf16[4,128,512]{2,1,0:T(8,128)(2,1)S(1)} %bitcast.113), channel_id=1, replica_groups={{0,16,32,48},{1,17,33,49},{2,18,34,50},{3,19,35,51},{4,20,36,52},{5,21,..., dimensions={0} | all-to-all | bytes 1048576 | tf_op jit(solution)/shard_map/all_to_all | solution.py:55
  112.6 11.3 %all_to_all.42 = bf16[8,16,512]{2,1,0:T(8,128)(2,1)S(1)} all-to-all(bf16[8,16,512]{2,1,0:T(8,128)(2,1)S(1)} %bitcast.118), channel_id=1, replica_groups={{0,2,4,6,8,10,12,14},{1,3,5,7,9,11,13,15},{16,18,20,22,24,26,28,30},{17..., dimensions={0} | all-to-all | bytes 262144 | tf_op jit(solution)/shard_map/all_to_all | solution.py:55
  123.9 10.4 %all_to_all.43 = bf16[8,16,512]{2,1,0:T(8,128)(2,1)S(1)} all-to-all(bf16[8,16,512]{2,1,0:T(8,128)(2,1)S(1)} %broadcast_in_dim.9), channel_id=1, replica_groups={{0,2,4,6,8,10,12,14},{1,3,5,7,9,11,13,15},{16,18,20,22,24,26,28,30},{17..., dimensions={0} | all-to-all | bytes 262144 | tf_op jit(solution)/shard_map/all_to_all | solution.py:55
  134.3 9.3 %all_to_all.44 = bf16[4,128,512]{2,1,0:T(8,128)(2,1)S(1)} all-to-all(bf16[4,128,512]{2,1,0:T(8,128)(2,1)S(1)} %broadcast_in_dim.11), channel_id=1, replica_groups={{0,16,32,48},{1,17,33,49},{2,18,34,50},{3,19,35,51},{4,20,36,52},{5,21,..., dimensions={0} | all-to-all | bytes 1048576 | tf_op jit(solution)/shard_map/all_to_all | solution.py:55
  143.7 4.7 %collective-permute-start.4 = (bf16[512,512]{1,0:T(8,128)(2,1)S(1)}, bf16[512,512]{1,0:T(8,128)(2,1)}, u32[]{:S(2)}, u32[]{:S(2)}) collective-permute-start(bf16[512,512]{1,0:T(8,128)(2,1)S(1)} %bitcast.96), channel_id=1, source_target_pairs={{0,1},{1,0},{2,3},{3,2},{4,5},{5,4},{6,7},{7,6},{8,9},{9,8},{10,11... | collective-permute-start | bytes 1572872 | tf_op jit(solution)/shard_map/ppermute | solution.py:301
  150.1 6.2 %head.1 = (bf16[512,1024]{1,0:T(8,128)(2,1)S(1)}, f32[128,1152]{1,0:T(8,128)S(1)}, bf16[128,1152]{1,0:T(8,128)(2,1)S(1)}, bf16[128,1152]{1,0:T(8,128)(2,1)S(1)}, bf16[128,1152]{1,0:T(8,128)(2,1)S(1)}) custom-call(s32[2]{0:T(128)S(1)} %pad_add_fusion.place, bf16[512,512]{1,0:T(8,128)(2,1)S(1)} %bitcast.97, bf16[512,512]{1,0:T(8,128)(2,1)} %collective-permute-done.4.other_ref, ...), custom_call_target="tpu_custom_call" | custom-call | tf_op jit(solution)/shard_map/head/pallas_call | solution.py:142
  161.2 5.5 %first_layer.1 = (f32[196,256]{1,0:T(8,128)S(1)}, bf16[196,256]{1,0:T(8,128)(2,1)S(1)}, bf16[196,256]{1,0:T(8,128)(2,1)S(1)}, bf16[196,256]{1,0:T(8,128)(2,1)S(1)}) custom-call(s32[2]{0:T(128)S(1)} %pad_add_fusion.place, bf16[512,512]{1,0:T(8,128)(2,1)S(1)} %bitcast.98, bf16[512,512]{1,0:T(8,128)(2,1)} %collective-permute-done.4.other_ref, ...), custom_call_target="tpu_custom_call" | custom-call | tf_op jit(solution)/shard_map/first_layer/pallas_call | solution.py:185
  169.6 3.6 %collective-permute-done.6 = bf16[128,1152]{1,0:T(8,128)(2,1)S(1)} collective-permute-done((bf16[128,1152]{1,0:T(8,128)(2,1)S(1)}, bf16[128,1152]{1,0:T(8,128)(2,1)S(1)}, u32[]{:S(2)}, u32[]{:S(2)}) %collective-permute-start.6) | collective-permute-done | bytes 294944 | tf_op jit(solution)/shard_map/ppermute | solution.py:66
  174.4 3.8 %collective-permute-start.9 = (bf16[128,1152]{1,0:T(8,128)(2,1)S(1)}, bf16[128,1152]{1,0:T(8,128)(2,1)S(1)}, u32[]{:S(2)}, u32[]{:S(2)}) collective-permute-start(bf16[128,1152]{1,0:T(8,128)(2,1)S(1)} %add_convert_fusion.refs_0_), channel_id=1, source_target_pairs={{0,128},{64,192},{128,0},{192,64},{1,129},{65,193},{129,1},{193,65... | collective-permute-start | bytes 884744 | tf_op jit(solution)/shard_map/ppermute | solution.py:66
  183.2 4.1 %collective-permute-start.12 = (bf16[128,1152]{1,0:T(8,128)(2,1)S(1)}, bf16[128,1152]{1,0:T(8,128)(2,1)S(1)}, u32[]{:S(2)}, u32[]{:S(2)}) collective-permute-start(bf16[128,1152]{1,0:T(8,128)(2,1)S(1)} %collective-permute-done.8.refs_1_), channel_id=1, source_target_pairs={{0,1},{1,0},{2,3},{3,2},{4,5},{5,4},{6,7},{7,6},{8,9},{9,8},{10,11... | collective-permute-start | bytes 884744 | tf_op jit(solution)/shard_map/ppermute | solution.py:309
  187.3 3.7 %collective-permute-done.9.refs_2_ = bf16[128,1152]{1,0:T(8,128)(2,1)S(1)} collective-permute-done((bf16[128,1152]{1,0:T(8,128)(2,1)S(1)}, bf16[128,1152]{1,0:T(8,128)(2,1)S(1)}, u32[]{:S(2)}, u32[]{:S(2)}) %collective-permute-start.9) | collective-permute-done | bytes 294944 | tf_op jit(solution)/shard_map/ppermute | solution.py:66
  193.8 5.5 %collective-permute-done.19.refs_10_ = bf16[196,256]{1,0:T(8,128)(2,1)S(1)} collective-permute-done((bf16[196,256]{1,0:T(8,128)(2,1)S(1)}, bf16[196,256]{1,0:T(8,128)(2,1)S(1)}, u32[]{:S(2)}, u32[]{:S(2)}) %collective-permute-start.19) | collective-permute-done | bytes 100384 | tf_op jit(solution)/shard_map/ppermute | solution.py:66
  199.4 3.4 %collective-permute-done.20.refs_11_ = bf16[196,256]{1,0:T(8,128)(2,1)S(1)} collective-permute-done((bf16[196,256]{1,0:T(8,128)(2,1)S(1)}, bf16[196,256]{1,0:T(8,128)(2,1)S(1)}, u32[]{:S(2)}, u32[]{:S(2)}) %collective-permute-start.20) | collective-permute-done | bytes 100384 | tf_op jit(solution)/shard_map/ppermute | solution.py:66
  202.8 3.3 %assemble.1 = (f32[196,1024]{1,0:T(8,128)}, f32[1024,1024]{1,0:T(8,128)}, f32[81,1024]{1,0:T(8,128)}) custom-call(s32[2]{0:T(128)S(1)} %pad_add_fusion.place, bf16[128,1152]{1,0:T(8,128)(2,1)S(1)} %add_convert_fusion.refs_0_, bf16[128,1152]{1,0:T(8,128)(2,1)S(1)} %collective-permute-done.8.refs_1_, bf16[128,1152]{1,0:T(8,128)(2,1)S(1)} %collective-permute-done.9.refs_2_, ...), custom_call_target="tpu_custom_call" | custom-call | tf_op jit(solution)/shard_map/assemble/pallas_call | solution.py:219
  (88 shorter events, 52.3 us)
Async XLA Ops:
  2.3 67.1 %collective-permute-start.2 = (bf16[196,512]{1,0:T(8,128)(2,1)}, bf16[196,512]{1,0:T(8,128)(2,1)}, u32[]{:S(2)}, u32[]{:S(2)}) collective-permute-start(bf16[196,512]{1,0:T(8,128)(2,1)} %constant_dynamic-slice_fusion), channel_id=1, source_target_pairs={{0,1},{1,0},{2,3},{3,2},{4,5},{5,4},{6,7},{7,6},{8,9},{9,8},{10,11... | collective-permute-start | bytes 602120 | tf_op jit(solution)/shard_map/ppermute | solution.py:269
  7.4 37.6 %collective-permute-start = (bf16[1,1,512,256]{3,2,1,0:T(8,128)(2,1)}, bf16[1,1,512,256]{3,2,1,0:T(8,128)(2,1)}, u32[]{:S(2)}, u32[]{:S(2)}) collective-permute-start(bf16[1,1,512,256]{3,2,1,0:T(8,128)(2,1)} %get-tuple-element.42), channel_id=1, source_target_pairs={{0,1},{1,2},{2,3},{3,4},{4,5},{5,6},{6,7},{7,8},{8,9},{9,10},{10,1... | collective-permute-start | bytes 786440 | tf_op jit(solution)/shard_map/ppermute | solution.py:22
  9.3 35.7 %collective-permute-start.1 = (bf16[1,1,512,256]{3,2,1,0:T(8,128)(2,1)}, bf16[1,1,512,256]{3,2,1,0:T(8,128)(2,1)}, u32[]{:S(2)}, u32[]{:S(2)}) collective-permute-start(bf16[1,1,512,256]{3,2,1,0:T(8,128)(2,1)} %get-tuple-element.43), channel_id=1, source_target_pairs={{1,0},{2,1},{3,2},{4,3},{5,4},{6,5},{7,6},{8,7},{9,8},{10,9},{11,1... | collective-permute-start | bytes 786440 | tf_op jit(solution)/shard_map/ppermute | solution.py:23
  23.7 45.8 %all-to-all-start = ((bf16[64,32,256]{2,1,0:T(8,128)(2,1)}), bf16[64,32,256]{2,1,0:T(8,128)(2,1)S(1)}, u32[]{:S(2)}, u32[]{:S(2)}) async-start(bf16[64,32,256]{2,1,0:T(8,128)(2,1)} %bitcast.2), calls=%async_computation | async-start | bytes 2097152 | tf_op jit(solution)/shard_map/all_to_all | solution.py:264
  75.0 22.5 %all-to-all-start.1 = ((bf16[8,64,197]{2,0,1:T(8,128)(2,1)}), bf16[8,64,197]{2,0,1:T(8,128)(2,1)S(1)}, u32[]{:S(2)}, u32[]{:S(2)}) async-start(bf16[8,64,197]{2,0,1:T(8,128)(2,1)} %copy.31), calls=%async_computation.1 | async-start | bytes 524288 | tf_op jit(solution)/shard_map/all_to_all | solution.py:287
  97.5 1.6 collective-permute-start.3
  112.6 37.5 %copy-start.1 = (bf16[1024,1024]{1,0:T(8,128)(2,1)S(1)}, bf16[1024,1024]{1,0:T(8,128)(2,1)}, u32[]{:S(2)}) copy-start(bf16[1024,1024]{1,0:T(8,128)(2,1)} %fc2_ref.3) | copy-start | bytes 6291460
  143.7 6.4 %collective-permute-start.4 = (bf16[512,512]{1,0:T(8,128)(2,1)S(1)}, bf16[512,512]{1,0:T(8,128)(2,1)}, u32[]{:S(2)}, u32[]{:S(2)}) collective-permute-start(bf16[512,512]{1,0:T(8,128)(2,1)S(1)} %bitcast.96), channel_id=1, source_target_pairs={{0,1},{1,0},{2,3},{3,2},{4,5},{5,4},{6,7},{7,6},{8,9},{9,8},{10,11... | collective-permute-start | bytes 1572872 | tf_op jit(solution)/shard_map/ppermute | solution.py:301
  156.3 11.6 %collective-permute-start.5 = (bf16[128,1152]{1,0:T(8,128)(2,1)S(1)}, bf16[128,1152]{1,0:T(8,128)(2,1)S(1)}, u32[]{:S(2)}, u32[]{:S(2)}) collective-permute-start(bf16[128,1152]{1,0:T(8,128)(2,1)S(1)} %get-tuple-element.23), channel_id=1, source_target_pairs={{0,64},{64,128},{128,192},{192,0},{1,65},{65,129},{129,193},{193,1... | collective-permute-start | bytes 884744 | tf_op jit(solution)/shard_map/ppermute | solution.py:66
  157.6 15.6 %collective-permute-start.6 = (bf16[128,1152]{1,0:T(8,128)(2,1)S(1)}, bf16[128,1152]{1,0:T(8,128)(2,1)S(1)}, u32[]{:S(2)}, u32[]{:S(2)}) collective-permute-start(bf16[128,1152]{1,0:T(8,128)(2,1)S(1)} %get-tuple-element.24), channel_id=1, source_target_pairs={{0,128},{64,192},{128,0},{192,64},{1,129},{65,193},{129,1},{193,65... | collective-permute-start | bytes 884744 | tf_op jit(solution)/shard_map/ppermute | solution.py:66
  160.1 13.1 %collective-permute-start.7 = (bf16[128,1152]{1,0:T(8,128)(2,1)S(1)}, bf16[128,1152]{1,0:T(8,128)(2,1)S(1)}, u32[]{:S(2)}, u32[]{:S(2)}) collective-permute-start(bf16[128,1152]{1,0:T(8,128)(2,1)S(1)} %get-tuple-element.25), channel_id=1, source_target_pairs={{0,192},{64,0},{128,64},{192,128},{1,193},{65,1},{129,65},{193,129... | collective-permute-start | bytes 884744 | tf_op jit(solution)/shard_map/ppermute | solution.py:66
  166.7 11.6 %collective-permute-start.15 = (bf16[196,256]{1,0:T(8,128)(2,1)S(1)}, bf16[196,256]{1,0:T(8,128)(2,1)S(1)}, u32[]{:S(2)}, u32[]{:S(2)}) collective-permute-start(bf16[196,256]{1,0:T(8,128)(2,1)S(1)} %get-tuple-element.28), channel_id=1, source_target_pairs={{0,64},{64,128},{128,192},{192,0},{1,65},{65,129},{129,193},{193,1... | collective-permute-start | bytes 301064 | tf_op jit(solution)/shard_map/ppermute | solution.py:66
  167.1 11.2 %collective-permute-start.16 = (bf16[196,256]{1,0:T(8,128)(2,1)S(1)}, bf16[196,256]{1,0:T(8,128)(2,1)S(1)}, u32[]{:S(2)}, u32[]{:S(2)}) collective-permute-start(bf16[196,256]{1,0:T(8,128)(2,1)S(1)} %get-tuple-element.29), channel_id=1, source_target_pairs={{0,128},{64,192},{128,0},{192,64},{1,129},{65,193},{129,1},{193,65... | collective-permute-start | bytes 301064 | tf_op jit(solution)/shard_map/ppermute | solution.py:66
  168.0 10.3 %collective-permute-start.17 = (bf16[196,256]{1,0:T(8,128)(2,1)S(1)}, bf16[196,256]{1,0:T(8,128)(2,1)S(1)}, u32[]{:S(2)}, u32[]{:S(2)}) collective-permute-start(bf16[196,256]{1,0:T(8,128)(2,1)S(1)} %get-tuple-element.30), channel_id=1, source_target_pairs={{0,192},{64,0},{128,64},{192,128},{1,193},{65,1},{129,65},{193,129... | collective-permute-start | bytes 301064 | tf_op jit(solution)/shard_map/ppermute | solution.py:66
  173.3 9.9 %collective-permute-start.8 = (bf16[128,1152]{1,0:T(8,128)(2,1)S(1)}, bf16[128,1152]{1,0:T(8,128)(2,1)S(1)}, u32[]{:S(2)}, u32[]{:S(2)}) collective-permute-start(bf16[128,1152]{1,0:T(8,128)(2,1)S(1)} %add_convert_fusion.refs_0_), channel_id=1, source_target_pairs={{0,64},{64,128},{128,192},{192,0},{1,65},{65,129},{129,193},{193,1... | collective-permute-start | bytes 884744 | tf_op jit(solution)/shard_map/ppermute | solution.py:66
  174.4 16.6 %collective-permute-start.9 = (bf16[128,1152]{1,0:T(8,128)(2,1)S(1)}, bf16[128,1152]{1,0:T(8,128)(2,1)S(1)}, u32[]{:S(2)}, u32[]{:S(2)}) collective-permute-start(bf16[128,1152]{1,0:T(8,128)(2,1)S(1)} %add_convert_fusion.refs_0_), channel_id=1, source_target_pairs={{0,128},{64,192},{128,0},{192,64},{1,129},{65,193},{129,1},{193,65... | collective-permute-start | bytes 884744 | tf_op jit(solution)/shard_map/ppermute | solution.py:66
  178.2 15.4 %collective-permute-start.10 = (bf16[128,1152]{1,0:T(8,128)(2,1)S(1)}, bf16[128,1152]{1,0:T(8,128)(2,1)S(1)}, u32[]{:S(2)}, u32[]{:S(2)}) collective-permute-start(bf16[128,1152]{1,0:T(8,128)(2,1)S(1)} %add_convert_fusion.refs_0_), channel_id=1, source_target_pairs={{0,192},{64,0},{128,64},{192,128},{1,193},{65,1},{129,65},{193,129... | collective-permute-start | bytes 884744 | tf_op jit(solution)/shard_map/ppermute | solution.py:66
  178.3 15.3 %collective-permute-start.18 = (bf16[196,256]{1,0:T(8,128)(2,1)S(1)}, bf16[196,256]{1,0:T(8,128)(2,1)S(1)}, u32[]{:S(2)}, u32[]{:S(2)}) collective-permute-start(bf16[196,256]{1,0:T(8,128)(2,1)S(1)} %add_convert_fusion.1.refs_8_), channel_id=1, source_target_pairs={{0,64},{64,128},{128,192},{192,0},{1,65},{65,129},{129,193},{193,1... | collective-permute-start | bytes 301064 | tf_op jit(solution)/shard_map/ppermute | solution.py:66
  179.9 23.0 %collective-permute-start.11 = (bf16[128,1152]{1,0:T(8,128)(2,1)S(1)}, bf16[128,1152]{1,0:T(8,128)(2,1)S(1)}, u32[]{:S(2)}, u32[]{:S(2)}) collective-permute-start(bf16[128,1152]{1,0:T(8,128)(2,1)S(1)} %add_convert_fusion.refs_0_), channel_id=1, source_target_pairs={{0,1},{1,0},{2,3},{3,2},{4,5},{5,4},{6,7},{7,6},{8,9},{9,8},{10,11... | collective-permute-start | bytes 884744 | tf_op jit(solution)/shard_map/ppermute | solution.py:309
  183.2 19.6 %collective-permute-start.12 = (bf16[128,1152]{1,0:T(8,128)(2,1)S(1)}, bf16[128,1152]{1,0:T(8,128)(2,1)S(1)}, u32[]{:S(2)}, u32[]{:S(2)}) collective-permute-start(bf16[128,1152]{1,0:T(8,128)(2,1)S(1)} %collective-permute-done.8.refs_1_), channel_id=1, source_target_pairs={{0,1},{1,0},{2,3},{3,2},{4,5},{5,4},{6,7},{7,6},{8,9},{9,8},{10,11... | collective-permute-start | bytes 884744 | tf_op jit(solution)/shard_map/ppermute | solution.py:309
  191.0 11.8 %collective-permute-start.13 = (bf16[128,1152]{1,0:T(8,128)(2,1)S(1)}, bf16[128,1152]{1,0:T(8,128)(2,1)S(1)}, u32[]{:S(2)}, u32[]{:S(2)}) collective-permute-start(bf16[128,1152]{1,0:T(8,128)(2,1)S(1)} %collective-permute-done.9.refs_2_), channel_id=1, source_target_pairs={{0,1},{1,0},{2,3},{3,2},{4,5},{5,4},{6,7},{7,6},{8,9},{9,8},{10,11... | collective-permute-start | bytes 884744 | tf_op jit(solution)/shard_map/ppermute | solution.py:309
  193.7 9.2 %collective-permute-start.14 = (bf16[128,1152]{1,0:T(8,128)(2,1)S(1)}, bf16[128,1152]{1,0:T(8,128)(2,1)S(1)}, u32[]{:S(2)}, u32[]{:S(2)}) collective-permute-start(bf16[128,1152]{1,0:T(8,128)(2,1)S(1)} %collective-permute-done.10.refs_3_), channel_id=1, source_target_pairs={{0,1},{1,0},{2,3},{3,2},{4,5},{5,4},{6,7},{7,6},{8,9},{9,8},{10,11... | collective-permute-start | bytes 884744 | tf_op jit(solution)/shard_map/ppermute | solution.py:309
  193.7 5.6 %collective-permute-start.19 = (bf16[196,256]{1,0:T(8,128)(2,1)S(1)}, bf16[196,256]{1,0:T(8,128)(2,1)S(1)}, u32[]{:S(2)}, u32[]{:S(2)}) collective-permute-start(bf16[196,256]{1,0:T(8,128)(2,1)S(1)} %add_convert_fusion.1.refs_8_), channel_id=1, source_target_pairs={{0,128},{64,192},{128,0},{192,64},{1,129},{65,193},{129,1},{193,65... | collective-permute-start | bytes 301064 | tf_op jit(solution)/shard_map/ppermute | solution.py:66
  199.3 3.5 %collective-permute-start.20 = (bf16[196,256]{1,0:T(8,128)(2,1)S(1)}, bf16[196,256]{1,0:T(8,128)(2,1)S(1)}, u32[]{:S(2)}, u32[]{:S(2)}) collective-permute-start(bf16[196,256]{1,0:T(8,128)(2,1)S(1)} %add_convert_fusion.1.refs_8_), channel_id=1, source_target_pairs={{0,192},{64,0},{128,64},{192,128},{1,193},{65,1},{129,65},{193,129... | collective-permute-start | bytes 301064 | tf_op jit(solution)/shard_map/ppermute | solution.py:66
  (5 other events, 32.2 us)

commit v3 on v2

--- a/solution.py
+++ b/solution.py
@@ -19,36 +19,61 @@
     devices = lax.axis_size("band")
     up = [(i, i + 1) for i in range(devices - 1)]
     down = [(j, i) for i, j in up]
-    before = lax.ppermute(array[:, -1:], "band", up)
-    after = lax.ppermute(array[:, :1], "band", down)
-    return jnp.concatenate([before, array, after], axis=1)
-
-
-def side_pad(array):
-    return jnp.pad(array, ((0, 0), (0, 0), (1, 1), (0, 0)))
-
-
-def conv_rows(source, w_rpn, count):
-    batch = source.shape[0]
-    width = source.shape[2] - 2
-    channels = source.shape[3]
-    total = jnp.zeros((batch * count * width, w_rpn.shape[3]), F32)
-    for dy in range(3):
+    before = lax.ppermute(array[0, -1:], "band", up)
+    after = lax.ppermute(array[0, :1], "band", down)
+    return before, after
+
+
+def rpn_kernel(before_ref, feat_ref, after_ref, rpn_ref, anchor_ref, out_ref, rows, held):
+    count = feat_ref.shape[0]
+    width = feat_ref.shape[1]
+    rows[0] = before_ref[0]
+    rows[pl.ds(1, count)] = feat_ref[...]
+    rows[count + 1] = after_ref[0]
+
+    def line(y, carry):
+        sides = []
         for dx in range(3):
-            window = source[:, dy : dy + count, dx : dx + width, :].reshape(
-                batch * count * width, channels
-            )
-            total = total + jnp.dot(window, w_rpn[dy, dx], preferred_element_type=F32)
-    return total
-
-
-def rpn(features, w_rpn, w_anchor):
-    batch, rows, width, channels = features.shape
-    conv = conv_rows(side_pad(halo(features)), w_rpn, rows)
-    hidden = jnp.maximum(conv, 0.0).astype(BF16)
+            total = dot(rows[y], rpn_ref[0, dx], (1, 0))
+            total = total + dot(rows[y + 1], rpn_ref[1, dx], (1, 0))
+            sides.append(total + dot(rows[y + 2], rpn_ref[2, dx], (1, 0)))
+        place = lax.broadcasted_iota(jnp.int32, sides[0].shape, 0)
+        left = jnp.where(place == 0, 0.0, pltpu.roll(sides[0], 1, 0))
+        right = jnp.where(place == width - 1, 0.0, pltpu.roll(sides[2], width - 1, 0))
+        hidden = jnp.maximum(left + sides[1] + right, 0.0).astype(BF16)
+        held[y] = dot(anchor_ref[...], hidden, (1, 1))
+        return carry
+
+    lax.fori_loop(0, count, line, 0)
+    for y in range(count):
+        for a in range(out_ref.shape[0]):
+            out_ref[a, y : y + 1, :] = held[y, a : a + 1, :].astype(BF16)
+
+
+def rpn(before, features, after, w_rpn, w_anchor):
+    rows, width, channels = features.shape[1:]
     anchors = w_anchor.shape[1]
-    flat = jnp.dot(hidden, w_anchor, preferred_element_type=F32)
-    return jnp.transpose(flat.reshape(batch, rows, width, anchors), (0, 3, 1, 2)).astype(BF16)
+    out = pl.pallas_call(
+        rpn_kernel,
+        out_shape=jax.ShapeDtypeStruct((anchors, rows, width), BF16),
+        in_specs=vmem_spec(5),
+        out_specs=pl.BlockSpec(memory_space=pltpu.VMEM),
+        scratch_shapes=[
+            pltpu.VMEM((rows + 2, width, channels), BF16),
+            pltpu.VMEM((rows, anchors, width), F32),
+        ],
+        compiler_params=pltpu.CompilerParams(vmem_limit_bytes=40 * 2**20),
+        cost_estimate=pl.CostEstimate(flops=9 * 10**9, bytes_accessed=4 * 10**6, transcendentals=0),
+        name="rpn",
+    )(before, features[0], after, w_rpn, w_anchor.T)
+    return out[None]
+
+
+def vmem_spec(count):
+    return [pl.BlockSpec(memory_space=pltpu.VMEM)] * count
+
+
+SMEM_SPEC = pl.BlockSpec(memory_space=pltpu.SMEM)
 
 
 def exchange(array, groups):
@@ -124,13 +149,6 @@
         cols = pl.ds(pl.multiple_of(core * (hid // NC) + chunk * wide, wide), wide)
         out[:, :hid] = dot(h1[:, cols], da2_ref[...], (0, 0)).astype(out.dtype)
         out[:, hid:] = dot(dlog[...], h2[:, cols], (0, 0)).astype(out.dtype)
-
-
-def vmem_spec(count):
-    return [pl.BlockSpec(memory_space=pltpu.VMEM)] * count
-
-
-SMEM_SPEC = pl.BlockSpec(memory_space=pltpu.SMEM)
 
 
 def head(place, mine, other, labels, w_fc2, w_class, classes):
@@ -193,48 +211,78 @@
     )(place, mine, other, da2, w_fc2, x_cols)
 
 
-def assemble_kernel(depth, place, *refs):
+SUM_ROWS = 192
+
+
+def sum_kernel(*refs):
+    heads, firsts, out_ref = refs[:4], refs[4:8], refs[8]
+    tall, wide = heads[0].shape
+    total = heads[0][...]
+    for ref in heads[1:]:
+        total = total + ref[...].astype(F32)
+    out_ref[:tall, :] = total.astype(BF16)
+    first = firsts[0][...]
+    for ref in firsts[1:]:
+        first = first + ref[...].astype(F32)
+    depth, cols = first.shape
+    quarter = depth // 4
+    rest = jnp.zeros((SUM_ROWS - tall, wide), BF16)
+    out_ref[tall:, :] = rest
+    for q in range(4):
+        part = first[q * quarter : (q + 1) * quarter].astype(BF16)
+        out_ref[tall : tall + quarter, q * cols : (q + 1) * cols] = part
+
+
+def sum_parts(heads, firsts):
+    wide = heads[0].shape[1]
+    return pl.pallas_call(
+        sum_kernel,
+        out_shape=jax.ShapeDtypeStruct((SUM_ROWS, wide), BF16),
+        in_specs=vmem_spec(8),
+        out_specs=pl.BlockSpec(memory_space=pltpu.VMEM),
+        compiler_params=pltpu.CompilerParams(vmem_limit_bytes=40 * 2**20),
+        name="sum_parts",
+    )(*heads, *firsts)
+
+
+def assemble_kernel(place, *refs):
     core, image = place[0], place[1]
-    mine, other, first = refs[:4], refs[4:8], refs[8:12]
-    fc1_ref, fc2_ref, class_ref = refs[12:]
+    mine, other = refs[:4], refs[4:8]
+    fc1_ref, fc2_ref, class_ref = refs[8:]
     hid = fc2_ref.shape[1]
     images = 4
     classes = class_ref.shape[0]
-    tall = mine[0].shape[0]
+    tall = other[0].shape[0]
+    depth = fc1_ref.shape[0]
+    quarter = depth // 4
+    wide = hid // images
     for step in range(images):
         chunk = lax.rem(image + images - step, images)
         for side, ref in ((core, mine[step]), (1 - core, other[step])):
             at = pl.ds(pl.multiple_of(side * (hid // NC) + chunk * tall, tall), tall)
-            fc2_ref[at, :] = ref[:, :hid].astype(F32)
+            fc2_ref[at, :] = ref[:tall, :hid].astype(F32)
             class_ref[:, at] = ref[:classes, hid:].astype(F32)
-        wide = hid // images
         cols = pl.ds(pl.multiple_of(chunk * wide, wide), wide)
-        fc1_ref[:, cols] = first[step][...].astype(F32)
-
-
-def assemble(place, mine, other, first, classes):
+        for q in range(4):
+            part = mine[step][tall : tall + quarter, q * wide : (q + 1) * wide]
+            fc1_ref[q * quarter : (q + 1) * quarter, cols] = part.astype(F32)
+
+
+def assemble(place, mine, other, depth, classes):
     hid = mine[0].shape[1] - 128
-    depth = first[0].shape[0]
     struct = jax.ShapeDtypeStruct
     return pl.pallas_call(
-        functools.partial(assemble_kernel, depth),
+        assemble_kernel,
         out_shape=[struct((depth, hid), F32), struct((hid, hid), F32), struct((classes, hid), F32)],
-        in_specs=[SMEM_SPEC] + vmem_spec(12),
+        in_specs=[SMEM_SPEC] + vmem_spec(8),
         out_specs=vmem_spec(3),
         compiler_params=pltpu.CompilerParams(vmem_limit_bytes=40 * 2**20),
         name="assemble",
-    )(place, *mine, *other, *first)
-
-
-def sum_img(own, sent):
-    total = own
-    for step, part in enumerate(sent, 1):
-        total = total + shift_img(part, step).astype(F32)
-    return total.astype(BF16)
-
-
-def spread_img(chunk):
-    return [chunk] + [shift_img(chunk, step) for step in range(1, lax.axis_size("img"))]
+    )(place, *mine, *other)
+
+
+def shift_all(sent):
+    return [shift_img(part, step) for step, part in enumerate(sent, 1)]
 
 
 def shards(
@@ -263,9 +311,11 @@
     sending = flat[wanted].reshape(nband, capacity, channels)
     received = lax.all_to_all(sending, "band", split_axis=0, concat_axis=0, tiled=True)
 
-    rpn_out = rpn(features, w_rpn, w_anchor)
-    w_mine = lax.dynamic_slice_in_dim(w_fc1, core * half, half, 1)
-    w_theirs = lax.dynamic_slice_in_dim(w_fc1, (1 - core) * half, half, 1)
+    edges, w_first = lax.optimization_barrier((features, w_fc1, sending))[:2]
+    before, after = halo(edges)
+    rpn_out = rpn(before, features, after, w_rpn, w_anchor)
+    w_mine = lax.dynamic_slice_in_dim(w_first, core * half, half, 1)
+    w_theirs = lax.dynamic_slice_in_dim(w_first, (1 - core) * half, half, 1)
     w_other = lax.ppermute(w_theirs, "band", CORE_SWAP)
     received, rpn_out, w_other = lax.optimization_barrier((received, rpn_out, w_other))
 
@@ -302,13 +352,13 @@
     classes = w_class.shape[1]
     class_wide = jnp.pad(w_class, ((0, 0), (0, 128 - classes)))
     da2, *parts = head(place, a1_mine, a1_other, labels, w_fc2, class_wide, classes)
-    total_head = sum_img(parts[0], parts[1:])
+    head_own, head_got = parts[0], shift_all(parts[1:])
     parts = first_layer(place, a1_mine, a1_other, da2, w_fc2, x_cols)
-    total_fc1 = sum_img(parts[0], parts[1:])
-    mine = spread_img(total_head)
-    other = [lax.ppermute(part, "band", CORE_SWAP) for part in mine]
-    fc1 = spread_img(total_fc1)
-    grad_fc1, grad_fc2, grad_class = assemble(place, mine, other, fc1, classes)
+    total = sum_parts([head_own] + head_got, [parts[0]] + shift_all(parts[1:]))
+    mine = [total] + [shift_img(total, step) for step in range(1, 4)]
+    tall = head_own.shape[0]
+    other = [lax.ppermute(part[:tall], "band", CORE_SWAP) for part in mine]
+    grad_fc1, grad_fc2, grad_class = assemble(place, mine, other, depth, classes)
     return (rpn_out, grad_fc1, grad_fc2, grad_class.T)
 
 

time: 208 us -> 204 us (0.981)
  waiting for transfers between devices: 31 us -> 57.5 us
  matrix products: 20.8 us -> 5.8 us
  local copies, waits for them, and re-layouts: 30 us -> 17.2 us
  Pallas kernels: 15 us -> 24.1 us
  starting transfers between devices: 58.8 us -> 52.9 us
  other arithmetic: 6.52 us -> 1.59 us
    ppermute x6, waiting for transfers between devices: 0.02 us -> 19.9 us  [the longest x1 18.7 us: halo(): after = lax.ppermute(array[0, :1], 'band', down)]
    dot_general x9 -> x0, matrix products: 15.5 us -> none  [the longest x8 9.95 us: conv_rows(): total = total + jnp.dot(window, w_rpn[dy, dx], preferred_element_type=F32)]
    pallas_call x1 -> x3, Pallas kernels: 3.29 us -> 12.4 us  [the longest x1 8.82 us: rpn(): pl.pallas_call(rpn_kernel, out_shape=jax.ShapeDtypeStruct((anchors, rows,...]
    ppermute x12 -> x9, waiting for transfers between devices: 17.8 us -> 24.4 us  [shift_img(): lax.ppermute(array, 'img', [(i, (i + step) % size) for i in range(size)])]
    ppermute x12 -> x9, starting transfers between devices: 14.4 us -> 7.97 us  [shift_img(): lax.ppermute(array, 'img', [(i, (i + step) % size) for i in range(size)])]
    concatenate x2 -> x0, other arithmetic: 4.66 us -> none  [halo(): return jnp.concatenate([before, array, after], axis=1)]
    slice x2 -> x4, local copies, waits for them, and re-layouts: 4.35 us -> 0.09 us  [shards(): other = [lax.ppermute(part[:tall], 'band', CORE_SWAP) for part in mine]]
    unnamed x17 -> x24, local copies, waits for them, and re-layouts: 6.5 us -> 3.26 us
  transfers between devices with their start and end apart: 23 -> 20, of which waited for: 8 -> 10; matrix products, arithmetic and copies ran while one was open for 24% -> 2% of each run, Pallas kernels for 3% -> 7%
where the time goes in v3:
time: 204 us; the launch traced here: 203 us
  waiting for transfers between devices  57.5 us (28%)
  starting transfers between devices  52.9 us (26%)
  blocking collectives  43.1 us (21%)
  Pallas kernels  24.1 us (12%)
  local copies, waits for them, and re-layouts  17.2 us (8%)
  matrix products  5.8 us (3%)
    all_to_all x4, blocking collectives, exchange(): lax.all_to_all(array, 'band', split_axis=0, concat_axis=0, tiled=True, ax...  43.1 us
    ppermute x9, waiting for transfers between devices, shift_img(): lax.ppermute(array, 'img', [(i, (i + step) % size) for i in range(size)])  24.4 us
    ppermute x1, waiting for transfers between devices, halo(): after = lax.ppermute(array[0, :1], 'band', down)  18.7 us
    all_to_all x1, starting transfers between devices, shards(): lax.all_to_all(sending, 'band', split_axis=0, concat_axis=0, tiled=True)  13.5 us
    all_to_all x1, waiting for transfers between devices, shards(): lax.all_to_all(x_local, 'band', split_axis=1, concat_axis=0, tiled=True)  12 us
    ppermute x4, starting transfers between devices, shards(): other = [lax.ppermute(part[:tall], 'band', CORE_SWAP) for part in mine]  10.9 us
    gather x1, local copies, waits for them, and re-layouts, shards(): sending = flat[wanted].reshape(nband, capacity, channels)  10.5 us
    all_to_all x1, starting transfers between devices, shards(): lax.all_to_all(x_local, 'band', split_axis=1, concat_axis=0, tiled=True)  9.15 us
  transfers between devices with their start and end apart: 20, of which 10 were waited for; matrix products, arithmetic and copies ran while one was open for 2% of the time, Pallas kernels for 7%

profile of v3, /device:TPU:1, one launch (start us, length us, event | category | flops | bytes accessed | tf_op | source)
XLA Modules:
  0.0 203.2 jit_solution(2954184065323002539)
XLA Ops:
  1.6 10.5 %gather_fusion = bf16[2048,256]{1,0:T(8,128)(2,1)} fusion(bf16[4096,256]{1,0:T(8,128)(2,1)} %bitcast.48, s32[2048]{0:T(1024)S(1)} %broadcast_clamp_fusion), kind=kCustom, calls=%fused_computation | custom fusion | bytes 2105344 | tf_op jit(solution)/shard_map/gather | solution.py:311
  12.1 13.5 %all-to-all-start = ((bf16[64,32,256]{2,1,0:T(8,128)(2,1)}), bf16[64,32,256]{2,1,0:T(8,128)(2,1)}, u32[]{:S(2)}, u32[]{:S(2)}) async-start(bf16[64,32,256]{2,1,0:T(8,128)(2,1)} %bitcast.58), calls=%async_computation | async-start | bytes 2097152 | tf_op jit(solution)/shard_map/all_to_all | solution.py:312
  29.0 3.6 %collective-permute-start = (bf16[1,512,256]{2,1,0:T(8,128)(2,1)S(1)}, bf16[1,512,256]{2,1,0:T(8,128)(2,1)S(1)}, u32[]{:S(2)}, u32[]{:S(2)}) collective-permute-start(bf16[1,512,256]{2,1,0:T(8,128)(2,1)S(1)} %get-tuple-element.39), channel_id=1, source_target_pairs={{0,1},{1,2},{2,3},{3,4},{4,5},{5,6},{6,7},{7,8},{8,9},{9,10},{10,1... | collective-permute-start | bytes 786440 | tf_op jit(solution)/shard_map/ppermute | solution.py:22
  34.6 18.7 %collective-permute-done.1.after_ref = bf16[1,512,256]{2,1,0:T(8,128)(2,1)S(1)} collective-permute-done((bf16[1,512,256]{2,1,0:T(8,128)(2,1)}, bf16[1,512,256]{2,1,0:T(8,128)(2,1)S(1)}, u32[]{:S(2)}, u32[]{:S(2)}) %collective-permute-start.1) | collective-permute-done | bytes 262176 | tf_op jit(solution)/shard_map/ppermute | solution.py:23
  54.6 8.8 %rpn.1 = bf16[15,8,512]{2,1,0:T(8,128)(2,1)} custom-call(bf16[1,512,256]{2,1,0:T(8,128)(2,1)S(1)} %collective-permute-done.before_ref, bf16[8,512,256]{2,1,0:T(8,128)(2,1)S(1)} %bitcast.49, bf16[1,512,256]{2,1,0:T(8,128)(2,1)S(1)} %collective-permute-done.1.after_ref, bf16[3,3,256,256]{3,2,1,0:T(8,128)(2,1)S(1)} %copy-done.3, bf16[15,256]{1,0:T(8,128)(2,1)S(1)} %bitcast.57), custom_call_target="tpu_custom_call" | custom-call | flops 8999999488 | bytes 4000000 | tf_op jit(solution)/shard_map/rpn/pallas_call | solution.py:56
  63.4 4.3 %fusion.18 = bf16[392,256]{1,0:T(8,128)(2,1)S(1)} fusion(bf16[2048,256]{1,0:T(8,128)(2,1)} %bitcast.18, f32[392]{0:T(512)S(1)} %bitcast.69, s32[392]{0:T(512)S(1)} %bitcast.65, f32[392]{0:T(512)S(1)} %bitcast.70, s32[392]{0:T(512)S(1)} %bitcast.66, f32[392]{0:T(512)S(1)} %bitcast.71, s32[392]{0:T(512)S(1)} %bitcast.67, f32[392]{0:T(512)S(1)} %bitcast.68, ...), kind=kOutput, calls=%fused_computation.24 | convolution fusion | flops 2475182080 | bytes 1261824 | tf_op jit(solution)/shard_map/dot_general | solution.py:331
  69.5 9.1 %all-to-all-start.1 = ((bf16[8,64,197]{2,0,1:T(8,128)(2,1)}), bf16[8,64,197]{2,0,1:T(8,128)(2,1)S(1)}, u32[]{:S(2)}, u32[]{:S(2)}) async-start(bf16[8,64,197]{2,0,1:T(8,128)(2,1)} %copy.31), calls=%async_computation.1 | async-start | bytes 524288 | tf_op jit(solution)/shard_map/all_to_all | solution.py:337
  78.7 12.0 %all-to-all-done.1 = bf16[8,64,197]{2,0,1:T(8,128)(2,1)S(1)} async-done(((bf16[8,64,197]{2,0,1:T(8,128)(2,1)}), bf16[8,64,197]{2,0,1:T(8,128)(2,1)S(1)}, u32[]{:S(2)}, u32[]{:S(2)}) %all-to-all-start.1) | async-done | bytes 201760 | tf_op jit(solution)/shard_map/all_to_all | solution.py:337
  93.5 12.3 %all_to_all.41 = bf16[4,128,512]{2,1,0:T(8,128)(2,1)S(1)} all-to-all(bf16[4,128,512]{2,1,0:T(8,128)(2,1)S(1)} %bitcast.59), channel_id=1, replica_groups={{0,16,32,48},{1,17,33,49},{2,18,34,50},{3,19,35,51},{4,20,36,52},{5,21,..., dimensions={0} | all-to-all | bytes 1048576 | tf_op jit(solution)/shard_map/all_to_all | solution.py:80
  105.9 11.1 %all_to_all.42 = bf16[8,16,512]{2,1,0:T(8,128)(2,1)S(1)} all-to-all(bf16[8,16,512]{2,1,0:T(8,128)(2,1)S(1)} %bitcast.62), channel_id=1, replica_groups={{0,2,4,6,8,10,12,14},{1,3,5,7,9,11,13,15},{16,18,20,22,24,26,28,30},{17..., dimensions={0} | all-to-all | bytes 262144 | tf_op jit(solution)/shard_map/all_to_all | solution.py:80
  117.1 10.4 %all_to_all.43 = bf16[8,16,512]{2,1,0:T(8,128)(2,1)S(1)} all-to-all(bf16[8,16,512]{2,1,0:T(8,128)(2,1)S(1)} %broadcast_in_dim.12), channel_id=1, replica_groups={{0,2,4,6,8,10,12,14},{1,3,5,7,9,11,13,15},{16,18,20,22,24,26,28,30},{17..., dimensions={0} | all-to-all | bytes 262144 | tf_op jit(solution)/shard_map/all_to_all | solution.py:80
  127.5 9.3 %all_to_all.44 = bf16[4,128,512]{2,1,0:T(8,128)(2,1)S(1)} all-to-all(bf16[4,128,512]{2,1,0:T(8,128)(2,1)S(1)} %broadcast_in_dim.28), channel_id=1, replica_groups={{0,16,32,48},{1,17,33,49},{2,18,34,50},{3,19,35,51},{4,20,36,52},{5,21,..., dimensions={0} | all-to-all | bytes 1048576 | tf_op jit(solution)/shard_map/all_to_all | solution.py:80
  136.9 4.7 %collective-permute-start.4 = (bf16[512,512]{1,0:T(8,128)(2,1)S(1)}, bf16[512,512]{1,0:T(8,128)(2,1)}, u32[]{:S(2)}, u32[]{:S(2)}) collective-permute-start(bf16[512,512]{1,0:T(8,128)(2,1)S(1)} %bitcast.50), channel_id=1, source_target_pairs={{0,1},{1,0},{2,3},{3,2},{4,5},{5,4},{6,7},{7,6},{8,9},{9,8},{10,11... | collective-permute-start | bytes 1572872 | tf_op jit(solution)/shard_map/ppermute | solution.py:351
  143.3 6.2 %head.1 = (bf16[512,1024]{1,0:T(8,128)(2,1)S(1)}, f32[128,1152]{1,0:T(8,128)S(1)}, bf16[128,1152]{1,0:T(8,128)(2,1)S(1)}, bf16[128,1152]{1,0:T(8,128)(2,1)S(1)}, bf16[128,1152]{1,0:T(8,128)(2,1)S(1)}) custom-call(s32[2]{0:T(128)S(1)} %pad_add_fusion.place, bf16[512,512]{1,0:T(8,128)(2,1)S(1)} %bitcast.51, bf16[512,512]{1,0:T(8,128)(2,1)} %collective-permute-done.4.other_ref, ...), custom_call_target="tpu_custom_call" | custom-call | tf_op jit(solution)/shard_map/head/pallas_call | solution.py:160
  150.8 2.5 %collective-permute-start.6 = (bf16[128,1152]{1,0:T(8,128)(2,1)S(1)}, bf16[128,1152]{1,0:T(8,128)(2,1)S(1)}, u32[]{:S(2)}, u32[]{:S(2)}) collective-permute-start(bf16[128,1152]{1,0:T(8,128)(2,1)S(1)} %get-tuple-element.28), channel_id=1, source_target_pairs={{0,128},{64,192},{128,0},{192,64},{1,129},{65,193},{129,1},{193,65... | collective-permute-start | bytes 884744 | tf_op jit(solution)/shard_map/ppermute | solution.py:91
  154.4 5.5 %first_layer.1 = (f32[196,256]{1,0:T(8,128)S(1)}, bf16[196,256]{1,0:T(8,128)(2,1)S(1)}, bf16[196,256]{1,0:T(8,128)(2,1)S(1)}, bf16[196,256]{1,0:T(8,128)(2,1)S(1)}) custom-call(s32[2]{0:T(128)S(1)} %pad_add_fusion.place, bf16[512,512]{1,0:T(8,128)(2,1)S(1)} %bitcast.52, bf16[512,512]{1,0:T(8,128)(2,1)} %collective-permute-done.4.other_ref, ...), custom_call_target="tpu_custom_call" | custom-call | tf_op jit(solution)/shard_map/first_layer/pallas_call | solution.py:203
  161.1 8.7 %collective-permute-done.8.refs_5_ = bf16[196,256]{1,0:T(8,128)(2,1)S(1)} collective-permute-done((bf16[196,256]{1,0:T(8,128)(2,1)S(1)}, bf16[196,256]{1,0:T(8,128)(2,1)S(1)}, u32[]{:S(2)}, u32[]{:S(2)}) %collective-permute-start.8) | collective-permute-done | bytes 100384 | tf_op jit(solution)/shard_map/ppermute | solution.py:91
  170.8 3.0 %collective-permute-done.10.refs_7_ = bf16[196,256]{1,0:T(8,128)(2,1)S(1)} collective-permute-done((bf16[196,256]{1,0:T(8,128)(2,1)S(1)}, bf16[196,256]{1,0:T(8,128)(2,1)S(1)}, u32[]{:S(2)}, u32[]{:S(2)}) %collective-permute-start.10) | collective-permute-done | bytes 100384 | tf_op jit(solution)/shard_map/ppermute | solution.py:91
  175.9 2.6 %collective-permute-start.14 = (bf16[128,1152]{1,0:T(8,128)(2,1)S(1)}, bf16[128,1152]{1,0:T(8,128)(2,1)S(1)}, u32[]{:S(2)}, u32[]{:S(2)}) collective-permute-start(bf16[128,1152]{1,0:T(8,128)(2,1)S(1)} %slice.76), channel_id=1, source_target_pairs={{0,1},{1,0},{2,3},{3,2},{4,5},{5,4},{6,7},{7,6},{8,9},{9,8},{10,11... | collective-permute-start | bytes 884744 | tf_op jit(solution)/shard_map/ppermute | solution.py:360
  178.5 5.9 %collective-permute-done.13.refs_3_ = bf16[192,1152]{1,0:T(8,128)(2,1)S(1)} collective-permute-done((bf16[192,1152]{1,0:T(8,128)(2,1)S(1)}, bf16[192,1152]{1,0:T(8,128)(2,1)S(1)}, u32[]{:S(2)}, u32[]{:S(2)}) %collective-permute-start.13) | collective-permute-done | bytes 442400 | tf_op jit(solution)/shard_map/ppermute | solution.py:91
  184.4 4.4 %collective-permute-start.17 = (bf16[128,1152]{1,0:T(8,128)(2,1)S(1)}, bf16[128,1152]{1,0:T(8,128)(2,1)S(1)}, u32[]{:S(2)}, u32[]{:S(2)}) collective-permute-start(bf16[128,1152]{1,0:T(8,128)(2,1)S(1)} %slice.79), channel_id=1, source_target_pairs={{0,1},{1,0},{2,3},{3,2},{4,5},{5,4},{6,7},{7,6},{8,9},{9,8},{10,11... | collective-permute-start | bytes 884744 | tf_op jit(solution)/shard_map/ppermute | solution.py:360
  188.8 3.3 %collective-permute-start.16 = (bf16[128,1152]{1,0:T(8,128)(2,1)S(1)}, bf16[128,1152]{1,0:T(8,128)(2,1)S(1)}, u32[]{:S(2)}, u32[]{:S(2)}) collective-permute-start(bf16[128,1152]{1,0:T(8,128)(2,1)S(1)} %slice.78), channel_id=1, source_target_pairs={{0,1},{1,0},{2,3},{3,2},{4,5},{5,4},{6,7},{7,6},{8,9},{9,8},{10,11... | collective-permute-start | bytes 884744 | tf_op jit(solution)/shard_map/ppermute | solution.py:360
  192.1 6.0 %collective-permute-done.11.refs_1_ = bf16[192,1152]{1,0:T(8,128)(2,1)S(1)} collective-permute-done((bf16[192,1152]{1,0:T(8,128)(2,1)S(1)}, bf16[192,1152]{1,0:T(8,128)(2,1)S(1)}, u32[]{:S(2)}, u32[]{:S(2)}) %collective-permute-start.11) | collective-permute-done | bytes 442400 | tf_op jit(solution)/shard_map/ppermute | solution.py:91
  199.9 3.3 %assemble.1 = (f32[196,1024]{1,0:T(8,128)}, f32[1024,1024]{1,0:T(8,128)}, f32[81,1024]{1,0:T(8,128)}) custom-call(s32[2]{0:T(128)S(1)} %pad_add_fusion.place, bf16[192,1152]{1,0:T(8,128)(2,1)S(1)} %sum_parts.1.refs_0_, bf16[192,1152]{1,0:T(8,128)(2,1)S(1)} %collective-permute-done.11.refs_1_, bf16[192,1152]{1,0:T(8,128)(2,1)S(1)} %collective-permute-done.12.refs_2_, ...), custom_call_target="tpu_custom_call" | custom-call | tf_op jit(solution)/shard_map/assemble/pallas_call | solution.py:274
  (80 shorter events, 22.5 us)
Async XLA Ops:
  0.6 25.0 %copy-start = (bf16[196,1024]{1,0:T(8,128)(2,1)S(1)}, bf16[196,1024]{1,0:T(8,128)(2,1)}, u32[]{:S(2)}) copy-start(bf16[196,1024]{1,0:T(8,128)(2,1)} %param.17) | copy-start | bytes 1204228
  1.6 24.7 %copy-start.1 = (bf16[1,8,512,256]{3,2,1,0:T(8,128)(2,1)S(1)}, bf16[1,8,512,256]{3,2,1,0:T(8,128)(2,1)}, u32[]{:S(2)}) copy-start(bf16[1,8,512,256]{3,2,1,0:T(8,128)(2,1)} %param.10) | copy-start | bytes 6291460
  12.1 41.2 %copy-start.4 = (bf16[256,15]{0,1:T(8,128)(2,1)S(1)}, bf16[256,15]{0,1:T(8,128)(2,1)}, u32[]{:S(2)}) copy-start(bf16[256,15]{0,1:T(8,128)(2,1)} %param.12) | copy-start | bytes 23044
  12.1 51.3 %all-to-all-start = ((bf16[64,32,256]{2,1,0:T(8,128)(2,1)}), bf16[64,32,256]{2,1,0:T(8,128)(2,1)}, u32[]{:S(2)}, u32[]{:S(2)}) async-start(bf16[64,32,256]{2,1,0:T(8,128)(2,1)} %bitcast.58), calls=%async_computation | async-start | bytes 2097152 | tf_op jit(solution)/shard_map/all_to_all | solution.py:312
  25.7 37.7 %collective-permute-start.2 = (bf16[196,512]{1,0:T(8,128)(2,1)S(1)}, bf16[196,512]{1,0:T(8,128)(2,1)}, u32[]{:S(2)}, u32[]{:S(2)}) collective-permute-start(bf16[196,512]{1,0:T(8,128)(2,1)S(1)} %constant_dynamic-slice_fusion), channel_id=1, source_target_pairs={{0,1},{1,0},{2,3},{3,2},{4,5},{5,4},{6,7},{7,6},{8,9},{9,8},{10,11... | collective-permute-start | bytes 602120 | tf_op jit(solution)/shard_map/ppermute | solution.py:319
  27.1 26.3 %collective-permute-start.1 = (bf16[1,512,256]{2,1,0:T(8,128)(2,1)}, bf16[1,512,256]{2,1,0:T(8,128)(2,1)S(1)}, u32[]{:S(2)}, u32[]{:S(2)}) collective-permute-start(bf16[1,512,256]{2,1,0:T(8,128)(2,1)} %get-tuple-element.38), channel_id=1, source_target_pairs={{1,0},{2,1},{3,2},{4,3},{5,4},{6,5},{7,6},{8,7},{9,8},{10,9},{11,1... | collective-permute-start | bytes 786440 | tf_op jit(solution)/shard_map/ppermute | solution.py:23
  29.0 24.3 %collective-permute-start = (bf16[1,512,256]{2,1,0:T(8,128)(2,1)S(1)}, bf16[1,512,256]{2,1,0:T(8,128)(2,1)S(1)}, u32[]{:S(2)}, u32[]{:S(2)}) collective-permute-start(bf16[1,512,256]{2,1,0:T(8,128)(2,1)S(1)} %get-tuple-element.39), channel_id=1, source_target_pairs={{0,1},{1,2},{2,3},{3,4},{4,5},{5,6},{6,7},{7,8},{8,9},{9,10},{10,1... | collective-permute-start | bytes 786440 | tf_op jit(solution)/shard_map/ppermute | solution.py:22
  69.5 21.2 %all-to-all-start.1 = ((bf16[8,64,197]{2,0,1:T(8,128)(2,1)}), bf16[8,64,197]{2,0,1:T(8,128)(2,1)S(1)}, u32[]{:S(2)}, u32[]{:S(2)}) async-start(bf16[8,64,197]{2,0,1:T(8,128)(2,1)} %copy.31), calls=%async_computation.1 | async-start | bytes 524288 | tf_op jit(solution)/shard_map/all_to_all | solution.py:337
  90.7 1.6 collective-permute-start.3
  93.5 49.7 %copy-start.2 = (bf16[1024,1024]{1,0:T(8,128)(2,1)S(1)}, bf16[1024,1024]{1,0:T(8,128)(2,1)}, u32[]{:S(2)}) copy-start(bf16[1024,1024]{1,0:T(8,128)(2,1)} %fc2_ref.3) | copy-start | bytes 6291460
  136.9 6.4 %collective-permute-start.4 = (bf16[512,512]{1,0:T(8,128)(2,1)S(1)}, bf16[512,512]{1,0:T(8,128)(2,1)}, u32[]{:S(2)}, u32[]{:S(2)}) collective-permute-start(bf16[512,512]{1,0:T(8,128)(2,1)S(1)} %bitcast.50), channel_id=1, source_target_pairs={{0,1},{1,0},{2,3},{3,2},{4,5},{5,4},{6,7},{7,6},{8,9},{9,8},{10,11... | collective-permute-start | bytes 1572872 | tf_op jit(solution)/shard_map/ppermute | solution.py:351
  149.5 24.2 %collective-permute-start.5 = (bf16[128,1152]{1,0:T(8,128)(2,1)S(1)}, bf16[128,1152]{1,0:T(8,128)(2,1)S(1)}, u32[]{:S(2)}, u32[]{:S(2)}) collective-permute-start(bf16[128,1152]{1,0:T(8,128)(2,1)S(1)} %get-tuple-element.27), channel_id=1, source_target_pairs={{0,64},{64,128},{128,192},{192,0},{1,65},{65,129},{129,193},{193,1... | collective-permute-start | bytes 884744 | tf_op jit(solution)/shard_map/ppermute | solution.py:91
  150.8 23.0 %collective-permute-start.6 = (bf16[128,1152]{1,0:T(8,128)(2,1)S(1)}, bf16[128,1152]{1,0:T(8,128)(2,1)S(1)}, u32[]{:S(2)}, u32[]{:S(2)}) collective-permute-start(bf16[128,1152]{1,0:T(8,128)(2,1)S(1)} %get-tuple-element.28), channel_id=1, source_target_pairs={{0,128},{64,192},{128,0},{192,64},{1,129},{65,193},{129,1},{193,65... | collective-permute-start | bytes 884744 | tf_op jit(solution)/shard_map/ppermute | solution.py:91
  153.2 20.5 %collective-permute-start.7 = (bf16[128,1152]{1,0:T(8,128)(2,1)S(1)}, bf16[128,1152]{1,0:T(8,128)(2,1)S(1)}, u32[]{:S(2)}, u32[]{:S(2)}) collective-permute-start(bf16[128,1152]{1,0:T(8,128)(2,1)S(1)} %get-tuple-element.29), channel_id=1, source_target_pairs={{0,192},{64,0},{128,64},{192,128},{1,193},{65,1},{129,65},{193,129... | collective-permute-start | bytes 884744 | tf_op jit(solution)/shard_map/ppermute | solution.py:91
  159.9 10.0 %collective-permute-start.8 = (bf16[196,256]{1,0:T(8,128)(2,1)S(1)}, bf16[196,256]{1,0:T(8,128)(2,1)S(1)}, u32[]{:S(2)}, u32[]{:S(2)}) collective-permute-start(bf16[196,256]{1,0:T(8,128)(2,1)S(1)} %get-tuple-element.32), channel_id=1, source_target_pairs={{0,64},{64,128},{128,192},{192,0},{1,65},{65,129},{129,193},{193,1... | collective-permute-start | bytes 301064 | tf_op jit(solution)/shard_map/ppermute | solution.py:91
  160.3 10.5 %collective-permute-start.9 = (bf16[196,256]{1,0:T(8,128)(2,1)S(1)}, bf16[196,256]{1,0:T(8,128)(2,1)S(1)}, u32[]{:S(2)}, u32[]{:S(2)}) collective-permute-start(bf16[196,256]{1,0:T(8,128)(2,1)S(1)} %get-tuple-element.33), channel_id=1, source_target_pairs={{0,128},{64,192},{128,0},{192,64},{1,129},{65,193},{129,1},{193,65... | collective-permute-start | bytes 301064 | tf_op jit(solution)/shard_map/ppermute | solution.py:91
  169.9 3.8 %collective-permute-start.10 = (bf16[196,256]{1,0:T(8,128)(2,1)S(1)}, bf16[196,256]{1,0:T(8,128)(2,1)S(1)}, u32[]{:S(2)}, u32[]{:S(2)}) collective-permute-start(bf16[196,256]{1,0:T(8,128)(2,1)S(1)} %get-tuple-element.34), channel_id=1, source_target_pairs={{0,192},{64,0},{128,64},{192,128},{1,193},{65,1},{129,65},{193,129... | collective-permute-start | bytes 301064 | tf_op jit(solution)/shard_map/ppermute | solution.py:91
  174.1 10.3 %collective-permute-start.13 = (bf16[192,1152]{1,0:T(8,128)(2,1)S(1)}, bf16[192,1152]{1,0:T(8,128)(2,1)S(1)}, u32[]{:S(2)}, u32[]{:S(2)}) collective-permute-start(bf16[192,1152]{1,0:T(8,128)(2,1)S(1)} %sum_parts.1.refs_0_), channel_id=1, source_target_pairs={{0,192},{64,0},{128,64},{192,128},{1,193},{65,1},{129,65},{193,129... | collective-permute-start | bytes 1327112 | tf_op jit(solution)/shard_map/ppermute | solution.py:91
  175.0 13.8 %collective-permute-start.12 = (bf16[192,1152]{1,0:T(8,128)(2,1)S(1)}, bf16[192,1152]{1,0:T(8,128)(2,1)S(1)}, u32[]{:S(2)}, u32[]{:S(2)}) collective-permute-start(bf16[192,1152]{1,0:T(8,128)(2,1)S(1)} %sum_parts.1.refs_0_), channel_id=1, source_target_pairs={{0,128},{64,192},{128,0},{192,64},{1,129},{65,193},{129,1},{193,65... | collective-permute-start | bytes 1327112 | tf_op jit(solution)/shard_map/ppermute | solution.py:91
  175.2 22.9 %collective-permute-start.11 = (bf16[192,1152]{1,0:T(8,128)(2,1)S(1)}, bf16[192,1152]{1,0:T(8,128)(2,1)S(1)}, u32[]{:S(2)}, u32[]{:S(2)}) collective-permute-start(bf16[192,1152]{1,0:T(8,128)(2,1)S(1)} %sum_parts.1.refs_0_), channel_id=1, source_target_pairs={{0,64},{64,128},{128,192},{192,0},{1,65},{65,129},{129,193},{193,1... | collective-permute-start | bytes 1327112 | tf_op jit(solution)/shard_map/ppermute | solution.py:91
  175.9 22.8 %collective-permute-start.14 = (bf16[128,1152]{1,0:T(8,128)(2,1)S(1)}, bf16[128,1152]{1,0:T(8,128)(2,1)S(1)}, u32[]{:S(2)}, u32[]{:S(2)}) collective-permute-start(bf16[128,1152]{1,0:T(8,128)(2,1)S(1)} %slice.76), channel_id=1, source_target_pairs={{0,1},{1,0},{2,3},{3,2},{4,5},{5,4},{6,7},{7,6},{8,9},{9,8},{10,11... | collective-permute-start | bytes 884744 | tf_op jit(solution)/shard_map/ppermute | solution.py:360
  184.4 14.3 %collective-permute-start.17 = (bf16[128,1152]{1,0:T(8,128)(2,1)S(1)}, bf16[128,1152]{1,0:T(8,128)(2,1)S(1)}, u32[]{:S(2)}, u32[]{:S(2)}) collective-permute-start(bf16[128,1152]{1,0:T(8,128)(2,1)S(1)} %slice.79), channel_id=1, source_target_pairs={{0,1},{1,0},{2,3},{3,2},{4,5},{5,4},{6,7},{7,6},{8,9},{9,8},{10,11... | collective-permute-start | bytes 884744 | tf_op jit(solution)/shard_map/ppermute | solution.py:360
  188.8 9.9 %collective-permute-start.16 = (bf16[128,1152]{1,0:T(8,128)(2,1)S(1)}, bf16[128,1152]{1,0:T(8,128)(2,1)S(1)}, u32[]{:S(2)}, u32[]{:S(2)}) collective-permute-start(bf16[128,1152]{1,0:T(8,128)(2,1)S(1)} %slice.78), channel_id=1, source_target_pairs={{0,1},{1,0},{2,3},{3,2},{4,5},{5,4},{6,7},{7,6},{8,9},{9,8},{10,11... | collective-permute-start | bytes 884744 | tf_op jit(solution)/shard_map/ppermute | solution.py:360
  198.1 1.8 collective-permute-start.15
  (6 other events, 66.8 us)

commit v4 on v3

--- a/solution.py
+++ b/solution.py
@@ -311,13 +311,11 @@
     sending = flat[wanted].reshape(nband, capacity, channels)
     received = lax.all_to_all(sending, "band", split_axis=0, concat_axis=0, tiled=True)
 
-    edges, w_first = lax.optimization_barrier((features, w_fc1, sending))[:2]
-    before, after = halo(edges)
-    rpn_out = rpn(before, features, after, w_rpn, w_anchor)
+    w_first = lax.optimization_barrier((w_fc1, sending))[0]
     w_mine = lax.dynamic_slice_in_dim(w_first, core * half, half, 1)
     w_theirs = lax.dynamic_slice_in_dim(w_first, (1 - core) * half, half, 1)
     w_other = lax.ppermute(w_theirs, "band", CORE_SWAP)
-    received, rpn_out, w_other = lax.optimization_barrier((received, rpn_out, w_other))
+    received, w_other = lax.optimization_barrier((received, w_other))
 
     received = received.reshape(nband * capacity, channels).astype(F32)
     roi_count, bins = sample_slot.shape[1:3]
@@ -354,8 +352,14 @@
     da2, *parts = head(place, a1_mine, a1_other, labels, w_fc2, class_wide, classes)
     head_own, head_got = parts[0], shift_all(parts[1:])
     parts = first_layer(place, a1_mine, a1_other, da2, w_fc2, x_cols)
-    total = sum_parts([head_own] + head_got, [parts[0]] + shift_all(parts[1:]))
+    head_got, parts = lax.optimization_barrier((head_got, parts))
+    first_got = shift_all(parts[1:])
+    total = sum_parts([head_own] + head_got, [parts[0]] + first_got)
+    total, inner = lax.optimization_barrier((total, features))
     mine = [total] + [shift_img(total, step) for step in range(1, 4)]
+    before, after = halo(inner)
+    rpn_out = rpn(before, inner, after, w_rpn, w_anchor)
+    mine[2], rpn_out = lax.optimization_barrier((mine[2], rpn_out))
     tall = head_own.shape[0]
     other = [lax.ppermute(part[:tall], "band", CORE_SWAP) for part in mine]
     grad_fc1, grad_fc2, grad_class = assemble(place, mine, other, depth, classes)

time: 204 us -> 197 us (0.966)
  local copies, waits for them, and re-layouts: 17.2 us -> 14.5 us
  waiting for transfers between devices: 57.5 us -> 55.1 us
  matrix products: 5.8 us -> 3.64 us
    all_to_all x1, waiting for transfers between devices: 0.01 us -> 26.9 us  [shards(): lax.all_to_all(sending, 'band', split_axis=0, concat_axis=0, tiled=True)]
    ppermute x1, waiting for transfers between devices: 18.7 us -> 0.01 us  [halo(): after = lax.ppermute(array[0, :1], 'band', down)]
    ppermute x9, waiting for transfers between devices: 24.4 us -> 12.7 us  [shift_img(): lax.ppermute(array, 'img', [(i, (i + step) % size) for i in range(size)])]
    ppermute x9, starting transfers between devices: 7.97 us -> 12.5 us  [shift_img(): lax.ppermute(array, 'img', [(i, (i + step) % size) for i in range(size)])]
    all_to_all x1, starting transfers between devices: 9.15 us -> 6.19 us  [shards(): lax.all_to_all(x_local, 'band', split_axis=1, concat_axis=0, tiled=True)]
  transfers between devices with their start and end apart: 20 -> 20, of which waited for: 10 -> 12; matrix products, arithmetic and copies ran while one was open for 2% -> 1% of each run, Pallas kernels for 7% -> 7%
where the time goes in v4:
time: 197 us
  waiting for transfers between devices  55.1 us (28%)
  starting transfers between devices  54.7 us (28%)
  blocking collectives  43 us (22%)
  Pallas kernels  24.5 us (12%)
  local copies, waits for them, and re-layouts  14.5 us (7%)
  matrix products  3.64 us (2%)
    all_to_all x4, blocking collectives, exchange(): lax.all_to_all(array, 'band', split_axis=0, concat_axis=0, tiled=True, ax...  43 us
    all_to_all x1, waiting for transfers between devices, shards(): lax.all_to_all(sending, 'band', split_axis=0, concat_axis=0, tiled=True)  26.9 us
    all_to_all x1, starting transfers between devices, shards(): lax.all_to_all(sending, 'band', split_axis=0, concat_axis=0, tiled=True)  13.2 us
    ppermute x9, waiting for transfers between devices, shift_img(): lax.ppermute(array, 'img', [(i, (i + step) % size) for i in range(size)])  12.7 us
    ppermute x9, starting transfers between devices, shift_img(): lax.ppermute(array, 'img', [(i, (i + step) % size) for i in range(size)])  12.5 us
    all_to_all x1, waiting for transfers between devices, shards(): lax.all_to_all(x_local, 'band', split_axis=1, concat_axis=0, tiled=True)  12 us
    ppermute x4, starting transfers between devices, shards(): other = [lax.ppermute(part[:tall], 'band', CORE_SWAP) for part in mine]  11.4 us
    gather x1, local copies, waits for them, and re-layouts, shards(): sending = flat[wanted].reshape(nband, capacity, channels)  10.4 us
  transfers between devices with their start and end apart: 20, of which 12 were waited for; matrix products, arithmetic and copies ran while one was open for 1% of the time, Pallas kernels for 7%

profile of v4, /device:TPU:1, one launch (start us, length us, event | category | flops | bytes accessed | tf_op | source)
XLA Modules:
  0.0 196.8 jit_solution(5573947995438095616)
XLA Ops:
  1.7 10.4 %gather_fusion = bf16[2048,256]{1,0:T(8,128)(2,1)} fusion(bf16[4096,256]{1,0:T(8,128)(2,1)} %bitcast.48, s32[2048]{0:T(1024)S(1)} %broadcast_clamp_fusion), kind=kCustom, calls=%fused_computation | custom fusion | bytes 2105344 | tf_op jit(solution)/shard_map/gather | solution.py:311
  12.0 13.2 %all-to-all-start = ((bf16[64,32,256]{2,1,0:T(8,128)(2,1)}), bf16[64,32,256]{2,1,0:T(8,128)(2,1)S(1)}, u32[]{:S(2)}, u32[]{:S(2)}) async-start(bf16[64,32,256]{2,1,0:T(8,128)(2,1)} %bitcast.12), calls=%async_computation | async-start | bytes 2097152 | tf_op jit(solution)/shard_map/all_to_all | solution.py:312
  26.9 26.9 %all-to-all-done = bf16[64,32,256]{2,1,0:T(8,128)(2,1)S(1)} async-done(((bf16[64,32,256]{2,1,0:T(8,128)(2,1)}), bf16[64,32,256]{2,1,0:T(8,128)(2,1)S(1)}, u32[]{:S(2)}, u32[]{:S(2)}) %all-to-all-start) | async-done | bytes 1048608 | tf_op jit(solution)/shard_map/all_to_all | solution.py:312
  53.7 3.1 %fusion.18 = bf16[392,256]{1,0:T(8,128)(2,1)S(1)} fusion(bf16[2048,256]{1,0:T(8,128)(2,1)S(1)} %bitcast.59, f32[392]{0:T(512)S(1)} %bitcast.69, s32[392]{0:T(512)S(1)} %bitcast.65, f32[392]{0:T(512)S(1)} %bitcast.70, s32[392]{0:T(512)S(1)} %bitcast.66, f32[392]{0:T(512)S(1)} %bitcast.71, s32[392]{0:T(512)S(1)} %bitcast.67, f32[392]{0:T(512)S(1)} %bitcast.68, ...), kind=kOutput, calls=%fused_computation.24 | convolution fusion | flops 2475182080 | bytes 1261824 | tf_op jit(solution)/shard_map/dot_general | solution.py:329
  58.6 6.2 %all-to-all-start.1 = ((bf16[8,64,197]{2,0,1:T(8,128)(2,1)}), bf16[8,64,197]{2,0,1:T(8,128)(2,1)S(1)}, u32[]{:S(2)}, u32[]{:S(2)}) async-start(bf16[8,64,197]{2,0,1:T(8,128)(2,1)} %copy.31), calls=%async_computation.1 | async-start | bytes 524288 | tf_op jit(solution)/shard_map/all_to_all | solution.py:335
  64.8 12.0 %all-to-all-done.1 = bf16[8,64,197]{2,0,1:T(8,128)(2,1)S(1)} async-done(((bf16[8,64,197]{2,0,1:T(8,128)(2,1)}), bf16[8,64,197]{2,0,1:T(8,128)(2,1)S(1)}, u32[]{:S(2)}, u32[]{:S(2)}) %all-to-all-start.1) | async-done | bytes 201760 | tf_op jit(solution)/shard_map/all_to_all | solution.py:335
  78.7 12.3 %all_to_all.41 = bf16[4,128,512]{2,1,0:T(8,128)(2,1)S(1)} all-to-all(bf16[4,128,512]{2,1,0:T(8,128)(2,1)S(1)} %bitcast.58), channel_id=1, replica_groups={{0,16,32,48},{1,17,33,49},{2,18,34,50},{3,19,35,51},{4,20,36,52},{5,21,..., dimensions={0} | all-to-all | bytes 1048576 | tf_op jit(solution)/shard_map/all_to_all | solution.py:80
  91.1 11.0 %all_to_all.42 = bf16[8,16,512]{2,1,0:T(8,128)(2,1)S(1)} all-to-all(bf16[8,16,512]{2,1,0:T(8,128)(2,1)S(1)} %bitcast.62), channel_id=1, replica_groups={{0,2,4,6,8,10,12,14},{1,3,5,7,9,11,13,15},{16,18,20,22,24,26,28,30},{17..., dimensions={0} | all-to-all | bytes 262144 | tf_op jit(solution)/shard_map/all_to_all | solution.py:80
  102.1 10.3 %all_to_all.43 = bf16[8,16,512]{2,1,0:T(8,128)(2,1)S(1)} all-to-all(bf16[8,16,512]{2,1,0:T(8,128)(2,1)S(1)} %broadcast_in_dim.11), channel_id=1, replica_groups={{0,2,4,6,8,10,12,14},{1,3,5,7,9,11,13,15},{16,18,20,22,24,26,28,30},{17..., dimensions={0} | all-to-all | bytes 262144 | tf_op jit(solution)/shard_map/all_to_all | solution.py:80
  112.5 9.3 %all_to_all.44 = bf16[4,128,512]{2,1,0:T(8,128)(2,1)S(1)} all-to-all(bf16[4,128,512]{2,1,0:T(8,128)(2,1)S(1)} %broadcast_in_dim.13), channel_id=1, replica_groups={{0,16,32,48},{1,17,33,49},{2,18,34,50},{3,19,35,51},{4,20,36,52},{5,21,..., dimensions={0} | all-to-all | bytes 1048576 | tf_op jit(solution)/shard_map/all_to_all | solution.py:80
  121.8 4.9 %collective-permute-start.2 = (bf16[512,512]{1,0:T(8,128)(2,1)S(1)}, bf16[512,512]{1,0:T(8,128)(2,1)}, u32[]{:S(2)}, u32[]{:S(2)}) collective-permute-start(bf16[512,512]{1,0:T(8,128)(2,1)S(1)} %bitcast.50), channel_id=1, source_target_pairs={{0,1},{1,0},{2,3},{3,2},{4,5},{5,4},{6,7},{7,6},{8,9},{9,8},{10,11... | collective-permute-start | bytes 1572872 | tf_op jit(solution)/shard_map/ppermute | solution.py:349
  128.4 6.3 %head.1 = (bf16[512,1024]{1,0:T(8,128)(2,1)S(1)}, f32[128,1152]{1,0:T(8,128)S(1)}, bf16[128,1152]{1,0:T(8,128)(2,1)S(1)}, bf16[128,1152]{1,0:T(8,128)(2,1)S(1)}, bf16[128,1152]{1,0:T(8,128)(2,1)S(1)}) custom-call(s32[2]{0:T(128)S(1)} %pad_add_fusion.place, bf16[512,512]{1,0:T(8,128)(2,1)S(1)} %bitcast.51, bf16[512,512]{1,0:T(8,128)(2,1)} %collective-permute-done.2.other_ref, ...), custom_call_target="tpu_custom_call" | custom-call | tf_op jit(solution)/shard_map/head/pallas_call | solution.py:160
  136.2 2.4 %collective-permute-start.4 = (bf16[128,1152]{1,0:T(8,128)(2,1)S(1)}, bf16[128,1152]{1,0:T(8,128)(2,1)S(1)}, u32[]{:S(2)}, u32[]{:S(2)}) collective-permute-start(bf16[128,1152]{1,0:T(8,128)(2,1)S(1)} %get-tuple-element.35), channel_id=1, source_target_pairs={{0,128},{64,192},{128,0},{192,64},{1,129},{65,193},{129,1},{193,65... | collective-permute-start | bytes 884744 | tf_op jit(solution)/shard_map/ppermute | solution.py:91
  139.8 5.6 %first_layer.1 = (f32[196,256]{1,0:T(8,128)S(1)}, bf16[196,256]{1,0:T(8,128)(2,1)S(1)}, bf16[196,256]{1,0:T(8,128)(2,1)S(1)}, bf16[196,256]{1,0:T(8,128)(2,1)S(1)}) custom-call(s32[2]{0:T(128)S(1)} %pad_add_fusion.place, bf16[512,512]{1,0:T(8,128)(2,1)S(1)} %bitcast.52, bf16[512,512]{1,0:T(8,128)(2,1)} %collective-permute-done.2.other_ref, ...), custom_call_target="tpu_custom_call" | custom-call | tf_op jit(solution)/shard_map/first_layer/pallas_call | solution.py:203
  145.4 6.2 %collective-permute-done.4.refs_2_ = bf16[128,1152]{1,0:T(8,128)(2,1)S(1)} collective-permute-done((bf16[128,1152]{1,0:T(8,128)(2,1)S(1)}, bf16[128,1152]{1,0:T(8,128)(2,1)S(1)}, u32[]{:S(2)}, u32[]{:S(2)}) %collective-permute-start.4) | collective-permute-done | bytes 294944 | tf_op jit(solution)/shard_map/ppermute | solution.py:91
  152.8 2.8 %collective-permute-start.7 = (bf16[196,256]{1,0:T(8,128)(2,1)S(1)}, bf16[196,256]{1,0:T(8,128)(2,1)S(1)}, u32[]{:S(2)}, u32[]{:S(2)}) collective-permute-start(bf16[196,256]{1,0:T(8,128)(2,1)S(1)} %get-tuple-element.47), channel_id=1, source_target_pairs={{0,128},{64,192},{128,0},{192,64},{1,129},{65,193},{129,1},{193,65... | collective-permute-start | bytes 301064 | tf_op jit(solution)/shard_map/ppermute | solution.py:91
  156.4 3.8 %collective-permute-done.7.refs_6_ = bf16[196,256]{1,0:T(8,128)(2,1)S(1)} collective-permute-done((bf16[196,256]{1,0:T(8,128)(2,1)S(1)}, bf16[196,256]{1,0:T(8,128)(2,1)S(1)}, u32[]{:S(2)}, u32[]{:S(2)}) %collective-permute-start.7) | collective-permute-done | bytes 100384 | tf_op jit(solution)/shard_map/ppermute | solution.py:91
  160.9 3.2 %collective-permute-start.11 = (bf16[1,512,256]{2,1,0:T(8,128)(2,1)S(1)}, bf16[1,512,256]{2,1,0:T(8,128)(2,1)S(1)}, u32[]{:S(2)}, u32[]{:S(2)}) collective-permute-start(bf16[1,512,256]{2,1,0:T(8,128)(2,1)S(1)} %get-tuple-element.56), channel_id=1, source_target_pairs={{1,0},{2,1},{3,2},{4,3},{5,4},{6,5},{7,6},{8,7},{9,8},{10,9},{11,1... | collective-permute-start | bytes 786440 | tf_op jit(solution)/shard_map/ppermute | solution.py:23
  164.1 2.3 %collective-permute-start.10 = (bf16[1,512,256]{2,1,0:T(8,128)(2,1)S(1)}, bf16[1,512,256]{2,1,0:T(8,128)(2,1)S(1)}, u32[]{:S(2)}, u32[]{:S(2)}) collective-permute-start(bf16[1,512,256]{2,1,0:T(8,128)(2,1)S(1)} %get-tuple-element.57), channel_id=1, source_target_pairs={{0,1},{1,2},{2,3},{3,4},{4,5},{5,6},{6,7},{7,8},{8,9},{9,10},{10,1... | collective-permute-start | bytes 786440 | tf_op jit(solution)/shard_map/ppermute | solution.py:22
  166.5 2.0 collective-permute-start.13
  170.6 8.9 %rpn.1 = bf16[15,8,512]{2,1,0:T(8,128)(2,1)} custom-call(bf16[1,512,256]{2,1,0:T(8,128)(2,1)S(1)} %collective-permute-done.10.before_ref, bf16[8,512,256]{2,1,0:T(8,128)(2,1)S(1)} %bitcast.49, bf16[1,512,256]{2,1,0:T(8,128)(2,1)S(1)} %collective-permute-done.11.after_ref, bf16[3,3,256,256]{3,2,1,0:T(8,128)(2,1)S(1)} %copy-done.3, bf16[15,256]{1,0:T(8,128)(2,1)S(1)} %bitcast.57), custom_call_target="tpu_custom_call" | custom-call | flops 8999999488 | bytes 4000000 | tf_op jit(solution)/shard_map/rpn/pallas_call | solution.py:56
  179.6 8.9 %collective-permute-start.17 = (bf16[128,1152]{1,0:T(8,128)(2,1)S(1)}, bf16[128,1152]{1,0:T(8,128)(2,1)S(1)}, u32[]{:S(2)}, u32[]{:S(2)}) collective-permute-start(bf16[128,1152]{1,0:T(8,128)(2,1)S(1)} %slice.77), channel_id=1, source_target_pairs={{0,1},{1,0},{2,3},{3,2},{4,5},{5,4},{6,7},{7,6},{8,9},{9,8},{10,11... | collective-permute-start | bytes 884744 | tf_op jit(solution)/shard_map/ppermute | solution.py:364
  188.4 1.8 collective-permute-done.12.refs_1_
  193.5 3.3 %assemble.1 = (f32[196,1024]{1,0:T(8,128)}, f32[1024,1024]{1,0:T(8,128)}, f32[81,1024]{1,0:T(8,128)}) custom-call(s32[2]{0:T(128)S(1)} %pad_add_fusion.place, bf16[192,1152]{1,0:T(8,128)(2,1)S(1)} %sum_parts.1.refs_0_, bf16[192,1152]{1,0:T(8,128)(2,1)S(1)} %collective-permute-done.12.refs_1_, bf16[192,1152]{1,0:T(8,128)(2,1)S(1)} %collective-permute-done.9.refs_2_, ...), custom_call_target="tpu_custom_call" | custom-call | tf_op jit(solution)/shard_map/assemble/pallas_call | solution.py:274
  (76 shorter events, 18.6 us)
Async XLA Ops:
  0.6 24.6 %copy-start = (bf16[196,1024]{1,0:T(8,128)(2,1)S(1)}, bf16[196,1024]{1,0:T(8,128)(2,1)}, u32[]{:S(2)}) copy-start(bf16[196,1024]{1,0:T(8,128)(2,1)} %param.17) | copy-start | bytes 1204228
  12.0 41.7 %all-to-all-start = ((bf16[64,32,256]{2,1,0:T(8,128)(2,1)}), bf16[64,32,256]{2,1,0:T(8,128)(2,1)S(1)}, u32[]{:S(2)}, u32[]{:S(2)}) async-start(bf16[64,32,256]{2,1,0:T(8,128)(2,1)} %bitcast.12), calls=%async_computation | async-start | bytes 2097152 | tf_op jit(solution)/shard_map/all_to_all | solution.py:312
  25.2 1.6 collective-permute-start
  58.6 18.2 %all-to-all-start.1 = ((bf16[8,64,197]{2,0,1:T(8,128)(2,1)}), bf16[8,64,197]{2,0,1:T(8,128)(2,1)S(1)}, u32[]{:S(2)}, u32[]{:S(2)}) async-start(bf16[8,64,197]{2,0,1:T(8,128)(2,1)} %copy.31), calls=%async_computation.1 | async-start | bytes 524288 | tf_op jit(solution)/shard_map/all_to_all | solution.py:335
  76.8 1.6 collective-permute-start.1
  78.7 49.7 %copy-start.2 = (bf16[1024,1024]{1,0:T(8,128)(2,1)S(1)}, bf16[1024,1024]{1,0:T(8,128)(2,1)}, u32[]{:S(2)}) copy-start(bf16[1024,1024]{1,0:T(8,128)(2,1)} %fc2_ref.3) | copy-start | bytes 6291460
  121.8 6.6 %collective-permute-start.2 = (bf16[512,512]{1,0:T(8,128)(2,1)S(1)}, bf16[512,512]{1,0:T(8,128)(2,1)}, u32[]{:S(2)}, u32[]{:S(2)}) collective-permute-start(bf16[512,512]{1,0:T(8,128)(2,1)S(1)} %bitcast.50), channel_id=1, source_target_pairs={{0,1},{1,0},{2,3},{3,2},{4,5},{5,4},{6,7},{7,6},{8,9},{9,8},{10,11... | collective-permute-start | bytes 1572872 | tf_op jit(solution)/shard_map/ppermute | solution.py:349
  134.7 10.7 %collective-permute-start.3 = (bf16[128,1152]{1,0:T(8,128)(2,1)S(1)}, bf16[128,1152]{1,0:T(8,128)(2,1)S(1)}, u32[]{:S(2)}, u32[]{:S(2)}) collective-permute-start(bf16[128,1152]{1,0:T(8,128)(2,1)S(1)} %get-tuple-element.34), channel_id=1, source_target_pairs={{0,64},{64,128},{128,192},{192,0},{1,65},{65,129},{129,193},{193,1... | collective-permute-start | bytes 884744 | tf_op jit(solution)/shard_map/ppermute | solution.py:91
  136.2 15.5 %collective-permute-start.4 = (bf16[128,1152]{1,0:T(8,128)(2,1)S(1)}, bf16[128,1152]{1,0:T(8,128)(2,1)S(1)}, u32[]{:S(2)}, u32[]{:S(2)}) collective-permute-start(bf16[128,1152]{1,0:T(8,128)(2,1)S(1)} %get-tuple-element.35), channel_id=1, source_target_pairs={{0,128},{64,192},{128,0},{192,64},{1,129},{65,193},{129,1},{193,65... | collective-permute-start | bytes 884744 | tf_op jit(solution)/shard_map/ppermute | solution.py:91
  138.6 13.1 %collective-permute-start.5 = (bf16[128,1152]{1,0:T(8,128)(2,1)S(1)}, bf16[128,1152]{1,0:T(8,128)(2,1)S(1)}, u32[]{:S(2)}, u32[]{:S(2)}) collective-permute-start(bf16[128,1152]{1,0:T(8,128)(2,1)S(1)} %get-tuple-element.36), channel_id=1, source_target_pairs={{0,192},{64,0},{128,64},{192,128},{1,193},{65,1},{129,65},{193,129... | collective-permute-start | bytes 884744 | tf_op jit(solution)/shard_map/ppermute | solution.py:91
  139.8 30.8 %copy-start.3 = (bf16[3,3,256,256]{3,2,1,0:T(8,128)(2,1)S(1)}, bf16[3,3,256,256]{3,2,1,0:T(8,128)(2,1)}, u32[]{:S(2)}) copy-start(bf16[3,3,256,256]{3,2,1,0:T(8,128)(2,1)} %rpn_ref.1) | copy-start | bytes 3538948
  139.8 30.8 %copy-start.4 = (bf16[256,15]{0,1:T(8,128)(2,1)S(1)}, bf16[256,15]{0,1:T(8,128)(2,1)}, u32[]{:S(2)}) copy-start(bf16[256,15]{0,1:T(8,128)(2,1)} %param.12) | copy-start | bytes 23044
  151.7 4.7 %collective-permute-start.6 = (bf16[196,256]{1,0:T(8,128)(2,1)S(1)}, bf16[196,256]{1,0:T(8,128)(2,1)S(1)}, u32[]{:S(2)}, u32[]{:S(2)}) collective-permute-start(bf16[196,256]{1,0:T(8,128)(2,1)S(1)} %get-tuple-element.46), channel_id=1, source_target_pairs={{0,64},{64,128},{128,192},{192,0},{1,65},{65,129},{129,193},{193,1... | collective-permute-start | bytes 301064 | tf_op jit(solution)/shard_map/ppermute | solution.py:91
  152.8 7.5 %collective-permute-start.7 = (bf16[196,256]{1,0:T(8,128)(2,1)S(1)}, bf16[196,256]{1,0:T(8,128)(2,1)S(1)}, u32[]{:S(2)}, u32[]{:S(2)}) collective-permute-start(bf16[196,256]{1,0:T(8,128)(2,1)S(1)} %get-tuple-element.47), channel_id=1, source_target_pairs={{0,128},{64,192},{128,0},{192,64},{1,129},{65,193},{129,1},{193,65... | collective-permute-start | bytes 301064 | tf_op jit(solution)/shard_map/ppermute | solution.py:91
  155.6 4.9 %collective-permute-start.8 = (bf16[196,256]{1,0:T(8,128)(2,1)S(1)}, bf16[196,256]{1,0:T(8,128)(2,1)S(1)}, u32[]{:S(2)}, u32[]{:S(2)}) collective-permute-start(bf16[196,256]{1,0:T(8,128)(2,1)S(1)} %get-tuple-element.48), channel_id=1, source_target_pairs={{0,192},{64,0},{128,64},{192,128},{1,193},{65,1},{129,65},{193,129... | collective-permute-start | bytes 301064 | tf_op jit(solution)/shard_map/ppermute | solution.py:91
  160.9 8.8 %collective-permute-start.11 = (bf16[1,512,256]{2,1,0:T(8,128)(2,1)S(1)}, bf16[1,512,256]{2,1,0:T(8,128)(2,1)S(1)}, u32[]{:S(2)}, u32[]{:S(2)}) collective-permute-start(bf16[1,512,256]{2,1,0:T(8,128)(2,1)S(1)} %get-tuple-element.56), channel_id=1, source_target_pairs={{1,0},{2,1},{3,2},{4,3},{5,4},{6,5},{7,6},{8,7},{9,8},{10,9},{11,1... | collective-permute-start | bytes 786440 | tf_op jit(solution)/shard_map/ppermute | solution.py:23
  164.1 6.5 %collective-permute-start.10 = (bf16[1,512,256]{2,1,0:T(8,128)(2,1)S(1)}, bf16[1,512,256]{2,1,0:T(8,128)(2,1)S(1)}, u32[]{:S(2)}, u32[]{:S(2)}) collective-permute-start(bf16[1,512,256]{2,1,0:T(8,128)(2,1)S(1)} %get-tuple-element.57), channel_id=1, source_target_pairs={{0,1},{1,2},{2,3},{3,4},{4,5},{5,6},{6,7},{7,8},{8,9},{9,10},{10,1... | collective-permute-start | bytes 786440 | tf_op jit(solution)/shard_map/ppermute | solution.py:22
  166.5 13.1 %collective-permute-start.13 = (bf16[192,1152]{1,0:T(8,128)(2,1)S(1)}, bf16[192,1152]{1,0:T(8,128)(2,1)S(1)}, u32[]{:S(2)}, u32[]{:S(2)}) collective-permute-start(bf16[192,1152]{1,0:T(8,128)(2,1)S(1)} %sum_parts.1.refs_0_), channel_id=1, source_target_pairs={{0,192},{64,0},{128,64},{192,128},{1,193},{65,1},{129,65},{193,129... | collective-permute-start | bytes 1327112 | tf_op jit(solution)/shard_map/ppermute | solution.py:91
  168.4 21.8 %collective-permute-start.12 = (bf16[192,1152]{1,0:T(8,128)(2,1)S(1)}, bf16[192,1152]{1,0:T(8,128)(2,1)S(1)}, u32[]{:S(2)}, u32[]{:S(2)}) collective-permute-start(bf16[192,1152]{1,0:T(8,128)(2,1)S(1)} %sum_parts.1.refs_0_), channel_id=1, source_target_pairs={{0,64},{64,128},{128,192},{192,0},{1,65},{65,129},{129,193},{193,1... | collective-permute-start | bytes 1327112 | tf_op jit(solution)/shard_map/ppermute | solution.py:91
  168.4 23.4 %collective-permute-start.9 = (bf16[192,1152]{1,0:T(8,128)(2,1)S(1)}, bf16[192,1152]{1,0:T(8,128)(2,1)S(1)}, u32[]{:S(2)}, u32[]{:S(2)}) collective-permute-start(bf16[192,1152]{1,0:T(8,128)(2,1)S(1)} %sum_parts.1.refs_0_), channel_id=1, source_target_pairs={{0,128},{64,192},{128,0},{192,64},{1,129},{65,193},{129,1},{193,65... | collective-permute-start | bytes 1327112 | tf_op jit(solution)/shard_map/ppermute | solution.py:91
  169.7 22.3 %collective-permute-start.14 = (bf16[128,1152]{1,0:T(8,128)(2,1)S(1)}, bf16[128,1152]{1,0:T(8,128)(2,1)S(1)}, u32[]{:S(2)}, u32[]{:S(2)}) collective-permute-start(bf16[128,1152]{1,0:T(8,128)(2,1)S(1)} %slice.60), channel_id=1, source_target_pairs={{0,1},{1,0},{2,3},{3,2},{4,5},{5,4},{6,7},{7,6},{8,9},{9,8},{10,11... | collective-permute-start | bytes 884744 | tf_op jit(solution)/shard_map/ppermute | solution.py:364
  179.6 12.4 %collective-permute-start.17 = (bf16[128,1152]{1,0:T(8,128)(2,1)S(1)}, bf16[128,1152]{1,0:T(8,128)(2,1)S(1)}, u32[]{:S(2)}, u32[]{:S(2)}) collective-permute-start(bf16[128,1152]{1,0:T(8,128)(2,1)S(1)} %slice.77), channel_id=1, source_target_pairs={{0,1},{1,0},{2,3},{3,2},{4,5},{5,4},{6,7},{7,6},{8,9},{9,8},{10,11... | collective-permute-start | bytes 884744 | tf_op jit(solution)/shard_map/ppermute | solution.py:364
  190.3 2.8 %collective-permute-start.15 = (bf16[128,1152]{1,0:T(8,128)(2,1)S(1)}, bf16[128,1152]{1,0:T(8,128)(2,1)S(1)}, u32[]{:S(2)}, u32[]{:S(2)}) collective-permute-start(bf16[128,1152]{1,0:T(8,128)(2,1)S(1)} %slice.76), channel_id=1, source_target_pairs={{0,1},{1,0},{2,3},{3,2},{4,5},{5,4},{6,7},{7,6},{8,9},{9,8},{10,11... | collective-permute-start | bytes 884744 | tf_op jit(solution)/shard_map/ppermute | solution.py:364
  191.8 1.7 collective-permute-start.16
  (4 other events, 93.8 us)

commit v5 on v4

--- a/solution.py
+++ b/solution.py
@@ -89,6 +89,161 @@
 def shift_img(array, step):
     size = lax.axis_size("img")
     return lax.ppermute(array, "img", [(i, (i + step) % size) for i in range(size)])
+
+
+def collect_kernel(slots_ref, feat_ref, out_ref, picks, spread):
+    pixels = feat_ref.shape[0]
+    per_head = slots_ref.shape[0]
+    heads = picks.shape[0] // per_head
+    column = lax.broadcasted_iota(jnp.int32, (per_head, pixels), 1)
+    groups = out_ref.shape[1] // 4
+    for part in range(slots_ref.shape[1] // heads):
+        for k in range(heads):
+            at = part * heads + k
+            hit = jnp.broadcast_to(slots_ref[:, at : at + 1], (per_head, pixels)) == column
+            picks[k * per_head : (k + 1) * per_head, :] = hit.astype(F32).astype(BF16)
+        found = dot(picks[...], feat_ref[...], (1, 0)).T
+        lanes = 128
+        for k in range(found.shape[1] // lanes):
+            group = part * (found.shape[1] // lanes) + k
+            spread[pl.ds(group, found.shape[0], stride=groups), :] = found[:, k * lanes : (k + 1) * lanes]
+    out_ref[...] = spread[...].reshape(out_ref.shape).astype(BF16)
+
+
+def collect(slots, flat, nband):
+    per_head, heads = slots.shape
+    pixels, channels = flat.shape
+    rows = channels * per_head * heads // 128
+    return pl.pallas_call(
+        collect_kernel,
+        out_shape=jax.ShapeDtypeStruct((nband, rows // nband, 128), BF16),
+        in_specs=vmem_spec(2),
+        out_specs=pl.BlockSpec(memory_space=pltpu.VMEM),
+        scratch_shapes=[pltpu.VMEM((16 * per_head, pixels), BF16), pltpu.VMEM((rows, 128), F32)],
+        compiler_params=pltpu.CompilerParams(vmem_limit_bytes=40 * 2**20),
+        cost_estimate=pl.CostEstimate(flops=4 * 10**9, bytes_accessed=3 * 10**6, transcendentals=0),
+        name="collect",
+    )(slots, flat)
+
+
+RECIPE_ROWS = 40
+
+
+def recipe_kernel(slots_ref, weights_ref, labels_ref, out_ref):
+    out_ref[...] = jnp.zeros(out_ref.shape, F32)
+    bins = slots_ref.shape[2]
+    for r in range(slots_ref.shape[0]):
+        rows = slice(r // 2 * 4, r // 2 * 4 + 4)
+        below = slice(16 + r // 2 * 4, 16 + r // 2 * 4 + 4)
+        lanes = slice(r % 2 * 64, r % 2 * 64 + bins)
+        out_ref[rows, lanes] = slots_ref[r].astype(F32)
+        out_ref[below, lanes] = weights_ref[r]
+    out_ref[32:33, : labels_ref.shape[1]] = labels_ref[...].astype(F32)
+
+
+def recipe(sample_slot, sample_weight, labels):
+    return pl.pallas_call(
+        recipe_kernel,
+        out_shape=jax.ShapeDtypeStruct((RECIPE_ROWS, 128), F32),
+        in_specs=vmem_spec(3),
+        out_specs=pl.BlockSpec(memory_space=pltpu.VMEM),
+        name="recipe",
+    )(jnp.transpose(sample_slot, (0, 2, 1)), jnp.transpose(sample_weight, (0, 2, 1)), labels)
+
+
+def pool_kernel(place, got_ref, recipe_ref, x_ref, label_ref, wide, pooled, marks):
+    y0, z0, c0 = place[2], place[3], place[0]
+    wide[...] = got_ref[...].astype(F32).reshape(wide.shape)
+    lane = lax.broadcasted_iota(jnp.int32, (16, 128), 1)
+    chunk_at = lax.broadcasted_iota(jnp.int32, (16, 128), 0)
+
+    def group_step(group, carry):
+        rows = []
+        for channel in range(4):
+            first = channel * 16 + group
+            rows.append([wide[pl.ds(first + 64 * b4, 16, stride=256), :] for b4 in range(4)])
+        for h4 in range(4):
+            head = group * 4 + h4
+            y, z, c = head // 16, (head // 2) % 8, head % 2
+            entry = entry_of(y, z, c, y0, z0, c0)
+            tables = []
+            for channel in range(4):
+                table = rows[channel][h4]
+                for b4 in range(4):
+                    if b4 != h4:
+                        moved = pltpu.roll(rows[channel][b4], (b4 - h4) * 32 % 128, 1)
+                        table = jnp.where(lane // 32 == b4, moved, table)
+                tables.append(table)
+            marks[pl.ds(head, 1), :] = recipe_ref[entry, 32:33, :]
+            for pair in range(4):
+                sums = [None] * 4
+                for corner in range(4):
+                    row = pair * 4 + corner
+                    slot = recipe_ref[entry, row : row + 1, :].astype(jnp.int32)
+                    weight = recipe_ref[entry, 16 + row : 17 + row, :]
+                    slot = jnp.broadcast_to(slot, (16, 128))
+                    weight = jnp.broadcast_to(weight, (16, 128))
+                    weight = jnp.where(lax.shift_right_logical(slot, 7) == chunk_at, weight, 0.0)
+                    place_in = jnp.bitwise_and(slot, 127)
+                    for channel in range(4):
+                        part = weight * jnp.take_along_axis(tables[channel], place_in, axis=1, mode="promise_in_bounds")
+                        sums[channel] = part if corner == 0 else sums[channel] + part
+                for channel in range(4):
+                    total = jnp.sum(sums[channel], axis=0, keepdims=True)
+                    pooled[channel * 4 + pair, pl.ds(head, 1), :] = total
+        return carry
+
+    lax.fori_loop(0, 16, group_step, 0)
+    low = lax.broadcasted_iota(jnp.int32, (64, 128), 1) < 64
+    for r in range(8):
+        for block in range(2):
+            left, right = pooled[8 * block + r // 2], pooled[8 * block + 4 + r // 2]
+            if r % 2 == 0:
+                right = pltpu.roll(right, 64, 1)
+            else:
+                left = pltpu.roll(left, 64, 1)
+            both = jnp.where(low, left, right).astype(BF16)
+            x_ref[r * 64 : (r + 1) * 64, block * 128 : (block + 1) * 128] = both
+        label_ref[r * 64 : (r + 1) * 64, :] = marks[:, r : r + 1].astype(jnp.int32)
+
+
+def pool(place, got, recipes):
+    struct = jax.ShapeDtypeStruct
+    nband = got.shape[0]
+    return pl.pallas_call(
+        pool_kernel,
+        out_shape=[struct((8 * nband, 256), BF16), struct((8 * nband, 1), jnp.int32)],
+        in_specs=[SMEM_SPEC] + vmem_spec(2),
+        out_specs=vmem_spec(2),
+        scratch_shapes=[
+            pltpu.VMEM((got.shape[0] * got.shape[1], 128), F32),
+            pltpu.VMEM((16, nband, 128), F32),
+            pltpu.VMEM((nband, 128), F32),
+        ],
+        compiler_params=pltpu.CompilerParams(vmem_limit_bytes=40 * 2**20),
+        name="pool",
+    )(place, got, recipes)
+
+
+def entry_of(y, z, c, y0, z0, c0):
+    dz = jnp.bitwise_xor(z, z0)
+    dy = jnp.bitwise_xor(y, y0)
+    d1, d2 = lax.shift_right_logical(dz, 1), lax.shift_right_logical(dz, 2)
+    z_bits = jnp.bitwise_and(jnp.bitwise_xor(dz, d1), 1) * 4
+    z_bits = z_bits + jnp.bitwise_and(jnp.bitwise_xor(d1, d2), 1) * 2 + d2
+    e1 = lax.shift_right_logical(dy, 1)
+    y_bits = jnp.bitwise_and(jnp.bitwise_xor(dy, e1), 1) * 2 + e1
+    return jnp.bitwise_xor(c, c0) * 32 + y_bits * 8 + z_bits
+
+
+def swap_bands(array, pattern):
+    y, z, c = pattern
+    perm = [(b, b ^ (y * NZ * NC + z * NC + c)) for b in range(BAND)]
+    return lax.ppermute(array, "band", perm)
+
+
+def doubled(array, pattern):
+    return jnp.concatenate([array, swap_bands(array, pattern)], axis=0)
 
 
 def gelu_parts(value):
@@ -303,38 +458,28 @@
     core = band % NC
     hid = w_fc2.shape[0]
     half = hid // NC
-    place = jnp.stack([core, image]).astype(jnp.int32)
+    z_at, y_at = (band // NC) % NZ, band // (NC * NZ)
+    place = jnp.stack([core, image, y_at, z_at]).astype(jnp.int32)
 
     flat = features.reshape(rows * width, channels)
-    capacity = pixel_slots.shape[3]
-    wanted = pixel_slots[0, :, 0, :].reshape(nband * capacity)
-    sending = flat[wanted].reshape(nband, capacity, channels)
+    recipes = recipe(sample_slot[0], sample_weight[0], roi_labels)[None]
+    for pattern in ((0, 7, 0), (0, 3, 0), (0, 1, 0)):
+        recipes = doubled(recipes, pattern)
+    sending = collect(jnp.transpose(pixel_slots[0, :, 0, :]), flat, nband)
+    sending, recipes = lax.optimization_barrier((sending, recipes))
     received = lax.all_to_all(sending, "band", split_axis=0, concat_axis=0, tiled=True)
+    for pattern in ((3, 0, 0), (1, 0, 0), (0, 0, 1)):
+        recipes = doubled(recipes, pattern)
 
     w_first = lax.optimization_barrier((w_fc1, sending))[0]
+    depth = w_first.shape[0]
+    w_first = jnp.pad(w_first.reshape(4, depth // 4, hid), ((0, 0), (0, 64 - depth // 4), (0, 0)))
+    w_first = w_first.reshape(256, hid)
     w_mine = lax.dynamic_slice_in_dim(w_first, core * half, half, 1)
     w_theirs = lax.dynamic_slice_in_dim(w_first, (1 - core) * half, half, 1)
     w_other = lax.ppermute(w_theirs, "band", CORE_SWAP)
-    received, w_other = lax.optimization_barrier((received, w_other))
-
-    received = received.reshape(nband * capacity, channels).astype(F32)
-    roi_count, bins = sample_slot.shape[1:3]
-    corner_slots = sample_slot[0].reshape(roi_count * bins, 4)
-    corner_weights = sample_weight[0].reshape(roi_count * bins, 4)
-    slot_ids = jnp.arange(nband * capacity, dtype=jnp.int32)[None, :]
-    pooling = jnp.zeros((roi_count * bins, nband * capacity), F32)
-    for corner in range(4):
-        hits = (corner_slots[:, corner : corner + 1] == slot_ids).astype(F32)
-        pooling = pooling + hits * corner_weights[:, corner : corner + 1]
-    pooled = jnp.dot(pooling, received, precision=lax.Precision.HIGHEST, preferred_element_type=F32)
-    pooled = pooled.astype(BF16).reshape(roi_count, bins, channels)
-    depth = w_fc1.shape[0]
-    x_local = jnp.transpose(pooled, (0, 2, 1)).reshape(roi_count, nband, depth)
-    label_column = jnp.broadcast_to(roi_labels[0].astype(BF16)[:, None, None], (roi_count, nband, 1))
-    x_local = jnp.concatenate([x_local, label_column], axis=2).reshape(roi_count, nband * (depth + 1))
-    x_cols = lax.all_to_all(x_local, "band", split_axis=1, concat_axis=0, tiled=True)
-    labels = x_cols[:, depth:].astype(jnp.int32)
-    x_cols = x_cols[:, :depth]
+    received, w_other, recipes = lax.optimization_barrier((received, w_other, recipes))
+    x_cols, labels = pool(place, received, recipes)
 
     x_other = lax.ppermute(x_cols, "band", CORE_SWAP)
     partial = dot(x_cols, w_mine, (1, 0)) + dot(x_other, w_other, (1, 0))

time: 197 us -> 217 us (1.10)
  Pallas kernels: 24.5 us -> 50.3 us
  waiting for transfers between devices: 55.1 us -> 42.7 us
  starting transfers between devices: 54.7 us -> 62.3 us
  local copies, waits for them, and re-layouts: 14.5 us -> 8.14 us
  blocking collectives: 43 us -> 47.3 us
  other arithmetic: 0.42 us -> 2.98 us
    pallas_call x0 -> x3, Pallas kernels: none -> 27.3 us  [the longest x1 19.5 us: pool(): pl.pallas_call(pool_kernel, out_shape=[struct((8 * nband, 256), BF16), st...]
    all_to_all x1, waiting for transfers between devices: 26.9 us -> 0.01 us  [shards(): lax.all_to_all(sending, 'band', split_axis=0, concat_axis=0, tiled=True)]
    ppermute x0 -> x6, waiting for transfers between devices: none -> 25.5 us  [swap_bands(): return lax.ppermute(array, 'band', perm)]
    ppermute x0 -> x6, starting transfers between devices: none -> 13.4 us  [swap_bands(): return lax.ppermute(array, 'band', perm)]
    all_to_all x1 -> x0, waiting for transfers between devices: 12 us -> none  [shards(): lax.all_to_all(x_local, 'band', split_axis=1, concat_axis=0, tiled=True)]
    gather x1 -> x0, local copies, waits for them, and re-layouts: 10.4 us -> none  [shards(): sending = flat[wanted].reshape(nband, capacity, channels)]
    all_to_all x1 -> x0, starting transfers between devices: 6.19 us -> none  [shards(): lax.all_to_all(x_local, 'band', split_axis=1, concat_axis=0, tiled=True)]
    all_to_all x4, blocking collectives: 43 us -> 47.3 us  [exchange(): lax.all_to_all(array, 'band', split_axis=0, concat_axis=0, tiled=True, ax...]
  transfers between devices with their start and end apart: 20 -> 25, of which waited for: 12 -> 13; matrix products, arithmetic and copies ran while one was open for 1% -> 3% of each run, Pallas kernels for 7% -> 9%
where the time goes in v5:
time: 217 us; the launch traced here: 216 us
  starting transfers between devices  62.3 us (29%)
  Pallas kernels  50.3 us (23%)
  blocking collectives  47.3 us (22%)
  waiting for transfers between devices  42.7 us (20%)
  local copies, waits for them, and re-layouts  8.14 us (4%)
  other arithmetic  2.98 us (1%)
    all_to_all x4, blocking collectives, exchange(): lax.all_to_all(array, 'band', split_axis=0, concat_axis=0, tiled=True, ax...  47.3 us
    ppermute x6, waiting for transfers between devices, swap_bands(): return lax.ppermute(array, 'band', perm)  25.5 us
    pallas_call x1, Pallas kernels, pool(): pl.pallas_call(pool_kernel, out_shape=[struct((8 * nband, 256), BF16), st...  19.5 us
    ppermute x9, waiting for transfers between devices, shift_img(): lax.ppermute(array, 'img', [(i, (i + step) % size) for i in range(size)])  14.6 us
    ppermute x6, starting transfers between devices, swap_bands(): return lax.ppermute(array, 'band', perm)  13.4 us
    all_to_all x1, starting transfers between devices, shards(): lax.all_to_all(sending, 'band', split_axis=0, concat_axis=0, tiled=True)  12.7 us
    ppermute x9, starting transfers between devices, shift_img(): lax.ppermute(array, 'img', [(i, (i + step) % size) for i in range(size)])  12.6 us
    ppermute x4, starting transfers between devices, shards(): other = [lax.ppermute(part[:tall], 'band', CORE_SWAP) for part in mine]  11.3 us
  transfers between devices with their start and end apart: 25, of which 13 were waited for; matrix products, arithmetic and copies ran while one was open for 3% of the time, Pallas kernels for 9%

profile of v5, /device:TPU:1, one launch (start us, length us, event | category | flops | bytes accessed | tf_op | source)
XLA Modules:
  0.0 216.1 jit_solution(8290478922234765573)
XLA Ops:
  2.0 6.4 %collective-permute-start = (f32[1,40,128]{2,1,0:T(8,128)}, f32[1,40,128]{2,1,0:T(8,128)S(1)}, u32[]{:S(2)}, u32[]{:S(2)}) collective-permute-start(f32[1,40,128]{2,1,0:T(8,128)} %bitcast.43), channel_id=1, source_target_pairs={{0,14},{1,15},{2,12},{3,13},{4,10},{5,11},{6,8},{7,9},{8,6},{9,7},... | collective-permute-start | bytes 61448 | tf_op jit(solution)/shard_map/ppermute | solution.py:242
  12.2 3.0 %collective-permute-done.1 = f32[2,40,128]{2,1,0:T(8,128)S(1)} collective-permute-done((f32[2,40,128]{2,1,0:T(8,128)S(1)}, f32[2,40,128]{2,1,0:T(8,128)S(1)}, u32[]{:S(2)}, u32[]{:S(2)}) %collective-permute-start.1) | collective-permute-done | bytes 40992 | tf_op jit(solution)/shard_map/ppermute | solution.py:242
  18.3 6.3 %collect.1 = bf16[64,64,128]{2,1,0:T(8,128)(2,1)} custom-call(s32[32,64]{1,0:T(8,128)S(1)} %bitcast.36, bf16[4096,256]{1,0:T(8,128)(2,1)S(1)} %bitcast.34), custom_call_target="tpu_custom_call" | custom-call | flops 4000000000 | bytes 3000000 | tf_op jit(solution)/shard_map/collect/pallas_call | solution.py:117
  24.6 12.7 %all-to-all-start = ((bf16[64,64,128]{2,1,0:T(8,128)(2,1)}), bf16[64,64,128]{2,1,0:T(8,128)(2,1)S(1)}, u32[]{:S(2)}, u32[]{:S(2)}) async-start(bf16[64,64,128]{2,1,0:T(8,128)(2,1)} %collect.1), calls=%async_computation | async-start | bytes 2097152 | tf_op jit(solution)/shard_map/all_to_all | solution.py:470
  37.4 2.9 %collective-permute-start.4 = (f32[8,40,128]{2,1,0:T(8,128)S(1)}, f32[8,40,128]{2,1,0:T(8,128)S(1)}, u32[]{:S(2)}, u32[]{:S(2)}) collective-permute-start(f32[8,40,128]{2,1,0:T(8,128)S(1)} %pad_maximum_fusion.3), channel_id=1, source_target_pairs={{0,48},{1,49},{2,50},{3,51},{4,52},{5,53},{6,54},{7,55},{8,56},{9,... | collective-permute-start | bytes 491528 | tf_op jit(solution)/shard_map/ppermute | solution.py:242
  40.3 7.0 %collective-permute-done.4 = f32[8,40,128]{2,1,0:T(8,128)S(1)} collective-permute-done((f32[8,40,128]{2,1,0:T(8,128)S(1)}, f32[8,40,128]{2,1,0:T(8,128)S(1)}, u32[]{:S(2)}, u32[]{:S(2)}) %collective-permute-start.4) | collective-permute-done | bytes 163872 | tf_op jit(solution)/shard_map/ppermute | solution.py:242
  47.7 14.1 %collective-permute-done.5 = f32[16,40,128]{2,1,0:T(8,128)S(1)} collective-permute-done((f32[16,40,128]{2,1,0:T(8,128)S(1)}, f32[16,40,128]{2,1,0:T(8,128)S(1)}, u32[]{:S(2)}, u32[]{:S(2)}) %collective-permute-start.5) | collective-permute-done | bytes 327712 | tf_op jit(solution)/shard_map/ppermute | solution.py:242
  67.9 19.5 %pool.1 = (bf16[512,256]{1,0:T(8,128)(2,1)S(1)}, s32[512,1]{1,0:T(8,128)S(1)}) custom-call(s32[4]{0:T(128)S(1)} %pad_add_fusion.place, bf16[64,64,128]{2,1,0:T(8,128)(2,1)S(1)} %all-to-all-done.got_ref, f32[64,40,128]{2,1,0:T(8,128)S(1)} %pad_maximum_fusion.recipe_ref), custom_call_target="tpu_custom_call" | custom-call | tf_op jit(solution)/shard_map/pool/pallas_call | solution.py:213
  90.5 11.7 %all_to_all.25 = bf16[4,128,512]{2,1,0:T(8,128)(2,1)S(1)} all-to-all(bf16[4,128,512]{2,1,0:T(8,128)(2,1)S(1)} %bitcast.40), channel_id=1, replica_groups={{0,16,32,48},{1,17,33,49},{2,18,34,50},{3,19,35,51},{4,20,36,52},{5,21,..., dimensions={0} | all-to-all | bytes 1048576 | tf_op jit(solution)/shard_map/all_to_all | solution.py:80
  102.3 15.8 %all_to_all.26 = bf16[8,16,512]{2,1,0:T(8,128)(2,1)S(1)} all-to-all(bf16[8,16,512]{2,1,0:T(8,128)(2,1)S(1)} %bitcast.42), channel_id=1, replica_groups={{0,2,4,6,8,10,12,14},{1,3,5,7,9,11,13,15},{16,18,20,22,24,26,28,30},{17..., dimensions={0} | all-to-all | bytes 262144 | tf_op jit(solution)/shard_map/all_to_all | solution.py:80
  118.1 10.4 %all_to_all.27 = bf16[8,16,512]{2,1,0:T(8,128)(2,1)S(1)} all-to-all(bf16[8,16,512]{2,1,0:T(8,128)(2,1)S(1)} %broadcast_in_dim.20), channel_id=1, replica_groups={{0,2,4,6,8,10,12,14},{1,3,5,7,9,11,13,15},{16,18,20,22,24,26,28,30},{17..., dimensions={0} | all-to-all | bytes 262144 | tf_op jit(solution)/shard_map/all_to_all | solution.py:80
  128.6 9.5 %all_to_all.28 = bf16[4,128,512]{2,1,0:T(8,128)(2,1)S(1)} all-to-all(bf16[4,128,512]{2,1,0:T(8,128)(2,1)S(1)} %broadcast_in_dim.22), channel_id=1, replica_groups={{0,16,32,48},{1,17,33,49},{2,18,34,50},{3,19,35,51},{4,20,36,52},{5,21,..., dimensions={0} | all-to-all | bytes 1048576 | tf_op jit(solution)/shard_map/all_to_all | solution.py:80
  138.0 5.3 %collective-permute-start.8 = (bf16[512,512]{1,0:T(8,128)(2,1)S(1)}, bf16[512,512]{1,0:T(8,128)(2,1)S(1)}, u32[]{:S(2)}, u32[]{:S(2)}) collective-permute-start(bf16[512,512]{1,0:T(8,128)(2,1)S(1)} %bitcast.31), channel_id=1, source_target_pairs={{0,1},{1,0},{2,3},{3,2},{4,5},{5,4},{6,7},{7,6},{8,9},{9,8},{10,11... | collective-permute-start | bytes 1572872 | tf_op jit(solution)/shard_map/ppermute | solution.py:494
  147.1 5.8 %head.1 = (bf16[512,1024]{1,0:T(8,128)(2,1)S(1)}, f32[128,1152]{1,0:T(8,128)S(1)}, bf16[128,1152]{1,0:T(8,128)(2,1)S(1)}, bf16[128,1152]{1,0:T(8,128)(2,1)S(1)}, bf16[128,1152]{1,0:T(8,128)(2,1)S(1)}) custom-call(s32[4]{0:T(128)S(1)} %pad_add_fusion.place, bf16[512,512]{1,0:T(8,128)(2,1)S(1)} %bitcast.32, ...), custom_call_target="tpu_custom_call" | custom-call | tf_op jit(solution)/shard_map/head/pallas_call | solution.py:315
  154.2 2.5 %collective-permute-start.10 = (bf16[128,1152]{1,0:T(8,128)(2,1)S(1)}, bf16[128,1152]{1,0:T(8,128)(2,1)S(1)}, u32[]{:S(2)}, u32[]{:S(2)}) collective-permute-start(bf16[128,1152]{1,0:T(8,128)(2,1)S(1)} %get-tuple-element.45), channel_id=1, source_target_pairs={{0,128},{64,192},{128,0},{192,64},{1,129},{65,193},{129,1},{193,65... | collective-permute-start | bytes 884744 | tf_op jit(solution)/shard_map/ppermute | solution.py:91
  157.8 5.0 %first_layer.1 = (f32[256,256]{1,0:T(8,128)S(1)}, bf16[256,256]{1,0:T(8,128)(2,1)S(1)}, bf16[256,256]{1,0:T(8,128)(2,1)S(1)}, bf16[256,256]{1,0:T(8,128)(2,1)S(1)}) custom-call(s32[4]{0:T(128)S(1)} %pad_add_fusion.place, bf16[512,512]{1,0:T(8,128)(2,1)S(1)} %bitcast.33, bf16[512,512]{1,0:T(8,128)(2,1)S(1)} %collective-permute-done.8.other_ref, ...), custom_call_target="tpu_custom_call" | custom-call | tf_op jit(solution)/shard_map/first_layer/pallas_call | solution.py:358
  162.9 7.3 %collective-permute-done.10.refs_2_ = bf16[128,1152]{1,0:T(8,128)(2,1)S(1)} collective-permute-done((bf16[128,1152]{1,0:T(8,128)(2,1)S(1)}, bf16[128,1152]{1,0:T(8,128)(2,1)S(1)}, u32[]{:S(2)}, u32[]{:S(2)}) %collective-permute-start.10) | collective-permute-done | bytes 294944 | tf_op jit(solution)/shard_map/ppermute | solution.py:91
  170.8 2.8 %collective-permute-start.13 = (bf16[256,256]{1,0:T(8,128)(2,1)S(1)}, bf16[256,256]{1,0:T(8,128)(2,1)S(1)}, u32[]{:S(2)}, u32[]{:S(2)}) collective-permute-start(bf16[256,256]{1,0:T(8,128)(2,1)S(1)} %get-tuple-element.57), channel_id=1, source_target_pairs={{0,128},{64,192},{128,0},{192,64},{1,129},{65,193},{129,1},{193,65... | collective-permute-start | bytes 393224 | tf_op jit(solution)/shard_map/ppermute | solution.py:91
  175.6 3.9 %collective-permute-done.13.refs_6_ = bf16[256,256]{1,0:T(8,128)(2,1)S(1)} collective-permute-done((bf16[256,256]{1,0:T(8,128)(2,1)S(1)}, bf16[256,256]{1,0:T(8,128)(2,1)S(1)}, u32[]{:S(2)}, u32[]{:S(2)}) %collective-permute-start.13) | collective-permute-done | bytes 131104 | tf_op jit(solution)/shard_map/ppermute | solution.py:91
  179.8 3.4 %collective-permute-start.17 = (bf16[1,512,256]{2,1,0:T(8,128)(2,1)S(1)}, bf16[1,512,256]{2,1,0:T(8,128)(2,1)S(1)}, u32[]{:S(2)}, u32[]{:S(2)}) collective-permute-start(bf16[1,512,256]{2,1,0:T(8,128)(2,1)S(1)} %get-tuple-element.66), channel_id=1, source_target_pairs={{1,0},{2,1},{3,2},{4,3},{5,4},{6,5},{7,6},{8,7},{9,8},{10,9},{11,1... | collective-permute-start | bytes 786440 | tf_op jit(solution)/shard_map/ppermute | solution.py:23
  183.2 2.3 %collective-permute-start.16 = (bf16[1,512,256]{2,1,0:T(8,128)(2,1)S(1)}, bf16[1,512,256]{2,1,0:T(8,128)(2,1)S(1)}, u32[]{:S(2)}, u32[]{:S(2)}) collective-permute-start(bf16[1,512,256]{2,1,0:T(8,128)(2,1)S(1)} %get-tuple-element.67), channel_id=1, source_target_pairs={{0,1},{1,2},{2,3},{3,4},{4,5},{5,6},{6,7},{7,8},{8,9},{9,10},{10,1... | collective-permute-start | bytes 786440 | tf_op jit(solution)/shard_map/ppermute | solution.py:22
  189.9 8.8 %rpn.1 = bf16[15,8,512]{2,1,0:T(8,128)(2,1)} custom-call(bf16[1,512,256]{2,1,0:T(8,128)(2,1)S(1)} %collective-permute-done.16.before_ref, bf16[8,512,256]{2,1,0:T(8,128)(2,1)S(1)} %bitcast.35, bf16[1,512,256]{2,1,0:T(8,128)(2,1)S(1)} %collective-permute-done.17.after_ref, bf16[3,3,256,256]{3,2,1,0:T(8,128)(2,1)S(1)} %copy-done.5, bf16[15,256]{1,0:T(8,128)(2,1)S(1)} %bitcast.37), custom_call_target="tpu_custom_call" | custom-call | flops 8999999488 | bytes 4000000 | tf_op jit(solution)/shard_map/rpn/pallas_call | solution.py:56
  198.7 9.0 %collective-permute-start.23 = (bf16[128,1152]{1,0:T(8,128)(2,1)S(1)}, bf16[128,1152]{1,0:T(8,128)(2,1)S(1)}, u32[]{:S(2)}, u32[]{:S(2)}) collective-permute-start(bf16[128,1152]{1,0:T(8,128)(2,1)S(1)} %slice.25), channel_id=1, source_target_pairs={{0,1},{1,0},{2,3},{3,2},{4,5},{5,4},{6,7},{7,6},{8,9},{9,8},{10,11... | collective-permute-start | bytes 884744 | tf_op jit(solution)/shard_map/ppermute | solution.py:509
  212.8 3.3 %assemble.1 = (f32[196,1024]{1,0:T(8,128)}, f32[1024,1024]{1,0:T(8,128)}, f32[81,1024]{1,0:T(8,128)}) custom-call(s32[4]{0:T(128)S(1)} %pad_add_fusion.place, bf16[192,1152]{1,0:T(8,128)(2,1)S(1)} %sum_parts.1.refs_0_, bf16[192,1152]{1,0:T(8,128)(2,1)S(1)} %collective-permute-done.18.refs_1_, bf16[192,1152]{1,0:T(8,128)(2,1)S(1)} %collective-permute-done.15.refs_2_, ...), custom_call_target="tpu_custom_call" | custom-call | tf_op jit(solution)/shard_map/assemble/pallas_call | solution.py:429
  (81 shorter events, 36.6 us)
Async XLA Ops:
  2.0 7.8 %collective-permute-start = (f32[1,40,128]{2,1,0:T(8,128)}, f32[1,40,128]{2,1,0:T(8,128)S(1)}, u32[]{:S(2)}, u32[]{:S(2)}) collective-permute-start(f32[1,40,128]{2,1,0:T(8,128)} %bitcast.43), channel_id=1, source_target_pairs={{0,14},{1,15},{2,12},{3,13},{4,10},{5,11},{6,8},{7,9},{8,6},{9,7},... | collective-permute-start | bytes 61448 | tf_op jit(solution)/shard_map/ppermute | solution.py:242
  10.6 4.7 %collective-permute-start.1 = (f32[2,40,128]{2,1,0:T(8,128)S(1)}, f32[2,40,128]{2,1,0:T(8,128)S(1)}, u32[]{:S(2)}, u32[]{:S(2)}) collective-permute-start(f32[2,40,128]{2,1,0:T(8,128)S(1)} %pad_maximum_fusion.5), channel_id=1, source_target_pairs={{0,6},{1,7},{2,4},{3,5},{4,2},{5,3},{6,0},{7,1},{8,14},{9,15},{10,... | collective-permute-start | bytes 122888 | tf_op jit(solution)/shard_map/ppermute | solution.py:242
  16.0 8.7 %collective-permute-start.2 = (f32[4,40,128]{2,1,0:T(8,128)S(1)}, f32[4,40,128]{2,1,0:T(8,128)S(1)}, u32[]{:S(2)}, u32[]{:S(2)}) collective-permute-start(f32[4,40,128]{2,1,0:T(8,128)S(1)} %pad_maximum_fusion.4), channel_id=1, source_target_pairs={{0,2},{1,3},{2,0},{3,1},{4,6},{5,7},{6,4},{7,5},{8,10},{9,11},{10,... | collective-permute-start | bytes 245768 | tf_op jit(solution)/shard_map/ppermute | solution.py:242
  24.6 43.3 %all-to-all-start = ((bf16[64,64,128]{2,1,0:T(8,128)(2,1)}), bf16[64,64,128]{2,1,0:T(8,128)(2,1)S(1)}, u32[]{:S(2)}, u32[]{:S(2)}) async-start(bf16[64,64,128]{2,1,0:T(8,128)(2,1)} %collect.1), calls=%async_computation | async-start | bytes 2097152 | tf_op jit(solution)/shard_map/all_to_all | solution.py:470
  37.4 9.9 %collective-permute-start.4 = (f32[8,40,128]{2,1,0:T(8,128)S(1)}, f32[8,40,128]{2,1,0:T(8,128)S(1)}, u32[]{:S(2)}, u32[]{:S(2)}) collective-permute-start(f32[8,40,128]{2,1,0:T(8,128)S(1)} %pad_maximum_fusion.3), channel_id=1, source_target_pairs={{0,48},{1,49},{2,50},{3,51},{4,52},{5,53},{6,54},{7,55},{8,56},{9,... | collective-permute-start | bytes 491528 | tf_op jit(solution)/shard_map/ppermute | solution.py:242
  47.3 14.5 %collective-permute-start.5 = (f32[16,40,128]{2,1,0:T(8,128)S(1)}, f32[16,40,128]{2,1,0:T(8,128)S(1)}, u32[]{:S(2)}, u32[]{:S(2)}) collective-permute-start(f32[16,40,128]{2,1,0:T(8,128)S(1)} %pad_maximum_fusion.2), channel_id=1, source_target_pairs={{0,16},{1,17},{2,18},{3,19},{4,20},{5,21},{6,22},{7,23},{8,24},{9,... | collective-permute-start | bytes 983048 | tf_op jit(solution)/shard_map/ppermute | solution.py:242
  61.8 4.7 %collective-permute-start.6 = (f32[32,40,128]{2,1,0:T(8,128)S(1)}, f32[32,40,128]{2,1,0:T(8,128)}, u32[]{:S(2)}, u32[]{:S(2)}) collective-permute-start(f32[32,40,128]{2,1,0:T(8,128)S(1)} %pad_maximum_fusion.1), channel_id=1, source_target_pairs={{0,1},{1,0},{2,3},{3,2},{4,5},{5,4},{6,7},{7,6},{8,9},{9,8},{10,11... | collective-permute-start | bytes 1966088 | tf_op jit(solution)/shard_map/ppermute | solution.py:242
  65.8 2.1 collective-permute-start.3
  87.5 1.8 collective-permute-start.7
  138.0 8.1 %collective-permute-start.8 = (bf16[512,512]{1,0:T(8,128)(2,1)S(1)}, bf16[512,512]{1,0:T(8,128)(2,1)S(1)}, u32[]{:S(2)}, u32[]{:S(2)}) collective-permute-start(bf16[512,512]{1,0:T(8,128)(2,1)S(1)} %bitcast.31), channel_id=1, source_target_pairs={{0,1},{1,0},{2,3},{3,2},{4,5},{5,4},{6,7},{7,6},{8,9},{9,8},{10,11... | collective-permute-start | bytes 1572872 | tf_op jit(solution)/shard_map/ppermute | solution.py:494
  152.9 10.0 %collective-permute-start.9 = (bf16[128,1152]{1,0:T(8,128)(2,1)S(1)}, bf16[128,1152]{1,0:T(8,128)(2,1)S(1)}, u32[]{:S(2)}, u32[]{:S(2)}) collective-permute-start(bf16[128,1152]{1,0:T(8,128)(2,1)S(1)} %get-tuple-element.44), channel_id=1, source_target_pairs={{0,64},{64,128},{128,192},{192,0},{1,65},{65,129},{129,193},{193,1... | collective-permute-start | bytes 884744 | tf_op jit(solution)/shard_map/ppermute | solution.py:91
  154.2 16.0 %collective-permute-start.10 = (bf16[128,1152]{1,0:T(8,128)(2,1)S(1)}, bf16[128,1152]{1,0:T(8,128)(2,1)S(1)}, u32[]{:S(2)}, u32[]{:S(2)}) collective-permute-start(bf16[128,1152]{1,0:T(8,128)(2,1)S(1)} %get-tuple-element.45), channel_id=1, source_target_pairs={{0,128},{64,192},{128,0},{192,64},{1,129},{65,193},{129,1},{193,65... | collective-permute-start | bytes 884744 | tf_op jit(solution)/shard_map/ppermute | solution.py:91
  156.6 13.5 %collective-permute-start.11 = (bf16[128,1152]{1,0:T(8,128)(2,1)S(1)}, bf16[128,1152]{1,0:T(8,128)(2,1)S(1)}, u32[]{:S(2)}, u32[]{:S(2)}) collective-permute-start(bf16[128,1152]{1,0:T(8,128)(2,1)S(1)} %get-tuple-element.46), channel_id=1, source_target_pairs={{0,192},{64,0},{128,64},{192,128},{1,193},{65,1},{129,65},{193,129... | collective-permute-start | bytes 884744 | tf_op jit(solution)/shard_map/ppermute | solution.py:91
  170.1 5.5 %collective-permute-start.12 = (bf16[256,256]{1,0:T(8,128)(2,1)S(1)}, bf16[256,256]{1,0:T(8,128)(2,1)S(1)}, u32[]{:S(2)}, u32[]{:S(2)}) collective-permute-start(bf16[256,256]{1,0:T(8,128)(2,1)S(1)} %get-tuple-element.56), channel_id=1, source_target_pairs={{0,64},{64,128},{128,192},{192,0},{1,65},{65,129},{129,193},{193,1... | collective-permute-start | bytes 393224 | tf_op jit(solution)/shard_map/ppermute | solution.py:91
  170.8 8.7 %collective-permute-start.13 = (bf16[256,256]{1,0:T(8,128)(2,1)S(1)}, bf16[256,256]{1,0:T(8,128)(2,1)S(1)}, u32[]{:S(2)}, u32[]{:S(2)}) collective-permute-start(bf16[256,256]{1,0:T(8,128)(2,1)S(1)} %get-tuple-element.57), channel_id=1, source_target_pairs={{0,128},{64,192},{128,0},{192,64},{1,129},{65,193},{129,1},{193,65... | collective-permute-start | bytes 393224 | tf_op jit(solution)/shard_map/ppermute | solution.py:91
  173.6 5.9 %collective-permute-start.14 = (bf16[256,256]{1,0:T(8,128)(2,1)S(1)}, bf16[256,256]{1,0:T(8,128)(2,1)S(1)}, u32[]{:S(2)}, u32[]{:S(2)}) collective-permute-start(bf16[256,256]{1,0:T(8,128)(2,1)S(1)} %get-tuple-element.58), channel_id=1, source_target_pairs={{0,192},{64,0},{128,64},{192,128},{1,193},{65,1},{129,65},{193,129... | collective-permute-start | bytes 393224 | tf_op jit(solution)/shard_map/ppermute | solution.py:91
  179.8 9.3 %collective-permute-start.17 = (bf16[1,512,256]{2,1,0:T(8,128)(2,1)S(1)}, bf16[1,512,256]{2,1,0:T(8,128)(2,1)S(1)}, u32[]{:S(2)}, u32[]{:S(2)}) collective-permute-start(bf16[1,512,256]{2,1,0:T(8,128)(2,1)S(1)} %get-tuple-element.66), channel_id=1, source_target_pairs={{1,0},{2,1},{3,2},{4,3},{5,4},{6,5},{7,6},{8,7},{9,8},{10,9},{11,1... | collective-permute-start | bytes 786440 | tf_op jit(solution)/shard_map/ppermute | solution.py:23
  183.2 6.7 %collective-permute-start.16 = (bf16[1,512,256]{2,1,0:T(8,128)(2,1)S(1)}, bf16[1,512,256]{2,1,0:T(8,128)(2,1)S(1)}, u32[]{:S(2)}, u32[]{:S(2)}) collective-permute-start(bf16[1,512,256]{2,1,0:T(8,128)(2,1)S(1)} %get-tuple-element.67), channel_id=1, source_target_pairs={{0,1},{1,2},{2,3},{3,4},{4,5},{5,6},{6,7},{7,8},{8,9},{9,10},{10,1... | collective-permute-start | bytes 786440 | tf_op jit(solution)/shard_map/ppermute | solution.py:22
  185.5 13.2 %collective-permute-start.19 = (bf16[192,1152]{1,0:T(8,128)(2,1)S(1)}, bf16[192,1152]{1,0:T(8,128)(2,1)S(1)}, u32[]{:S(2)}, u32[]{:S(2)}) collective-permute-start(bf16[192,1152]{1,0:T(8,128)(2,1)S(1)} %sum_parts.1.refs_0_), channel_id=1, source_target_pairs={{0,192},{64,0},{128,64},{192,128},{1,193},{65,1},{129,65},{193,129... | collective-permute-start | bytes 1327112 | tf_op jit(solution)/shard_map/ppermute | solution.py:91
  187.8 22.0 %collective-permute-start.18 = (bf16[192,1152]{1,0:T(8,128)(2,1)S(1)}, bf16[192,1152]{1,0:T(8,128)(2,1)S(1)}, u32[]{:S(2)}, u32[]{:S(2)}) collective-permute-start(bf16[192,1152]{1,0:T(8,128)(2,1)S(1)} %sum_parts.1.refs_0_), channel_id=1, source_target_pairs={{0,64},{64,128},{128,192},{192,0},{1,65},{65,129},{129,193},{193,1... | collective-permute-start | bytes 1327112 | tf_op jit(solution)/shard_map/ppermute | solution.py:91
  187.8 23.4 %collective-permute-start.15 = (bf16[192,1152]{1,0:T(8,128)(2,1)S(1)}, bf16[192,1152]{1,0:T(8,128)(2,1)S(1)}, u32[]{:S(2)}, u32[]{:S(2)}) collective-permute-start(bf16[192,1152]{1,0:T(8,128)(2,1)S(1)} %sum_parts.1.refs_0_), channel_id=1, source_target_pairs={{0,128},{64,192},{128,0},{192,64},{1,129},{65,193},{129,1},{193,65... | collective-permute-start | bytes 1327112 | tf_op jit(solution)/shard_map/ppermute | solution.py:91
  189.1 22.2 %collective-permute-start.20 = (bf16[128,1152]{1,0:T(8,128)(2,1)S(1)}, bf16[128,1152]{1,0:T(8,128)(2,1)S(1)}, u32[]{:S(2)}, u32[]{:S(2)}) collective-permute-start(bf16[128,1152]{1,0:T(8,128)(2,1)S(1)} %slice.20), channel_id=1, source_target_pairs={{0,1},{1,0},{2,3},{3,2},{4,5},{5,4},{6,7},{7,6},{8,9},{9,8},{10,11... | collective-permute-start | bytes 884744 | tf_op jit(solution)/shard_map/ppermute | solution.py:509
  198.7 12.5 %collective-permute-start.23 = (bf16[128,1152]{1,0:T(8,128)(2,1)S(1)}, bf16[128,1152]{1,0:T(8,128)(2,1)S(1)}, u32[]{:S(2)}, u32[]{:S(2)}) collective-permute-start(bf16[128,1152]{1,0:T(8,128)(2,1)S(1)} %slice.25), channel_id=1, source_target_pairs={{0,1},{1,0},{2,3},{3,2},{4,5},{5,4},{6,7},{7,6},{8,9},{9,8},{10,11... | collective-permute-start | bytes 884744 | tf_op jit(solution)/shard_map/ppermute | solution.py:509
  209.8 2.6 %collective-permute-start.21 = (bf16[128,1152]{1,0:T(8,128)(2,1)S(1)}, bf16[128,1152]{1,0:T(8,128)(2,1)S(1)}, u32[]{:S(2)}, u32[]{:S(2)}) collective-permute-start(bf16[128,1152]{1,0:T(8,128)(2,1)S(1)} %slice.24), channel_id=1, source_target_pairs={{0,1},{1,0},{2,3},{3,2},{4,5},{5,4},{6,7},{7,6},{8,9},{9,8},{10,11... | collective-permute-start | bytes 884744 | tf_op jit(solution)/shard_map/ppermute | solution.py:509
  (11 other events, 71.4 us)

commit v6 on v4

--- a/solution.py
+++ b/solution.py
@@ -12,6 +12,7 @@
 F32, BF16 = jnp.float32, jnp.bfloat16
 CORE_SWAP = [(b, b ^ 1) for b in range(BAND)]
 Z_GROUPS = [[(y * NZ + z) * NC + c for z in range(NZ)] for y in range(NY) for c in range(NC)]
+ZC_GROUPS = [[y * NZ * NC + k for k in range(NZ * NC)] for y in range(NY)]
 Y_GROUPS = [[(y * NZ + z) * NC + c for y in range(NY)] for z in range(NZ) for c in range(NC)]
 
 
@@ -89,6 +90,68 @@
 def shift_img(array, step):
     size = lax.axis_size("img")
     return lax.ppermute(array, "img", [(i, (i + step) % size) for i in range(size)])
+
+
+def collect_kernel(slots_ref, feat_ref, out_ref, picks):
+    pixels = feat_ref.shape[0]
+    per_head = slots_ref.shape[0]
+    heads = picks.shape[0] // per_head
+    column = lax.broadcasted_iota(jnp.int32, (per_head, pixels), 1)
+    for part in range(slots_ref.shape[1] // heads):
+        for k in range(heads):
+            at = part * heads + k
+            hit = jnp.broadcast_to(slots_ref[:, at : at + 1], (per_head, pixels)) == column
+            picks[k * per_head : (k + 1) * per_head, :] = hit.astype(F32).astype(BF16)
+        found = dot(picks[...], feat_ref[...], (1, 0)).astype(BF16)
+        out_ref[part * heads : (part + 1) * heads] = found.reshape((heads, per_head, found.shape[1]))
+
+
+def collect(slots, flat):
+    per_head, heads = slots.shape
+    pixels, channels = flat.shape
+    return pl.pallas_call(
+        collect_kernel,
+        out_shape=jax.ShapeDtypeStruct((heads, per_head, channels), BF16),
+        in_specs=vmem_spec(2),
+        out_specs=pl.BlockSpec(memory_space=pltpu.VMEM),
+        scratch_shapes=[pltpu.VMEM((16 * per_head, pixels), BF16)],
+        compiler_params=pltpu.CompilerParams(vmem_limit_bytes=40 * 2**20),
+        cost_estimate=pl.CostEstimate(flops=4 * 10**9, bytes_accessed=3 * 10**6, transcendentals=0),
+        name="collect",
+    )(slots, flat)
+
+
+def partial_kernel(place, mine_ref, other_ref, *refs):
+    y_at = place[2]
+    weights, out_ref = refs[:NY], refs[NY]
+    depth = weights[0].shape[1]
+    total = None
+    for step in range(NY):
+        start = lax.rem(y_at + NY - step, NY) * PITCH
+        cols = pl.ds(pl.multiple_of(start, PITCH), PITCH)
+        for ref, weight in ((mine_ref, weights[step][0]), (other_ref, weights[step][1])):
+            part = dot(ref[:, cols][:, :depth], weight, (1, 0))
+            total = part if total is None else total + part
+    out_ref[...] = total.astype(BF16)
+
+
+PITCH = 256
+
+
+def partial_sums(place, mine, other, weights):
+    return pl.pallas_call(
+        partial_kernel,
+        out_shape=jax.ShapeDtypeStruct((mine.shape[0], weights[0].shape[2]), BF16),
+        in_specs=[SMEM_SPEC] + vmem_spec(2 + NY),
+        out_specs=pl.BlockSpec(memory_space=pltpu.VMEM),
+        compiler_params=pltpu.CompilerParams(vmem_limit_bytes=40 * 2**20),
+        name="partial_sums",
+    )(place, mine, other, *weights)
+
+
+def shift_y(array, step):
+    row = NZ * NC
+    return lax.ppermute(array, "band", [(b, (b + step * row) % BAND) for b in range(BAND)])
 
 
 def gelu_parts(value):
@@ -174,9 +237,9 @@
     )(place, mine, other, labels, w_fc2, w_class)
 
 
-def first_kernel(place, mine_ref, other_ref, da2_ref, fc2_ref, x_ref,
-                 own_ref, s1_ref, s2_ref, s3_ref, a1, da1):
-    core, image = place[0], place[1]
+def first_kernel(place, mine_ref, other_ref, da2_ref, fc2_ref, *refs):
+    core, image, y_at = place[0], place[1], place[2]
+    x_refs, outs, a1, da1 = refs[:NY], refs[NY : NY + 4], refs[NY + 4], refs[NY + 5]
     join_halves(core, mine_ref, other_ref, a1)
     count, hid = a1.shape
 
@@ -189,26 +252,32 @@
     lax.fori_loop(0, count // ROW_BLOCK, block, 0)
     images = 4
     wide = hid // images
-    for step, out in enumerate((own_ref, s1_ref, s2_ref, s3_ref)):
+    tall = count // NY
+    depth = outs[0].shape[0]
+    for step, out in enumerate(outs):
         chunk = lax.rem(image + step, images)
         cols = pl.ds(pl.multiple_of(chunk * wide, wide), wide)
-        out[...] = dot(x_ref[...], da1[:, cols], (0, 0)).astype(out.dtype)
-
-
-def first_layer(place, mine, other, da2, w_fc2, x_cols):
+        total = None
+        for back in range(NY):
+            start = lax.rem(y_at + NY - back, NY) * tall
+            part = dot(x_refs[back][...], da1[pl.ds(pl.multiple_of(start, tall), tall), cols], (0, 0))
+            total = part if total is None else total + part
+        out[...] = total[:depth].astype(out.dtype)
+
+
+def first_layer(place, mine, other, da2, w_fc2, x_blocks, depth):
     count, hid = da2.shape
-    depth = x_cols.shape[1]
     wide = hid // 4
     struct = jax.ShapeDtypeStruct
     return pl.pallas_call(
         first_kernel,
         out_shape=[struct((depth, wide), F32)] + [struct((depth, wide), BF16)] * 3,
-        in_specs=[SMEM_SPEC] + vmem_spec(5),
+        in_specs=[SMEM_SPEC] + vmem_spec(4 + NY),
         out_specs=vmem_spec(4),
         scratch_shapes=[pltpu.VMEM((count, hid), BF16), pltpu.VMEM((count, hid), BF16)],
         compiler_params=pltpu.CompilerParams(vmem_limit_bytes=40 * 2**20),
         name="first_layer",
-    )(place, mine, other, da2, w_fc2, x_cols)
+    )(place, mine, other, da2, w_fc2, *x_blocks)
 
 
 SUM_ROWS = 192
@@ -303,19 +372,22 @@
     core = band % NC
     hid = w_fc2.shape[0]
     half = hid // NC
-    place = jnp.stack([core, image]).astype(jnp.int32)
+    y_at = band // (NC * NZ)
+    place = jnp.stack([core, image, y_at]).astype(jnp.int32)
 
     flat = features.reshape(rows * width, channels)
     capacity = pixel_slots.shape[3]
-    wanted = pixel_slots[0, :, 0, :].reshape(nband * capacity)
-    sending = flat[wanted].reshape(nband, capacity, channels)
+    sending = collect(jnp.transpose(pixel_slots[0, :, 0, :]), flat)
     received = lax.all_to_all(sending, "band", split_axis=0, concat_axis=0, tiled=True)
 
-    w_first = lax.optimization_barrier((w_fc1, sending))[0]
+    w_first, labels = lax.optimization_barrier((w_fc1, roi_labels, sending))[:2]
+    depth = w_first.shape[0]
     w_mine = lax.dynamic_slice_in_dim(w_first, core * half, half, 1)
     w_theirs = lax.dynamic_slice_in_dim(w_first, (1 - core) * half, half, 1)
-    w_other = lax.ppermute(w_theirs, "band", CORE_SWAP)
-    received, w_other = lax.optimization_barrier((received, w_other))
+    w_pair = jnp.stack([w_mine, lax.ppermute(w_theirs, "band", CORE_SWAP)])
+    weights = [w_pair] + [shift_y(w_pair, step) for step in range(1, NY)]
+    labels = lax.all_gather(labels[0], "band", axis=0, tiled=True)[:, None]
+    received, weights, labels = lax.optimization_barrier((received, weights, labels))
 
     received = received.reshape(nband * capacity, channels).astype(F32)
     roi_count, bins = sample_slot.shape[1:3]
@@ -328,20 +400,16 @@
         pooling = pooling + hits * corner_weights[:, corner : corner + 1]
     pooled = jnp.dot(pooling, received, precision=lax.Precision.HIGHEST, preferred_element_type=F32)
     pooled = pooled.astype(BF16).reshape(roi_count, bins, channels)
-    depth = w_fc1.shape[0]
     x_local = jnp.transpose(pooled, (0, 2, 1)).reshape(roi_count, nband, depth)
-    label_column = jnp.broadcast_to(roi_labels[0].astype(BF16)[:, None, None], (roi_count, nband, 1))
-    x_local = jnp.concatenate([x_local, label_column], axis=2).reshape(roi_count, nband * (depth + 1))
-    x_cols = lax.all_to_all(x_local, "band", split_axis=1, concat_axis=0, tiled=True)
-    labels = x_cols[:, depth:].astype(jnp.int32)
-    x_cols = x_cols[:, :depth]
-
-    x_other = lax.ppermute(x_cols, "band", CORE_SWAP)
-    partial = dot(x_cols, w_mine, (1, 0)) + dot(x_other, w_other, (1, 0))
-    count = x_cols.shape[0]
-    by_y = exchange(partial.astype(BF16).reshape(NY, count // NY, half), Y_GROUPS)
-    by_y = jnp.sum(by_y.astype(F32), axis=0).astype(BF16)
-    by_z = exchange(by_y.reshape(NZ, count // NY // NZ, half), Z_GROUPS)
+    x_local = jnp.pad(x_local, ((0, 0), (0, 0), (0, PITCH - depth)))
+    x_local = x_local.reshape(roi_count, NY, NZ * NC, PITCH).transpose(2, 0, 1, 3)
+    x_part = exchange(x_local.reshape(NZ * NC, roi_count, NY * PITCH), ZC_GROUPS)
+    x_part = x_part.reshape(NZ * NC * roi_count, NY * PITCH)
+
+    x_other = lax.ppermute(x_part, "band", CORE_SWAP)
+    partial = partial_sums(place, x_part, x_other, weights)
+    count = roi_count * nband
+    by_z = exchange(partial.reshape(NZ, count // NY // NZ, half), Z_GROUPS)
     a1_own = jnp.sum(by_z.astype(F32), axis=0).astype(BF16)
     a1_z = exchange(jnp.broadcast_to(a1_own[None], (NZ,) + a1_own.shape), Z_GROUPS)
     a1_z = a1_z.reshape(1, count // NY, half)
@@ -351,7 +419,12 @@
     class_wide = jnp.pad(w_class, ((0, 0), (0, 128 - classes)))
     da2, *parts = head(place, a1_mine, a1_other, labels, w_fc2, class_wide, classes)
     head_own, head_got = parts[0], shift_all(parts[1:])
-    parts = first_layer(place, a1_mine, a1_other, da2, w_fc2, x_cols)
+    x_part = lax.optimization_barrier((x_part, da2))[0]
+    x_blocks = [lax.dynamic_slice_in_dim(x_part, y_at * PITCH, PITCH, 1)]
+    for step in range(1, NY):
+        to = (y_at + step) % NY
+        x_blocks.append(shift_y(lax.dynamic_slice_in_dim(x_part, to * PITCH, PITCH, 1), step))
+    parts = first_layer(place, a1_mine, a1_other, da2, w_fc2, x_blocks, depth)
     head_got, parts = lax.optimization_barrier((head_got, parts))
     first_got = shift_all(parts[1:])
     total = sum_parts([head_own] + head_got, [parts[0]] + first_got)

time: 197 us -> 225 us (1.14)
  blocking collectives: 43 us -> 83.4 us
  waiting for transfers between devices: 55.1 us -> 33.3 us
  Pallas kernels: 24.5 us -> 31.7 us
  local copies, waits for them, and re-layouts: 14.5 us -> 17.9 us
    unnamed x0 -> x1, blocking collectives: none -> 35.1 us
    all_to_all x1, waiting for transfers between devices: 26.9 us -> 0.01 us  [shards(): lax.all_to_all(sending, 'band', split_axis=0, concat_axis=0, tiled=True)]
    ppermute x2 -> x8, waiting for transfers between devices: 1.7 us -> 26.2 us  [the longest x6 24.8 us: shift_y(): lax.ppermute(array, 'band', [(b, (b + step * row) % BAND) for b in range(...]
    all_to_all x1 -> x0, waiting for transfers between devices: 12 us -> none  [shards(): lax.all_to_all(x_local, 'band', split_axis=1, concat_axis=0, tiled=True)]
    unnamed x20 -> x52, local copies, waits for them, and re-layouts: 1.99 us -> 13.2 us
    gather x1 -> x0, local copies, waits for them, and re-layouts: 10.4 us -> none  [shards(): sending = flat[wanted].reshape(nband, capacity, channels)]
    ppermute x9, waiting for transfers between devices: 12.7 us -> 5.54 us  [shift_img(): lax.ppermute(array, 'img', [(i, (i + step) % size) for i in range(size)])]
    pallas_call x0 -> x2, Pallas kernels: none -> 6.52 us  [the longest x1 5.55 us: collect(): pl.pallas_call(collect_kernel, out_shape=jax.ShapeDtypeStruct((heads, per...]
  transfers between devices with their start and end apart: 20 -> 25, of which waited for: 12 -> 12; matrix products, arithmetic and copies ran while one was open for 1% -> 3% of each run, Pallas kernels for 7% -> 6%
where the time goes in v6:
time: 225 us; the launch traced here: 224 us
  blocking collectives  83.4 us (37%)
  starting transfers between devices  52.8 us (23%)
  waiting for transfers between devices  33.3 us (15%)
  Pallas kernels  31.7 us (14%)
  local copies, waits for them, and re-layouts  17.9 us (8%)
  matrix products  3.07 us (1%)
    all_to_all x4, blocking collectives, exchange(): lax.all_to_all(array, 'band', split_axis=0, concat_axis=0, tiled=True, ax...  48.3 us
    unnamed x1, blocking collectives  35.1 us
    ppermute x6, waiting for transfers between devices, shift_y(): lax.ppermute(array, 'band', [(b, (b + step * row) % BAND) for b in range(...  24.8 us
    unnamed x52, local copies, waits for them, and re-layouts  13.2 us
    all_to_all x1, starting transfers between devices, shards(): lax.all_to_all(sending, 'band', split_axis=0, concat_axis=0, tiled=True)  13.2 us
    ppermute x4, starting transfers between devices, shards(): other = [lax.ppermute(part[:tall], 'band', CORE_SWAP) for part in mine]  11.6 us
    ppermute x9, starting transfers between devices, shift_img(): lax.ppermute(array, 'img', [(i, (i + step) % size) for i in range(size)])  11.1 us
    pallas_call x1, Pallas kernels, rpn(): pl.pallas_call(rpn_kernel, out_shape=jax.ShapeDtypeStruct((anchors, rows,...  8.82 us
  transfers between devices with their start and end apart: 25, of which 12 were waited for; matrix products, arithmetic and copies ran while one was open for 3% of the time, Pallas kernels for 6%

profile of v6, /device:TPU:1, one launch (start us, length us, event | category | flops | bytes accessed | tf_op | source)
XLA Modules:
  0.0 224.0 jit_solution(1113500693961163510)
XLA Ops:
  3.0 5.5 %collect.1 = bf16[64,32,256]{2,1,0:T(8,128)(2,1)} custom-call(s32[32,64]{1,0:T(8,128)S(1)} %bitcast.57, bf16[4096,256]{1,0:T(8,128)(2,1)S(1)} %bitcast.55), custom_call_target="tpu_custom_call" | custom-call | flops 4000000000 | bytes 3000000 | tf_op jit(solution)/shard_map/collect/pallas_call | solution.py:112
  8.5 13.2 %all-to-all-start = ((bf16[64,32,256]{2,1,0:T(8,128)(2,1)}), bf16[64,32,256]{2,1,0:T(8,128)(2,1)S(1)}, u32[]{:S(2)}, u32[]{:S(2)}) async-start(bf16[64,32,256]{2,1,0:T(8,128)(2,1)} %collect.1), calls=%async_computation | async-start | bytes 2097152 | tf_op jit(solution)/shard_map/all_to_all | solution.py:381
  23.9 35.1 %all-reduce.2 = s32[512]{0:T(512)} all-reduce(s32[512]{0:T(512)S(1)} %bitcast_dynamic-update-slice_fusion), channel_id=2, replica_groups=mesh['img'=4,'band'=64] {'band'}, use_global_device_ids=true, to_apply=%add.2 | all-reduce | flops 512 | bytes 4096
  61.1 4.8 %collective-permute-done.3.refs_3_ = bf16[2,196,512]{2,1,0:T(8,128)(2,1)S(1)} collective-permute-done((bf16[2,196,512]{2,1,0:T(8,128)(2,1)S(1)}, bf16[2,196,512]{2,1,0:T(8,128)(2,1)S(1)}, u32[]{:S(2)}, u32[]{:S(2)}) %collective-permute-start.3) | collective-permute-done | bytes 401440 | tf_op jit(solution)/shard_map/ppermute | solution.py:154
  65.9 2.7 %collective-permute-done.2.refs_2_ = bf16[2,196,512]{2,1,0:T(8,128)(2,1)S(1)} collective-permute-done((bf16[2,196,512]{2,1,0:T(8,128)(2,1)S(1)}, bf16[2,196,512]{2,1,0:T(8,128)(2,1)S(1)}, u32[]{:S(2)}, u32[]{:S(2)}) %collective-permute-start.2) | collective-permute-done | bytes 401440 | tf_op jit(solution)/shard_map/ppermute | solution.py:154
  69.3 11.4 %collective-permute-done.1.refs_1_ = bf16[2,196,512]{2,1,0:T(8,128)(2,1)S(1)} collective-permute-done((bf16[2,196,512]{2,1,0:T(8,128)(2,1)S(1)}, bf16[2,196,512]{2,1,0:T(8,128)(2,1)S(1)}, u32[]{:S(2)}, u32[]{:S(2)}) %collective-permute-start.1) | collective-permute-done | bytes 401440 | tf_op jit(solution)/shard_map/ppermute | solution.py:154
  81.5 3.1 %fusion.17 = bf16[392,256]{1,0:T(8,128)(2,1)S(1)} fusion(bf16[2048,256]{1,0:T(8,128)(2,1)S(1)} %bitcast.60, f32[392]{0:T(512)S(1)} %bitcast.70, s32[392]{0:T(512)S(1)} %bitcast.66, f32[392]{0:T(512)S(1)} %bitcast.71, s32[392]{0:T(512)S(1)} %bitcast.67, f32[392]{0:T(512)S(1)} %bitcast.72, s32[392]{0:T(512)S(1)} %bitcast.68, f32[392]{0:T(512)S(1)} %bitcast.69, ...), kind=kOutput, calls=%fused_computation.21 | convolution fusion | flops 2475182080 | bytes 1261824 | tf_op jit(solution)/shard_map/dot_general | solution.py:401
  85.6 17.6 %all_to_all.25 = bf16[16,8,1024]{2,1,0:T(8,128)(2,1)S(1)} all-to-all(bf16[16,8,1024]{2,1,0:T(8,128)(2,1)S(1)} %reshape.43), channel_id=1, replica_groups={{0,1,2,3,4,5,6,7,8,9,10,11,12,13,14,15},{16,17,18,19,20,21,22,23,24,25,..., dimensions={0} | all-to-all | bytes 524288 | tf_op jit(solution)/shard_map/all_to_all | solution.py:81
  107.8 10.9 %all_to_all.26 = bf16[8,16,512]{2,1,0:T(8,128)(2,1)S(1)} all-to-all(bf16[8,16,512]{2,1,0:T(8,128)(2,1)S(1)} %bitcast.54), channel_id=1, replica_groups={{0,2,4,6,8,10,12,14},{1,3,5,7,9,11,13,15},{16,18,20,22,24,26,28,30},{17..., dimensions={0} | all-to-all | bytes 262144 | tf_op jit(solution)/shard_map/all_to_all | solution.py:81
  118.7 10.3 %all_to_all.27 = bf16[8,16,512]{2,1,0:T(8,128)(2,1)S(1)} all-to-all(bf16[8,16,512]{2,1,0:T(8,128)(2,1)S(1)} %broadcast_in_dim.21), channel_id=1, replica_groups={{0,2,4,6,8,10,12,14},{1,3,5,7,9,11,13,15},{16,18,20,22,24,26,28,30},{17..., dimensions={0} | all-to-all | bytes 262144 | tf_op jit(solution)/shard_map/all_to_all | solution.py:81
  129.1 9.4 %all_to_all.28 = bf16[4,128,512]{2,1,0:T(8,128)(2,1)S(1)} all-to-all(bf16[4,128,512]{2,1,0:T(8,128)(2,1)S(1)} %broadcast_in_dim.23), channel_id=1, replica_groups={{0,16,32,48},{1,17,33,49},{2,18,34,50},{3,19,35,51},{4,20,36,52},{5,21,..., dimensions={0} | all-to-all | bytes 1048576 | tf_op jit(solution)/shard_map/all_to_all | solution.py:81
  138.5 4.1 %collective-permute-start.5 = (bf16[512,512]{1,0:T(8,128)(2,1)S(1)}, bf16[512,512]{1,0:T(8,128)(2,1)S(1)}, u32[]{:S(2)}, u32[]{:S(2)}) collective-permute-start(bf16[512,512]{1,0:T(8,128)(2,1)S(1)} %bitcast.48), channel_id=1, source_target_pairs={{0,1},{1,0},{2,3},{3,2},{4,5},{5,4},{6,7},{7,6},{8,9},{9,8},{10,11... | collective-permute-start | bytes 1572872 | tf_op jit(solution)/shard_map/ppermute | solution.py:417
  142.6 1.8 copy.24
  149.6 6.5 %head.1 = (bf16[512,1024]{1,0:T(8,128)(2,1)S(1)}, f32[128,1152]{1,0:T(8,128)S(1)}, bf16[128,1152]{1,0:T(8,128)(2,1)}, bf16[128,1152]{1,0:T(8,128)(2,1)}, bf16[128,1152]{1,0:T(8,128)(2,1)}) custom-call(s32[3]{0:T(128)S(1)} %copy-done.14, bf16[512,512]{1,0:T(8,128)(2,1)S(1)} %bitcast.49, bf16[512,512]{1,0:T(8,128)(2,1)S(1)} %collective-permute-done.5.other_ref, ...), custom_call_target="tpu_custom_call" | custom-call | tf_op jit(solution)/shard_map/head/pallas_call | solution.py:223
  159.0 2.4 %collective-permute-start.7 = (bf16[128,1152]{1,0:T(8,128)(2,1)}, bf16[128,1152]{1,0:T(8,128)(2,1)}, u32[]{:S(2)}, u32[]{:S(2)}) collective-permute-start(bf16[128,1152]{1,0:T(8,128)(2,1)} %get-tuple-element.46), channel_id=1, source_target_pairs={{0,128},{64,192},{128,0},{192,64},{1,129},{65,193},{129,1},{193,65... | collective-permute-start | bytes 884744 | tf_op jit(solution)/shard_map/ppermute | solution.py:92
  168.2 2.7 %collective-permute-done.9.refs_1_ = bf16[128,256]{1,0:T(8,128)(2,1)S(1)} collective-permute-done((bf16[128,256]{1,0:T(8,128)(2,1)S(1)}, bf16[128,256]{1,0:T(8,128)(2,1)S(1)}, u32[]{:S(2)}, u32[]{:S(2)}) %collective-permute-start.9) | collective-permute-done | bytes 65568 | tf_op jit(solution)/shard_map/ppermute | solution.py:154
  172.2 5.2 %first_layer.1 = (f32[196,256]{1,0:T(8,128)S(1)}, bf16[196,256]{1,0:T(8,128)(2,1)S(1)}, bf16[196,256]{1,0:T(8,128)(2,1)S(1)}, bf16[196,256]{1,0:T(8,128)(2,1)S(1)}) custom-call(s32[3]{0:T(128)S(1)} %copy-done.14, bf16[512,512]{1,0:T(8,128)(2,1)S(1)} %bitcast.50, bf16[512,512]{1,0:T(8,128)(2,1)S(1)} %collective-permute-done.5.other_ref, ...), custom_call_target="tpu_custom_call" | custom-call | tf_op jit(solution)/shard_map/first_layer/pallas_call | solution.py:272
  180.2 3.1 %collective-permute-done.12.refs_5_ = bf16[196,256]{1,0:T(8,128)(2,1)S(1)} collective-permute-done((bf16[196,256]{1,0:T(8,128)(2,1)S(1)}, bf16[196,256]{1,0:T(8,128)(2,1)S(1)}, u32[]{:S(2)}, u32[]{:S(2)}) %collective-permute-start.12) | collective-permute-done | bytes 100384 | tf_op jit(solution)/shard_map/ppermute | solution.py:92
  185.4 5.8 %collective-permute-start.17 = (bf16[1,512,256]{2,1,0:T(8,128)(2,1)S(1)}, bf16[1,512,256]{2,1,0:T(8,128)(2,1)S(1)}, u32[]{:S(2)}, u32[]{:S(2)}) collective-permute-start(bf16[1,512,256]{2,1,0:T(8,128)(2,1)S(1)} %get-tuple-element.68), channel_id=1, source_target_pairs={{1,0},{2,1},{3,2},{4,3},{5,4},{6,5},{7,6},{8,7},{9,8},{10,9},{11,1... | collective-permute-start | bytes 786440 | tf_op jit(solution)/shard_map/ppermute | solution.py:24
  191.2 2.1 collective-permute-start.16
  193.4 2.3 %collective-permute-start.19 = (bf16[192,1152]{1,0:T(8,128)(2,1)S(1)}, bf16[192,1152]{1,0:T(8,128)(2,1)S(1)}, u32[]{:S(2)}, u32[]{:S(2)}) collective-permute-start(bf16[192,1152]{1,0:T(8,128)(2,1)S(1)} %sum_parts.1.refs_0_), channel_id=1, source_target_pairs={{0,192},{64,0},{128,64},{192,128},{1,193},{65,1},{129,65},{193,129... | collective-permute-start | bytes 1327112 | tf_op jit(solution)/shard_map/ppermute | solution.py:92
  197.8 8.8 %rpn.1 = bf16[15,8,512]{2,1,0:T(8,128)(2,1)} custom-call(bf16[1,512,256]{2,1,0:T(8,128)(2,1)S(1)} %collective-permute-done.16.before_ref, bf16[8,512,256]{2,1,0:T(8,128)(2,1)S(1)} %bitcast.56, bf16[1,512,256]{2,1,0:T(8,128)(2,1)S(1)} %collective-permute-done.17.after_ref, bf16[3,3,256,256]{3,2,1,0:T(8,128)(2,1)S(1)} %copy-done.15, bf16[15,256]{1,0:T(8,128)(2,1)S(1)} %bitcast.58), custom_call_target="tpu_custom_call" | custom-call | flops 8999999488 | bytes 4000000 | tf_op jit(solution)/shard_map/rpn/pallas_call | solution.py:57
  206.7 9.0 %collective-permute-start.23 = (bf16[128,1152]{1,0:T(8,128)(2,1)S(1)}, bf16[128,1152]{1,0:T(8,128)(2,1)S(1)}, u32[]{:S(2)}, u32[]{:S(2)}) collective-permute-start(bf16[128,1152]{1,0:T(8,128)(2,1)S(1)} %slice.65), channel_id=1, source_target_pairs={{0,1},{1,0},{2,3},{3,2},{4,5},{5,4},{6,7},{7,6},{8,9},{9,8},{10,11... | collective-permute-start | bytes 884744 | tf_op jit(solution)/shard_map/ppermute | solution.py:437
  220.7 3.3 %assemble.1 = (f32[196,1024]{1,0:T(8,128)}, f32[1024,1024]{1,0:T(8,128)}, f32[81,1024]{1,0:T(8,128)}) custom-call(s32[3]{0:T(128)S(1)} %copy-done.14, bf16[192,1152]{1,0:T(8,128)(2,1)S(1)} %sum_parts.1.refs_0_, bf16[192,1152]{1,0:T(8,128)(2,1)S(1)} %collective-permute-done.18.refs_1_, bf16[192,1152]{1,0:T(8,128)(2,1)S(1)} %collective-permute-done.15.refs_2_, ...), custom_call_target="tpu_custom_call" | custom-call | tf_op jit(solution)/shard_map/assemble/pallas_call | solution.py:343
  (115 shorter events, 41.3 us)
Async XLA Ops:
  8.5 73.0 %all-to-all-start = ((bf16[64,32,256]{2,1,0:T(8,128)(2,1)}), bf16[64,32,256]{2,1,0:T(8,128)(2,1)S(1)}, u32[]{:S(2)}, u32[]{:S(2)}) async-start(bf16[64,32,256]{2,1,0:T(8,128)(2,1)} %collect.1), calls=%async_computation | async-start | bytes 2097152 | tf_op jit(solution)/shard_map/all_to_all | solution.py:381
  21.8 37.2 %collective-permute-start = (bf16[196,512]{1,0:T(8,128)(2,1)S(1)}, bf16[196,512]{1,0:T(8,128)(2,1)S(1)}, u32[]{:S(2)}, u32[]{:S(2)}) collective-permute-start(bf16[196,512]{1,0:T(8,128)(2,1)S(1)} %get-tuple-element.71), channel_id=1, source_target_pairs={{0,1},{1,0},{2,3},{3,2},{4,5},{5,4},{6,7},{7,6},{8,9},{9,8},{10,11... | collective-permute-start | bytes 602120 | tf_op jit(solution)/shard_map/ppermute | solution.py:387
  59.0 6.9 %collective-permute-start.3 = (bf16[2,196,512]{2,1,0:T(8,128)(2,1)S(1)}, bf16[2,196,512]{2,1,0:T(8,128)(2,1)S(1)}, u32[]{:S(2)}, u32[]{:S(2)}) collective-permute-start(bf16[2,196,512]{2,1,0:T(8,128)(2,1)S(1)} %pad_maximum_fusion.refs_0_), channel_id=1, source_target_pairs={{0,48},{1,49},{2,50},{3,51},{4,52},{5,53},{6,54},{7,55},{8,56},{9,... | collective-permute-start | bytes 1204232 | tf_op jit(solution)/shard_map/ppermute | solution.py:154
  59.7 8.9 %collective-permute-start.2 = (bf16[2,196,512]{2,1,0:T(8,128)(2,1)S(1)}, bf16[2,196,512]{2,1,0:T(8,128)(2,1)S(1)}, u32[]{:S(2)}, u32[]{:S(2)}) collective-permute-start(bf16[2,196,512]{2,1,0:T(8,128)(2,1)S(1)} %pad_maximum_fusion.refs_0_), channel_id=1, source_target_pairs={{0,32},{1,33},{2,34},{3,35},{4,36},{5,37},{6,38},{7,39},{8,40},{9,... | collective-permute-start | bytes 1204232 | tf_op jit(solution)/shard_map/ppermute | solution.py:154
  61.0 19.7 %collective-permute-start.1 = (bf16[2,196,512]{2,1,0:T(8,128)(2,1)S(1)}, bf16[2,196,512]{2,1,0:T(8,128)(2,1)S(1)}, u32[]{:S(2)}, u32[]{:S(2)}) collective-permute-start(bf16[2,196,512]{2,1,0:T(8,128)(2,1)S(1)} %pad_maximum_fusion.refs_0_), channel_id=1, source_target_pairs={{0,16},{1,17},{2,18},{3,19},{4,20},{5,21},{6,22},{7,23},{8,24},{9,... | collective-permute-start | bytes 1204232 | tf_op jit(solution)/shard_map/ppermute | solution.py:154
  138.5 9.1 %collective-permute-start.5 = (bf16[512,512]{1,0:T(8,128)(2,1)S(1)}, bf16[512,512]{1,0:T(8,128)(2,1)S(1)}, u32[]{:S(2)}, u32[]{:S(2)}) collective-permute-start(bf16[512,512]{1,0:T(8,128)(2,1)S(1)} %bitcast.48), channel_id=1, source_target_pairs={{0,1},{1,0},{2,3},{3,2},{4,5},{5,4},{6,7},{7,6},{8,9},{9,8},{10,11... | collective-permute-start | bytes 1572872 | tf_op jit(solution)/shard_map/ppermute | solution.py:417
  157.8 19.6 %collective-permute-start.6 = (bf16[128,1152]{1,0:T(8,128)(2,1)}, bf16[128,1152]{1,0:T(8,128)(2,1)}, u32[]{:S(2)}, u32[]{:S(2)}) collective-permute-start(bf16[128,1152]{1,0:T(8,128)(2,1)} %get-tuple-element.45), channel_id=1, source_target_pairs={{0,64},{64,128},{128,192},{192,0},{1,65},{65,129},{129,193},{193,1... | collective-permute-start | bytes 884744 | tf_op jit(solution)/shard_map/ppermute | solution.py:92
  159.0 18.4 %collective-permute-start.7 = (bf16[128,1152]{1,0:T(8,128)(2,1)}, bf16[128,1152]{1,0:T(8,128)(2,1)}, u32[]{:S(2)}, u32[]{:S(2)}) collective-permute-start(bf16[128,1152]{1,0:T(8,128)(2,1)} %get-tuple-element.46), channel_id=1, source_target_pairs={{0,128},{64,192},{128,0},{192,64},{1,129},{65,193},{129,1},{193,65... | collective-permute-start | bytes 884744 | tf_op jit(solution)/shard_map/ppermute | solution.py:92
  161.5 15.9 %collective-permute-start.8 = (bf16[128,1152]{1,0:T(8,128)(2,1)}, bf16[128,1152]{1,0:T(8,128)(2,1)}, u32[]{:S(2)}, u32[]{:S(2)}) collective-permute-start(bf16[128,1152]{1,0:T(8,128)(2,1)} %get-tuple-element.47), channel_id=1, source_target_pairs={{0,192},{64,0},{128,64},{192,128},{1,193},{65,1},{129,65},{193,129... | collective-permute-start | bytes 884744 | tf_op jit(solution)/shard_map/ppermute | solution.py:92
  162.6 3.6 %collective-permute-start.11 = (bf16[128,256]{1,0:T(8,128)(2,1)S(1)}, bf16[128,256]{1,0:T(8,128)(2,1)S(1)}, u32[]{:S(2)}, u32[]{:S(2)}) collective-permute-start(bf16[128,256]{1,0:T(8,128)(2,1)S(1)} %get-tuple-element.72), channel_id=1, source_target_pairs={{0,48},{1,49},{2,50},{3,51},{4,52},{5,53},{6,54},{7,55},{8,56},{9,... | collective-permute-start | bytes 196616 | tf_op jit(solution)/shard_map/ppermute | solution.py:154
  163.6 4.6 %collective-permute-start.10 = (bf16[128,256]{1,0:T(8,128)(2,1)S(1)}, bf16[128,256]{1,0:T(8,128)(2,1)S(1)}, u32[]{:S(2)}, u32[]{:S(2)}) collective-permute-start(bf16[128,256]{1,0:T(8,128)(2,1)S(1)} %get-tuple-element.73), channel_id=1, source_target_pairs={{0,32},{1,33},{2,34},{3,35},{4,36},{5,37},{6,38},{7,39},{8,40},{9,... | collective-permute-start | bytes 196616 | tf_op jit(solution)/shard_map/ppermute | solution.py:154
  166.2 4.7 %collective-permute-start.9 = (bf16[128,256]{1,0:T(8,128)(2,1)S(1)}, bf16[128,256]{1,0:T(8,128)(2,1)S(1)}, u32[]{:S(2)}, u32[]{:S(2)}) collective-permute-start(bf16[128,256]{1,0:T(8,128)(2,1)S(1)} %get-tuple-element.74), channel_id=1, source_target_pairs={{0,16},{1,17},{2,18},{3,19},{4,20},{5,21},{6,22},{7,23},{8,24},{9,... | collective-permute-start | bytes 196616 | tf_op jit(solution)/shard_map/ppermute | solution.py:154
  177.4 5.9 %collective-permute-start.12 = (bf16[196,256]{1,0:T(8,128)(2,1)S(1)}, bf16[196,256]{1,0:T(8,128)(2,1)S(1)}, u32[]{:S(2)}, u32[]{:S(2)}) collective-permute-start(bf16[196,256]{1,0:T(8,128)(2,1)S(1)} %get-tuple-element.58), channel_id=1, source_target_pairs={{0,64},{64,128},{128,192},{192,0},{1,65},{65,129},{129,193},{193,1... | collective-permute-start | bytes 301064 | tf_op jit(solution)/shard_map/ppermute | solution.py:92
  177.7 5.6 %collective-permute-start.13 = (bf16[196,256]{1,0:T(8,128)(2,1)S(1)}, bf16[196,256]{1,0:T(8,128)(2,1)S(1)}, u32[]{:S(2)}, u32[]{:S(2)}) collective-permute-start(bf16[196,256]{1,0:T(8,128)(2,1)S(1)} %get-tuple-element.59), channel_id=1, source_target_pairs={{0,128},{64,192},{128,0},{192,64},{1,129},{65,193},{129,1},{193,65... | collective-permute-start | bytes 301064 | tf_op jit(solution)/shard_map/ppermute | solution.py:92
  178.7 5.2 %collective-permute-start.14 = (bf16[196,256]{1,0:T(8,128)(2,1)S(1)}, bf16[196,256]{1,0:T(8,128)(2,1)S(1)}, u32[]{:S(2)}, u32[]{:S(2)}) collective-permute-start(bf16[196,256]{1,0:T(8,128)(2,1)S(1)} %get-tuple-element.60), channel_id=1, source_target_pairs={{0,192},{64,0},{128,64},{192,128},{1,193},{65,1},{129,65},{193,129... | collective-permute-start | bytes 301064 | tf_op jit(solution)/shard_map/ppermute | solution.py:92
  185.4 11.5 %collective-permute-start.17 = (bf16[1,512,256]{2,1,0:T(8,128)(2,1)S(1)}, bf16[1,512,256]{2,1,0:T(8,128)(2,1)S(1)}, u32[]{:S(2)}, u32[]{:S(2)}) collective-permute-start(bf16[1,512,256]{2,1,0:T(8,128)(2,1)S(1)} %get-tuple-element.68), channel_id=1, source_target_pairs={{1,0},{2,1},{3,2},{4,3},{5,4},{6,5},{7,6},{8,7},{9,8},{10,9},{11,1... | collective-permute-start | bytes 786440 | tf_op jit(solution)/shard_map/ppermute | solution.py:24
  191.2 6.6 %collective-permute-start.16 = (bf16[1,512,256]{2,1,0:T(8,128)(2,1)S(1)}, bf16[1,512,256]{2,1,0:T(8,128)(2,1)S(1)}, u32[]{:S(2)}, u32[]{:S(2)}) collective-permute-start(bf16[1,512,256]{2,1,0:T(8,128)(2,1)S(1)} %get-tuple-element.69), channel_id=1, source_target_pairs={{0,1},{1,2},{2,3},{3,4},{4,5},{5,6},{6,7},{7,8},{8,9},{9,10},{10,1... | collective-permute-start | bytes 786440 | tf_op jit(solution)/shard_map/ppermute | solution.py:23
  193.4 13.3 %collective-permute-start.19 = (bf16[192,1152]{1,0:T(8,128)(2,1)S(1)}, bf16[192,1152]{1,0:T(8,128)(2,1)S(1)}, u32[]{:S(2)}, u32[]{:S(2)}) collective-permute-start(bf16[192,1152]{1,0:T(8,128)(2,1)S(1)} %sum_parts.1.refs_0_), channel_id=1, source_target_pairs={{0,192},{64,0},{128,64},{192,128},{1,193},{65,1},{129,65},{193,129... | collective-permute-start | bytes 1327112 | tf_op jit(solution)/shard_map/ppermute | solution.py:92
  195.6 21.8 %collective-permute-start.18 = (bf16[192,1152]{1,0:T(8,128)(2,1)S(1)}, bf16[192,1152]{1,0:T(8,128)(2,1)S(1)}, u32[]{:S(2)}, u32[]{:S(2)}) collective-permute-start(bf16[192,1152]{1,0:T(8,128)(2,1)S(1)} %sum_parts.1.refs_0_), channel_id=1, source_target_pairs={{0,64},{64,128},{128,192},{192,0},{1,65},{65,129},{129,193},{193,1... | collective-permute-start | bytes 1327112 | tf_op jit(solution)/shard_map/ppermute | solution.py:92
  195.6 23.4 %collective-permute-start.15 = (bf16[192,1152]{1,0:T(8,128)(2,1)S(1)}, bf16[192,1152]{1,0:T(8,128)(2,1)S(1)}, u32[]{:S(2)}, u32[]{:S(2)}) collective-permute-start(bf16[192,1152]{1,0:T(8,128)(2,1)S(1)} %sum_parts.1.refs_0_), channel_id=1, source_target_pairs={{0,128},{64,192},{128,0},{192,64},{1,129},{65,193},{129,1},{193,65... | collective-permute-start | bytes 1327112 | tf_op jit(solution)/shard_map/ppermute | solution.py:92
  196.9 22.3 %collective-permute-start.20 = (bf16[128,1152]{1,0:T(8,128)(2,1)S(1)}, bf16[128,1152]{1,0:T(8,128)(2,1)S(1)}, u32[]{:S(2)}, u32[]{:S(2)}) collective-permute-start(bf16[128,1152]{1,0:T(8,128)(2,1)S(1)} %slice.52), channel_id=1, source_target_pairs={{0,1},{1,0},{2,3},{3,2},{4,5},{5,4},{6,7},{7,6},{8,9},{9,8},{10,11... | collective-permute-start | bytes 884744 | tf_op jit(solution)/shard_map/ppermute | solution.py:437
  206.7 12.5 %collective-permute-start.23 = (bf16[128,1152]{1,0:T(8,128)(2,1)S(1)}, bf16[128,1152]{1,0:T(8,128)(2,1)S(1)}, u32[]{:S(2)}, u32[]{:S(2)}) collective-permute-start(bf16[128,1152]{1,0:T(8,128)(2,1)S(1)} %slice.65), channel_id=1, source_target_pairs={{0,1},{1,0},{2,3},{3,2},{4,5},{5,4},{6,7},{7,6},{8,9},{9,8},{10,11... | collective-permute-start | bytes 884744 | tf_op jit(solution)/shard_map/ppermute | solution.py:437
  217.4 2.8 %collective-permute-start.21 = (bf16[128,1152]{1,0:T(8,128)(2,1)S(1)}, bf16[128,1152]{1,0:T(8,128)(2,1)S(1)}, u32[]{:S(2)}, u32[]{:S(2)}) collective-permute-start(bf16[128,1152]{1,0:T(8,128)(2,1)S(1)} %slice.64), channel_id=1, source_target_pairs={{0,1},{1,0},{2,3},{3,2},{4,5},{5,4},{6,7},{7,6},{8,9},{9,8},{10,11... | collective-permute-start | bytes 884744 | tf_op jit(solution)/shard_map/ppermute | solution.py:437
  219.1 1.7 collective-permute-start.22
  (24 other events, 292.8 us)

commit v7 on v6

--- a/solution.py
+++ b/solution.py
@@ -10,9 +10,9 @@
 NY, NZ, NC = 4, 8, 2
 BAND = NY * NZ * NC
 F32, BF16 = jnp.float32, jnp.bfloat16
+VMEM = 24 * 2**20
 CORE_SWAP = [(b, b ^ 1) for b in range(BAND)]
 Z_GROUPS = [[(y * NZ + z) * NC + c for z in range(NZ)] for y in range(NY) for c in range(NC)]
-ZC_GROUPS = [[y * NZ * NC + k for k in range(NZ * NC)] for y in range(NY)]
 Y_GROUPS = [[(y * NZ + z) * NC + c for y in range(NY)] for z in range(NZ) for c in range(NC)]
 
 
@@ -63,7 +63,7 @@
             pltpu.VMEM((rows + 2, width, channels), BF16),
             pltpu.VMEM((rows, anchors, width), F32),
         ],
-        compiler_params=pltpu.CompilerParams(vmem_limit_bytes=40 * 2**20),
+        compiler_params=pltpu.CompilerParams(vmem_limit_bytes=VMEM),
         cost_estimate=pl.CostEstimate(flops=9 * 10**9, bytes_accessed=4 * 10**6, transcendentals=0),
         name="rpn",
     )(before, features[0], after, w_rpn, w_anchor.T)
@@ -115,38 +115,58 @@
         in_specs=vmem_spec(2),
         out_specs=pl.BlockSpec(memory_space=pltpu.VMEM),
         scratch_shapes=[pltpu.VMEM((16 * per_head, pixels), BF16)],
-        compiler_params=pltpu.CompilerParams(vmem_limit_bytes=40 * 2**20),
+        compiler_params=pltpu.CompilerParams(vmem_limit_bytes=VMEM),
         cost_estimate=pl.CostEstimate(flops=4 * 10**9, bytes_accessed=3 * 10**6, transcendentals=0),
         name="collect",
     )(slots, flat)
 
 
-def partial_kernel(place, mine_ref, other_ref, *refs):
-    y_at = place[2]
+def pair_kernel(mine_ref, other_ref, out_ref):
+    depth = mine_ref.shape[0]
+    out_ref[...] = jnp.zeros_like(out_ref)
+    out_ref[:depth, :] = mine_ref[...]
+    out_ref[TALL : TALL + depth, :] = other_ref[...]
+
+
+def pair(mine, other):
+    return pl.pallas_call(
+        pair_kernel,
+        out_shape=jax.ShapeDtypeStruct((TALL + SHORT,) + mine.shape[1:], BF16),
+        in_specs=vmem_spec(2),
+        out_specs=pl.BlockSpec(memory_space=pltpu.VMEM),
+        name="pair",
+    )(mine, other)
+
+
+def partial_kernel(place, x_ref, *refs):
+    core, y_at = place[0], place[2]
     weights, out_ref = refs[:NY], refs[NY]
-    depth = weights[0].shape[1]
     total = None
     for step in range(NY):
-        start = lax.rem(y_at + NY - step, NY) * PITCH
-        cols = pl.ds(pl.multiple_of(start, PITCH), PITCH)
-        for ref, weight in ((mine_ref, weights[step][0]), (other_ref, weights[step][1])):
-            part = dot(ref[:, cols][:, :depth], weight, (1, 0))
+        row = lax.rem(y_at + NY - step, NY)
+        for index, side in enumerate((core, 1 - core)):
+            start = (side * NY + row) * PITCH
+            cols = pl.ds(pl.multiple_of(start, PITCH), PITCH)
+            size = (TALL, SHORT)[index]
+            weight = weights[step][index * TALL : index * TALL + size, :]
+            part = dot(x_ref[:, cols][:, :size], weight, (1, 0))
             total = part if total is None else total + part
     out_ref[...] = total.astype(BF16)
 
 
 PITCH = 256
-
-
-def partial_sums(place, mine, other, weights):
+TALL, SHORT = 208, 200
+
+
+def partial_sums(place, x_part, weights):
     return pl.pallas_call(
         partial_kernel,
-        out_shape=jax.ShapeDtypeStruct((mine.shape[0], weights[0].shape[2]), BF16),
-        in_specs=[SMEM_SPEC] + vmem_spec(2 + NY),
-        out_specs=pl.BlockSpec(memory_space=pltpu.VMEM),
-        compiler_params=pltpu.CompilerParams(vmem_limit_bytes=40 * 2**20),
+        out_shape=jax.ShapeDtypeStruct((x_part.shape[0], weights[0].shape[1]), BF16),
+        in_specs=[SMEM_SPEC] + vmem_spec(1 + NY),
+        out_specs=pl.BlockSpec(memory_space=pltpu.VMEM),
+        compiler_params=pltpu.CompilerParams(vmem_limit_bytes=VMEM),
         name="partial_sums",
-    )(place, mine, other, *weights)
+    )(place, x_part, *weights)
 
 
 def shift_y(array, step):
@@ -173,111 +193,120 @@
 ROW_BLOCK = 128
 
 
-def join_halves(core, mine_ref, other_ref, whole_ref):
-    half = mine_ref.shape[1]
-    whole_ref[:, pl.ds(pl.multiple_of(core * half, half), half)] = mine_ref[...]
-    whole_ref[:, pl.ds(pl.multiple_of((1 - core) * half, half), half)] = other_ref[...]
-
-
-def head_kernel(classes, place, mine_ref, other_ref, labels_ref, fc2_ref, class_ref,
-                da2_ref, own_ref, s1_ref, s2_ref, s3_ref, a1, h1, h2, dlog):
+def order_rows(y_at, x_refs, whole_ref, lanes):
+    tall = x_refs[0].shape[0] // NC
+    for back, ref in enumerate(x_refs):
+        row = lax.rem(y_at + NY - back, NY) * tall
+        for side in range(NC):
+            at = pl.ds(pl.multiple_of(side * NY * tall + row, tall), tall)
+            whole_ref[at, :] = ref[side * tall : (side + 1) * tall, lanes].astype(whole_ref.dtype)
+
+
+def head_kernel(place, mine_ref, other_ref, fc2_ref, class_ref, da2_ref, *refs):
+    sends, (h1, h2, dlog) = refs[:4], refs[4:]
     core, image = place[0], place[1]
-    join_halves(core, mine_ref, other_ref, a1)
-    count, hid = a1.shape
-    lanes = class_ref.shape[1]
-
-    def block(step, carry):
-        rows = pl.ds(pl.multiple_of(step * ROW_BLOCK, ROW_BLOCK), ROW_BLOCK)
-        hidden = gelu_of(a1[rows, :].astype(F32)).astype(BF16)
+    classes = class_ref.shape[0]
+    hid = fc2_ref.shape[0]
+    for step in range(da2_ref.shape[0] // ROW_BLOCK):
+        rows = slice(step * ROW_BLOCK, (step + 1) * ROW_BLOCK)
+        steps = mine_ref.shape[0] // ROW_BLOCK
+        ref = mine_ref if step < steps else other_ref
+        at = step % steps * ROW_BLOCK
+        hidden = gelu_of(ref[at : at + ROW_BLOCK, :hid].astype(F32)).astype(BF16)
         h1[rows, :] = hidden
         a2 = dot(hidden, fc2_ref[...], (1, 0))
         second = gelu_of(a2).astype(BF16)
         h2[rows, :] = second
-        logits = dot(second, class_ref[...], (1, 0))
-        column = lax.broadcasted_iota(jnp.int32, (ROW_BLOCK, lanes), 1)
-        expo = jnp.where(column < classes, jnp.exp(logits), 0.0)
+        logits = dot(second, class_ref[...], (1, 1))
+        column = lax.broadcasted_iota(jnp.int32, (ROW_BLOCK, classes), 1)
+        expo = jnp.exp(logits)
         prob = expo / jnp.sum(expo, axis=1, keepdims=True)
-        onehot = (labels_ref[rows, :] == column).astype(F32)
+        labels = ref[at : at + ROW_BLOCK, hid:].astype(F32)[:, :1].astype(jnp.int32)
+        onehot = (labels == column).astype(F32)
         dlogits = (prob - onehot).astype(BF16)
         dlog[rows, :] = dlogits
-        dh2 = dot(dlogits, class_ref[...], (1, 1))
+        dh2 = dot(dlogits, class_ref[...], (1, 0))
         da2_ref[rows, :] = (dh2 * slope_of(a2)).astype(BF16)
-        return carry
-
-    lax.fori_loop(0, count // ROW_BLOCK, block, 0)
     images = 4
     wide = hid // NC // images
-    for step, out in enumerate((own_ref, s1_ref, s2_ref, s3_ref)):
+    for step, out in enumerate(sends):
         chunk = lax.rem(image + step, images)
         cols = pl.ds(pl.multiple_of(core * (hid // NC) + chunk * wide, wide), wide)
         out[:, :hid] = dot(h1[:, cols], da2_ref[...], (0, 0)).astype(out.dtype)
-        out[:, hid:] = dot(dlog[...], h2[:, cols], (0, 0)).astype(out.dtype)
-
-
-def head(place, mine, other, labels, w_fc2, w_class, classes):
-    count, half = mine.shape
-    hid = w_fc2.shape[0]
-    lanes = w_class.shape[1]
-    wide = half // 4
+        out[:, hid:] = jnp.zeros((wide, out.shape[1] - hid), out.dtype)
+        out[:classes, hid:] = dot(dlog[...], h2[:, cols], (0, 0)).astype(out.dtype)
+
+
+def head(place, mine, other, w_fc2, w_class):
+    count, hid = 2 * mine.shape[0], w_fc2.shape[0]
+    classes = w_class.shape[1]
+    wide = hid // NC // 4
     struct = jax.ShapeDtypeStruct
     return pl.pallas_call(
-        functools.partial(head_kernel, classes),
-        out_shape=[struct((count, hid), BF16), struct((wide, hid + lanes), F32)]
-        + [struct((wide, hid + lanes), BF16)] * 3,
-        in_specs=[SMEM_SPEC] + vmem_spec(5),
+        head_kernel,
+        out_shape=[struct((count, hid), BF16), struct((wide, hid + 128), F32)]
+        + [struct((wide, hid + 128), BF16)] * 3,
+        in_specs=[SMEM_SPEC] + vmem_spec(4),
         out_specs=vmem_spec(5),
         scratch_shapes=[
             pltpu.VMEM((count, hid), BF16),
             pltpu.VMEM((count, hid), BF16),
-            pltpu.VMEM((count, hid), BF16),
-            pltpu.VMEM((count, lanes), BF16),
+            pltpu.VMEM((count, classes), BF16),
         ],
-        compiler_params=pltpu.CompilerParams(vmem_limit_bytes=40 * 2**20),
+        compiler_params=pltpu.CompilerParams(vmem_limit_bytes=VMEM),
         name="head",
-    )(place, mine, other, labels, w_fc2, w_class)
-
-
-def first_kernel(place, mine_ref, other_ref, da2_ref, fc2_ref, *refs):
-    core, image, y_at = place[0], place[1], place[2]
-    x_refs, outs, a1, da1 = refs[:NY], refs[NY : NY + 4], refs[NY + 4], refs[NY + 5]
-    join_halves(core, mine_ref, other_ref, a1)
-    count, hid = a1.shape
-
-    def block(step, carry):
-        rows = pl.ds(pl.multiple_of(step * ROW_BLOCK, ROW_BLOCK), ROW_BLOCK)
+    )(place, mine, other, w_fc2, w_class.T)
+
+
+def back_kernel(mine_ref, other_ref, da2_ref, fc2_ref, da1_ref):
+    count, hid = da2_ref.shape
+    for step in range(count // ROW_BLOCK):
+        rows = slice(step * ROW_BLOCK, (step + 1) * ROW_BLOCK)
+        steps = mine_ref.shape[0] // ROW_BLOCK
+        ref = mine_ref if step < steps else other_ref
+        at = step % steps * ROW_BLOCK
         dh1 = dot(da2_ref[rows, :], fc2_ref[...], (1, 1))
-        da1[rows, :] = (dh1 * slope_of(a1[rows, :].astype(F32))).astype(BF16)
-        return carry
-
-    lax.fori_loop(0, count // ROW_BLOCK, block, 0)
+        da1_ref[rows, :] = (dh1 * slope_of(ref[at : at + ROW_BLOCK, :hid].astype(F32))).astype(BF16)
+
+
+def back(mine, other, da2, w_fc2):
+    return pl.pallas_call(
+        back_kernel,
+        out_shape=jax.ShapeDtypeStruct(da2.shape, BF16),
+        in_specs=vmem_spec(4),
+        out_specs=pl.BlockSpec(memory_space=pltpu.VMEM),
+        compiler_params=pltpu.CompilerParams(vmem_limit_bytes=VMEM),
+        cost_estimate=pl.CostEstimate(flops=2 * 10**9, bytes_accessed=5 * 10**6, transcendentals=0),
+        name="back",
+    )(mine, other, da2, w_fc2)
+
+
+def first_kernel(place, da1_ref, *refs):
+    image, y_at = place[1], place[2]
+    x_refs, outs, rois = refs[:NY], refs[NY : NY + 4], refs[NY + 4]
+    order_rows(y_at, x_refs, rois, slice(None))
     images = 4
-    wide = hid // images
-    tall = count // NY
+    wide = da1_ref.shape[1] // images
     depth = outs[0].shape[0]
     for step, out in enumerate(outs):
         chunk = lax.rem(image + step, images)
         cols = pl.ds(pl.multiple_of(chunk * wide, wide), wide)
-        total = None
-        for back in range(NY):
-            start = lax.rem(y_at + NY - back, NY) * tall
-            part = dot(x_refs[back][...], da1[pl.ds(pl.multiple_of(start, tall), tall), cols], (0, 0))
-            total = part if total is None else total + part
-        out[...] = total[:depth].astype(out.dtype)
-
-
-def first_layer(place, mine, other, da2, w_fc2, x_blocks, depth):
-    count, hid = da2.shape
+        out[...] = dot(rois[...], da1_ref[:, cols], (0, 0))[:depth].astype(out.dtype)
+
+
+def first_layer(place, da1, x_blocks, depth):
+    count, hid = da1.shape
     wide = hid // 4
     struct = jax.ShapeDtypeStruct
     return pl.pallas_call(
         first_kernel,
         out_shape=[struct((depth, wide), F32)] + [struct((depth, wide), BF16)] * 3,
-        in_specs=[SMEM_SPEC] + vmem_spec(4 + NY),
+        in_specs=[SMEM_SPEC] + vmem_spec(1 + NY),
         out_specs=vmem_spec(4),
-        scratch_shapes=[pltpu.VMEM((count, hid), BF16), pltpu.VMEM((count, hid), BF16)],
-        compiler_params=pltpu.CompilerParams(vmem_limit_bytes=40 * 2**20),
+        scratch_shapes=[pltpu.VMEM((count, PITCH), BF16)],
+        compiler_params=pltpu.CompilerParams(vmem_limit_bytes=VMEM),
         name="first_layer",
-    )(place, mine, other, da2, w_fc2, *x_blocks)
+    )(place, da1, *x_blocks)
 
 
 SUM_ROWS = 192
@@ -309,7 +338,7 @@
         out_shape=jax.ShapeDtypeStruct((SUM_ROWS, wide), BF16),
         in_specs=vmem_spec(8),
         out_specs=pl.BlockSpec(memory_space=pltpu.VMEM),
-        compiler_params=pltpu.CompilerParams(vmem_limit_bytes=40 * 2**20),
+        compiler_params=pltpu.CompilerParams(vmem_limit_bytes=VMEM),
         name="sum_parts",
     )(*heads, *firsts)
 
@@ -345,7 +374,7 @@
         out_shape=[struct((depth, hid), F32), struct((hid, hid), F32), struct((classes, hid), F32)],
         in_specs=[SMEM_SPEC] + vmem_spec(8),
         out_specs=vmem_spec(3),
-        compiler_params=pltpu.CompilerParams(vmem_limit_bytes=40 * 2**20),
+        compiler_params=pltpu.CompilerParams(vmem_limit_bytes=VMEM),
         name="assemble",
     )(place, *mine, *other)
 
@@ -371,7 +400,6 @@
     band, image = lax.axis_index("band"), lax.axis_index("img")
     core = band % NC
     hid = w_fc2.shape[0]
-    half = hid // NC
     y_at = band // (NC * NZ)
     place = jnp.stack([core, image, y_at]).astype(jnp.int32)
 
@@ -380,14 +408,11 @@
     sending = collect(jnp.transpose(pixel_slots[0, :, 0, :]), flat)
     received = lax.all_to_all(sending, "band", split_axis=0, concat_axis=0, tiled=True)
 
-    w_first, labels = lax.optimization_barrier((w_fc1, roi_labels, sending))[:2]
+    w_first = lax.optimization_barrier((w_fc1, sending))[0]
     depth = w_first.shape[0]
-    w_mine = lax.dynamic_slice_in_dim(w_first, core * half, half, 1)
-    w_theirs = lax.dynamic_slice_in_dim(w_first, (1 - core) * half, half, 1)
-    w_pair = jnp.stack([w_mine, lax.ppermute(w_theirs, "band", CORE_SWAP)])
+    w_pair = pair(w_first, lax.ppermute(w_first, "band", CORE_SWAP))
     weights = [w_pair] + [shift_y(w_pair, step) for step in range(1, NY)]
-    labels = lax.all_gather(labels[0], "band", axis=0, tiled=True)[:, None]
-    received, weights, labels = lax.optimization_barrier((received, weights, labels))
+    received, weights = lax.optimization_barrier((received, weights))
 
     received = received.reshape(nband * capacity, channels).astype(F32)
     roi_count, bins = sample_slot.shape[1:3]
@@ -402,35 +427,42 @@
     pooled = pooled.astype(BF16).reshape(roi_count, bins, channels)
     x_local = jnp.transpose(pooled, (0, 2, 1)).reshape(roi_count, nband, depth)
     x_local = jnp.pad(x_local, ((0, 0), (0, 0), (0, PITCH - depth)))
-    x_local = x_local.reshape(roi_count, NY, NZ * NC, PITCH).transpose(2, 0, 1, 3)
-    x_part = exchange(x_local.reshape(NZ * NC, roi_count, NY * PITCH), ZC_GROUPS)
-    x_part = x_part.reshape(NZ * NC * roi_count, NY * PITCH)
-
-    x_other = lax.ppermute(x_part, "band", CORE_SWAP)
-    partial = partial_sums(place, x_part, x_other, weights)
-    count = roi_count * nband
-    by_z = exchange(partial.reshape(NZ, count // NY // NZ, half), Z_GROUPS)
+    x_local = x_local.reshape(roi_count, NY, NZ, NC, PITCH).transpose(2, 0, 3, 1, 4)
+    x_part = exchange(x_local.reshape(NZ, roi_count, NC * NY * PITCH), Z_GROUPS)
+    x_part = x_part.reshape(NZ * roi_count, NC * NY * PITCH)
+
+    across = NY * PITCH
+    x_mine = lax.dynamic_slice_in_dim(x_part, core * across, across, 1)
+    x_theirs = lax.dynamic_slice_in_dim(x_part, (1 - core) * across, across, 1)
+    x_both = jnp.concatenate([x_mine, lax.ppermute(x_theirs, "band", CORE_SWAP)], axis=0)
+    partial = partial_sums(place, x_part, weights)
+    partial, x_both = lax.optimization_barrier((partial, x_both))
+    by_z = exchange(partial.reshape(NZ, roi_count, hid), Z_GROUPS)
     a1_own = jnp.sum(by_z.astype(F32), axis=0).astype(BF16)
+    marks = jnp.broadcast_to(roi_labels[0].astype(BF16)[:, None], (roi_count, 128))
+    a1_own = jnp.concatenate([a1_own, marks], axis=1)
     a1_z = exchange(jnp.broadcast_to(a1_own[None], (NZ,) + a1_own.shape), Z_GROUPS)
-    a1_z = a1_z.reshape(1, count // NY, half)
-    a1_mine = exchange(jnp.broadcast_to(a1_z, (NY,) + a1_z.shape[1:]), Y_GROUPS).reshape(count, half)
+    a1_z = a1_z.reshape(1, NZ * roi_count, hid + 128)
+    a1_mine = exchange(jnp.broadcast_to(a1_z, (NY,) + a1_z.shape[1:]), Y_GROUPS)
+    a1_mine = a1_mine.reshape(NY * NZ * roi_count, hid + 128)
     a1_other = lax.ppermute(a1_mine, "band", CORE_SWAP)
     classes = w_class.shape[1]
-    class_wide = jnp.pad(w_class, ((0, 0), (0, 128 - classes)))
-    da2, *parts = head(place, a1_mine, a1_other, labels, w_fc2, class_wide, classes)
+    da2, *parts = head(place, a1_mine, a1_other, w_fc2, w_class)
     head_own, head_got = parts[0], shift_all(parts[1:])
-    x_part = lax.optimization_barrier((x_part, da2))[0]
-    x_blocks = [lax.dynamic_slice_in_dim(x_part, y_at * PITCH, PITCH, 1)]
+    x_both = lax.optimization_barrier((x_both, da2))[0]
+    x_blocks = [lax.dynamic_slice_in_dim(x_both, y_at * PITCH, PITCH, 1)]
     for step in range(1, NY):
         to = (y_at + step) % NY
-        x_blocks.append(shift_y(lax.dynamic_slice_in_dim(x_part, to * PITCH, PITCH, 1), step))
-    parts = first_layer(place, a1_mine, a1_other, da2, w_fc2, x_blocks, depth)
+        x_blocks.append(shift_y(lax.dynamic_slice_in_dim(x_both, to * PITCH, PITCH, 1), step))
+    da1 = back(a1_mine, a1_other, da2, w_fc2)
+    parts = first_layer(place, da1, x_blocks, depth)
+    inner = lax.optimization_barrier((features, parts[0]))[0]
+    before, after = halo(inner)
     head_got, parts = lax.optimization_barrier((head_got, parts))
     first_got = shift_all(parts[1:])
     total = sum_parts([head_own] + head_got, [parts[0]] + first_got)
-    total, inner = lax.optimization_barrier((total, features))
+    total, inner = lax.optimization_barrier((total, inner))
     mine = [total] + [shift_img(total, step) for step in range(1, 4)]
-    before, after = halo(inner)
     rpn_out = rpn(before, inner, after, w_rpn, w_anchor)
     mine[2], rpn_out = lax.optimization_barrier((mine[2], rpn_out))
     tall = head_own.shape[0]

time: 225 us -> 214 us (0.951)
  blocking collectives: 83.4 us -> 21.5 us
  waiting for transfers between devices: 33.3 us -> 65.7 us
  starting transfers between devices: 52.8 us -> 65.9 us
    unnamed x1 -> x0, blocking collectives: 35.1 us -> none
    all_to_all x4 -> x2, blocking collectives: 48.3 us -> 21.5 us  [exchange(): lax.all_to_all(array, 'band', split_axis=0, concat_axis=0, tiled=True, ax...]
    all_to_all x0 -> x2, waiting for transfers between devices: none -> 20.1 us  [exchange(): lax.all_to_all(array, 'band', split_axis=0, concat_axis=0, tiled=True, ax...]
    ppermute x6, waiting for transfers between devices: 24.8 us -> 37.5 us  [shift_y(): lax.ppermute(array, 'band', [(b, (b + step * row) % BAND) for b in range(...]
    all_to_all x0 -> x2, starting transfers between devices: none -> 8.6 us  [exchange(): lax.all_to_all(array, 'band', split_axis=0, concat_axis=0, tiled=True, ax...]
    pallas_call x2 -> x4, Pallas kernels: 7.44 us -> 14.1 us  [the longest x1 5.57 us: head(): pl.pallas_call(head_kernel, out_shape=[struct((count, hid), BF16), struct...]
    pallas_call x1, Pallas kernels: 5.18 us -> 1.05 us  [first_layer(): pl.pallas_call(first_kernel, out_shape=[struct((depth, wide), F32)] + [st...]
    unnamed x52 -> x37, local copies, waits for them, and re-layouts: 13.2 us -> 10.3 us
  transfers between devices with their start and end apart: 25 -> 27, of which waited for: 12 -> 11; matrix products, arithmetic and copies ran while one was open for 3% -> 4% of each run, Pallas kernels for 6% -> 9%
where the time goes in v7:
time: 214 us; the launch traced here: 213 us
  starting transfers between devices  65.9 us (31%)
  waiting for transfers between devices  65.7 us (31%)
  Pallas kernels  33.1 us (15%)
  blocking collectives  21.5 us (10%)
  local copies, waits for them, and re-layouts  19.8 us (9%)
  matrix products  4.96 us (2%)
    ppermute x6, waiting for transfers between devices, shift_y(): lax.ppermute(array, 'band', [(b, (b + step * row) % BAND) for b in range(...  37.5 us
    all_to_all x2, blocking collectives, exchange(): lax.all_to_all(array, 'band', split_axis=0, concat_axis=0, tiled=True, ax...  21.5 us
    all_to_all x2, waiting for transfers between devices, exchange(): lax.all_to_all(array, 'band', split_axis=0, concat_axis=0, tiled=True, ax...  20.1 us
    ppermute x9, starting transfers between devices, shift_img(): lax.ppermute(array, 'img', [(i, (i + step) % size) for i in range(size)])  13.4 us
    ppermute x4, starting transfers between devices, shards(): other = [lax.ppermute(part[:tall], 'band', CORE_SWAP) for part in mine]  13.3 us
    all_to_all x1, starting transfers between devices, shards(): lax.all_to_all(sending, 'band', split_axis=0, concat_axis=0, tiled=True)  13.2 us
    unnamed x37, local copies, waits for them, and re-layouts  10.3 us
    pallas_call x1, Pallas kernels, rpn(): pl.pallas_call(rpn_kernel, out_shape=jax.ShapeDtypeStruct((anchors, rows,...  8.82 us
  transfers between devices with their start and end apart: 27, of which 11 were waited for; matrix products, arithmetic and copies ran while one was open for 4% of the time, Pallas kernels for 9%

profile of v7, /device:TPU:1, one launch (start us, length us, event | category | flops | bytes accessed | tf_op | source)
XLA Modules:
  0.0 212.9 jit_solution(12645655105162597195)
XLA Ops:
  2.9 5.5 %collect.1 = bf16[64,32,256]{2,1,0:T(8,128)(2,1)} custom-call(s32[32,64]{1,0:T(8,128)S(1)} %bitcast.52, bf16[4096,256]{1,0:T(8,128)(2,1)S(1)} %bitcast.50), custom_call_target="tpu_custom_call" | custom-call | flops 4000000000 | bytes 3000000 | tf_op jit(solution)/shard_map/collect/pallas_call | solution.py:112
  8.5 13.2 %all-to-all-start = ((bf16[64,32,256]{2,1,0:T(8,128)(2,1)}), bf16[64,32,256]{2,1,0:T(8,128)(2,1)S(1)}, u32[]{:S(2)}, u32[]{:S(2)}) async-start(bf16[64,32,256]{2,1,0:T(8,128)(2,1)} %collect.1), calls=%async_computation | async-start | bytes 2097152 | tf_op jit(solution)/shard_map/all_to_all | solution.py:409
  26.4 2.7 %collective-permute-start.3 = (bf16[408,1024]{1,0:T(8,128)(2,1)}, bf16[408,1024]{1,0:T(8,128)(2,1)S(1)}, u32[]{:S(2)}, u32[]{:S(2)}) collective-permute-start(bf16[408,1024]{1,0:T(8,128)(2,1)} %pair.1.refs_0_), channel_id=1, source_target_pairs={{0,48},{1,49},{2,50},{3,51},{4,52},{5,53},{6,54},{7,55},{8,56},{9,... | collective-permute-start | bytes 2506760 | tf_op jit(solution)/shard_map/ppermute | solution.py:174
  38.6 16.5 %collective-permute-done.3.refs_3_ = bf16[408,1024]{1,0:T(8,128)(2,1)S(1)} collective-permute-done((bf16[408,1024]{1,0:T(8,128)(2,1)}, bf16[408,1024]{1,0:T(8,128)(2,1)S(1)}, u32[]{:S(2)}, u32[]{:S(2)}) %collective-permute-start.3) | collective-permute-done | bytes 835616 | tf_op jit(solution)/shard_map/ppermute | solution.py:174
  56.0 2.6 %collective-permute-done.2.refs_2_ = bf16[408,1024]{1,0:T(8,128)(2,1)S(1)} collective-permute-done((bf16[408,1024]{1,0:T(8,128)(2,1)}, bf16[408,1024]{1,0:T(8,128)(2,1)S(1)}, u32[]{:S(2)}, u32[]{:S(2)}) %collective-permute-start.2) | collective-permute-done | bytes 835616 | tf_op jit(solution)/shard_map/ppermute | solution.py:174
  58.6 18.4 %collective-permute-done.1.refs_1_ = bf16[408,1024]{1,0:T(8,128)(2,1)S(1)} collective-permute-done((bf16[408,1024]{1,0:T(8,128)(2,1)}, bf16[408,1024]{1,0:T(8,128)(2,1)S(1)}, u32[]{:S(2)}, u32[]{:S(2)}) %collective-permute-start.1) | collective-permute-done | bytes 835616 | tf_op jit(solution)/shard_map/ppermute | solution.py:174
  77.0 5.0 %fusion.17 = bf16[392,256]{1,0:T(8,128)(2,1)} fusion(bf16[2048,256]{1,0:T(8,128)(2,1)S(1)} %bitcast.55, f32[392]{0:T(512)} %bitcast.63, s32[392]{0:T(512)} %bitcast.59, f32[392]{0:T(512)} %bitcast.64, s32[392]{0:T(512)} %bitcast.60, f32[392]{0:T(512)} %bitcast.65, s32[392]{0:T(512)} %bitcast.61, f32[392]{0:T(512)} %bitcast.62, s32[392]{0:T(512)} %bitcast.58), kind=kOutput, calls=%fused_computation.21 | convolution fusion | flops 2475182080 | bytes 1261824 | tf_op jit(solution)/shard_map/dot_general | solution.py:426
  85.0 5.2 %all-to-all-start.1 = ((bf16[8,8,2048]{2,1,0:T(8,128)(2,1)}), bf16[8,8,2048]{2,1,0:T(8,128)(2,1)S(1)}, u32[]{:S(2)}, u32[]{:S(2)}) async-start(bf16[8,8,2048]{2,1,0:T(8,128)(2,1)} %reshape.49), calls=%async_computation.1 | async-start | bytes 524288 | tf_op jit(solution)/shard_map/all_to_all | solution.py:81
  90.2 10.7 %all-to-all-done.1 = bf16[8,8,2048]{2,1,0:T(8,128)(2,1)S(1)} async-done(((bf16[8,8,2048]{2,1,0:T(8,128)(2,1)}), bf16[8,8,2048]{2,1,0:T(8,128)(2,1)S(1)}, u32[]{:S(2)}, u32[]{:S(2)}) %all-to-all-start.1) | async-done | bytes 262176 | tf_op jit(solution)/shard_map/all_to_all | solution.py:81
  110.1 3.4 %all-to-all-start.2 = ((bf16[8,8,1024]{2,1,0:T(8,128)(2,1)}), bf16[8,8,1024]{2,1,0:T(8,128)(2,1)S(1)}, u32[]{:S(2)}, u32[]{:S(2)}) async-start(bf16[8,8,1024]{2,1,0:T(8,128)(2,1)} %bitcast.19), calls=%async_computation.2 | async-start | bytes 262144 | tf_op jit(solution)/shard_map/all_to_all | solution.py:81
  113.5 9.4 %all-to-all-done.2 = bf16[8,8,1024]{2,1,0:T(8,128)(2,1)S(1)} async-done(((bf16[8,8,1024]{2,1,0:T(8,128)(2,1)}), bf16[8,8,1024]{2,1,0:T(8,128)(2,1)S(1)}, u32[]{:S(2)}, u32[]{:S(2)}) %all-to-all-start.2) | async-done | bytes 131104 | tf_op jit(solution)/shard_map/all_to_all | solution.py:81
  123.0 10.8 %all_to_all.25 = bf16[8,8,1152]{2,1,0:T(8,128)(2,1)S(1)} all-to-all(bf16[8,8,1152]{2,1,0:T(8,128)(2,1)S(1)} %broadcast_in_dim.11), channel_id=1, replica_groups={{0,2,4,6,8,10,12,14},{1,3,5,7,9,11,13,15},{16,18,20,22,24,26,28,30},{17..., dimensions={0} | all-to-all | bytes 294912 | tf_op jit(solution)/shard_map/all_to_all | solution.py:81
  133.8 10.7 %all_to_all.26 = bf16[4,64,1152]{2,1,0:T(8,128)(2,1)S(1)} all-to-all(bf16[4,64,1152]{2,1,0:T(8,128)(2,1)S(1)} %broadcast_in_dim.26), channel_id=1, replica_groups={{0,16,32,48},{1,17,33,49},{2,18,34,50},{3,19,35,51},{4,20,36,52},{5,21,..., dimensions={0} | all-to-all | bytes 1179648 | tf_op jit(solution)/shard_map/all_to_all | solution.py:81
  144.6 3.2 %collective-permute-start.5 = (bf16[256,1152]{1,0:T(8,128)(2,1)S(1)}, bf16[256,1152]{1,0:T(8,128)(2,1)}, u32[]{:S(2)}, u32[]{:S(2)}) collective-permute-start(bf16[256,1152]{1,0:T(8,128)(2,1)S(1)} %bitcast.46), channel_id=1, source_target_pairs={{0,1},{1,0},{2,3},{3,2},{4,5},{5,4},{6,7},{7,6},{8,9},{9,8},{10,11... | collective-permute-start | bytes 1769480 | tf_op jit(solution)/shard_map/ppermute | solution.py:448
  149.5 5.6 %head.1 = (bf16[512,1024]{1,0:T(8,128)(2,1)S(1)}, f32[128,1152]{1,0:T(8,128)S(1)}, bf16[128,1152]{1,0:T(8,128)(2,1)S(1)}, bf16[128,1152]{1,0:T(8,128)(2,1)S(1)}, bf16[128,1152]{1,0:T(8,128)(2,1)S(1)}) custom-call(s32[3]{0:T(128)S(1)} %pad_add_fusion.place, bf16[256,1152]{1,0:T(8,128)(2,1)S(1)} %bitcast.47, ...), custom_call_target="tpu_custom_call" | custom-call | tf_op jit(solution)/shard_map/head/pallas_call | solution.py:245
  161.0 4.5 %back.1.da1_ref = bf16[512,1024]{1,0:T(8,128)(2,1)S(1)} custom-call(bf16[256,1152]{1,0:T(8,128)(2,1)S(1)} %bitcast.48, bf16[256,1152]{1,0:T(8,128)(2,1)} %collective-permute-done.5.other_ref, bf16[512,1024]{1,0:T(8,128)(2,1)S(1)} %get-tuple-element.48.da2_ref, bf16[1024,1024]{1,0:T(8,128)(2,1)S(1)} %copy-done.1), custom_call_target="tpu_custom_call" | custom-call | flops 2000000000 | bytes 5000000 | tf_op jit(solution)/shard_map/back/pallas_call | solution.py:273
  168.0 3.7 %collective-permute-start.17 = (bf16[1,512,256]{2,1,0:T(8,128)(2,1)S(1)}, bf16[1,512,256]{2,1,0:T(8,128)(2,1)S(1)}, u32[]{:S(2)}, u32[]{:S(2)}) collective-permute-start(bf16[1,512,256]{2,1,0:T(8,128)(2,1)S(1)} %get-tuple-element.70), channel_id=1, source_target_pairs={{1,0},{2,1},{3,2},{4,3},{5,4},{6,5},{7,6},{8,7},{9,8},{10,9},{11,1... | collective-permute-start | bytes 786440 | tf_op jit(solution)/shard_map/ppermute | solution.py:24
  178.5 3.2 %collective-permute-done.13.refs_6_ = bf16[196,256]{1,0:T(8,128)(2,1)S(1)} collective-permute-done((bf16[196,256]{1,0:T(8,128)(2,1)S(1)}, bf16[196,256]{1,0:T(8,128)(2,1)S(1)}, u32[]{:S(2)}, u32[]{:S(2)}) %collective-permute-start.13) | collective-permute-done | bytes 100384 | tf_op jit(solution)/shard_map/ppermute | solution.py:92
  182.0 2.5 %collective-permute-start.19 = (bf16[192,1152]{1,0:T(8,128)(2,1)S(1)}, bf16[192,1152]{1,0:T(8,128)(2,1)S(1)}, u32[]{:S(2)}, u32[]{:S(2)}) collective-permute-start(bf16[192,1152]{1,0:T(8,128)(2,1)S(1)} %sum_parts.1.refs_0_), channel_id=1, source_target_pairs={{0,192},{64,0},{128,64},{192,128},{1,193},{65,1},{129,65},{193,129... | collective-permute-start | bytes 1327112 | tf_op jit(solution)/shard_map/ppermute | solution.py:92
  185.8 2.5 %collective-permute-start.20 = (bf16[128,1152]{1,0:T(8,128)(2,1)S(1)}, bf16[128,1152]{1,0:T(8,128)(2,1)S(1)}, u32[]{:S(2)}, u32[]{:S(2)}) collective-permute-start(bf16[128,1152]{1,0:T(8,128)(2,1)S(1)} %slice.52), channel_id=1, source_target_pairs={{0,1},{1,0},{2,3},{3,2},{4,5},{5,4},{6,7},{7,6},{8,9},{9,8},{10,11... | collective-permute-start | bytes 884744 | tf_op jit(solution)/shard_map/ppermute | solution.py:469
  188.3 8.8 %rpn.1 = bf16[15,8,512]{2,1,0:T(8,128)(2,1)} custom-call(bf16[1,512,256]{2,1,0:T(8,128)(2,1)S(1)} %collective-permute-done.16.before_ref, bf16[8,512,256]{2,1,0:T(8,128)(2,1)S(1)} %bitcast.51, bf16[1,512,256]{2,1,0:T(8,128)(2,1)S(1)} %collective-permute-done.17.after_ref, bf16[3,3,256,256]{3,2,1,0:T(8,128)(2,1)S(1)} %copy-done.11, bf16[15,256]{1,0:T(8,128)(2,1)S(1)} %bitcast.53), custom_call_target="tpu_custom_call" | custom-call | flops 8999999488 | bytes 4000000 | tf_op jit(solution)/shard_map/rpn/pallas_call | solution.py:57
  197.2 7.3 %collective-permute-start.23 = (bf16[128,1152]{1,0:T(8,128)(2,1)S(1)}, bf16[128,1152]{1,0:T(8,128)(2,1)S(1)}, u32[]{:S(2)}, u32[]{:S(2)}) collective-permute-start(bf16[128,1152]{1,0:T(8,128)(2,1)S(1)} %slice.65), channel_id=1, source_target_pairs={{0,1},{1,0},{2,3},{3,2},{4,5},{5,4},{6,7},{7,6},{8,9},{9,8},{10,11... | collective-permute-start | bytes 884744 | tf_op jit(solution)/shard_map/ppermute | solution.py:469
  204.6 3.3 %collective-permute-start.21 = (bf16[128,1152]{1,0:T(8,128)(2,1)S(1)}, bf16[128,1152]{1,0:T(8,128)(2,1)S(1)}, u32[]{:S(2)}, u32[]{:S(2)}) collective-permute-start(bf16[128,1152]{1,0:T(8,128)(2,1)S(1)} %slice.64), channel_id=1, source_target_pairs={{0,1},{1,0},{2,3},{3,2},{4,5},{5,4},{6,7},{7,6},{8,9},{9,8},{10,11... | collective-permute-start | bytes 884744 | tf_op jit(solution)/shard_map/ppermute | solution.py:469
  209.6 3.3 %assemble.1 = (f32[196,1024]{1,0:T(8,128)}, f32[1024,1024]{1,0:T(8,128)}, f32[81,1024]{1,0:T(8,128)}) custom-call(s32[3]{0:T(128)S(1)} %pad_add_fusion.place, bf16[192,1152]{1,0:T(8,128)(2,1)S(1)} %sum_parts.1.refs_0_, bf16[192,1152]{1,0:T(8,128)(2,1)S(1)} %collective-permute-done.18.refs_1_, bf16[192,1152]{1,0:T(8,128)(2,1)S(1)} %collective-permute-done.15.refs_2_, ...), custom_call_target="tpu_custom_call" | custom-call | tf_op jit(solution)/shard_map/assemble/pallas_call | solution.py:372
  (104 shorter events, 50.0 us)
Async XLA Ops:
  8.5 68.5 %all-to-all-start = ((bf16[64,32,256]{2,1,0:T(8,128)(2,1)}), bf16[64,32,256]{2,1,0:T(8,128)(2,1)S(1)}, u32[]{:S(2)}, u32[]{:S(2)}) async-start(bf16[64,32,256]{2,1,0:T(8,128)(2,1)} %collect.1), calls=%async_computation | async-start | bytes 2097152 | tf_op jit(solution)/shard_map/all_to_all | solution.py:409
  26.4 28.6 %collective-permute-start.3 = (bf16[408,1024]{1,0:T(8,128)(2,1)}, bf16[408,1024]{1,0:T(8,128)(2,1)S(1)}, u32[]{:S(2)}, u32[]{:S(2)}) collective-permute-start(bf16[408,1024]{1,0:T(8,128)(2,1)} %pair.1.refs_0_), channel_id=1, source_target_pairs={{0,48},{1,49},{2,50},{3,51},{4,52},{5,53},{6,54},{7,55},{8,56},{9,... | collective-permute-start | bytes 2506760 | tf_op jit(solution)/shard_map/ppermute | solution.py:174
  29.2 29.4 %collective-permute-start.2 = (bf16[408,1024]{1,0:T(8,128)(2,1)}, bf16[408,1024]{1,0:T(8,128)(2,1)S(1)}, u32[]{:S(2)}, u32[]{:S(2)}) collective-permute-start(bf16[408,1024]{1,0:T(8,128)(2,1)} %pair.1.refs_0_), channel_id=1, source_target_pairs={{0,32},{1,33},{2,34},{3,35},{4,36},{5,37},{6,38},{7,39},{8,40},{9,... | collective-permute-start | bytes 2506760 | tf_op jit(solution)/shard_map/ppermute | solution.py:174
  29.5 47.4 %collective-permute-start.1 = (bf16[408,1024]{1,0:T(8,128)(2,1)}, bf16[408,1024]{1,0:T(8,128)(2,1)S(1)}, u32[]{:S(2)}, u32[]{:S(2)}) collective-permute-start(bf16[408,1024]{1,0:T(8,128)(2,1)} %pair.1.refs_0_), channel_id=1, source_target_pairs={{0,16},{1,17},{2,18},{3,19},{4,20},{5,21},{6,22},{7,23},{8,24},{9,... | collective-permute-start | bytes 2506760 | tf_op jit(solution)/shard_map/ppermute | solution.py:174
  85.0 15.9 %all-to-all-start.1 = ((bf16[8,8,2048]{2,1,0:T(8,128)(2,1)}), bf16[8,8,2048]{2,1,0:T(8,128)(2,1)S(1)}, u32[]{:S(2)}, u32[]{:S(2)}) async-start(bf16[8,8,2048]{2,1,0:T(8,128)(2,1)} %reshape.49), calls=%async_computation.1 | async-start | bytes 524288 | tf_op jit(solution)/shard_map/all_to_all | solution.py:81
  101.5 7.6 %collective-permute-start.4 = (bf16[64,1024]{1,0:T(8,128)(2,1)}, bf16[64,1024]{1,0:T(8,128)(2,1)}, u32[]{:S(2)}, u32[]{:S(2)}) collective-permute-start(bf16[64,1024]{1,0:T(8,128)(2,1)} %get-tuple-element.77), channel_id=1, source_target_pairs={{0,1},{1,0},{2,3},{3,2},{4,5},{5,4},{6,7},{7,6},{8,9},{9,8},{10,11... | collective-permute-start | bytes 393224 | tf_op jit(solution)/shard_map/ppermute | solution.py:437
  110.1 12.8 %all-to-all-start.2 = ((bf16[8,8,1024]{2,1,0:T(8,128)(2,1)}), bf16[8,8,1024]{2,1,0:T(8,128)(2,1)S(1)}, u32[]{:S(2)}, u32[]{:S(2)}) async-start(bf16[8,8,1024]{2,1,0:T(8,128)(2,1)} %bitcast.19), calls=%async_computation.2 | async-start | bytes 262144 | tf_op jit(solution)/shard_map/all_to_all | solution.py:81
  144.6 4.9 %collective-permute-start.5 = (bf16[256,1152]{1,0:T(8,128)(2,1)S(1)}, bf16[256,1152]{1,0:T(8,128)(2,1)}, u32[]{:S(2)}, u32[]{:S(2)}) collective-permute-start(bf16[256,1152]{1,0:T(8,128)(2,1)S(1)} %bitcast.46), channel_id=1, source_target_pairs={{0,1},{1,0},{2,3},{3,2},{4,5},{5,4},{6,7},{7,6},{8,9},{9,8},{10,11... | collective-permute-start | bytes 1769480 | tf_op jit(solution)/shard_map/ppermute | solution.py:448
  155.1 10.3 %collective-permute-start.11 = (bf16[128,256]{1,0:T(8,128)(2,1)S(1)}, bf16[128,256]{1,0:T(8,128)(2,1)S(1)}, u32[]{:S(2)}, u32[]{:S(2)}) collective-permute-start(bf16[128,256]{1,0:T(8,128)(2,1)S(1)} %get-tuple-element.72), channel_id=1, source_target_pairs={{0,48},{1,49},{2,50},{3,51},{4,52},{5,53},{6,54},{7,55},{8,56},{9,... | collective-permute-start | bytes 196616 | tf_op jit(solution)/shard_map/ppermute | solution.py:174
  156.1 10.8 %collective-permute-start.10 = (bf16[128,256]{1,0:T(8,128)(2,1)S(1)}, bf16[128,256]{1,0:T(8,128)(2,1)S(1)}, u32[]{:S(2)}, u32[]{:S(2)}) collective-permute-start(bf16[128,256]{1,0:T(8,128)(2,1)S(1)} %get-tuple-element.73), channel_id=1, source_target_pairs={{0,32},{1,33},{2,34},{3,35},{4,36},{5,37},{6,38},{7,39},{8,40},{9,... | collective-permute-start | bytes 196616 | tf_op jit(solution)/shard_map/ppermute | solution.py:174
  157.3 9.6 %collective-permute-start.9 = (bf16[128,256]{1,0:T(8,128)(2,1)S(1)}, bf16[128,256]{1,0:T(8,128)(2,1)S(1)}, u32[]{:S(2)}, u32[]{:S(2)}) collective-permute-start(bf16[128,256]{1,0:T(8,128)(2,1)S(1)} %get-tuple-element.74), channel_id=1, source_target_pairs={{0,16},{1,17},{2,18},{3,19},{4,20},{5,21},{6,22},{7,23},{8,24},{9,... | collective-permute-start | bytes 196616 | tf_op jit(solution)/shard_map/ppermute | solution.py:174
  157.3 16.4 %collective-permute-start.6 = (bf16[128,1152]{1,0:T(8,128)(2,1)S(1)}, bf16[128,1152]{1,0:T(8,128)(2,1)S(1)}, u32[]{:S(2)}, u32[]{:S(2)}) collective-permute-start(bf16[128,1152]{1,0:T(8,128)(2,1)S(1)} %get-tuple-element.45), channel_id=1, source_target_pairs={{0,64},{64,128},{128,192},{192,0},{1,65},{65,129},{129,193},{193,1... | collective-permute-start | bytes 884744 | tf_op jit(solution)/shard_map/ppermute | solution.py:92
  158.5 15.2 %collective-permute-start.7 = (bf16[128,1152]{1,0:T(8,128)(2,1)S(1)}, bf16[128,1152]{1,0:T(8,128)(2,1)S(1)}, u32[]{:S(2)}, u32[]{:S(2)}) collective-permute-start(bf16[128,1152]{1,0:T(8,128)(2,1)S(1)} %get-tuple-element.46), channel_id=1, source_target_pairs={{0,128},{64,192},{128,0},{192,64},{1,129},{65,193},{129,1},{193,65... | collective-permute-start | bytes 884744 | tf_op jit(solution)/shard_map/ppermute | solution.py:92
  165.5 8.2 %collective-permute-start.8 = (bf16[128,1152]{1,0:T(8,128)(2,1)S(1)}, bf16[128,1152]{1,0:T(8,128)(2,1)S(1)}, u32[]{:S(2)}, u32[]{:S(2)}) collective-permute-start(bf16[128,1152]{1,0:T(8,128)(2,1)S(1)} %get-tuple-element.47), channel_id=1, source_target_pairs={{0,192},{64,0},{128,64},{192,128},{1,193},{65,1},{129,65},{193,129... | collective-permute-start | bytes 884744 | tf_op jit(solution)/shard_map/ppermute | solution.py:92
  168.0 17.8 %collective-permute-start.17 = (bf16[1,512,256]{2,1,0:T(8,128)(2,1)S(1)}, bf16[1,512,256]{2,1,0:T(8,128)(2,1)S(1)}, u32[]{:S(2)}, u32[]{:S(2)}) collective-permute-start(bf16[1,512,256]{2,1,0:T(8,128)(2,1)S(1)} %get-tuple-element.70), channel_id=1, source_target_pairs={{1,0},{2,1},{3,2},{4,3},{5,4},{6,5},{7,6},{8,7},{9,8},{10,9},{11,1... | collective-permute-start | bytes 786440 | tf_op jit(solution)/shard_map/ppermute | solution.py:24
  171.7 16.6 %collective-permute-start.16 = (bf16[1,512,256]{2,1,0:T(8,128)(2,1)S(1)}, bf16[1,512,256]{2,1,0:T(8,128)(2,1)S(1)}, u32[]{:S(2)}, u32[]{:S(2)}) collective-permute-start(bf16[1,512,256]{2,1,0:T(8,128)(2,1)S(1)} %get-tuple-element.71), channel_id=1, source_target_pairs={{0,1},{1,2},{2,3},{3,4},{4,5},{5,6},{6,7},{7,8},{8,9},{9,10},{10,1... | collective-permute-start | bytes 786440 | tf_op jit(solution)/shard_map/ppermute | solution.py:23
  173.7 4.8 %collective-permute-start.12 = (bf16[196,256]{1,0:T(8,128)(2,1)S(1)}, bf16[196,256]{1,0:T(8,128)(2,1)S(1)}, u32[]{:S(2)}, u32[]{:S(2)}) collective-permute-start(bf16[196,256]{1,0:T(8,128)(2,1)S(1)} %get-tuple-element.59), channel_id=1, source_target_pairs={{0,64},{64,128},{128,192},{192,0},{1,65},{65,129},{129,193},{193,1... | collective-permute-start | bytes 301064 | tf_op jit(solution)/shard_map/ppermute | solution.py:92
  175.9 5.8 %collective-permute-start.13 = (bf16[196,256]{1,0:T(8,128)(2,1)S(1)}, bf16[196,256]{1,0:T(8,128)(2,1)S(1)}, u32[]{:S(2)}, u32[]{:S(2)}) collective-permute-start(bf16[196,256]{1,0:T(8,128)(2,1)S(1)} %get-tuple-element.60), channel_id=1, source_target_pairs={{0,128},{64,192},{128,0},{192,64},{1,129},{65,193},{129,1},{193,65... | collective-permute-start | bytes 301064 | tf_op jit(solution)/shard_map/ppermute | solution.py:92
  176.3 5.4 %collective-permute-start.14 = (bf16[196,256]{1,0:T(8,128)(2,1)S(1)}, bf16[196,256]{1,0:T(8,128)(2,1)S(1)}, u32[]{:S(2)}, u32[]{:S(2)}) collective-permute-start(bf16[196,256]{1,0:T(8,128)(2,1)S(1)} %get-tuple-element.61), channel_id=1, source_target_pairs={{0,192},{64,0},{128,64},{192,128},{1,193},{65,1},{129,65},{193,129... | collective-permute-start | bytes 301064 | tf_op jit(solution)/shard_map/ppermute | solution.py:92
  182.0 15.1 %collective-permute-start.19 = (bf16[192,1152]{1,0:T(8,128)(2,1)S(1)}, bf16[192,1152]{1,0:T(8,128)(2,1)S(1)}, u32[]{:S(2)}, u32[]{:S(2)}) collective-permute-start(bf16[192,1152]{1,0:T(8,128)(2,1)S(1)} %sum_parts.1.refs_0_), channel_id=1, source_target_pairs={{0,192},{64,0},{128,64},{192,128},{1,193},{65,1},{129,65},{193,129... | collective-permute-start | bytes 1327112 | tf_op jit(solution)/shard_map/ppermute | solution.py:92
  184.5 20.0 %collective-permute-start.18 = (bf16[192,1152]{1,0:T(8,128)(2,1)S(1)}, bf16[192,1152]{1,0:T(8,128)(2,1)S(1)}, u32[]{:S(2)}, u32[]{:S(2)}) collective-permute-start(bf16[192,1152]{1,0:T(8,128)(2,1)S(1)} %sum_parts.1.refs_0_), channel_id=1, source_target_pairs={{0,64},{64,128},{128,192},{192,0},{1,65},{65,129},{129,193},{193,1... | collective-permute-start | bytes 1327112 | tf_op jit(solution)/shard_map/ppermute | solution.py:92
  184.5 23.4 %collective-permute-start.15 = (bf16[192,1152]{1,0:T(8,128)(2,1)S(1)}, bf16[192,1152]{1,0:T(8,128)(2,1)S(1)}, u32[]{:S(2)}, u32[]{:S(2)}) collective-permute-start(bf16[192,1152]{1,0:T(8,128)(2,1)S(1)} %sum_parts.1.refs_0_), channel_id=1, source_target_pairs={{0,128},{64,192},{128,0},{192,64},{1,129},{65,193},{129,1},{193,65... | collective-permute-start | bytes 1327112 | tf_op jit(solution)/shard_map/ppermute | solution.py:92
  185.8 22.3 %collective-permute-start.20 = (bf16[128,1152]{1,0:T(8,128)(2,1)S(1)}, bf16[128,1152]{1,0:T(8,128)(2,1)S(1)}, u32[]{:S(2)}, u32[]{:S(2)}) collective-permute-start(bf16[128,1152]{1,0:T(8,128)(2,1)S(1)} %slice.52), channel_id=1, source_target_pairs={{0,1},{1,0},{2,3},{3,2},{4,5},{5,4},{6,7},{7,6},{8,9},{9,8},{10,11... | collective-permute-start | bytes 884744 | tf_op jit(solution)/shard_map/ppermute | solution.py:469
  197.2 10.9 %collective-permute-start.23 = (bf16[128,1152]{1,0:T(8,128)(2,1)S(1)}, bf16[128,1152]{1,0:T(8,128)(2,1)S(1)}, u32[]{:S(2)}, u32[]{:S(2)}) collective-permute-start(bf16[128,1152]{1,0:T(8,128)(2,1)S(1)} %slice.65), channel_id=1, source_target_pairs={{0,1},{1,0},{2,3},{3,2},{4,5},{5,4},{6,7},{7,6},{8,9},{9,8},{10,11... | collective-permute-start | bytes 884744 | tf_op jit(solution)/shard_map/ppermute | solution.py:469
  (20 other events, 253.7 us)

commit v8 on v4

--- a/solution.py
+++ b/solution.py
@@ -91,6 +91,35 @@
     return lax.ppermute(array, "img", [(i, (i + step) % size) for i in range(size)])
 
 
+def collect_kernel(slots_ref, feat_ref, out_ref, picks):
+    pixels = feat_ref.shape[0]
+    per_head = slots_ref.shape[0]
+    heads = picks.shape[0] // per_head
+    column = lax.broadcasted_iota(jnp.int32, (per_head, pixels), 1)
+    for part in range(slots_ref.shape[1] // heads):
+        for k in range(heads):
+            at = part * heads + k
+            hit = jnp.broadcast_to(slots_ref[:, at : at + 1], (per_head, pixels)) == column
+            picks[k * per_head : (k + 1) * per_head, :] = hit.astype(F32).astype(BF16)
+        found = dot(picks[...], feat_ref[...], (1, 0)).astype(BF16)
+        out_ref[part * heads : (part + 1) * heads] = found.reshape((heads, per_head, found.shape[1]))
+
+
+def collect(slots, flat):
+    per_head, heads = slots.shape
+    pixels, channels = flat.shape
+    return pl.pallas_call(
+        collect_kernel,
+        out_shape=jax.ShapeDtypeStruct((heads, per_head, channels), BF16),
+        in_specs=vmem_spec(2),
+        out_specs=pl.BlockSpec(memory_space=pltpu.VMEM),
+        scratch_shapes=[pltpu.VMEM((16 * per_head, pixels), BF16)],
+        compiler_params=pltpu.CompilerParams(vmem_limit_bytes=40 * 2**20),
+        cost_estimate=pl.CostEstimate(flops=4 * 10**9, bytes_accessed=3 * 10**6, transcendentals=0),
+        name="collect",
+    )(slots, flat)
+
+
 def gelu_parts(value):
     cubic = 0.044715 * (value * value * value)
     tanh = jnp.tanh(0.7978845608028654 * (value + cubic))
@@ -116,62 +145,59 @@
     whole_ref[:, pl.ds(pl.multiple_of((1 - core) * half, half), half)] = other_ref[...]
 
 
-def head_kernel(classes, place, mine_ref, other_ref, labels_ref, fc2_ref, class_ref,
-                da2_ref, own_ref, s1_ref, s2_ref, s3_ref, a1, h1, h2, dlog):
+def head_kernel(place, mine_ref, other_ref, labels_ref, fc2_ref, class_ref, da2_ref, *refs):
+    sends, (a1, h1, h2, dlog) = refs[:4], refs[4:]
     core, image = place[0], place[1]
     join_halves(core, mine_ref, other_ref, a1)
+    classes = class_ref.shape[0]
     count, hid = a1.shape
-    lanes = class_ref.shape[1]
-
-    def block(step, carry):
-        rows = pl.ds(pl.multiple_of(step * ROW_BLOCK, ROW_BLOCK), ROW_BLOCK)
+    for step in range(count // ROW_BLOCK):
+        rows = slice(step * ROW_BLOCK, (step + 1) * ROW_BLOCK)
         hidden = gelu_of(a1[rows, :].astype(F32)).astype(BF16)
         h1[rows, :] = hidden
         a2 = dot(hidden, fc2_ref[...], (1, 0))
         second = gelu_of(a2).astype(BF16)
         h2[rows, :] = second
-        logits = dot(second, class_ref[...], (1, 0))
-        column = lax.broadcasted_iota(jnp.int32, (ROW_BLOCK, lanes), 1)
-        expo = jnp.where(column < classes, jnp.exp(logits), 0.0)
+        logits = dot(second, class_ref[...], (1, 1))
+        column = lax.broadcasted_iota(jnp.int32, (ROW_BLOCK, classes), 1)
+        expo = jnp.exp(logits)
         prob = expo / jnp.sum(expo, axis=1, keepdims=True)
         onehot = (labels_ref[rows, :] == column).astype(F32)
         dlogits = (prob - onehot).astype(BF16)
         dlog[rows, :] = dlogits
-        dh2 = dot(dlogits, class_ref[...], (1, 1))
+        dh2 = dot(dlogits, class_ref[...], (1, 0))
         da2_ref[rows, :] = (dh2 * slope_of(a2)).astype(BF16)
-        return carry
-
-    lax.fori_loop(0, count // ROW_BLOCK, block, 0)
     images = 4
     wide = hid // NC // images
-    for step, out in enumerate((own_ref, s1_ref, s2_ref, s3_ref)):
+    for step, out in enumerate(sends):
         chunk = lax.rem(image + step, images)
         cols = pl.ds(pl.multiple_of(core * (hid // NC) + chunk * wide, wide), wide)
         out[:, :hid] = dot(h1[:, cols], da2_ref[...], (0, 0)).astype(out.dtype)
-        out[:, hid:] = dot(dlog[...], h2[:, cols], (0, 0)).astype(out.dtype)
-
-
-def head(place, mine, other, labels, w_fc2, w_class, classes):
+        out[:, hid:] = jnp.zeros((wide, out.shape[1] - hid), out.dtype)
+        out[:classes, hid:] = dot(dlog[...], h2[:, cols], (0, 0)).astype(out.dtype)
+
+
+def head(place, mine, other, labels, w_fc2, w_class):
     count, half = mine.shape
     hid = w_fc2.shape[0]
-    lanes = w_class.shape[1]
+    classes = w_class.shape[1]
     wide = half // 4
     struct = jax.ShapeDtypeStruct
     return pl.pallas_call(
-        functools.partial(head_kernel, classes),
-        out_shape=[struct((count, hid), BF16), struct((wide, hid + lanes), F32)]
-        + [struct((wide, hid + lanes), BF16)] * 3,
+        head_kernel,
+        out_shape=[struct((count, hid), BF16), struct((wide, hid + 128), F32)]
+        + [struct((wide, hid + 128), BF16)] * 3,
         in_specs=[SMEM_SPEC] + vmem_spec(5),
         out_specs=vmem_spec(5),
         scratch_shapes=[
             pltpu.VMEM((count, hid), BF16),
             pltpu.VMEM((count, hid), BF16),
             pltpu.VMEM((count, hid), BF16),
-            pltpu.VMEM((count, lanes), BF16),
+            pltpu.VMEM((count, classes), BF16),
         ],
         compiler_params=pltpu.CompilerParams(vmem_limit_bytes=40 * 2**20),
         name="head",
-    )(place, mine, other, labels, w_fc2, w_class)
+    )(place, mine, other, labels, w_fc2, w_class.T)
 
 
 def first_kernel(place, mine_ref, other_ref, da2_ref, fc2_ref, x_ref,
@@ -180,13 +206,10 @@
     join_halves(core, mine_ref, other_ref, a1)
     count, hid = a1.shape
 
-    def block(step, carry):
-        rows = pl.ds(pl.multiple_of(step * ROW_BLOCK, ROW_BLOCK), ROW_BLOCK)
+    for step in range(count // ROW_BLOCK):
+        rows = slice(step * ROW_BLOCK, (step + 1) * ROW_BLOCK)
         dh1 = dot(da2_ref[rows, :], fc2_ref[...], (1, 1))
         da1[rows, :] = (dh1 * slope_of(a1[rows, :].astype(F32))).astype(BF16)
-        return carry
-
-    lax.fori_loop(0, count // ROW_BLOCK, block, 0)
     images = 4
     wide = hid // images
     for step, out in enumerate((own_ref, s1_ref, s2_ref, s3_ref)):
@@ -307,15 +330,15 @@
 
     flat = features.reshape(rows * width, channels)
     capacity = pixel_slots.shape[3]
-    wanted = pixel_slots[0, :, 0, :].reshape(nband * capacity)
-    sending = flat[wanted].reshape(nband, capacity, channels)
+    sending = collect(jnp.transpose(pixel_slots[0, :, 0, :]), flat)
     received = lax.all_to_all(sending, "band", split_axis=0, concat_axis=0, tiled=True)
 
-    w_first = lax.optimization_barrier((w_fc1, sending))[0]
+    w_first, edges = lax.optimization_barrier((w_fc1, features, sending))[:2]
+    before, after = halo(edges)
     w_mine = lax.dynamic_slice_in_dim(w_first, core * half, half, 1)
     w_theirs = lax.dynamic_slice_in_dim(w_first, (1 - core) * half, half, 1)
     w_other = lax.ppermute(w_theirs, "band", CORE_SWAP)
-    received, w_other = lax.optimization_barrier((received, w_other))
+    received, w_other, before, after = lax.optimization_barrier((received, w_other, before, after))
 
     received = received.reshape(nband * capacity, channels).astype(F32)
     roi_count, bins = sample_slot.shape[1:3]
@@ -348,16 +371,15 @@
     a1_mine = exchange(jnp.broadcast_to(a1_z, (NY,) + a1_z.shape[1:]), Y_GROUPS).reshape(count, half)
     a1_other = lax.ppermute(a1_mine, "band", CORE_SWAP)
     classes = w_class.shape[1]
-    class_wide = jnp.pad(w_class, ((0, 0), (0, 128 - classes)))
-    da2, *parts = head(place, a1_mine, a1_other, labels, w_fc2, class_wide, classes)
+    da2, *parts = head(place, a1_mine, a1_other, labels, w_fc2, w_class)
     head_own, head_got = parts[0], shift_all(parts[1:])
     parts = first_layer(place, a1_mine, a1_other, da2, w_fc2, x_cols)
-    head_got, parts = lax.optimization_barrier((head_got, parts))
-    first_got = shift_all(parts[1:])
+    first_got = [shift_img(parts[1], 1), None, shift_img(parts[3], 3)]
+    held, head_got[0], head_got[2] = lax.optimization_barrier((parts[2], head_got[0], head_got[2]))
+    first_got[1] = shift_img(held, 2)
     total = sum_parts([head_own] + head_got, [parts[0]] + first_got)
     total, inner = lax.optimization_barrier((total, features))
     mine = [total] + [shift_img(total, step) for step in range(1, 4)]
-    before, after = halo(inner)
     rpn_out = rpn(before, inner, after, w_rpn, w_anchor)
     mine[2], rpn_out = lax.optimization_barrier((mine[2], rpn_out))
     tall = head_own.shape[0]

time: 197 us -> 186 us (0.944)
  waiting for transfers between devices: 55.1 us -> 46 us
  local copies, waits for them, and re-layouts: 14.5 us -> 5.44 us
  Pallas kernels: 24.5 us -> 28.7 us
    all_to_all x1, waiting for transfers between devices: 26.9 us -> 0.99 us  [shards(): lax.all_to_all(sending, 'band', split_axis=0, concat_axis=0, tiled=True)]
    ppermute x1, waiting for transfers between devices: 0.01 us -> 20.2 us  [halo(): after = lax.ppermute(array[0, :1], 'band', down)]
    gather x1 -> x0, local copies, waits for them, and re-layouts: 10.4 us -> none  [shards(): sending = flat[wanted].reshape(nband, capacity, channels)]
    pallas_call x1 -> x2, Pallas kernels: 6.28 us -> 11.2 us  [the longest x1 5.63 us: head(): pl.pallas_call(head_kernel, out_shape=[struct((count, hid), BF16), struct...]
    ppermute x9, waiting for transfers between devices: 12.7 us -> 8.93 us  [shift_img(): lax.ppermute(array, 'img', [(i, (i + step) % size) for i in range(size)])]
    ppermute x9, starting transfers between devices: 12.5 us -> 9.86 us  [shift_img(): lax.ppermute(array, 'img', [(i, (i + step) % size) for i in range(size)])]
    all_to_all x1, starting transfers between devices: 6.19 us -> 8.26 us  [shards(): lax.all_to_all(x_local, 'band', split_axis=1, concat_axis=0, tiled=True)]
  transfers between devices with their start and end apart: 20 -> 20, of which waited for: 12 -> 9; matrix products, arithmetic and copies ran while one was open for 1% -> 1% of each run, Pallas kernels for 7% -> 8%
where the time goes in v8:
time: 186 us; the launch traced here: 185 us
  starting transfers between devices  56.4 us (30%)
  waiting for transfers between devices  46 us (25%)
  blocking collectives  43 us (23%)
  Pallas kernels  28.7 us (15%)
  local copies, waits for them, and re-layouts  5.44 us (3%)
  matrix products  3.64 us (2%)
    all_to_all x4, blocking collectives, exchange(): lax.all_to_all(array, 'band', split_axis=0, concat_axis=0, tiled=True, ax...  43 us
    ppermute x1, waiting for transfers between devices, halo(): after = lax.ppermute(array[0, :1], 'band', down)  20.2 us
    all_to_all x1, starting transfers between devices, shards(): lax.all_to_all(sending, 'band', split_axis=0, concat_axis=0, tiled=True)  13.3 us
    ppermute x4, starting transfers between devices, shards(): other = [lax.ppermute(part[:tall], 'band', CORE_SWAP) for part in mine]  13.2 us
    all_to_all x1, waiting for transfers between devices, shards(): lax.all_to_all(x_local, 'band', split_axis=1, concat_axis=0, tiled=True)  12 us
    ppermute x9, starting transfers between devices, shift_img(): lax.ppermute(array, 'img', [(i, (i + step) % size) for i in range(size)])  9.86 us
    ppermute x9, waiting for transfers between devices, shift_img(): lax.ppermute(array, 'img', [(i, (i + step) % size) for i in range(size)])  8.93 us
    pallas_call x1, Pallas kernels, rpn(): pl.pallas_call(rpn_kernel, out_shape=jax.ShapeDtypeStruct((anchors, rows,...  8.91 us
  transfers between devices with their start and end apart: 20, of which 9 were waited for; matrix products, arithmetic and copies ran while one was open for 1% of the time, Pallas kernels for 8%

profile of v8, /device:TPU:1, one launch (start us, length us, event | category | flops | bytes accessed | tf_op | source)
XLA Modules:
  0.0 185.3 jit_solution(18033578728876399130)
XLA Ops:
  0.7 1.6 copy-done.3
  3.0 5.5 %collect.1 = bf16[64,32,256]{2,1,0:T(8,128)(2,1)} custom-call(s32[32,64]{1,0:T(8,128)S(1)} %bitcast.56, bf16[4096,256]{1,0:T(8,128)(2,1)S(1)} %bitcast.54), custom_call_target="tpu_custom_call" | custom-call | flops 4000000000 | bytes 3000000 | tf_op jit(solution)/shard_map/collect/pallas_call | solution.py:111
  8.6 13.3 %all-to-all-start = ((bf16[64,32,256]{2,1,0:T(8,128)(2,1)}), bf16[64,32,256]{2,1,0:T(8,128)(2,1)S(1)}, u32[]{:S(2)}, u32[]{:S(2)}) async-start(bf16[64,32,256]{2,1,0:T(8,128)(2,1)} %collect.1), calls=%async_computation | async-start | bytes 2097152 | tf_op jit(solution)/shard_map/all_to_all | solution.py:334
  23.5 2.0 %collective-permute-start.2 = (bf16[1,512,256]{2,1,0:T(8,128)(2,1)S(1)}, bf16[1,512,256]{2,1,0:T(8,128)(2,1)S(1)}, u32[]{:S(2)}, u32[]{:S(2)}) collective-permute-start(bf16[1,512,256]{2,1,0:T(8,128)(2,1)S(1)} %get-tuple-element.54), channel_id=1, source_target_pairs={{1,0},{2,1},{3,2},{4,3},{5,4},{6,5},{7,6},{8,7},{9,8},{10,9},{11,1... | collective-permute-start | bytes 786440 | tf_op jit(solution)/shard_map/ppermute | solution.py:23
  25.5 3.6 %collective-permute-start.1 = (bf16[1,512,256]{2,1,0:T(8,128)(2,1)S(1)}, bf16[1,512,256]{2,1,0:T(8,128)(2,1)S(1)}, u32[]{:S(2)}, u32[]{:S(2)}) collective-permute-start(bf16[1,512,256]{2,1,0:T(8,128)(2,1)S(1)} %get-tuple-element.55), channel_id=1, source_target_pairs={{0,1},{1,2},{2,3},{3,4},{4,5},{5,6},{6,7},{7,8},{8,9},{9,10},{10,1... | collective-permute-start | bytes 786440 | tf_op jit(solution)/shard_map/ppermute | solution.py:22
  29.4 20.2 %collective-permute-done.2.after_ref = bf16[1,512,256]{2,1,0:T(8,128)(2,1)S(1)} collective-permute-done((bf16[1,512,256]{2,1,0:T(8,128)(2,1)S(1)}, bf16[1,512,256]{2,1,0:T(8,128)(2,1)S(1)}, u32[]{:S(2)}, u32[]{:S(2)}) %collective-permute-start.2) | collective-permute-done | bytes 262176 | tf_op jit(solution)/shard_map/ppermute | solution.py:23
  50.6 3.1 %fusion.18 = bf16[392,256]{1,0:T(8,128)(2,1)S(1)} fusion(bf16[2048,256]{1,0:T(8,128)(2,1)S(1)} %bitcast.59, f32[392]{0:T(512)S(1)} %bitcast.68, s32[392]{0:T(512)S(1)} %bitcast.64, f32[392]{0:T(512)S(1)} %bitcast.69, s32[392]{0:T(512)S(1)} %bitcast.65, f32[392]{0:T(512)S(1)} %bitcast.70, s32[392]{0:T(512)S(1)} %bitcast.66, f32[392]{0:T(512)S(1)} %bitcast.67, ...), kind=kOutput, calls=%fused_computation.23 | convolution fusion | flops 2475182080 | bytes 1261824 | tf_op jit(solution)/shard_map/dot_general | solution.py:352
  55.5 8.3 %all-to-all-start.1 = ((bf16[8,64,197]{2,0,1:T(8,128)(2,1)}), bf16[8,64,197]{2,0,1:T(8,128)(2,1)S(1)}, u32[]{:S(2)}, u32[]{:S(2)}) async-start(bf16[8,64,197]{2,0,1:T(8,128)(2,1)} %copy.25), calls=%async_computation.1 | async-start | bytes 524288 | tf_op jit(solution)/shard_map/all_to_all | solution.py:358
  63.7 12.0 %all-to-all-done.1 = bf16[8,64,197]{2,0,1:T(8,128)(2,1)S(1)} async-done(((bf16[8,64,197]{2,0,1:T(8,128)(2,1)}), bf16[8,64,197]{2,0,1:T(8,128)(2,1)S(1)}, u32[]{:S(2)}, u32[]{:S(2)}) %all-to-all-start.1) | async-done | bytes 201760 | tf_op jit(solution)/shard_map/all_to_all | solution.py:358
  77.6 12.2 %all_to_all.41 = bf16[4,128,512]{2,1,0:T(8,128)(2,1)S(1)} all-to-all(bf16[4,128,512]{2,1,0:T(8,128)(2,1)S(1)} %bitcast.58), channel_id=1, replica_groups={{0,16,32,48},{1,17,33,49},{2,18,34,50},{3,19,35,51},{4,20,36,52},{5,21,..., dimensions={0} | all-to-all | bytes 1048576 | tf_op jit(solution)/shard_map/all_to_all | solution.py:80
  90.5 11.2 %all_to_all.42 = bf16[8,16,512]{2,1,0:T(8,128)(2,1)S(1)} all-to-all(bf16[8,16,512]{2,1,0:T(8,128)(2,1)} %bitcast.62), channel_id=1, replica_groups={{0,2,4,6,8,10,12,14},{1,3,5,7,9,11,13,15},{16,18,20,22,24,26,28,30},{17..., dimensions={0} | all-to-all | bytes 262144 | tf_op jit(solution)/shard_map/all_to_all | solution.py:80
  101.8 10.3 %all_to_all.43 = bf16[8,16,512]{2,1,0:T(8,128)(2,1)S(1)} all-to-all(bf16[8,16,512]{2,1,0:T(8,128)(2,1)S(1)} %broadcast_in_dim.11), channel_id=1, replica_groups={{0,2,4,6,8,10,12,14},{1,3,5,7,9,11,13,15},{16,18,20,22,24,26,28,30},{17..., dimensions={0} | all-to-all | bytes 262144 | tf_op jit(solution)/shard_map/all_to_all | solution.py:80
  112.2 9.3 %all_to_all.44 = bf16[4,128,512]{2,1,0:T(8,128)(2,1)S(1)} all-to-all(bf16[4,128,512]{2,1,0:T(8,128)(2,1)S(1)} %broadcast_in_dim.26), channel_id=1, replica_groups={{0,16,32,48},{1,17,33,49},{2,18,34,50},{3,19,35,51},{4,20,36,52},{5,21,..., dimensions={0} | all-to-all | bytes 1048576 | tf_op jit(solution)/shard_map/all_to_all | solution.py:80
  121.5 5.2 %collective-permute-start.4 = (bf16[512,512]{1,0:T(8,128)(2,1)S(1)}, bf16[512,512]{1,0:T(8,128)(2,1)}, u32[]{:S(2)}, u32[]{:S(2)}) collective-permute-start(bf16[512,512]{1,0:T(8,128)(2,1)S(1)} %bitcast.46), channel_id=1, source_target_pairs={{0,1},{1,0},{2,3},{3,2},{4,5},{5,4},{6,7},{7,6},{8,9},{9,8},{10,11... | collective-permute-start | bytes 1572872 | tf_op jit(solution)/shard_map/ppermute | solution.py:372
  126.9 1.5 collective-permute-done.4.other_ref
  128.4 5.6 %head.1 = (bf16[512,1024]{1,0:T(8,128)(2,1)S(1)}, f32[128,1152]{1,0:T(8,128)S(1)}, bf16[128,1152]{1,0:T(8,128)(2,1)S(1)}, bf16[128,1152]{1,0:T(8,128)(2,1)S(1)}, bf16[128,1152]{1,0:T(8,128)(2,1)S(1)}) custom-call(s32[2]{0:T(128)S(1)} %pad_add_fusion.place, bf16[512,512]{1,0:T(8,128)(2,1)S(1)} %bitcast.47, bf16[512,512]{1,0:T(8,128)(2,1)} %collective-permute-done.4.other_ref, ...), custom_call_target="tpu_custom_call" | custom-call | tf_op jit(solution)/shard_map/head/pallas_call | solution.py:186
  136.8 1.5 collective-permute-start.7
  138.3 5.0 %first_layer.1 = (f32[196,256]{1,0:T(8,128)S(1)}, bf16[196,256]{1,0:T(8,128)(2,1)S(1)}, bf16[196,256]{1,0:T(8,128)(2,1)S(1)}, bf16[196,256]{1,0:T(8,128)(2,1)S(1)}) custom-call(s32[2]{0:T(128)S(1)} %pad_add_fusion.place, bf16[512,512]{1,0:T(8,128)(2,1)S(1)} %bitcast.48, bf16[512,512]{1,0:T(8,128)(2,1)} %collective-permute-done.4.other_ref, ...), custom_call_target="tpu_custom_call" | custom-call | tf_op jit(solution)/shard_map/first_layer/pallas_call | solution.py:226
  143.8 2.4 %collective-permute-start.10 = (bf16[196,256]{1,0:T(8,128)(2,1)S(1)}, bf16[196,256]{1,0:T(8,128)(2,1)S(1)}, u32[]{:S(2)}, u32[]{:S(2)}) collective-permute-start(bf16[196,256]{1,0:T(8,128)(2,1)S(1)} %get-tuple-element.44), channel_id=1, source_target_pairs={{0,192},{64,0},{128,64},{192,128},{1,193},{65,1},{129,65},{193,129... | collective-permute-start | bytes 301064 | tf_op jit(solution)/shard_map/ppermute | solution.py:91
  146.4 8.0 %collective-permute-done.8.refs_5_ = bf16[196,256]{1,0:T(8,128)(2,1)S(1)} collective-permute-done((bf16[196,256]{1,0:T(8,128)(2,1)S(1)}, bf16[196,256]{1,0:T(8,128)(2,1)S(1)}, u32[]{:S(2)}, u32[]{:S(2)}) %collective-permute-start.8) | collective-permute-done | bytes 100384 | tf_op jit(solution)/shard_map/ppermute | solution.py:91
  158.2 3.3 %collective-permute-start.14 = (bf16[128,1152]{1,0:T(8,128)(2,1)S(1)}, bf16[128,1152]{1,0:T(8,128)(2,1)S(1)}, u32[]{:S(2)}, u32[]{:S(2)}) collective-permute-start(bf16[128,1152]{1,0:T(8,128)(2,1)S(1)} %slice.60), channel_id=1, source_target_pairs={{0,1},{1,0},{2,3},{3,2},{4,5},{5,4},{6,7},{7,6},{8,9},{9,8},{10,11... | collective-permute-start | bytes 884744 | tf_op jit(solution)/shard_map/ppermute | solution.py:386
  161.6 8.9 %rpn.1 = bf16[15,8,512]{2,1,0:T(8,128)(2,1)} custom-call(bf16[1,512,256]{2,1,0:T(8,128)(2,1)S(1)} %copy-done.9, bf16[8,512,256]{2,1,0:T(8,128)(2,1)S(1)} %bitcast.55, bf16[1,512,256]{2,1,0:T(8,128)(2,1)S(1)} %copy-done.7, bf16[3,3,256,256]{3,2,1,0:T(8,128)(2,1)S(1)} %copy-done.5, bf16[15,256]{1,0:T(8,128)(2,1)S(1)} %bitcast.57), custom_call_target="tpu_custom_call" | custom-call | flops 8999999488 | bytes 4000000 | tf_op jit(solution)/shard_map/rpn/pallas_call | solution.py:56
  170.7 9.7 %collective-permute-start.15 = (bf16[128,1152]{1,0:T(8,128)(2,1)S(1)}, bf16[128,1152]{1,0:T(8,128)(2,1)S(1)}, u32[]{:S(2)}, u32[]{:S(2)}) collective-permute-start(bf16[128,1152]{1,0:T(8,128)(2,1)S(1)} %slice.74), channel_id=1, source_target_pairs={{0,1},{1,0},{2,3},{3,2},{4,5},{5,4},{6,7},{7,6},{8,9},{9,8},{10,11... | collective-permute-start | bytes 884744 | tf_op jit(solution)/shard_map/ppermute | solution.py:386
  182.0 3.3 %assemble.1 = (f32[196,1024]{1,0:T(8,128)}, f32[1024,1024]{1,0:T(8,128)}, f32[81,1024]{1,0:T(8,128)}) custom-call(s32[2]{0:T(128)S(1)} %pad_add_fusion.place, bf16[192,1152]{1,0:T(8,128)(2,1)S(1)} %sum_parts.1.refs_0_, bf16[192,1152]{1,0:T(8,128)(2,1)S(1)} %collective-permute-done.12.refs_1_, bf16[192,1152]{1,0:T(8,128)(2,1)S(1)} %collective-permute-done.11.refs_2_, ...), custom_call_target="tpu_custom_call" | custom-call | tf_op jit(solution)/shard_map/assemble/pallas_call | solution.py:297
  (84 shorter events, 17.3 us)
Async XLA Ops:
  8.6 42.0 %all-to-all-start = ((bf16[64,32,256]{2,1,0:T(8,128)(2,1)}), bf16[64,32,256]{2,1,0:T(8,128)(2,1)S(1)}, u32[]{:S(2)}, u32[]{:S(2)}) async-start(bf16[64,32,256]{2,1,0:T(8,128)(2,1)} %collect.1), calls=%async_computation | async-start | bytes 2097152 | tf_op jit(solution)/shard_map/all_to_all | solution.py:334
  21.9 7.5 %collective-permute-start = (bf16[196,512]{1,0:T(8,128)(2,1)S(1)}, bf16[196,512]{1,0:T(8,128)(2,1)S(1)}, u32[]{:S(2)}, u32[]{:S(2)}) collective-permute-start(bf16[196,512]{1,0:T(8,128)(2,1)S(1)} %constant_dynamic-slice_fusion), channel_id=1, source_target_pairs={{0,1},{1,0},{2,3},{3,2},{4,5},{5,4},{6,7},{7,6},{8,9},{9,8},{10,11... | collective-permute-start | bytes 602120 | tf_op jit(solution)/shard_map/ppermute | solution.py:340
  23.5 26.1 %collective-permute-start.2 = (bf16[1,512,256]{2,1,0:T(8,128)(2,1)S(1)}, bf16[1,512,256]{2,1,0:T(8,128)(2,1)S(1)}, u32[]{:S(2)}, u32[]{:S(2)}) collective-permute-start(bf16[1,512,256]{2,1,0:T(8,128)(2,1)S(1)} %get-tuple-element.54), channel_id=1, source_target_pairs={{1,0},{2,1},{3,2},{4,3},{5,4},{6,5},{7,6},{8,7},{9,8},{10,9},{11,1... | collective-permute-start | bytes 786440 | tf_op jit(solution)/shard_map/ppermute | solution.py:23
  25.5 24.1 %collective-permute-start.1 = (bf16[1,512,256]{2,1,0:T(8,128)(2,1)S(1)}, bf16[1,512,256]{2,1,0:T(8,128)(2,1)S(1)}, u32[]{:S(2)}, u32[]{:S(2)}) collective-permute-start(bf16[1,512,256]{2,1,0:T(8,128)(2,1)S(1)} %get-tuple-element.55), channel_id=1, source_target_pairs={{0,1},{1,2},{2,3},{3,4},{4,5},{5,6},{6,7},{7,8},{8,9},{9,10},{10,1... | collective-permute-start | bytes 786440 | tf_op jit(solution)/shard_map/ppermute | solution.py:22
  55.5 20.3 %all-to-all-start.1 = ((bf16[8,64,197]{2,0,1:T(8,128)(2,1)}), bf16[8,64,197]{2,0,1:T(8,128)(2,1)S(1)}, u32[]{:S(2)}, u32[]{:S(2)}) async-start(bf16[8,64,197]{2,0,1:T(8,128)(2,1)} %copy.25), calls=%async_computation.1 | async-start | bytes 524288 | tf_op jit(solution)/shard_map/all_to_all | solution.py:358
  75.7 1.6 collective-permute-start.3
  76.5 51.9 %copy-start.1 = (bf16[1024,1024]{1,0:T(8,128)(2,1)S(1)}, bf16[1024,1024]{1,0:T(8,128)(2,1)}, u32[]{:S(2)}) copy-start(bf16[1024,1024]{1,0:T(8,128)(2,1)} %fc2_ref.3) | copy-start | bytes 6291460
  76.5 51.9 %copy-start.2 = (bf16[1024,81]{0,1:T(8,128)(2,1)S(1)}, bf16[1024,81]{0,1:T(8,128)(2,1)}, u32[]{:S(2)}) copy-start(bf16[1024,81]{0,1:T(8,128)(2,1)} %param.19) | copy-start | bytes 497668
  121.5 6.9 %collective-permute-start.4 = (bf16[512,512]{1,0:T(8,128)(2,1)S(1)}, bf16[512,512]{1,0:T(8,128)(2,1)}, u32[]{:S(2)}, u32[]{:S(2)}) collective-permute-start(bf16[512,512]{1,0:T(8,128)(2,1)S(1)} %bitcast.46), channel_id=1, source_target_pairs={{0,1},{1,0},{2,3},{3,2},{4,5},{5,4},{6,7},{7,6},{8,9},{9,8},{10,11... | collective-permute-start | bytes 1572872 | tf_op jit(solution)/shard_map/ppermute | solution.py:372
  134.0 12.1 %collective-permute-start.5 = (bf16[128,1152]{1,0:T(8,128)(2,1)S(1)}, bf16[128,1152]{1,0:T(8,128)(2,1)S(1)}, u32[]{:S(2)}, u32[]{:S(2)}) collective-permute-start(bf16[128,1152]{1,0:T(8,128)(2,1)S(1)} %get-tuple-element.36), channel_id=1, source_target_pairs={{0,64},{64,128},{128,192},{192,0},{1,65},{65,129},{129,193},{193,1... | collective-permute-start | bytes 884744 | tf_op jit(solution)/shard_map/ppermute | solution.py:91
  135.3 10.8 %collective-permute-start.6 = (bf16[128,1152]{1,0:T(8,128)(2,1)S(1)}, bf16[128,1152]{1,0:T(8,128)(2,1)S(1)}, u32[]{:S(2)}, u32[]{:S(2)}) collective-permute-start(bf16[128,1152]{1,0:T(8,128)(2,1)S(1)} %get-tuple-element.37), channel_id=1, source_target_pairs={{0,192},{64,0},{128,64},{192,128},{1,193},{65,1},{129,65},{193,129... | collective-permute-start | bytes 884744 | tf_op jit(solution)/shard_map/ppermute | solution.py:91
  136.8 17.6 %collective-permute-start.7 = (bf16[128,1152]{1,0:T(8,128)(2,1)S(1)}, bf16[128,1152]{1,0:T(8,128)(2,1)S(1)}, u32[]{:S(2)}, u32[]{:S(2)}) collective-permute-start(bf16[128,1152]{1,0:T(8,128)(2,1)S(1)} %get-tuple-element.39), channel_id=1, source_target_pairs={{0,128},{64,192},{128,0},{192,64},{1,129},{65,193},{129,1},{193,65... | collective-permute-start | bytes 884744 | tf_op jit(solution)/shard_map/ppermute | solution.py:91
  138.3 23.3 %copy-start.9 = (bf16[1,512,256]{2,1,0:T(8,128)(2,1)S(1)}, bf16[1,512,256]{2,1,0:T(8,128)(2,1)}, u32[]{:S(2)}) copy-start(bf16[1,512,256]{2,1,0:T(8,128)(2,1)} %copy-done.8) | copy-start | bytes 786436
  138.3 23.3 %copy-start.11 = (bf16[256,15]{0,1:T(8,128)(2,1)S(1)}, bf16[256,15]{0,1:T(8,128)(2,1)}, u32[]{:S(2)}) copy-start(bf16[256,15]{0,1:T(8,128)(2,1)} %param.12) | copy-start | bytes 23044
  143.4 11.0 %collective-permute-start.8 = (bf16[196,256]{1,0:T(8,128)(2,1)S(1)}, bf16[196,256]{1,0:T(8,128)(2,1)S(1)}, u32[]{:S(2)}, u32[]{:S(2)}) collective-permute-start(bf16[196,256]{1,0:T(8,128)(2,1)S(1)} %get-tuple-element.42), channel_id=1, source_target_pairs={{0,64},{64,128},{128,192},{192,0},{1,65},{65,129},{129,193},{193,1... | collective-permute-start | bytes 301064 | tf_op jit(solution)/shard_map/ppermute | solution.py:91
  143.8 10.6 %collective-permute-start.10 = (bf16[196,256]{1,0:T(8,128)(2,1)S(1)}, bf16[196,256]{1,0:T(8,128)(2,1)S(1)}, u32[]{:S(2)}, u32[]{:S(2)}) collective-permute-start(bf16[196,256]{1,0:T(8,128)(2,1)S(1)} %get-tuple-element.44), channel_id=1, source_target_pairs={{0,192},{64,0},{128,64},{192,128},{1,193},{65,1},{129,65},{193,129... | collective-permute-start | bytes 301064 | tf_op jit(solution)/shard_map/ppermute | solution.py:91
  146.1 9.2 %collective-permute-start.9 = (bf16[196,256]{1,0:T(8,128)(2,1)S(1)}, bf16[196,256]{1,0:T(8,128)(2,1)S(1)}, u32[]{:S(2)}, u32[]{:S(2)}) collective-permute-start(bf16[196,256]{1,0:T(8,128)(2,1)S(1)} %get-tuple-element.43), channel_id=1, source_target_pairs={{0,128},{64,192},{128,0},{192,64},{1,129},{65,193},{129,1},{193,65... | collective-permute-start | bytes 301064 | tf_op jit(solution)/shard_map/ppermute | solution.py:91
  155.6 14.9 %collective-permute-start.13 = (bf16[192,1152]{1,0:T(8,128)(2,1)S(1)}, bf16[192,1152]{1,0:T(8,128)(2,1)S(1)}, u32[]{:S(2)}, u32[]{:S(2)}) collective-permute-start(bf16[192,1152]{1,0:T(8,128)(2,1)S(1)} %sum_parts.1.refs_0_), channel_id=1, source_target_pairs={{0,192},{64,0},{128,64},{192,128},{1,193},{65,1},{129,65},{193,129... | collective-permute-start | bytes 1327112 | tf_op jit(solution)/shard_map/ppermute | solution.py:91
  157.0 13.7 %collective-permute-start.12 = (bf16[192,1152]{1,0:T(8,128)(2,1)S(1)}, bf16[192,1152]{1,0:T(8,128)(2,1)S(1)}, u32[]{:S(2)}, u32[]{:S(2)}) collective-permute-start(bf16[192,1152]{1,0:T(8,128)(2,1)S(1)} %sum_parts.1.refs_0_), channel_id=1, source_target_pairs={{0,64},{64,128},{128,192},{192,0},{1,65},{65,129},{129,193},{193,1... | collective-permute-start | bytes 1327112 | tf_op jit(solution)/shard_map/ppermute | solution.py:91
  157.2 23.2 %collective-permute-start.11 = (bf16[192,1152]{1,0:T(8,128)(2,1)S(1)}, bf16[192,1152]{1,0:T(8,128)(2,1)S(1)}, u32[]{:S(2)}, u32[]{:S(2)}) collective-permute-start(bf16[192,1152]{1,0:T(8,128)(2,1)S(1)} %sum_parts.1.refs_0_), channel_id=1, source_target_pairs={{0,128},{64,192},{128,0},{192,64},{1,129},{65,193},{129,1},{193,65... | collective-permute-start | bytes 1327112 | tf_op jit(solution)/shard_map/ppermute | solution.py:91
  158.2 22.3 %collective-permute-start.14 = (bf16[128,1152]{1,0:T(8,128)(2,1)S(1)}, bf16[128,1152]{1,0:T(8,128)(2,1)S(1)}, u32[]{:S(2)}, u32[]{:S(2)}) collective-permute-start(bf16[128,1152]{1,0:T(8,128)(2,1)S(1)} %slice.60), channel_id=1, source_target_pairs={{0,1},{1,0},{2,3},{3,2},{4,5},{5,4},{6,7},{7,6},{8,9},{9,8},{10,11... | collective-permute-start | bytes 884744 | tf_op jit(solution)/shard_map/ppermute | solution.py:386
  170.5 10.0 %collective-permute-start.17 = (bf16[128,1152]{1,0:T(8,128)(2,1)S(1)}, bf16[128,1152]{1,0:T(8,128)(2,1)S(1)}, u32[]{:S(2)}, u32[]{:S(2)}) collective-permute-start(bf16[128,1152]{1,0:T(8,128)(2,1)S(1)} %slice.75), channel_id=1, source_target_pairs={{0,1},{1,0},{2,3},{3,2},{4,5},{5,4},{6,7},{7,6},{8,9},{9,8},{10,11... | collective-permute-start | bytes 884744 | tf_op jit(solution)/shard_map/ppermute | solution.py:386
  170.7 10.9 %collective-permute-start.15 = (bf16[128,1152]{1,0:T(8,128)(2,1)S(1)}, bf16[128,1152]{1,0:T(8,128)(2,1)S(1)}, u32[]{:S(2)}, u32[]{:S(2)}) collective-permute-start(bf16[128,1152]{1,0:T(8,128)(2,1)S(1)} %slice.74), channel_id=1, source_target_pairs={{0,1},{1,0},{2,3},{3,2},{4,5},{5,4},{6,7},{7,6},{8,9},{9,8},{10,11... | collective-permute-start | bytes 884744 | tf_op jit(solution)/shard_map/ppermute | solution.py:386
  180.4 1.7 collective-permute-start.16
  (11 other events, 163.5 us)

commit v9 on v7

--- a/solution.py
+++ b/solution.py
@@ -10,9 +10,10 @@
 NY, NZ, NC = 4, 8, 2
 BAND = NY * NZ * NC
 F32, BF16 = jnp.float32, jnp.bfloat16
-VMEM = 24 * 2**20
+VMEM = 40 * 2**20
 CORE_SWAP = [(b, b ^ 1) for b in range(BAND)]
 Z_GROUPS = [[(y * NZ + z) * NC + c for z in range(NZ)] for y in range(NY) for c in range(NC)]
+ZC_GROUPS = [[y * NZ * NC + k for k in range(NZ * NC)] for y in range(NY)]
 Y_GROUPS = [[(y * NZ + z) * NC + c for y in range(NY)] for z in range(NZ) for c in range(NC)]
 
 
@@ -121,52 +122,56 @@
     )(slots, flat)
 
 
-def pair_kernel(mine_ref, other_ref, out_ref):
-    depth = mine_ref.shape[0]
-    out_ref[...] = jnp.zeros_like(out_ref)
-    out_ref[:depth, :] = mine_ref[...]
-    out_ref[TALL : TALL + depth, :] = other_ref[...]
-
-
-def pair(mine, other):
-    return pl.pallas_call(
-        pair_kernel,
-        out_shape=jax.ShapeDtypeStruct((TALL + SHORT,) + mine.shape[1:], BF16),
-        in_specs=vmem_spec(2),
-        out_specs=pl.BlockSpec(memory_space=pltpu.VMEM),
-        name="pair",
-    )(mine, other)
-
-
-def partial_kernel(place, x_ref, *refs):
-    core, y_at = place[0], place[2]
-    weights, out_ref = refs[:NY], refs[NY]
+PITCH = 256
+SHORT = 200
+
+
+def halves_kernel(place, *refs):
+    core = place[0]
+    sources, keep_ref, send_ref = refs[:NY], refs[NY], refs[NY + 1]
+    depth = sources[0].shape[0]
+    wide = keep_ref.shape[1]
+    for ref, side in ((keep_ref, core), (send_ref, 1 - core)):
+        ref[...] = jnp.zeros_like(ref)
+        for k, source in enumerate(sources):
+            cols = pl.ds(pl.multiple_of(side * wide, wide), wide)
+            ref[k * SHORT : k * SHORT + depth, :] = source[:, cols]
+
+
+def halves(place, slices):
+    shape = (NY * SHORT + 8, slices[0].shape[1] // NC)
+    return pl.pallas_call(
+        halves_kernel,
+        out_shape=[jax.ShapeDtypeStruct(shape, BF16)] * 2,
+        in_specs=[SMEM_SPEC] + vmem_spec(NY),
+        out_specs=vmem_spec(2),
+        compiler_params=pltpu.CompilerParams(vmem_limit_bytes=VMEM),
+        name="halves",
+    )(place, *slices)
+
+
+def partial_kernel(place, mine_ref, other_ref, keep_ref, got_ref, out_ref):
+    y_at = place[2]
     total = None
     for step in range(NY):
-        row = lax.rem(y_at + NY - step, NY)
-        for index, side in enumerate((core, 1 - core)):
-            start = (side * NY + row) * PITCH
-            cols = pl.ds(pl.multiple_of(start, PITCH), PITCH)
-            size = (TALL, SHORT)[index]
-            weight = weights[step][index * TALL : index * TALL + size, :]
-            part = dot(x_ref[:, cols][:, :size], weight, (1, 0))
+        start = lax.rem(y_at + NY - step, NY) * PITCH
+        cols = pl.ds(pl.multiple_of(start, PITCH), PITCH)
+        rows = slice(step * SHORT, (step + 1) * SHORT)
+        for ref, weight in ((mine_ref, keep_ref), (other_ref, got_ref)):
+            part = dot(ref[:, cols][:, :SHORT], weight[rows, :], (1, 0))
             total = part if total is None else total + part
     out_ref[...] = total.astype(BF16)
 
 
-PITCH = 256
-TALL, SHORT = 208, 200
-
-
-def partial_sums(place, x_part, weights):
+def partial_sums(place, mine, other, keep, got):
     return pl.pallas_call(
         partial_kernel,
-        out_shape=jax.ShapeDtypeStruct((x_part.shape[0], weights[0].shape[1]), BF16),
-        in_specs=[SMEM_SPEC] + vmem_spec(1 + NY),
+        out_shape=jax.ShapeDtypeStruct((mine.shape[0], keep.shape[1]), BF16),
+        in_specs=[SMEM_SPEC] + vmem_spec(4),
         out_specs=pl.BlockSpec(memory_space=pltpu.VMEM),
         compiler_params=pltpu.CompilerParams(vmem_limit_bytes=VMEM),
         name="partial_sums",
-    )(place, x_part, *weights)
+    )(place, mine, other, keep, got)
 
 
 def shift_y(array, step):
@@ -193,26 +198,21 @@
 ROW_BLOCK = 128
 
 
-def order_rows(y_at, x_refs, whole_ref, lanes):
-    tall = x_refs[0].shape[0] // NC
-    for back, ref in enumerate(x_refs):
-        row = lax.rem(y_at + NY - back, NY) * tall
-        for side in range(NC):
-            at = pl.ds(pl.multiple_of(side * NY * tall + row, tall), tall)
-            whole_ref[at, :] = ref[side * tall : (side + 1) * tall, lanes].astype(whole_ref.dtype)
+def join_halves(core, mine_ref, other_ref, whole_ref):
+    half = whole_ref.shape[1] // NC
+    whole_ref[:, pl.ds(pl.multiple_of(core * half, half), half)] = mine_ref[:, :half]
+    whole_ref[:, pl.ds(pl.multiple_of((1 - core) * half, half), half)] = other_ref[:, :half]
 
 
 def head_kernel(place, mine_ref, other_ref, fc2_ref, class_ref, da2_ref, *refs):
-    sends, (h1, h2, dlog) = refs[:4], refs[4:]
+    sends, (a1, h1, h2, dlog) = refs[:4], refs[4:]
     core, image = place[0], place[1]
+    join_halves(core, mine_ref, other_ref, a1)
     classes = class_ref.shape[0]
-    hid = fc2_ref.shape[0]
-    for step in range(da2_ref.shape[0] // ROW_BLOCK):
+    count, hid = a1.shape
+    for step in range(count // ROW_BLOCK):
         rows = slice(step * ROW_BLOCK, (step + 1) * ROW_BLOCK)
-        steps = mine_ref.shape[0] // ROW_BLOCK
-        ref = mine_ref if step < steps else other_ref
-        at = step % steps * ROW_BLOCK
-        hidden = gelu_of(ref[at : at + ROW_BLOCK, :hid].astype(F32)).astype(BF16)
+        hidden = gelu_of(a1[rows, :].astype(F32)).astype(BF16)
         h1[rows, :] = hidden
         a2 = dot(hidden, fc2_ref[...], (1, 0))
         second = gelu_of(a2).astype(BF16)
@@ -221,7 +221,7 @@
         column = lax.broadcasted_iota(jnp.int32, (ROW_BLOCK, classes), 1)
         expo = jnp.exp(logits)
         prob = expo / jnp.sum(expo, axis=1, keepdims=True)
-        labels = ref[at : at + ROW_BLOCK, hid:].astype(F32)[:, :1].astype(jnp.int32)
+        labels = mine_ref[rows, hid // NC :].astype(F32)[:, :1].astype(jnp.int32)
         onehot = (labels == column).astype(F32)
         dlogits = (prob - onehot).astype(BF16)
         dlog[rows, :] = dlogits
@@ -238,9 +238,10 @@
 
 
 def head(place, mine, other, w_fc2, w_class):
-    count, hid = 2 * mine.shape[0], w_fc2.shape[0]
+    count, half = mine.shape[0], w_fc2.shape[0] // NC
+    hid = w_fc2.shape[0]
     classes = w_class.shape[1]
-    wide = hid // NC // 4
+    wide = half // 4
     struct = jax.ShapeDtypeStruct
     return pl.pallas_call(
         head_kernel,
@@ -251,6 +252,7 @@
         scratch_shapes=[
             pltpu.VMEM((count, hid), BF16),
             pltpu.VMEM((count, hid), BF16),
+            pltpu.VMEM((count, hid), BF16),
             pltpu.VMEM((count, classes), BF16),
         ],
         compiler_params=pltpu.CompilerParams(vmem_limit_bytes=VMEM),
@@ -258,33 +260,34 @@
     )(place, mine, other, w_fc2, w_class.T)
 
 
-def back_kernel(mine_ref, other_ref, da2_ref, fc2_ref, da1_ref):
-    count, hid = da2_ref.shape
-    for step in range(count // ROW_BLOCK):
+def back_kernel(place, mine_ref, other_ref, da2_ref, fc2_ref, da1_ref, a1):
+    join_halves(place[0], mine_ref, other_ref, a1)
+    for step in range(a1.shape[0] // ROW_BLOCK):
         rows = slice(step * ROW_BLOCK, (step + 1) * ROW_BLOCK)
-        steps = mine_ref.shape[0] // ROW_BLOCK
-        ref = mine_ref if step < steps else other_ref
-        at = step % steps * ROW_BLOCK
         dh1 = dot(da2_ref[rows, :], fc2_ref[...], (1, 1))
-        da1_ref[rows, :] = (dh1 * slope_of(ref[at : at + ROW_BLOCK, :hid].astype(F32))).astype(BF16)
-
-
-def back(mine, other, da2, w_fc2):
+        da1_ref[rows, :] = (dh1 * slope_of(a1[rows, :].astype(F32))).astype(BF16)
+
+
+def back(place, mine, other, da2, w_fc2):
     return pl.pallas_call(
         back_kernel,
         out_shape=jax.ShapeDtypeStruct(da2.shape, BF16),
-        in_specs=vmem_spec(4),
+        in_specs=[SMEM_SPEC] + vmem_spec(4),
         out_specs=pl.BlockSpec(memory_space=pltpu.VMEM),
+        scratch_shapes=[pltpu.VMEM(da2.shape, BF16)],
         compiler_params=pltpu.CompilerParams(vmem_limit_bytes=VMEM),
         cost_estimate=pl.CostEstimate(flops=2 * 10**9, bytes_accessed=5 * 10**6, transcendentals=0),
         name="back",
-    )(mine, other, da2, w_fc2)
+    )(place, mine, other, da2, w_fc2)
 
 
 def first_kernel(place, da1_ref, *refs):
     image, y_at = place[1], place[2]
     x_refs, outs, rois = refs[:NY], refs[NY : NY + 4], refs[NY + 4]
-    order_rows(y_at, x_refs, rois, slice(None))
+    tall = x_refs[0].shape[0]
+    for step, ref in enumerate(x_refs):
+        start = lax.rem(y_at + NY - step, NY) * tall
+        rois[pl.ds(pl.multiple_of(start, tall), tall), :] = ref[...]
     images = 4
     wide = da1_ref.shape[1] // images
     depth = outs[0].shape[0]
@@ -400,6 +403,7 @@
     band, image = lax.axis_index("band"), lax.axis_index("img")
     core = band % NC
     hid = w_fc2.shape[0]
+    half = hid // NC
     y_at = band // (NC * NZ)
     place = jnp.stack([core, image, y_at]).astype(jnp.int32)
 
@@ -408,11 +412,13 @@
     sending = collect(jnp.transpose(pixel_slots[0, :, 0, :]), flat)
     received = lax.all_to_all(sending, "band", split_axis=0, concat_axis=0, tiled=True)
 
-    w_first = lax.optimization_barrier((w_fc1, sending))[0]
-    depth = w_first.shape[0]
-    w_pair = pair(w_first, lax.ppermute(w_first, "band", CORE_SWAP))
-    weights = [w_pair] + [shift_y(w_pair, step) for step in range(1, NY)]
-    received, weights = lax.optimization_barrier((received, weights))
+    depth = w_fc1.shape[0]
+    w_first, edges, labels = lax.optimization_barrier((w_fc1, features, roi_labels, sending))[:3]
+    slices = [w_first] + [shift_y(w_first, step) for step in range(1, NY)]
+    before, after = halo(edges)
+    marks = jnp.broadcast_to(labels[0].astype(BF16)[:, None], (labels.shape[1], 128))
+    others = lax.ppermute(marks, "band", CORE_SWAP)
+    marks = jnp.where(core == 0, jnp.concatenate([marks, others]), jnp.concatenate([others, marks]))
 
     received = received.reshape(nband * capacity, channels).astype(F32)
     roi_count, bins = sample_slot.shape[1:3]
@@ -427,47 +433,46 @@
     pooled = pooled.astype(BF16).reshape(roi_count, bins, channels)
     x_local = jnp.transpose(pooled, (0, 2, 1)).reshape(roi_count, nband, depth)
     x_local = jnp.pad(x_local, ((0, 0), (0, 0), (0, PITCH - depth)))
-    x_local = x_local.reshape(roi_count, NY, NZ, NC, PITCH).transpose(2, 0, 3, 1, 4)
-    x_part = exchange(x_local.reshape(NZ, roi_count, NC * NY * PITCH), Z_GROUPS)
-    x_part = x_part.reshape(NZ * roi_count, NC * NY * PITCH)
-
-    across = NY * PITCH
-    x_mine = lax.dynamic_slice_in_dim(x_part, core * across, across, 1)
-    x_theirs = lax.dynamic_slice_in_dim(x_part, (1 - core) * across, across, 1)
-    x_both = jnp.concatenate([x_mine, lax.ppermute(x_theirs, "band", CORE_SWAP)], axis=0)
-    partial = partial_sums(place, x_part, weights)
-    partial, x_both = lax.optimization_barrier((partial, x_both))
-    by_z = exchange(partial.reshape(NZ, roi_count, hid), Z_GROUPS)
+    x_local = x_local.reshape(roi_count, NY, NZ * NC, PITCH).transpose(2, 0, 1, 3)
+    x_local, slices, before, after, marks = lax.optimization_barrier(
+        (x_local, slices, before, after, marks)
+    )
+    keep, send = halves(place, slices)
+    got = lax.ppermute(send, "band", CORE_SWAP)
+    x_part = exchange(x_local.reshape(NZ * NC, roi_count, NY * PITCH), ZC_GROUPS)
+    x_part = x_part.reshape(NZ * NC * roi_count, NY * PITCH)
+
+    x_other = lax.ppermute(x_part, "band", CORE_SWAP)
+    partial = partial_sums(place, x_part, x_other, keep, got)
+    count = roi_count * nband
+    by_z = exchange(partial.reshape(NZ, count // NY // NZ, half), Z_GROUPS)
     a1_own = jnp.sum(by_z.astype(F32), axis=0).astype(BF16)
-    marks = jnp.broadcast_to(roi_labels[0].astype(BF16)[:, None], (roi_count, 128))
     a1_own = jnp.concatenate([a1_own, marks], axis=1)
     a1_z = exchange(jnp.broadcast_to(a1_own[None], (NZ,) + a1_own.shape), Z_GROUPS)
-    a1_z = a1_z.reshape(1, NZ * roi_count, hid + 128)
+    a1_z = a1_z.reshape(1, count // NY, half + 128)
     a1_mine = exchange(jnp.broadcast_to(a1_z, (NY,) + a1_z.shape[1:]), Y_GROUPS)
-    a1_mine = a1_mine.reshape(NY * NZ * roi_count, hid + 128)
+    a1_mine = a1_mine.reshape(count, half + 128)
     a1_other = lax.ppermute(a1_mine, "band", CORE_SWAP)
-    classes = w_class.shape[1]
     da2, *parts = head(place, a1_mine, a1_other, w_fc2, w_class)
     head_own, head_got = parts[0], shift_all(parts[1:])
-    x_both = lax.optimization_barrier((x_both, da2))[0]
-    x_blocks = [lax.dynamic_slice_in_dim(x_both, y_at * PITCH, PITCH, 1)]
+    x_part = lax.optimization_barrier((x_part, da2))[0]
+    x_blocks = [lax.dynamic_slice_in_dim(x_part, y_at * PITCH, PITCH, 1)]
     for step in range(1, NY):
         to = (y_at + step) % NY
-        x_blocks.append(shift_y(lax.dynamic_slice_in_dim(x_both, to * PITCH, PITCH, 1), step))
-    da1 = back(a1_mine, a1_other, da2, w_fc2)
+        x_blocks.append(shift_y(lax.dynamic_slice_in_dim(x_part, to * PITCH, PITCH, 1), step))
+    da1 = back(place, a1_mine, a1_other, da2, w_fc2)
     parts = first_layer(place, da1, x_blocks, depth)
-    inner = lax.optimization_barrier((features, parts[0]))[0]
-    before, after = halo(inner)
-    head_got, parts = lax.optimization_barrier((head_got, parts))
-    first_got = shift_all(parts[1:])
+    first_got = [shift_img(parts[1], 1), None, shift_img(parts[3], 3)]
+    held, head_got[0], head_got[2] = lax.optimization_barrier((parts[2], head_got[0], head_got[2]))
+    first_got[1] = shift_img(held, 2)
     total = sum_parts([head_own] + head_got, [parts[0]] + first_got)
-    total, inner = lax.optimization_barrier((total, inner))
+    total, inner = lax.optimization_barrier((total, features))
     mine = [total] + [shift_img(total, step) for step in range(1, 4)]
     rpn_out = rpn(before, inner, after, w_rpn, w_anchor)
     mine[2], rpn_out = lax.optimization_barrier((mine[2], rpn_out))
     tall = head_own.shape[0]
     other = [lax.ppermute(part[:tall], "band", CORE_SWAP) for part in mine]
-    grad_fc1, grad_fc2, grad_class = assemble(place, mine, other, depth, classes)
+    grad_fc1, grad_fc2, grad_class = assemble(place, mine, other, depth, w_class.shape[1])
     return (rpn_out, grad_fc1, grad_fc2, grad_class.T)
 
 

time: 214 us -> 176 us (0.82)
  waiting for transfers between devices: 65.7 us -> 26.5 us
  blocking collectives: 21.5 us -> 50 us
  starting transfers between devices: 65.9 us -> 52.5 us
  local copies, waits for them, and re-layouts: 19.8 us -> 8.59 us
    ppermute x6, waiting for transfers between devices: 37.5 us -> 0.02 us  [shift_y(): lax.ppermute(array, 'band', [(b, (b + step * row) % BAND) for b in range(...]
    all_to_all x2 -> x4, blocking collectives: 21.5 us -> 50 us  [exchange(): lax.all_to_all(array, 'band', split_axis=0, concat_axis=0, tiled=True, ax...]
    all_to_all x2 -> x0, waiting for transfers between devices: 20.1 us -> none  [exchange(): lax.all_to_all(array, 'band', split_axis=0, concat_axis=0, tiled=True, ax...]
    all_to_all x1, waiting for transfers between devices: 0.01 us -> 15.8 us  [shards(): lax.all_to_all(sending, 'band', split_axis=0, concat_axis=0, tiled=True)]
    all_to_all x2 -> x0, starting transfers between devices: 8.6 us -> none  [exchange(): lax.all_to_all(array, 'band', split_axis=0, concat_axis=0, tiled=True, ax...]
    unnamed x37 -> x32, local copies, waits for them, and re-layouts: 10.3 us -> 4.43 us
    ppermute x9, starting transfers between devices: 13.4 us -> 9.14 us  [shift_img(): lax.ppermute(array, 'img', [(i, (i + step) % size) for i in range(size)])]
    ppermute x9, waiting for transfers between devices: 3.42 us -> 5.69 us  [shift_img(): lax.ppermute(array, 'img', [(i, (i + step) % size) for i in range(size)])]
  transfers between devices with their start and end apart: 27 -> 26, of which waited for: 11 -> 7; matrix products, arithmetic and copies ran while one was open for 4% -> 5% of each run, Pallas kernels for 9% -> 8%
where the time goes in v9:
time: 176 us; the launch traced here: 175 us
  starting transfers between devices  52.5 us (30%)
  blocking collectives  50 us (28%)
  Pallas kernels  32.5 us (18%)
  waiting for transfers between devices  26.5 us (15%)
  local copies, waits for them, and re-layouts  8.59 us (5%)
  matrix products  4.04 us (2%)
    all_to_all x4, blocking collectives, exchange(): lax.all_to_all(array, 'band', split_axis=0, concat_axis=0, tiled=True, ax...  50 us
    all_to_all x1, waiting for transfers between devices, shards(): lax.all_to_all(sending, 'band', split_axis=0, concat_axis=0, tiled=True)  15.8 us
    ppermute x4, starting transfers between devices, shards(): other = [lax.ppermute(part[:tall], 'band', CORE_SWAP) for part in mine]  13.3 us
    all_to_all x1, starting transfers between devices, shards(): lax.all_to_all(sending, 'band', split_axis=0, concat_axis=0, tiled=True)  13.3 us
    ppermute x9, starting transfers between devices, shift_img(): lax.ppermute(array, 'img', [(i, (i + step) % size) for i in range(size)])  9.14 us
    pallas_call x1, Pallas kernels, rpn(): pl.pallas_call(rpn_kernel, out_shape=jax.ShapeDtypeStruct((anchors, rows,...  8.83 us
    ppermute x6, starting transfers between devices, shift_y(): lax.ppermute(array, 'band', [(b, (b + step * row) % BAND) for b in range(...  6.18 us
    pallas_call x1, Pallas kernels, head(): pl.pallas_call(head_kernel, out_shape=[struct((count, hid), BF16), struct...  5.76 us
  transfers between devices with their start and end apart: 26, of which 7 were waited for; matrix products, arithmetic and copies ran while one was open for 5% of the time, Pallas kernels for 8%

profile of v9, /device:TPU:1, one launch (start us, length us, event | category | flops | bytes accessed | tf_op | source)
XLA Modules:
  0.0 175.3 jit_solution(2070419502754110398)
XLA Ops:
  3.0 5.6 %collect.1 = bf16[64,32,256]{2,1,0:T(8,128)(2,1)} custom-call(s32[32,64]{1,0:T(8,128)S(1)} %bitcast.54, bf16[4096,256]{1,0:T(8,128)(2,1)S(1)} %bitcast.52), custom_call_target="tpu_custom_call" | custom-call | flops 4000000000 | bytes 3000000 | tf_op jit(solution)/shard_map/collect/pallas_call | solution.py:113
  8.5 13.3 %all-to-all-start = ((bf16[64,32,256]{2,1,0:T(8,128)(2,1)}), bf16[64,32,256]{2,1,0:T(8,128)(2,1)S(1)}, u32[]{:S(2)}, u32[]{:S(2)}) async-start(bf16[64,32,256]{2,1,0:T(8,128)(2,1)} %collect.1), calls=%async_computation | async-start | bytes 2097152 | tf_op jit(solution)/shard_map/all_to_all | solution.py:413
  21.8 2.9 %collective-permute-start.2 = (bf16[196,1024]{1,0:T(8,128)(2,1)S(1)}, bf16[196,1024]{1,0:T(8,128)(2,1)S(1)}, u32[]{:S(2)}, u32[]{:S(2)}) collective-permute-start(bf16[196,1024]{1,0:T(8,128)(2,1)S(1)} %copy-done.3), channel_id=1, source_target_pairs={{0,48},{1,49},{2,50},{3,51},{4,52},{5,53},{6,54},{7,55},{8,56},{9,... | collective-permute-start | bytes 1204232 | tf_op jit(solution)/shard_map/ppermute | solution.py:179
  27.0 1.8 %slice_bitcast_fusion = (bf16[1,512,256]{2,1,0:T(8,128)(2,1)}, bf16[1,512,256]{2,1,0:T(8,128)(2,1)S(1)}) fusion(bf16[1,8,512,256]{3,2,1,0:T(8,128)(2,1)} %param.10), kind=kLoop, calls=%fused_computation.22 | loop fusion | bytes 1048576 | tf_op jit(solution)/shard_map/squeeze | solution.py:25
  28.8 1.9 %collective-permute-start.4 = (bf16[1,512,256]{2,1,0:T(8,128)(2,1)}, bf16[1,512,256]{2,1,0:T(8,128)(2,1)S(1)}, u32[]{:S(2)}, u32[]{:S(2)}) collective-permute-start(bf16[1,512,256]{2,1,0:T(8,128)(2,1)} %get-tuple-element.70), channel_id=1, source_target_pairs={{1,0},{2,1},{3,2},{4,3},{5,4},{6,5},{7,6},{8,7},{9,8},{10,9},{11,1... | collective-permute-start | bytes 786440 | tf_op jit(solution)/shard_map/ppermute | solution.py:25
  31.1 3.6 %collective-permute-start.3 = (bf16[1,512,256]{2,1,0:T(8,128)(2,1)S(1)}, bf16[1,512,256]{2,1,0:T(8,128)(2,1)S(1)}, u32[]{:S(2)}, u32[]{:S(2)}) collective-permute-start(bf16[1,512,256]{2,1,0:T(8,128)(2,1)S(1)} %get-tuple-element.71), channel_id=1, source_target_pairs={{0,1},{1,2},{2,3},{3,4},{4,5},{5,6},{6,7},{7,8},{8,9},{9,10},{10,1... | collective-permute-start | bytes 786440 | tf_op jit(solution)/shard_map/ppermute | solution.py:24
  34.7 15.8 %all-to-all-done = bf16[64,32,256]{2,1,0:T(8,128)(2,1)S(1)} async-done(((bf16[64,32,256]{2,1,0:T(8,128)(2,1)}), bf16[64,32,256]{2,1,0:T(8,128)(2,1)S(1)}, u32[]{:S(2)}, u32[]{:S(2)}) %all-to-all-start) | async-done | bytes 1048608 | tf_op jit(solution)/shard_map/all_to_all | solution.py:413
  50.6 4.0 %fusion.17 = bf16[392,256]{1,0:T(8,128)(2,1)} fusion(bf16[2048,256]{1,0:T(8,128)(2,1)S(1)} %bitcast.57, f32[392]{0:T(512)S(1)} %bitcast.65, s32[392]{0:T(512)S(1)} %bitcast.61, f32[392]{0:T(512)S(1)} %bitcast.66, s32[392]{0:T(512)S(1)} %bitcast.62, f32[392]{0:T(512)S(1)} %bitcast.67, s32[392]{0:T(512)S(1)} %bitcast.63, f32[392]{0:T(512)S(1)} %bitcast.64, ...), kind=kOutput, calls=%fused_computation.21 | convolution fusion | flops 2475182080 | bytes 1261824 | tf_op jit(solution)/shard_map/dot_general | solution.py:432
  59.5 17.6 %all_to_all.25 = bf16[16,8,1024]{2,1,0:T(8,128)(2,1)S(1)} all-to-all(bf16[16,8,1024]{2,1,0:T(8,128)(2,1)S(1)} %reshape.49), channel_id=1, replica_groups={{0,1,2,3,4,5,6,7,8,9,10,11,12,13,14,15},{16,17,18,19,20,21,22,23,24,25,..., dimensions={0} | all-to-all | bytes 524288 | tf_op jit(solution)/shard_map/all_to_all | solution.py:82
  81.3 10.9 %all_to_all.26 = bf16[8,16,512]{2,1,0:T(8,128)(2,1)S(1)} all-to-all(bf16[8,16,512]{2,1,0:T(8,128)(2,1)S(1)} %bitcast.50), channel_id=1, replica_groups={{0,2,4,6,8,10,12,14},{1,3,5,7,9,11,13,15},{16,18,20,22,24,26,28,30},{17..., dimensions={0} | all-to-all | bytes 262144 | tf_op jit(solution)/shard_map/all_to_all | solution.py:82
  92.3 10.8 %all_to_all.27 = bf16[8,16,640]{2,1,0:T(8,128)(2,1)S(1)} all-to-all(bf16[8,16,640]{2,1,0:T(8,128)(2,1)S(1)} %broadcast_in_dim.11), channel_id=1, replica_groups={{0,2,4,6,8,10,12,14},{1,3,5,7,9,11,13,15},{16,18,20,22,24,26,28,30},{17..., dimensions={0} | all-to-all | bytes 327680 | tf_op jit(solution)/shard_map/all_to_all | solution.py:82
  103.1 10.7 %all_to_all.28 = bf16[4,128,640]{2,1,0:T(8,128)(2,1)S(1)} all-to-all(bf16[4,128,640]{2,1,0:T(8,128)(2,1)S(1)} %broadcast_in_dim.26), channel_id=1, replica_groups={{0,16,32,48},{1,17,33,49},{2,18,34,50},{3,19,35,51},{4,20,36,52},{5,21,..., dimensions={0} | all-to-all | bytes 1310720 | tf_op jit(solution)/shard_map/all_to_all | solution.py:82
  113.9 3.5 %collective-permute-start.8 = (bf16[512,640]{1,0:T(8,128)(2,1)S(1)}, bf16[512,640]{1,0:T(8,128)(2,1)}, u32[]{:S(2)}, u32[]{:S(2)}) collective-permute-start(bf16[512,640]{1,0:T(8,128)(2,1)S(1)} %bitcast.44), channel_id=1, source_target_pairs={{0,1},{1,0},{2,3},{3,2},{4,5},{5,4},{6,7},{7,6},{8,9},{9,8},{10,11... | collective-permute-start | bytes 1966088 | tf_op jit(solution)/shard_map/ppermute | solution.py:455
  117.3 1.9 %collective-permute-done.8.other_ref = bf16[512,640]{1,0:T(8,128)(2,1)} collective-permute-done((bf16[512,640]{1,0:T(8,128)(2,1)S(1)}, bf16[512,640]{1,0:T(8,128)(2,1)}, u32[]{:S(2)}, u32[]{:S(2)}) %collective-permute-start.8) | collective-permute-done | bytes 655392 | tf_op jit(solution)/shard_map/ppermute | solution.py:455
  119.2 5.8 %head.1 = (bf16[512,1024]{1,0:T(8,128)(2,1)S(1)}, f32[128,1152]{1,0:T(8,128)S(1)}, bf16[128,1152]{1,0:T(8,128)(2,1)S(1)}, bf16[128,1152]{1,0:T(8,128)(2,1)S(1)}, bf16[128,1152]{1,0:T(8,128)(2,1)S(1)}) custom-call(s32[3]{0:T(128)S(1)} %pad_add_fusion.place, bf16[512,640]{1,0:T(8,128)(2,1)S(1)} %bitcast.45, bf16[512,640]{1,0:T(8,128)(2,1)} %collective-permute-done.8.other_ref, ...), custom_call_target="tpu_custom_call" | custom-call | tf_op jit(solution)/shard_map/head/pallas_call | solution.py:246
  131.5 4.6 %back.1.da1_ref = bf16[512,1024]{1,0:T(8,128)(2,1)S(1)} custom-call(s32[3]{0:T(128)S(1)} %pad_add_fusion.place, bf16[512,640]{1,0:T(8,128)(2,1)S(1)} %bitcast.46, bf16[512,640]{1,0:T(8,128)(2,1)} %collective-permute-done.8.other_ref, bf16[512,1024]{1,0:T(8,128)(2,1)S(1)} %get-tuple-element.49.da2_ref, bf16[1024,1024]{1,0:T(8,128)(2,1)S(1)} %copy-done), custom_call_target="tpu_custom_call" | custom-call | flops 2000000000 | bytes 5000000 | tf_op jit(solution)/shard_map/back/pallas_call | solution.py:272
  137.5 2.5 %collective-permute-start.17 = (bf16[196,256]{1,0:T(8,128)(2,1)S(1)}, bf16[196,256]{1,0:T(8,128)(2,1)S(1)}, u32[]{:S(2)}, u32[]{:S(2)}) collective-permute-start(bf16[196,256]{1,0:T(8,128)(2,1)S(1)} %get-tuple-element.60), channel_id=1, source_target_pairs={{0,192},{64,0},{128,64},{192,128},{1,193},{65,1},{129,65},{193,129... | collective-permute-start | bytes 301064 | tf_op jit(solution)/shard_map/ppermute | solution.py:93
  140.3 3.1 %collective-permute-done.15.refs_5_ = bf16[196,256]{1,0:T(8,128)(2,1)S(1)} collective-permute-done((bf16[196,256]{1,0:T(8,128)(2,1)S(1)}, bf16[196,256]{1,0:T(8,128)(2,1)S(1)}, u32[]{:S(2)}, u32[]{:S(2)}) %collective-permute-start.15) | collective-permute-done | bytes 100384 | tf_op jit(solution)/shard_map/ppermute | solution.py:93
  143.4 2.6 %collective-permute-done.16.refs_6_ = bf16[196,256]{1,0:T(8,128)(2,1)S(1)} collective-permute-done((bf16[196,256]{1,0:T(8,128)(2,1)S(1)}, bf16[196,256]{1,0:T(8,128)(2,1)S(1)}, u32[]{:S(2)}, u32[]{:S(2)}) %collective-permute-start.16) | collective-permute-done | bytes 100384 | tf_op jit(solution)/shard_map/ppermute | solution.py:93
  148.2 4.5 %collective-permute-start.21 = (bf16[128,1152]{1,0:T(8,128)(2,1)S(1)}, bf16[128,1152]{1,0:T(8,128)(2,1)S(1)}, u32[]{:S(2)}, u32[]{:S(2)}) collective-permute-start(bf16[128,1152]{1,0:T(8,128)(2,1)S(1)} %slice.52), channel_id=1, source_target_pairs={{0,1},{1,0},{2,3},{3,2},{4,5},{5,4},{6,7},{7,6},{8,9},{9,8},{10,11... | collective-permute-start | bytes 884744 | tf_op jit(solution)/shard_map/ppermute | solution.py:474
  152.7 8.8 %rpn.1 = bf16[15,8,512]{2,1,0:T(8,128)(2,1)} custom-call(bf16[1,512,256]{2,1,0:T(8,128)(2,1)S(1)} %copy-done.9, bf16[8,512,256]{2,1,0:T(8,128)(2,1)S(1)} %bitcast.53, bf16[1,512,256]{2,1,0:T(8,128)(2,1)S(1)} %collective-permute-done.4.after_ref, bf16[3,3,256,256]{3,2,1,0:T(8,128)(2,1)S(1)} %copy-done.7, bf16[15,256]{1,0:T(8,128)(2,1)S(1)} %bitcast.55), custom_call_target="tpu_custom_call" | custom-call | flops 8999999488 | bytes 4000000 | tf_op jit(solution)/shard_map/rpn/pallas_call | solution.py:58
  161.5 1.7 collective-permute-start.24
  163.2 7.1 %collective-permute-start.22 = (bf16[128,1152]{1,0:T(8,128)(2,1)S(1)}, bf16[128,1152]{1,0:T(8,128)(2,1)S(1)}, u32[]{:S(2)}, u32[]{:S(2)}) collective-permute-start(bf16[128,1152]{1,0:T(8,128)(2,1)S(1)} %slice.64), channel_id=1, source_target_pairs={{0,1},{1,0},{2,3},{3,2},{4,5},{5,4},{6,7},{7,6},{8,9},{9,8},{10,11... | collective-permute-start | bytes 884744 | tf_op jit(solution)/shard_map/ppermute | solution.py:474
  172.0 3.3 %assemble.1 = (f32[196,1024]{1,0:T(8,128)}, f32[1024,1024]{1,0:T(8,128)}, f32[81,1024]{1,0:T(8,128)}) custom-call(s32[3]{0:T(128)S(1)} %pad_add_fusion.place, bf16[192,1152]{1,0:T(8,128)(2,1)S(1)} %sum_parts.1.refs_0_, bf16[192,1152]{1,0:T(8,128)(2,1)S(1)} %collective-permute-done.19.refs_1_, bf16[192,1152]{1,0:T(8,128)(2,1)S(1)} %collective-permute-done.18.refs_2_, ...), custom_call_target="tpu_custom_call" | custom-call | tf_op jit(solution)/shard_map/assemble/pallas_call | solution.py:375
  (98 shorter events, 26.3 us)
Async XLA Ops:
  8.5 42.0 %all-to-all-start = ((bf16[64,32,256]{2,1,0:T(8,128)(2,1)}), bf16[64,32,256]{2,1,0:T(8,128)(2,1)S(1)}, u32[]{:S(2)}, u32[]{:S(2)}) async-start(bf16[64,32,256]{2,1,0:T(8,128)(2,1)} %collect.1), calls=%async_computation | async-start | bytes 2097152 | tf_op jit(solution)/shard_map/all_to_all | solution.py:413
  21.8 34.5 %collective-permute-start.2 = (bf16[196,1024]{1,0:T(8,128)(2,1)S(1)}, bf16[196,1024]{1,0:T(8,128)(2,1)S(1)}, u32[]{:S(2)}, u32[]{:S(2)}) collective-permute-start(bf16[196,1024]{1,0:T(8,128)(2,1)S(1)} %copy-done.3), channel_id=1, source_target_pairs={{0,48},{1,49},{2,50},{3,51},{4,52},{5,53},{6,54},{7,55},{8,56},{9,... | collective-permute-start | bytes 1204232 | tf_op jit(solution)/shard_map/ppermute | solution.py:179
  24.7 31.6 %collective-permute-start.1 = (bf16[196,1024]{1,0:T(8,128)(2,1)S(1)}, bf16[196,1024]{1,0:T(8,128)(2,1)S(1)}, u32[]{:S(2)}, u32[]{:S(2)}) collective-permute-start(bf16[196,1024]{1,0:T(8,128)(2,1)S(1)} %copy-done.3), channel_id=1, source_target_pairs={{0,32},{1,33},{2,34},{3,35},{4,36},{5,37},{6,38},{7,39},{8,40},{9,... | collective-permute-start | bytes 1204232 | tf_op jit(solution)/shard_map/ppermute | solution.py:179
  25.1 31.2 %collective-permute-start = (bf16[196,1024]{1,0:T(8,128)(2,1)S(1)}, bf16[196,1024]{1,0:T(8,128)(2,1)S(1)}, u32[]{:S(2)}, u32[]{:S(2)}) collective-permute-start(bf16[196,1024]{1,0:T(8,128)(2,1)S(1)} %copy-done.3), channel_id=1, source_target_pairs={{0,16},{1,17},{2,18},{3,19},{4,20},{5,21},{6,22},{7,23},{8,24},{9,... | collective-permute-start | bytes 1204232 | tf_op jit(solution)/shard_map/ppermute | solution.py:179
  25.8 5.3 %collective-permute-start.5 = (bf16[8,128]{1,0:T(8,128)(2,1)S(1)}, bf16[8,128]{1,0:T(8,128)(2,1)S(1)}, u32[]{:S(2)}, u32[]{:S(2)}) collective-permute-start(bf16[8,128]{1,0:T(8,128)(2,1)S(1)} %broadcast_in_dim.10), channel_id=1, source_target_pairs={{0,1},{1,0},{2,3},{3,2},{4,5},{5,4},{6,7},{7,6},{8,9},{9,8},{10,11... | collective-permute-start | bytes 6152 | tf_op jit(solution)/shard_map/ppermute | solution.py:420
  28.8 27.4 %collective-permute-start.4 = (bf16[1,512,256]{2,1,0:T(8,128)(2,1)}, bf16[1,512,256]{2,1,0:T(8,128)(2,1)S(1)}, u32[]{:S(2)}, u32[]{:S(2)}) collective-permute-start(bf16[1,512,256]{2,1,0:T(8,128)(2,1)} %get-tuple-element.70), channel_id=1, source_target_pairs={{1,0},{2,1},{3,2},{4,3},{5,4},{6,5},{7,6},{8,7},{9,8},{10,9},{11,1... | collective-permute-start | bytes 786440 | tf_op jit(solution)/shard_map/ppermute | solution.py:25
  31.1 25.2 %collective-permute-start.3 = (bf16[1,512,256]{2,1,0:T(8,128)(2,1)S(1)}, bf16[1,512,256]{2,1,0:T(8,128)(2,1)S(1)}, u32[]{:S(2)}, u32[]{:S(2)}) collective-permute-start(bf16[1,512,256]{2,1,0:T(8,128)(2,1)S(1)} %get-tuple-element.71), channel_id=1, source_target_pairs={{0,1},{1,2},{2,3},{3,4},{4,5},{5,6},{6,7},{7,8},{8,9},{9,10},{10,1... | collective-permute-start | bytes 786440 | tf_op jit(solution)/shard_map/ppermute | solution.py:24
  58.8 19.8 %collective-permute-start.7 = (bf16[808,512]{1,0:T(8,128)(2,1)}, bf16[808,512]{1,0:T(8,128)(2,1)}, u32[]{:S(2)}, u32[]{:S(2)}) collective-permute-start(bf16[808,512]{1,0:T(8,128)(2,1)} %get-tuple-element.46), channel_id=1, source_target_pairs={{0,1},{1,0},{2,3},{3,2},{4,5},{5,4},{6,7},{7,6},{8,9},{9,8},{10,11... | collective-permute-start | bytes 2482184 | tf_op jit(solution)/shard_map/ppermute | solution.py:441
  113.9 5.4 %collective-permute-start.8 = (bf16[512,640]{1,0:T(8,128)(2,1)S(1)}, bf16[512,640]{1,0:T(8,128)(2,1)}, u32[]{:S(2)}, u32[]{:S(2)}) collective-permute-start(bf16[512,640]{1,0:T(8,128)(2,1)S(1)} %bitcast.44), channel_id=1, source_target_pairs={{0,1},{1,0},{2,3},{3,2},{4,5},{5,4},{6,7},{7,6},{8,9},{9,8},{10,11... | collective-permute-start | bytes 1966088 | tf_op jit(solution)/shard_map/ppermute | solution.py:455
  125.0 15.0 %collective-permute-start.12 = (bf16[128,1152]{1,0:T(8,128)(2,1)S(1)}, bf16[128,1152]{1,0:T(8,128)(2,1)S(1)}, u32[]{:S(2)}, u32[]{:S(2)}) collective-permute-start(bf16[128,1152]{1,0:T(8,128)(2,1)S(1)} %get-tuple-element.52), channel_id=1, source_target_pairs={{0,64},{64,128},{128,192},{192,0},{1,65},{65,129},{129,193},{193,1... | collective-permute-start | bytes 884744 | tf_op jit(solution)/shard_map/ppermute | solution.py:93
  126.3 13.7 %collective-permute-start.13 = (bf16[128,1152]{1,0:T(8,128)(2,1)S(1)}, bf16[128,1152]{1,0:T(8,128)(2,1)S(1)}, u32[]{:S(2)}, u32[]{:S(2)}) collective-permute-start(bf16[128,1152]{1,0:T(8,128)(2,1)S(1)} %get-tuple-element.53), channel_id=1, source_target_pairs={{0,192},{64,0},{128,64},{192,128},{1,193},{65,1},{129,65},{193,129... | collective-permute-start | bytes 884744 | tf_op jit(solution)/shard_map/ppermute | solution.py:93
  127.8 3.7 %collective-permute-start.11 = (bf16[128,256]{1,0:T(8,128)(2,1)S(1)}, bf16[128,256]{1,0:T(8,128)(2,1)S(1)}, u32[]{:S(2)}, u32[]{:S(2)}) collective-permute-start(bf16[128,256]{1,0:T(8,128)(2,1)S(1)} %get-tuple-element.72), channel_id=1, source_target_pairs={{0,48},{1,49},{2,50},{3,51},{4,52},{5,53},{6,54},{7,55},{8,56},{9,... | collective-permute-start | bytes 196616 | tf_op jit(solution)/shard_map/ppermute | solution.py:179
  128.7 14.7 %collective-permute-start.14 = (bf16[128,1152]{1,0:T(8,128)(2,1)S(1)}, bf16[128,1152]{1,0:T(8,128)(2,1)S(1)}, u32[]{:S(2)}, u32[]{:S(2)}) collective-permute-start(bf16[128,1152]{1,0:T(8,128)(2,1)S(1)} %get-tuple-element.55), channel_id=1, source_target_pairs={{0,128},{64,192},{128,0},{192,64},{1,129},{65,193},{129,1},{193,65... | collective-permute-start | bytes 884744 | tf_op jit(solution)/shard_map/ppermute | solution.py:93
  130.3 5.9 %collective-permute-start.10 = (bf16[128,256]{1,0:T(8,128)(2,1)S(1)}, bf16[128,256]{1,0:T(8,128)(2,1)S(1)}, u32[]{:S(2)}, u32[]{:S(2)}) collective-permute-start(bf16[128,256]{1,0:T(8,128)(2,1)S(1)} %get-tuple-element.73), channel_id=1, source_target_pairs={{0,32},{1,33},{2,34},{3,35},{4,36},{5,37},{6,38},{7,39},{8,40},{9,... | collective-permute-start | bytes 196616 | tf_op jit(solution)/shard_map/ppermute | solution.py:179
  131.4 4.7 %collective-permute-start.9 = (bf16[128,256]{1,0:T(8,128)(2,1)S(1)}, bf16[128,256]{1,0:T(8,128)(2,1)S(1)}, u32[]{:S(2)}, u32[]{:S(2)}) collective-permute-start(bf16[128,256]{1,0:T(8,128)(2,1)S(1)} %get-tuple-element.74), channel_id=1, source_target_pairs={{0,16},{1,17},{2,18},{3,19},{4,20},{5,21},{6,22},{7,23},{8,24},{9,... | collective-permute-start | bytes 196616 | tf_op jit(solution)/shard_map/ppermute | solution.py:179
  137.3 6.1 %collective-permute-start.15 = (bf16[196,256]{1,0:T(8,128)(2,1)S(1)}, bf16[196,256]{1,0:T(8,128)(2,1)S(1)}, u32[]{:S(2)}, u32[]{:S(2)}) collective-permute-start(bf16[196,256]{1,0:T(8,128)(2,1)S(1)} %get-tuple-element.58), channel_id=1, source_target_pairs={{0,64},{64,128},{128,192},{192,0},{1,65},{65,129},{129,193},{193,1... | collective-permute-start | bytes 301064 | tf_op jit(solution)/shard_map/ppermute | solution.py:93
  137.5 5.9 %collective-permute-start.17 = (bf16[196,256]{1,0:T(8,128)(2,1)S(1)}, bf16[196,256]{1,0:T(8,128)(2,1)S(1)}, u32[]{:S(2)}, u32[]{:S(2)}) collective-permute-start(bf16[196,256]{1,0:T(8,128)(2,1)S(1)} %get-tuple-element.60), channel_id=1, source_target_pairs={{0,192},{64,0},{128,64},{192,128},{1,193},{65,1},{129,65},{193,129... | collective-permute-start | bytes 301064 | tf_op jit(solution)/shard_map/ppermute | solution.py:93
  140.0 6.0 %collective-permute-start.16 = (bf16[196,256]{1,0:T(8,128)(2,1)S(1)}, bf16[196,256]{1,0:T(8,128)(2,1)S(1)}, u32[]{:S(2)}, u32[]{:S(2)}) collective-permute-start(bf16[196,256]{1,0:T(8,128)(2,1)S(1)} %get-tuple-element.59), channel_id=1, source_target_pairs={{0,128},{64,192},{128,0},{192,64},{1,129},{65,193},{129,1},{193,65... | collective-permute-start | bytes 301064 | tf_op jit(solution)/shard_map/ppermute | solution.py:93
  146.4 15.1 %collective-permute-start.20 = (bf16[192,1152]{1,0:T(8,128)(2,1)S(1)}, bf16[192,1152]{1,0:T(8,128)(2,1)S(1)}, u32[]{:S(2)}, u32[]{:S(2)}) collective-permute-start(bf16[192,1152]{1,0:T(8,128)(2,1)S(1)} %sum_parts.1.refs_0_), channel_id=1, source_target_pairs={{0,192},{64,0},{128,64},{192,128},{1,193},{65,1},{129,65},{193,129... | collective-permute-start | bytes 1327112 | tf_op jit(solution)/shard_map/ppermute | solution.py:93
  146.9 16.3 %collective-permute-start.19 = (bf16[192,1152]{1,0:T(8,128)(2,1)S(1)}, bf16[192,1152]{1,0:T(8,128)(2,1)S(1)}, u32[]{:S(2)}, u32[]{:S(2)}) collective-permute-start(bf16[192,1152]{1,0:T(8,128)(2,1)S(1)} %sum_parts.1.refs_0_), channel_id=1, source_target_pairs={{0,64},{64,128},{128,192},{192,0},{1,65},{65,129},{129,193},{193,1... | collective-permute-start | bytes 1327112 | tf_op jit(solution)/shard_map/ppermute | solution.py:93
  147.9 22.4 %collective-permute-start.18 = (bf16[192,1152]{1,0:T(8,128)(2,1)S(1)}, bf16[192,1152]{1,0:T(8,128)(2,1)S(1)}, u32[]{:S(2)}, u32[]{:S(2)}) collective-permute-start(bf16[192,1152]{1,0:T(8,128)(2,1)S(1)} %sum_parts.1.refs_0_), channel_id=1, source_target_pairs={{0,128},{64,192},{128,0},{192,64},{1,129},{65,193},{129,1},{193,65... | collective-permute-start | bytes 1327112 | tf_op jit(solution)/shard_map/ppermute | solution.py:93
  148.2 22.3 %collective-permute-start.21 = (bf16[128,1152]{1,0:T(8,128)(2,1)S(1)}, bf16[128,1152]{1,0:T(8,128)(2,1)S(1)}, u32[]{:S(2)}, u32[]{:S(2)}) collective-permute-start(bf16[128,1152]{1,0:T(8,128)(2,1)S(1)} %slice.52), channel_id=1, source_target_pairs={{0,1},{1,0},{2,3},{3,2},{4,5},{5,4},{6,7},{7,6},{8,9},{9,8},{10,11... | collective-permute-start | bytes 884744 | tf_op jit(solution)/shard_map/ppermute | solution.py:474
  161.5 8.9 %collective-permute-start.24 = (bf16[128,1152]{1,0:T(8,128)(2,1)S(1)}, bf16[128,1152]{1,0:T(8,128)(2,1)S(1)}, u32[]{:S(2)}, u32[]{:S(2)}) collective-permute-start(bf16[128,1152]{1,0:T(8,128)(2,1)S(1)} %slice.65), channel_id=1, source_target_pairs={{0,1},{1,0},{2,3},{3,2},{4,5},{5,4},{6,7},{7,6},{8,9},{9,8},{10,11... | collective-permute-start | bytes 884744 | tf_op jit(solution)/shard_map/ppermute | solution.py:474
  163.2 8.3 %collective-permute-start.22 = (bf16[128,1152]{1,0:T(8,128)(2,1)S(1)}, bf16[128,1152]{1,0:T(8,128)(2,1)S(1)}, u32[]{:S(2)}, u32[]{:S(2)}) collective-permute-start(bf16[128,1152]{1,0:T(8,128)(2,1)S(1)} %slice.64), channel_id=1, source_target_pairs={{0,1},{1,0},{2,3},{3,2},{4,5},{5,4},{6,7},{7,6},{8,9},{9,8},{10,11... | collective-permute-start | bytes 884744 | tf_op jit(solution)/shard_map/ppermute | solution.py:474
  (17 other events, 288.3 us)

commit v10 on v9

--- a/solution.py
+++ b/solution.py
@@ -315,32 +315,39 @@
 SUM_ROWS = 192
 
 
+CLASS_ROWS = 11
+
+
 def sum_kernel(*refs):
-    heads, firsts, out_ref = refs[:4], refs[4:8], refs[8]
-    tall, wide = heads[0].shape
+    heads, firsts, out_ref, rest = refs[:4], refs[4:8], refs[8], refs[9]
+    tall = heads[0].shape[0]
+    hid = out_ref.shape[1]
     total = heads[0][...]
     for ref in heads[1:]:
         total = total + ref[...].astype(F32)
-    out_ref[:tall, :] = total.astype(BF16)
+    out_ref[:tall, :] = total[:, :hid].astype(BF16)
     first = firsts[0][...]
     for ref in firsts[1:]:
         first = first + ref[...].astype(F32)
     depth, cols = first.shape
     quarter = depth // 4
-    rest = jnp.zeros((SUM_ROWS - tall, wide), BF16)
-    out_ref[tall:, :] = rest
+    rest[...] = jnp.zeros_like(rest)
+    for k in range(hid // 128):
+        rest[:CLASS_ROWS, k * 128 : (k + 1) * 128] = total[k * CLASS_ROWS : (k + 1) * CLASS_ROWS, hid:]
     for q in range(4):
-        part = first[q * quarter : (q + 1) * quarter].astype(BF16)
-        out_ref[tall : tall + quarter, q * cols : (q + 1) * cols] = part
+        part = first[q * quarter : (q + 1) * quarter]
+        rest[CLASS_ROWS : CLASS_ROWS + quarter, q * cols : (q + 1) * cols] = part
+    out_ref[tall:, :] = rest[...].astype(BF16)
 
 
 def sum_parts(heads, firsts):
-    wide = heads[0].shape[1]
+    tall, wide = heads[0].shape[0], heads[0].shape[1] - 128
     return pl.pallas_call(
         sum_kernel,
         out_shape=jax.ShapeDtypeStruct((SUM_ROWS, wide), BF16),
         in_specs=vmem_spec(8),
         out_specs=pl.BlockSpec(memory_space=pltpu.VMEM),
+        scratch_shapes=[pltpu.VMEM((SUM_ROWS - tall, wide), F32)],
         compiler_params=pltpu.CompilerParams(vmem_limit_bytes=VMEM),
         name="sum_parts",
     )(*heads, *firsts)
@@ -353,7 +360,7 @@
     hid = fc2_ref.shape[1]
     images = 4
     classes = class_ref.shape[0]
-    tall = other[0].shape[0]
+    tall = hid // NC // images
     depth = fc1_ref.shape[0]
     quarter = depth // 4
     wide = hid // images
@@ -361,16 +368,21 @@
         chunk = lax.rem(image + images - step, images)
         for side, ref in ((core, mine[step]), (1 - core, other[step])):
             at = pl.ds(pl.multiple_of(side * (hid // NC) + chunk * tall, tall), tall)
-            fc2_ref[at, :] = ref[:tall, :hid].astype(F32)
-            class_ref[:, at] = ref[:classes, hid:].astype(F32)
+            fc2_ref[at, :] = ref[:tall, :].astype(F32)
+            rest = ref[tall : tall + 16, :].astype(F32)
+            for k in range(hid // 128):
+                count = min(CLASS_ROWS, classes - k * CLASS_ROWS)
+                part = rest[:count, k * 128 : (k + 1) * 128]
+                class_ref[k * CLASS_ROWS : k * CLASS_ROWS + count, at] = part
         cols = pl.ds(pl.multiple_of(chunk * wide, wide), wide)
+        rest = mine[step][tall:, :].astype(F32)
         for q in range(4):
-            part = mine[step][tall : tall + quarter, q * wide : (q + 1) * wide]
-            fc1_ref[q * quarter : (q + 1) * quarter, cols] = part.astype(F32)
+            part = rest[CLASS_ROWS : CLASS_ROWS + quarter, q * wide : (q + 1) * wide]
+            fc1_ref[q * quarter : (q + 1) * quarter, cols] = part
 
 
 def assemble(place, mine, other, depth, classes):
-    hid = mine[0].shape[1] - 128
+    hid = mine[0].shape[1]
     struct = jax.ShapeDtypeStruct
     return pl.pallas_call(
         assemble_kernel,
@@ -470,7 +482,7 @@
     mine = [total] + [shift_img(total, step) for step in range(1, 4)]
     rpn_out = rpn(before, inner, after, w_rpn, w_anchor)
     mine[2], rpn_out = lax.optimization_barrier((mine[2], rpn_out))
-    tall = head_own.shape[0]
+    tall = head_own.shape[0] + 16
     other = [lax.ppermute(part[:tall], "band", CORE_SWAP) for part in mine]
     grad_fc1, grad_fc2, grad_class = assemble(place, mine, other, depth, w_class.shape[1])
     return (rpn_out, grad_fc1, grad_fc2, grad_class.T)

time: 176 us -> 174 us (0.989)
  starting transfers between devices: 52.5 us -> 50.4 us
    ppermute x4, starting transfers between devices: 13.3 us -> 11.2 us  [shards(): other = [lax.ppermute(part[:tall], 'band', CORE_SWAP) for part in mine]]
where the time goes in v10:
time: 174 us; the launch traced here: 173 us
  starting transfers between devices  50.4 us (29%)
  blocking collectives  50 us (29%)
  Pallas kernels  32.5 us (19%)
  waiting for transfers between devices  26.5 us (15%)
  local copies, waits for them, and re-layouts  8.58 us (5%)
  matrix products  4.04 us (2%)
    all_to_all x4, blocking collectives, exchange(): lax.all_to_all(array, 'band', split_axis=0, concat_axis=0, tiled=True, ax...  50 us
    all_to_all x1, waiting for transfers between devices, shards(): lax.all_to_all(sending, 'band', split_axis=0, concat_axis=0, tiled=True)  15.8 us
    all_to_all x1, starting transfers between devices, shards(): lax.all_to_all(sending, 'band', split_axis=0, concat_axis=0, tiled=True)  13.3 us
    ppermute x4, starting transfers between devices, shards(): other = [lax.ppermute(part[:tall], 'band', CORE_SWAP) for part in mine]  11.2 us
    ppermute x9, starting transfers between devices, shift_img(): lax.ppermute(array, 'img', [(i, (i + step) % size) for i in range(size)])  9.14 us
    pallas_call x1, Pallas kernels, rpn(): pl.pallas_call(rpn_kernel, out_shape=jax.ShapeDtypeStruct((anchors, rows,...  8.83 us
    ppermute x6, starting transfers between devices, shift_y(): lax.ppermute(array, 'band', [(b, (b + step * row) % BAND) for b in range(...  6.18 us
    pallas_call x1, Pallas kernels, head(): pl.pallas_call(head_kernel, out_shape=[struct((count, hid), BF16), struct...  5.76 us
  transfers between devices with their start and end apart: 26, of which 7 were waited for; matrix products, arithmetic and copies ran while one was open for 5% of the time, Pallas kernels for 8%

profile of v10, /device:TPU:1, one launch (start us, length us, event | category | flops | bytes accessed | tf_op | source)
XLA Modules:
  0.0 173.2 jit_solution(6763710416327747350)
XLA Ops:
  0.6 1.6 copy-done.5
  3.0 5.6 %collect.1 = bf16[64,32,256]{2,1,0:T(8,128)(2,1)} custom-call(s32[32,64]{1,0:T(8,128)S(1)} %bitcast.54, bf16[4096,256]{1,0:T(8,128)(2,1)S(1)} %bitcast.52), custom_call_target="tpu_custom_call" | custom-call | flops 4000000000 | bytes 3000000 | tf_op jit(solution)/shard_map/collect/pallas_call | solution.py:113
  8.5 13.3 %all-to-all-start = ((bf16[64,32,256]{2,1,0:T(8,128)(2,1)}), bf16[64,32,256]{2,1,0:T(8,128)(2,1)S(1)}, u32[]{:S(2)}, u32[]{:S(2)}) async-start(bf16[64,32,256]{2,1,0:T(8,128)(2,1)} %collect.1), calls=%async_computation | async-start | bytes 2097152 | tf_op jit(solution)/shard_map/all_to_all | solution.py:425
  21.8 2.9 %collective-permute-start.2 = (bf16[196,1024]{1,0:T(8,128)(2,1)S(1)}, bf16[196,1024]{1,0:T(8,128)(2,1)S(1)}, u32[]{:S(2)}, u32[]{:S(2)}) collective-permute-start(bf16[196,1024]{1,0:T(8,128)(2,1)S(1)} %copy-done.3), channel_id=1, source_target_pairs={{0,48},{1,49},{2,50},{3,51},{4,52},{5,53},{6,54},{7,55},{8,56},{9,... | collective-permute-start | bytes 1204232 | tf_op jit(solution)/shard_map/ppermute | solution.py:179
  27.0 1.8 %slice_bitcast_fusion = (bf16[1,512,256]{2,1,0:T(8,128)(2,1)}, bf16[1,512,256]{2,1,0:T(8,128)(2,1)S(1)}) fusion(bf16[1,8,512,256]{3,2,1,0:T(8,128)(2,1)} %param.10), kind=kLoop, calls=%fused_computation.22 | loop fusion | bytes 1048576 | tf_op jit(solution)/shard_map/squeeze | solution.py:25
  28.8 1.9 %collective-permute-start.4 = (bf16[1,512,256]{2,1,0:T(8,128)(2,1)}, bf16[1,512,256]{2,1,0:T(8,128)(2,1)S(1)}, u32[]{:S(2)}, u32[]{:S(2)}) collective-permute-start(bf16[1,512,256]{2,1,0:T(8,128)(2,1)} %get-tuple-element.70), channel_id=1, source_target_pairs={{1,0},{2,1},{3,2},{4,3},{5,4},{6,5},{7,6},{8,7},{9,8},{10,9},{11,1... | collective-permute-start | bytes 786440 | tf_op jit(solution)/shard_map/ppermute | solution.py:25
  31.1 3.6 %collective-permute-start.3 = (bf16[1,512,256]{2,1,0:T(8,128)(2,1)S(1)}, bf16[1,512,256]{2,1,0:T(8,128)(2,1)S(1)}, u32[]{:S(2)}, u32[]{:S(2)}) collective-permute-start(bf16[1,512,256]{2,1,0:T(8,128)(2,1)S(1)} %get-tuple-element.71), channel_id=1, source_target_pairs={{0,1},{1,2},{2,3},{3,4},{4,5},{5,6},{6,7},{7,8},{8,9},{9,10},{10,1... | collective-permute-start | bytes 786440 | tf_op jit(solution)/shard_map/ppermute | solution.py:24
  34.7 15.8 %all-to-all-done = bf16[64,32,256]{2,1,0:T(8,128)(2,1)S(1)} async-done(((bf16[64,32,256]{2,1,0:T(8,128)(2,1)}), bf16[64,32,256]{2,1,0:T(8,128)(2,1)S(1)}, u32[]{:S(2)}, u32[]{:S(2)}) %all-to-all-start) | async-done | bytes 1048608 | tf_op jit(solution)/shard_map/all_to_all | solution.py:425
  50.6 4.0 %fusion.17 = bf16[392,256]{1,0:T(8,128)(2,1)} fusion(bf16[2048,256]{1,0:T(8,128)(2,1)S(1)} %bitcast.57, f32[392]{0:T(512)S(1)} %bitcast.65, s32[392]{0:T(512)S(1)} %bitcast.61, f32[392]{0:T(512)S(1)} %bitcast.66, s32[392]{0:T(512)S(1)} %bitcast.62, f32[392]{0:T(512)S(1)} %bitcast.67, s32[392]{0:T(512)S(1)} %bitcast.63, f32[392]{0:T(512)S(1)} %bitcast.64, ...), kind=kOutput, calls=%fused_computation.21 | convolution fusion | flops 2475182080 | bytes 1261824 | tf_op jit(solution)/shard_map/dot_general | solution.py:444
  59.5 17.6 %all_to_all.25 = bf16[16,8,1024]{2,1,0:T(8,128)(2,1)S(1)} all-to-all(bf16[16,8,1024]{2,1,0:T(8,128)(2,1)S(1)} %reshape.49), channel_id=1, replica_groups={{0,1,2,3,4,5,6,7,8,9,10,11,12,13,14,15},{16,17,18,19,20,21,22,23,24,25,..., dimensions={0} | all-to-all | bytes 524288 | tf_op jit(solution)/shard_map/all_to_all | solution.py:82
  81.3 10.9 %all_to_all.26 = bf16[8,16,512]{2,1,0:T(8,128)(2,1)S(1)} all-to-all(bf16[8,16,512]{2,1,0:T(8,128)(2,1)S(1)} %bitcast.50), channel_id=1, replica_groups={{0,2,4,6,8,10,12,14},{1,3,5,7,9,11,13,15},{16,18,20,22,24,26,28,30},{17..., dimensions={0} | all-to-all | bytes 262144 | tf_op jit(solution)/shard_map/all_to_all | solution.py:82
  92.3 10.8 %all_to_all.27 = bf16[8,16,640]{2,1,0:T(8,128)(2,1)S(1)} all-to-all(bf16[8,16,640]{2,1,0:T(8,128)(2,1)S(1)} %broadcast_in_dim.11), channel_id=1, replica_groups={{0,2,4,6,8,10,12,14},{1,3,5,7,9,11,13,15},{16,18,20,22,24,26,28,30},{17..., dimensions={0} | all-to-all | bytes 327680 | tf_op jit(solution)/shard_map/all_to_all | solution.py:82
  103.1 10.7 %all_to_all.28 = bf16[4,128,640]{2,1,0:T(8,128)(2,1)S(1)} all-to-all(bf16[4,128,640]{2,1,0:T(8,128)(2,1)S(1)} %broadcast_in_dim.26), channel_id=1, replica_groups={{0,16,32,48},{1,17,33,49},{2,18,34,50},{3,19,35,51},{4,20,36,52},{5,21,..., dimensions={0} | all-to-all | bytes 1310720 | tf_op jit(solution)/shard_map/all_to_all | solution.py:82
  113.9 3.5 %collective-permute-start.8 = (bf16[512,640]{1,0:T(8,128)(2,1)S(1)}, bf16[512,640]{1,0:T(8,128)(2,1)}, u32[]{:S(2)}, u32[]{:S(2)}) collective-permute-start(bf16[512,640]{1,0:T(8,128)(2,1)S(1)} %bitcast.44), channel_id=1, source_target_pairs={{0,1},{1,0},{2,3},{3,2},{4,5},{5,4},{6,7},{7,6},{8,9},{9,8},{10,11... | collective-permute-start | bytes 1966088 | tf_op jit(solution)/shard_map/ppermute | solution.py:467
  117.3 1.9 %collective-permute-done.8.other_ref = bf16[512,640]{1,0:T(8,128)(2,1)} collective-permute-done((bf16[512,640]{1,0:T(8,128)(2,1)S(1)}, bf16[512,640]{1,0:T(8,128)(2,1)}, u32[]{:S(2)}, u32[]{:S(2)}) %collective-permute-start.8) | collective-permute-done | bytes 655392 | tf_op jit(solution)/shard_map/ppermute | solution.py:467
  119.2 5.8 %head.1 = (bf16[512,1024]{1,0:T(8,128)(2,1)S(1)}, f32[128,1152]{1,0:T(8,128)S(1)}, bf16[128,1152]{1,0:T(8,128)(2,1)S(1)}, bf16[128,1152]{1,0:T(8,128)(2,1)S(1)}, bf16[128,1152]{1,0:T(8,128)(2,1)S(1)}) custom-call(s32[3]{0:T(128)S(1)} %pad_add_fusion.place, bf16[512,640]{1,0:T(8,128)(2,1)S(1)} %bitcast.45, bf16[512,640]{1,0:T(8,128)(2,1)} %collective-permute-done.8.other_ref, ...), custom_call_target="tpu_custom_call" | custom-call | tf_op jit(solution)/shard_map/head/pallas_call | solution.py:246
  131.5 4.6 %back.1.da1_ref = bf16[512,1024]{1,0:T(8,128)(2,1)S(1)} custom-call(s32[3]{0:T(128)S(1)} %pad_add_fusion.place, bf16[512,640]{1,0:T(8,128)(2,1)S(1)} %bitcast.46, bf16[512,640]{1,0:T(8,128)(2,1)} %collective-permute-done.8.other_ref, bf16[512,1024]{1,0:T(8,128)(2,1)S(1)} %get-tuple-element.49.da2_ref, bf16[1024,1024]{1,0:T(8,128)(2,1)S(1)} %copy-done), custom_call_target="tpu_custom_call" | custom-call | flops 2000000000 | bytes 5000000 | tf_op jit(solution)/shard_map/back/pallas_call | solution.py:272
  137.5 2.5 %collective-permute-start.17 = (bf16[196,256]{1,0:T(8,128)(2,1)S(1)}, bf16[196,256]{1,0:T(8,128)(2,1)S(1)}, u32[]{:S(2)}, u32[]{:S(2)}) collective-permute-start(bf16[196,256]{1,0:T(8,128)(2,1)S(1)} %get-tuple-element.60), channel_id=1, source_target_pairs={{0,192},{64,0},{128,64},{192,128},{1,193},{65,1},{129,65},{193,129... | collective-permute-start | bytes 301064 | tf_op jit(solution)/shard_map/ppermute | solution.py:93
  140.3 3.1 %collective-permute-done.15.refs_5_ = bf16[196,256]{1,0:T(8,128)(2,1)S(1)} collective-permute-done((bf16[196,256]{1,0:T(8,128)(2,1)S(1)}, bf16[196,256]{1,0:T(8,128)(2,1)S(1)}, u32[]{:S(2)}, u32[]{:S(2)}) %collective-permute-start.15) | collective-permute-done | bytes 100384 | tf_op jit(solution)/shard_map/ppermute | solution.py:93
  143.4 2.6 %collective-permute-done.16.refs_6_ = bf16[196,256]{1,0:T(8,128)(2,1)S(1)} collective-permute-done((bf16[196,256]{1,0:T(8,128)(2,1)S(1)}, bf16[196,256]{1,0:T(8,128)(2,1)S(1)}, u32[]{:S(2)}, u32[]{:S(2)}) %collective-permute-start.16) | collective-permute-done | bytes 100384 | tf_op jit(solution)/shard_map/ppermute | solution.py:93
  148.1 4.5 %collective-permute-start.21 = (bf16[144,1024]{1,0:T(8,128)(2,1)S(1)}, bf16[144,1024]{1,0:T(8,128)(2,1)S(1)}, u32[]{:S(2)}, u32[]{:S(2)}) collective-permute-start(bf16[144,1024]{1,0:T(8,128)(2,1)S(1)} %slice.52), channel_id=1, source_target_pairs={{0,1},{1,0},{2,3},{3,2},{4,5},{5,4},{6,7},{7,6},{8,9},{9,8},{10,11... | collective-permute-start | bytes 884744 | tf_op jit(solution)/shard_map/ppermute | solution.py:486
  152.6 8.8 %rpn.1 = bf16[15,8,512]{2,1,0:T(8,128)(2,1)} custom-call(bf16[1,512,256]{2,1,0:T(8,128)(2,1)S(1)} %copy-done.9, bf16[8,512,256]{2,1,0:T(8,128)(2,1)S(1)} %bitcast.53, bf16[1,512,256]{2,1,0:T(8,128)(2,1)S(1)} %collective-permute-done.4.after_ref, bf16[3,3,256,256]{3,2,1,0:T(8,128)(2,1)S(1)} %copy-done.7, bf16[15,256]{1,0:T(8,128)(2,1)S(1)} %bitcast.55), custom_call_target="tpu_custom_call" | custom-call | flops 8999999488 | bytes 4000000 | tf_op jit(solution)/shard_map/rpn/pallas_call | solution.py:58
  162.1 6.0 %collective-permute-start.22 = (bf16[144,1024]{1,0:T(8,128)(2,1)S(1)}, bf16[144,1024]{1,0:T(8,128)(2,1)S(1)}, u32[]{:S(2)}, u32[]{:S(2)}) collective-permute-start(bf16[144,1024]{1,0:T(8,128)(2,1)S(1)} %slice.64), channel_id=1, source_target_pairs={{0,1},{1,0},{2,3},{3,2},{4,5},{5,4},{6,7},{7,6},{8,9},{9,8},{10,11... | collective-permute-start | bytes 884744 | tf_op jit(solution)/shard_map/ppermute | solution.py:486
  169.9 3.3 %assemble.1 = (f32[196,1024]{1,0:T(8,128)}, f32[1024,1024]{1,0:T(8,128)}, f32[81,1024]{1,0:T(8,128)}) custom-call(s32[3]{0:T(128)S(1)} %pad_add_fusion.place, bf16[192,1024]{1,0:T(8,128)(2,1)S(1)} %sum_parts.1.refs_0_, bf16[192,1024]{1,0:T(8,128)(2,1)S(1)} %collective-permute-done.19.refs_1_, bf16[192,1024]{1,0:T(8,128)(2,1)S(1)} %collective-permute-done.18.refs_2_, ...), custom_call_target="tpu_custom_call" | custom-call | tf_op jit(solution)/shard_map/assemble/pallas_call | solution.py:387
  (98 shorter events, 25.2 us)
Async XLA Ops:
  8.5 42.0 %all-to-all-start = ((bf16[64,32,256]{2,1,0:T(8,128)(2,1)}), bf16[64,32,256]{2,1,0:T(8,128)(2,1)S(1)}, u32[]{:S(2)}, u32[]{:S(2)}) async-start(bf16[64,32,256]{2,1,0:T(8,128)(2,1)} %collect.1), calls=%async_computation | async-start | bytes 2097152 | tf_op jit(solution)/shard_map/all_to_all | solution.py:425
  21.8 34.5 %collective-permute-start.2 = (bf16[196,1024]{1,0:T(8,128)(2,1)S(1)}, bf16[196,1024]{1,0:T(8,128)(2,1)S(1)}, u32[]{:S(2)}, u32[]{:S(2)}) collective-permute-start(bf16[196,1024]{1,0:T(8,128)(2,1)S(1)} %copy-done.3), channel_id=1, source_target_pairs={{0,48},{1,49},{2,50},{3,51},{4,52},{5,53},{6,54},{7,55},{8,56},{9,... | collective-permute-start | bytes 1204232 | tf_op jit(solution)/shard_map/ppermute | solution.py:179
  24.7 31.6 %collective-permute-start.1 = (bf16[196,1024]{1,0:T(8,128)(2,1)S(1)}, bf16[196,1024]{1,0:T(8,128)(2,1)S(1)}, u32[]{:S(2)}, u32[]{:S(2)}) collective-permute-start(bf16[196,1024]{1,0:T(8,128)(2,1)S(1)} %copy-done.3), channel_id=1, source_target_pairs={{0,32},{1,33},{2,34},{3,35},{4,36},{5,37},{6,38},{7,39},{8,40},{9,... | collective-permute-start | bytes 1204232 | tf_op jit(solution)/shard_map/ppermute | solution.py:179
  25.1 31.2 %collective-permute-start = (bf16[196,1024]{1,0:T(8,128)(2,1)S(1)}, bf16[196,1024]{1,0:T(8,128)(2,1)S(1)}, u32[]{:S(2)}, u32[]{:S(2)}) collective-permute-start(bf16[196,1024]{1,0:T(8,128)(2,1)S(1)} %copy-done.3), channel_id=1, source_target_pairs={{0,16},{1,17},{2,18},{3,19},{4,20},{5,21},{6,22},{7,23},{8,24},{9,... | collective-permute-start | bytes 1204232 | tf_op jit(solution)/shard_map/ppermute | solution.py:179
  25.8 5.3 %collective-permute-start.5 = (bf16[8,128]{1,0:T(8,128)(2,1)S(1)}, bf16[8,128]{1,0:T(8,128)(2,1)S(1)}, u32[]{:S(2)}, u32[]{:S(2)}) collective-permute-start(bf16[8,128]{1,0:T(8,128)(2,1)S(1)} %broadcast_in_dim.10), channel_id=1, source_target_pairs={{0,1},{1,0},{2,3},{3,2},{4,5},{5,4},{6,7},{7,6},{8,9},{9,8},{10,11... | collective-permute-start | bytes 6152 | tf_op jit(solution)/shard_map/ppermute | solution.py:432
  28.8 27.4 %collective-permute-start.4 = (bf16[1,512,256]{2,1,0:T(8,128)(2,1)}, bf16[1,512,256]{2,1,0:T(8,128)(2,1)S(1)}, u32[]{:S(2)}, u32[]{:S(2)}) collective-permute-start(bf16[1,512,256]{2,1,0:T(8,128)(2,1)} %get-tuple-element.70), channel_id=1, source_target_pairs={{1,0},{2,1},{3,2},{4,3},{5,4},{6,5},{7,6},{8,7},{9,8},{10,9},{11,1... | collective-permute-start | bytes 786440 | tf_op jit(solution)/shard_map/ppermute | solution.py:25
  31.1 25.2 %collective-permute-start.3 = (bf16[1,512,256]{2,1,0:T(8,128)(2,1)S(1)}, bf16[1,512,256]{2,1,0:T(8,128)(2,1)S(1)}, u32[]{:S(2)}, u32[]{:S(2)}) collective-permute-start(bf16[1,512,256]{2,1,0:T(8,128)(2,1)S(1)} %get-tuple-element.71), channel_id=1, source_target_pairs={{0,1},{1,2},{2,3},{3,4},{4,5},{5,6},{6,7},{7,8},{8,9},{9,10},{10,1... | collective-permute-start | bytes 786440 | tf_op jit(solution)/shard_map/ppermute | solution.py:24
  58.8 19.8 %collective-permute-start.7 = (bf16[808,512]{1,0:T(8,128)(2,1)}, bf16[808,512]{1,0:T(8,128)(2,1)}, u32[]{:S(2)}, u32[]{:S(2)}) collective-permute-start(bf16[808,512]{1,0:T(8,128)(2,1)} %get-tuple-element.46), channel_id=1, source_target_pairs={{0,1},{1,0},{2,3},{3,2},{4,5},{5,4},{6,7},{7,6},{8,9},{9,8},{10,11... | collective-permute-start | bytes 2482184 | tf_op jit(solution)/shard_map/ppermute | solution.py:453
  113.9 5.4 %collective-permute-start.8 = (bf16[512,640]{1,0:T(8,128)(2,1)S(1)}, bf16[512,640]{1,0:T(8,128)(2,1)}, u32[]{:S(2)}, u32[]{:S(2)}) collective-permute-start(bf16[512,640]{1,0:T(8,128)(2,1)S(1)} %bitcast.44), channel_id=1, source_target_pairs={{0,1},{1,0},{2,3},{3,2},{4,5},{5,4},{6,7},{7,6},{8,9},{9,8},{10,11... | collective-permute-start | bytes 1966088 | tf_op jit(solution)/shard_map/ppermute | solution.py:467
  125.0 15.0 %collective-permute-start.12 = (bf16[128,1152]{1,0:T(8,128)(2,1)S(1)}, bf16[128,1152]{1,0:T(8,128)(2,1)S(1)}, u32[]{:S(2)}, u32[]{:S(2)}) collective-permute-start(bf16[128,1152]{1,0:T(8,128)(2,1)S(1)} %get-tuple-element.52), channel_id=1, source_target_pairs={{0,64},{64,128},{128,192},{192,0},{1,65},{65,129},{129,193},{193,1... | collective-permute-start | bytes 884744 | tf_op jit(solution)/shard_map/ppermute | solution.py:93
  126.3 13.7 %collective-permute-start.13 = (bf16[128,1152]{1,0:T(8,128)(2,1)S(1)}, bf16[128,1152]{1,0:T(8,128)(2,1)S(1)}, u32[]{:S(2)}, u32[]{:S(2)}) collective-permute-start(bf16[128,1152]{1,0:T(8,128)(2,1)S(1)} %get-tuple-element.53), channel_id=1, source_target_pairs={{0,192},{64,0},{128,64},{192,128},{1,193},{65,1},{129,65},{193,129... | collective-permute-start | bytes 884744 | tf_op jit(solution)/shard_map/ppermute | solution.py:93
  127.8 3.7 %collective-permute-start.11 = (bf16[128,256]{1,0:T(8,128)(2,1)S(1)}, bf16[128,256]{1,0:T(8,128)(2,1)S(1)}, u32[]{:S(2)}, u32[]{:S(2)}) collective-permute-start(bf16[128,256]{1,0:T(8,128)(2,1)S(1)} %get-tuple-element.72), channel_id=1, source_target_pairs={{0,48},{1,49},{2,50},{3,51},{4,52},{5,53},{6,54},{7,55},{8,56},{9,... | collective-permute-start | bytes 196616 | tf_op jit(solution)/shard_map/ppermute | solution.py:179
  128.7 14.7 %collective-permute-start.14 = (bf16[128,1152]{1,0:T(8,128)(2,1)S(1)}, bf16[128,1152]{1,0:T(8,128)(2,1)S(1)}, u32[]{:S(2)}, u32[]{:S(2)}) collective-permute-start(bf16[128,1152]{1,0:T(8,128)(2,1)S(1)} %get-tuple-element.55), channel_id=1, source_target_pairs={{0,128},{64,192},{128,0},{192,64},{1,129},{65,193},{129,1},{193,65... | collective-permute-start | bytes 884744 | tf_op jit(solution)/shard_map/ppermute | solution.py:93
  130.3 5.9 %collective-permute-start.10 = (bf16[128,256]{1,0:T(8,128)(2,1)S(1)}, bf16[128,256]{1,0:T(8,128)(2,1)S(1)}, u32[]{:S(2)}, u32[]{:S(2)}) collective-permute-start(bf16[128,256]{1,0:T(8,128)(2,1)S(1)} %get-tuple-element.73), channel_id=1, source_target_pairs={{0,32},{1,33},{2,34},{3,35},{4,36},{5,37},{6,38},{7,39},{8,40},{9,... | collective-permute-start | bytes 196616 | tf_op jit(solution)/shard_map/ppermute | solution.py:179
  131.4 4.7 %collective-permute-start.9 = (bf16[128,256]{1,0:T(8,128)(2,1)S(1)}, bf16[128,256]{1,0:T(8,128)(2,1)S(1)}, u32[]{:S(2)}, u32[]{:S(2)}) collective-permute-start(bf16[128,256]{1,0:T(8,128)(2,1)S(1)} %get-tuple-element.74), channel_id=1, source_target_pairs={{0,16},{1,17},{2,18},{3,19},{4,20},{5,21},{6,22},{7,23},{8,24},{9,... | collective-permute-start | bytes 196616 | tf_op jit(solution)/shard_map/ppermute | solution.py:179
  137.3 6.1 %collective-permute-start.15 = (bf16[196,256]{1,0:T(8,128)(2,1)S(1)}, bf16[196,256]{1,0:T(8,128)(2,1)S(1)}, u32[]{:S(2)}, u32[]{:S(2)}) collective-permute-start(bf16[196,256]{1,0:T(8,128)(2,1)S(1)} %get-tuple-element.58), channel_id=1, source_target_pairs={{0,64},{64,128},{128,192},{192,0},{1,65},{65,129},{129,193},{193,1... | collective-permute-start | bytes 301064 | tf_op jit(solution)/shard_map/ppermute | solution.py:93
  137.5 5.9 %collective-permute-start.17 = (bf16[196,256]{1,0:T(8,128)(2,1)S(1)}, bf16[196,256]{1,0:T(8,128)(2,1)S(1)}, u32[]{:S(2)}, u32[]{:S(2)}) collective-permute-start(bf16[196,256]{1,0:T(8,128)(2,1)S(1)} %get-tuple-element.60), channel_id=1, source_target_pairs={{0,192},{64,0},{128,64},{192,128},{1,193},{65,1},{129,65},{193,129... | collective-permute-start | bytes 301064 | tf_op jit(solution)/shard_map/ppermute | solution.py:93
  140.0 6.0 %collective-permute-start.16 = (bf16[196,256]{1,0:T(8,128)(2,1)S(1)}, bf16[196,256]{1,0:T(8,128)(2,1)S(1)}, u32[]{:S(2)}, u32[]{:S(2)}) collective-permute-start(bf16[196,256]{1,0:T(8,128)(2,1)S(1)} %get-tuple-element.59), channel_id=1, source_target_pairs={{0,128},{64,192},{128,0},{192,64},{1,129},{65,193},{129,1},{193,65... | collective-permute-start | bytes 301064 | tf_op jit(solution)/shard_map/ppermute | solution.py:93
  146.3 15.1 %collective-permute-start.20 = (bf16[192,1024]{1,0:T(8,128)(2,1)S(1)}, bf16[192,1024]{1,0:T(8,128)(2,1)S(1)}, u32[]{:S(2)}, u32[]{:S(2)}) collective-permute-start(bf16[192,1024]{1,0:T(8,128)(2,1)S(1)} %sum_parts.1.refs_0_), channel_id=1, source_target_pairs={{0,192},{64,0},{128,64},{192,128},{1,193},{65,1},{129,65},{193,129... | collective-permute-start | bytes 1179656 | tf_op jit(solution)/shard_map/ppermute | solution.py:93
  146.9 15.2 %collective-permute-start.19 = (bf16[192,1024]{1,0:T(8,128)(2,1)S(1)}, bf16[192,1024]{1,0:T(8,128)(2,1)S(1)}, u32[]{:S(2)}, u32[]{:S(2)}) collective-permute-start(bf16[192,1024]{1,0:T(8,128)(2,1)S(1)} %sum_parts.1.refs_0_), channel_id=1, source_target_pairs={{0,64},{64,128},{128,192},{192,0},{1,65},{65,129},{129,193},{193,1... | collective-permute-start | bytes 1179656 | tf_op jit(solution)/shard_map/ppermute | solution.py:93
  147.9 20.3 %collective-permute-start.18 = (bf16[192,1024]{1,0:T(8,128)(2,1)S(1)}, bf16[192,1024]{1,0:T(8,128)(2,1)S(1)}, u32[]{:S(2)}, u32[]{:S(2)}) collective-permute-start(bf16[192,1024]{1,0:T(8,128)(2,1)S(1)} %sum_parts.1.refs_0_), channel_id=1, source_target_pairs={{0,128},{64,192},{128,0},{192,64},{1,129},{65,193},{129,1},{193,65... | collective-permute-start | bytes 1179656 | tf_op jit(solution)/shard_map/ppermute | solution.py:93
  148.1 20.1 %collective-permute-start.21 = (bf16[144,1024]{1,0:T(8,128)(2,1)S(1)}, bf16[144,1024]{1,0:T(8,128)(2,1)S(1)}, u32[]{:S(2)}, u32[]{:S(2)}) collective-permute-start(bf16[144,1024]{1,0:T(8,128)(2,1)S(1)} %slice.52), channel_id=1, source_target_pairs={{0,1},{1,0},{2,3},{3,2},{4,5},{5,4},{6,7},{7,6},{8,9},{9,8},{10,11... | collective-permute-start | bytes 884744 | tf_op jit(solution)/shard_map/ppermute | solution.py:486
  161.5 6.8 %collective-permute-start.24 = (bf16[144,1024]{1,0:T(8,128)(2,1)S(1)}, bf16[144,1024]{1,0:T(8,128)(2,1)S(1)}, u32[]{:S(2)}, u32[]{:S(2)}) collective-permute-start(bf16[144,1024]{1,0:T(8,128)(2,1)S(1)} %slice.65), channel_id=1, source_target_pairs={{0,1},{1,0},{2,3},{3,2},{4,5},{5,4},{6,7},{7,6},{8,9},{9,8},{10,11... | collective-permute-start | bytes 884744 | tf_op jit(solution)/shard_map/ppermute | solution.py:486
  162.1 7.2 %collective-permute-start.22 = (bf16[144,1024]{1,0:T(8,128)(2,1)S(1)}, bf16[144,1024]{1,0:T(8,128)(2,1)S(1)}, u32[]{:S(2)}, u32[]{:S(2)}) collective-permute-start(bf16[144,1024]{1,0:T(8,128)(2,1)S(1)} %slice.64), channel_id=1, source_target_pairs={{0,1},{1,0},{2,3},{3,2},{4,5},{5,4},{6,7},{7,6},{8,9},{9,8},{10,11... | collective-permute-start | bytes 884744 | tf_op jit(solution)/shard_map/ppermute | solution.py:486
  (17 other events, 288.3 us)

commit v11 on v10

--- a/solution.py
+++ b/solution.py
@@ -123,55 +123,35 @@
 
 
 PITCH = 256
-SHORT = 200
-
-
-def halves_kernel(place, *refs):
-    core = place[0]
-    sources, keep_ref, send_ref = refs[:NY], refs[NY], refs[NY + 1]
-    depth = sources[0].shape[0]
-    wide = keep_ref.shape[1]
-    for ref, side in ((keep_ref, core), (send_ref, 1 - core)):
-        ref[...] = jnp.zeros_like(ref)
-        for k, source in enumerate(sources):
-            cols = pl.ds(pl.multiple_of(side * wide, wide), wide)
-            ref[k * SHORT : k * SHORT + depth, :] = source[:, cols]
-
-
-def halves(place, slices):
-    shape = (NY * SHORT + 8, slices[0].shape[1] // NC)
-    return pl.pallas_call(
-        halves_kernel,
-        out_shape=[jax.ShapeDtypeStruct(shape, BF16)] * 2,
-        in_specs=[SMEM_SPEC] + vmem_spec(NY),
-        out_specs=vmem_spec(2),
-        compiler_params=pltpu.CompilerParams(vmem_limit_bytes=VMEM),
-        name="halves",
-    )(place, *slices)
-
-
-def partial_kernel(place, mine_ref, other_ref, keep_ref, got_ref, out_ref):
-    y_at = place[2]
-    total = None
+
+
+def partial_kernel(place, x_ref, *refs):
+    core, y_at = place[0], place[2]
+    slices, outs = refs[:NY], refs[NY:]
+    depth = slices[0].shape[0]
+    blocks = []
     for step in range(NY):
         start = lax.rem(y_at + NY - step, NY) * PITCH
-        cols = pl.ds(pl.multiple_of(start, PITCH), PITCH)
-        rows = slice(step * SHORT, (step + 1) * SHORT)
-        for ref, weight in ((mine_ref, keep_ref), (other_ref, got_ref)):
-            part = dot(ref[:, cols][:, :SHORT], weight[rows, :], (1, 0))
-            total = part if total is None else total + part
-    out_ref[...] = total.astype(BF16)
-
-
-def partial_sums(place, mine, other, keep, got):
+        blocks.append(x_ref[:, pl.ds(pl.multiple_of(start, PITCH), PITCH)][:, :depth])
+    for out, side in zip(outs, (core, 1 - core)):
+        wide = out.shape[1]
+        cols = pl.ds(pl.multiple_of(side * wide, wide), wide)
+        total = dot(blocks[0], slices[0][:, cols], (1, 0))
+        for step in range(1, NY):
+            total = total + dot(blocks[step], slices[step][:, cols], (1, 0))
+        out[...] = total.astype(out.dtype)
+
+
+def partial_sums(place, x_part, slices):
+    shape = (x_part.shape[0], slices[0].shape[1] // NC)
     return pl.pallas_call(
         partial_kernel,
-        out_shape=jax.ShapeDtypeStruct((mine.shape[0], keep.shape[1]), BF16),
-        in_specs=[SMEM_SPEC] + vmem_spec(4),
-        out_specs=pl.BlockSpec(memory_space=pltpu.VMEM),
+        out_shape=[jax.ShapeDtypeStruct(shape, F32), jax.ShapeDtypeStruct(shape, BF16)],
+        in_specs=[SMEM_SPEC] + vmem_spec(1 + NY),
+        out_specs=vmem_spec(2),
         compiler_params=pltpu.CompilerParams(vmem_limit_bytes=VMEM),
         name="partial_sums",
-    )(place, mine, other, keep, got)
+    )(place, x_part, *slices)
 
 
 def shift_y(array, step):
@@ -449,13 +429,11 @@
     x_local, slices, before, after, marks = lax.optimization_barrier(
         (x_local, slices, before, after, marks)
     )
-    keep, send = halves(place, slices)
-    got = lax.ppermute(send, "band", CORE_SWAP)
     x_part = exchange(x_local.reshape(NZ * NC, roi_count, NY * PITCH), ZC_GROUPS)
     x_part = x_part.reshape(NZ * NC * roi_count, NY * PITCH)
 
-    x_other = lax.ppermute(x_part, "band", CORE_SWAP)
-    partial = partial_sums(place, x_part, x_other, keep, got)
+    keep, send = partial_sums(place, x_part, slices)
+    partial = (keep + lax.ppermute(send, "band", CORE_SWAP).astype(F32)).astype(BF16)
     count = roi_count * nband
     by_z = exchange(partial.reshape(NZ, count // NY // NZ, half), Z_GROUPS)
     a1_own = jnp.sum(by_z.astype(F32), axis=0).astype(BF16)

time: 174 us -> 174 us (level)
  blocking collectives: 50 us -> 32.4 us
  waiting for transfers between devices: 26.5 us -> 38.3 us
  starting transfers between devices: 50.4 us -> 56.6 us
  local copies, waits for them, and re-layouts: 8.58 us -> 11.5 us
  Pallas kernels: 32.5 us -> 30.4 us
    all_to_all x4 -> x3, blocking collectives: 50 us -> 32.4 us  [exchange(): lax.all_to_all(array, 'band', split_axis=0, concat_axis=0, tiled=True, ax...]
    all_to_all x0 -> x1, waiting for transfers between devices: none -> 11.6 us  [exchange(): lax.all_to_all(array, 'band', split_axis=0, concat_axis=0, tiled=True, ax...]
    all_to_all x0 -> x1, starting transfers between devices: none -> 6.45 us  [exchange(): lax.all_to_all(array, 'band', split_axis=0, concat_axis=0, tiled=True, ax...]
    unnamed x32 -> x40, local copies, waits for them, and re-layouts: 4.43 us -> 7.44 us
    pallas_call x2 -> x1, Pallas kernels: 3.13 us -> 1 us  [partial_sums(): pl.pallas_call(partial_kernel, out_shape=[jax.ShapeDtypeStruct(shape, F32...]
  transfers between devices with their start and end apart: 26 -> 26, of which waited for: 7 -> 9; matrix products, arithmetic and copies ran while one was open for 5% -> 4% of each run, Pallas kernels for 8% -> 8%
where the time goes in v11:
time: 174 us; the launch traced here: 173 us
  starting transfers between devices  56.6 us (33%)
  waiting for transfers between devices  38.3 us (22%)
  blocking collectives  32.4 us (19%)
  Pallas kernels  30.4 us (17%)
  local copies, waits for them, and re-layouts  11.5 us (7%)
  matrix products  3.07 us (2%)
    all_to_all x3, blocking collectives, exchange(): lax.all_to_all(array, 'band', split_axis=0, concat_axis=0, tiled=True, ax...  32.4 us
    all_to_all x1, waiting for transfers between devices, shards(): lax.all_to_all(sending, 'band', split_axis=0, concat_axis=0, tiled=True)  15.6 us
    all_to_all x1, starting transfers between devices, shards(): lax.all_to_all(sending, 'band', split_axis=0, concat_axis=0, tiled=True)  13.3 us
    all_to_all x1, waiting for transfers between devices, exchange(): lax.all_to_all(array, 'band', split_axis=0, concat_axis=0, tiled=True, ax...  11.6 us
    ppermute x4, starting transfers between devices, shards(): other = [lax.ppermute(part[:tall], 'band', CORE_SWAP) for part in mine]  11.1 us
    pallas_call x1, Pallas kernels, rpn(): pl.pallas_call(rpn_kernel, out_shape=jax.ShapeDtypeStruct((anchors, rows,...  8.93 us
    ppermute x9, starting transfers between devices, shift_img(): lax.ppermute(array, 'img', [(i, (i + step) % size) for i in range(size)])  8.78 us
    unnamed x40, local copies, waits for them, and re-layouts  7.44 us
  transfers between devices with their start and end apart: 26, of which 9 were waited for; matrix products, arithmetic and copies ran while one was open for 4% of the time, Pallas kernels for 8%

profile of v11, /device:TPU:1, one launch (start us, length us, event | category | flops | bytes accessed | tf_op | source)
XLA Modules:
  0.0 173.4 jit_solution(1441939277420443767)
XLA Ops:
  3.0 5.5 %collect.1 = bf16[64,32,256]{2,1,0:T(8,128)(2,1)} custom-call(s32[32,64]{1,0:T(8,128)S(1)} %bitcast.52, bf16[4096,256]{1,0:T(8,128)(2,1)S(1)} %bitcast.50), custom_call_target="tpu_custom_call" | custom-call | flops 4000000000 | bytes 3000000 | tf_op jit(solution)/shard_map/collect/pallas_call | solution.py:113
  8.5 13.3 %all-to-all-start = ((bf16[64,32,256]{2,1,0:T(8,128)(2,1)}), bf16[64,32,256]{2,1,0:T(8,128)(2,1)S(1)}, u32[]{:S(2)}, u32[]{:S(2)}) async-start(bf16[64,32,256]{2,1,0:T(8,128)(2,1)} %collect.1), calls=%async_computation | async-start | bytes 2097152 | tf_op jit(solution)/shard_map/all_to_all | solution.py:405
  21.8 2.9 %collective-permute-start.2 = (bf16[196,1024]{1,0:T(8,128)(2,1)S(1)}, bf16[196,1024]{1,0:T(8,128)(2,1)S(1)}, u32[]{:S(2)}, u32[]{:S(2)}) collective-permute-start(bf16[196,1024]{1,0:T(8,128)(2,1)S(1)} %copy-done.1), channel_id=1, source_target_pairs={{0,48},{1,49},{2,50},{3,51},{4,52},{5,53},{6,54},{7,55},{8,56},{9,... | collective-permute-start | bytes 1204232 | tf_op jit(solution)/shard_map/ppermute | solution.py:159
  27.0 1.9 %slice_bitcast_fusion = (bf16[1,512,256]{2,1,0:T(8,128)(2,1)}, bf16[1,512,256]{2,1,0:T(8,128)(2,1)}) fusion(bf16[1,8,512,256]{3,2,1,0:T(8,128)(2,1)} %param.10), kind=kLoop, calls=%fused_computation.23 | loop fusion | bytes 1048576 | tf_op jit(solution)/shard_map/squeeze | solution.py:25
  28.9 1.9 %collective-permute-start.4 = (bf16[1,512,256]{2,1,0:T(8,128)(2,1)}, bf16[1,512,256]{2,1,0:T(8,128)(2,1)S(1)}, u32[]{:S(2)}, u32[]{:S(2)}) collective-permute-start(bf16[1,512,256]{2,1,0:T(8,128)(2,1)} %get-tuple-element.70), channel_id=1, source_target_pairs={{1,0},{2,1},{3,2},{4,3},{5,4},{6,5},{7,6},{8,7},{9,8},{10,9},{11,1... | collective-permute-start | bytes 786440 | tf_op jit(solution)/shard_map/ppermute | solution.py:25
  31.1 3.8 %collective-permute-start.3 = (bf16[1,512,256]{2,1,0:T(8,128)(2,1)}, bf16[1,512,256]{2,1,0:T(8,128)(2,1)S(1)}, u32[]{:S(2)}, u32[]{:S(2)}) collective-permute-start(bf16[1,512,256]{2,1,0:T(8,128)(2,1)} %get-tuple-element.71), channel_id=1, source_target_pairs={{0,1},{1,2},{2,3},{3,4},{4,5},{5,6},{6,7},{7,8},{8,9},{9,10},{10,1... | collective-permute-start | bytes 786440 | tf_op jit(solution)/shard_map/ppermute | solution.py:24
  34.9 15.6 %all-to-all-done = bf16[64,32,256]{2,1,0:T(8,128)(2,1)S(1)} async-done(((bf16[64,32,256]{2,1,0:T(8,128)(2,1)}), bf16[64,32,256]{2,1,0:T(8,128)(2,1)S(1)}, u32[]{:S(2)}, u32[]{:S(2)}) %all-to-all-start) | async-done | bytes 1048608 | tf_op jit(solution)/shard_map/all_to_all | solution.py:405
  50.5 3.1 %fusion.17 = bf16[392,256]{1,0:T(8,128)(2,1)S(1)} fusion(bf16[2048,256]{1,0:T(8,128)(2,1)S(1)} %bitcast.55, f32[392]{0:T(512)S(1)} %bitcast.64, s32[392]{0:T(512)S(1)} %bitcast.60, f32[392]{0:T(512)S(1)} %bitcast.65, s32[392]{0:T(512)S(1)} %bitcast.61, f32[392]{0:T(512)S(1)} %bitcast.66, s32[392]{0:T(512)S(1)} %bitcast.62, f32[392]{0:T(512)S(1)} %bitcast.63, ...), kind=kOutput, calls=%fused_computation.21 | convolution fusion | flops 2475182080 | bytes 1261824 | tf_op jit(solution)/shard_map/dot_general | solution.py:424
  58.0 6.5 %all-to-all-start.1 = ((bf16[16,8,1024]{2,1,0:T(8,128)(2,1)}), bf16[16,8,1024]{2,1,0:T(8,128)(2,1)S(1)}, u32[]{:S(2)}, u32[]{:S(2)}) async-start(bf16[16,8,1024]{2,1,0:T(8,128)(2,1)} %reshape.49), calls=%async_computation.1 | async-start | bytes 524288 | tf_op jit(solution)/shard_map/all_to_all | solution.py:82
  64.5 11.6 %all-to-all-done.1 = bf16[16,8,1024]{2,1,0:T(8,128)(2,1)S(1)} async-done(((bf16[16,8,1024]{2,1,0:T(8,128)(2,1)}), bf16[16,8,1024]{2,1,0:T(8,128)(2,1)S(1)}, u32[]{:S(2)}, u32[]{:S(2)}) %all-to-all-start.1) | async-done | bytes 262176 | tf_op jit(solution)/shard_map/all_to_all | solution.py:82
  80.6 10.9 %all_to_all.25 = bf16[8,16,512]{2,1,0:T(8,128)(2,1)S(1)} all-to-all(bf16[8,16,512]{2,1,0:T(8,128)(2,1)S(1)} %bitcast.58), channel_id=1, replica_groups={{0,2,4,6,8,10,12,14},{1,3,5,7,9,11,13,15},{16,18,20,22,24,26,28,30},{17..., dimensions={0} | all-to-all | bytes 262144 | tf_op jit(solution)/shard_map/all_to_all | solution.py:82
  91.6 10.8 %all_to_all.26 = bf16[8,16,640]{2,1,0:T(8,128)(2,1)S(1)} all-to-all(bf16[8,16,640]{2,1,0:T(8,128)(2,1)S(1)} %broadcast_in_dim.11), channel_id=1, replica_groups={{0,2,4,6,8,10,12,14},{1,3,5,7,9,11,13,15},{16,18,20,22,24,26,28,30},{17..., dimensions={0} | all-to-all | bytes 327680 | tf_op jit(solution)/shard_map/all_to_all | solution.py:82
  102.4 10.8 %all_to_all.27 = bf16[4,128,640]{2,1,0:T(8,128)(2,1)S(1)} all-to-all(bf16[4,128,640]{2,1,0:T(8,128)(2,1)S(1)} %broadcast_in_dim.26), channel_id=1, replica_groups={{0,16,32,48},{1,17,33,49},{2,18,34,50},{3,19,35,51},{4,20,36,52},{5,21,..., dimensions={0} | all-to-all | bytes 1310720 | tf_op jit(solution)/shard_map/all_to_all | solution.py:82
  113.2 3.5 %collective-permute-start.7 = (bf16[512,640]{1,0:T(8,128)(2,1)S(1)}, bf16[512,640]{1,0:T(8,128)(2,1)}, u32[]{:S(2)}, u32[]{:S(2)}) collective-permute-start(bf16[512,640]{1,0:T(8,128)(2,1)S(1)} %bitcast.44), channel_id=1, source_target_pairs={{0,1},{1,0},{2,3},{3,2},{4,5},{5,4},{6,7},{7,6},{8,9},{9,8},{10,11... | collective-permute-start | bytes 1966088 | tf_op jit(solution)/shard_map/ppermute | solution.py:445
  116.6 1.9 %collective-permute-done.7.other_ref = bf16[512,640]{1,0:T(8,128)(2,1)} collective-permute-done((bf16[512,640]{1,0:T(8,128)(2,1)S(1)}, bf16[512,640]{1,0:T(8,128)(2,1)}, u32[]{:S(2)}, u32[]{:S(2)}) %collective-permute-start.7) | collective-permute-done | bytes 655392 | tf_op jit(solution)/shard_map/ppermute | solution.py:445
  119.4 5.7 %head.1 = (bf16[512,1024]{1,0:T(8,128)(2,1)S(1)}, f32[128,1152]{1,0:T(8,128)S(1)}, bf16[128,1152]{1,0:T(8,128)(2,1)S(1)}, bf16[128,1152]{1,0:T(8,128)(2,1)S(1)}, bf16[128,1152]{1,0:T(8,128)(2,1)S(1)}) custom-call(s32[3]{0:T(128)S(1)} %pad_add_fusion.place, bf16[512,640]{1,0:T(8,128)(2,1)S(1)} %bitcast.45, bf16[512,640]{1,0:T(8,128)(2,1)} %collective-permute-done.7.other_ref, ...), custom_call_target="tpu_custom_call" | custom-call | tf_op jit(solution)/shard_map/head/pallas_call | solution.py:226
  131.9 4.6 %back.1.da1_ref = bf16[512,1024]{1,0:T(8,128)(2,1)S(1)} custom-call(s32[3]{0:T(128)S(1)} %pad_add_fusion.place, bf16[512,640]{1,0:T(8,128)(2,1)S(1)} %bitcast.46, bf16[512,640]{1,0:T(8,128)(2,1)} %collective-permute-done.7.other_ref, bf16[512,1024]{1,0:T(8,128)(2,1)S(1)} %get-tuple-element.49.da2_ref, bf16[1024,1024]{1,0:T(8,128)(2,1)S(1)} %copy-done), custom_call_target="tpu_custom_call" | custom-call | flops 2000000000 | bytes 5000000 | tf_op jit(solution)/shard_map/back/pallas_call | solution.py:252
  137.9 2.5 %collective-permute-start.16 = (bf16[196,256]{1,0:T(8,128)(2,1)S(1)}, bf16[196,256]{1,0:T(8,128)(2,1)S(1)}, u32[]{:S(2)}, u32[]{:S(2)}) collective-permute-start(bf16[196,256]{1,0:T(8,128)(2,1)S(1)} %get-tuple-element.60), channel_id=1, source_target_pairs={{0,192},{64,0},{128,64},{192,128},{1,193},{65,1},{129,65},{193,129... | collective-permute-start | bytes 301064 | tf_op jit(solution)/shard_map/ppermute | solution.py:93
  140.6 2.9 %collective-permute-done.14.refs_5_ = bf16[196,256]{1,0:T(8,128)(2,1)S(1)} collective-permute-done((bf16[196,256]{1,0:T(8,128)(2,1)S(1)}, bf16[196,256]{1,0:T(8,128)(2,1)S(1)}, u32[]{:S(2)}, u32[]{:S(2)}) %collective-permute-start.14) | collective-permute-done | bytes 100384 | tf_op jit(solution)/shard_map/ppermute | solution.py:93
  143.5 2.9 %collective-permute-done.15.refs_6_ = bf16[196,256]{1,0:T(8,128)(2,1)S(1)} collective-permute-done((bf16[196,256]{1,0:T(8,128)(2,1)S(1)}, bf16[196,256]{1,0:T(8,128)(2,1)S(1)}, u32[]{:S(2)}, u32[]{:S(2)}) %collective-permute-start.15) | collective-permute-done | bytes 100384 | tf_op jit(solution)/shard_map/ppermute | solution.py:93
  148.3 4.5 %collective-permute-start.20 = (bf16[144,1024]{1,0:T(8,128)(2,1)S(1)}, bf16[144,1024]{1,0:T(8,128)(2,1)S(1)}, u32[]{:S(2)}, u32[]{:S(2)}) collective-permute-start(bf16[144,1024]{1,0:T(8,128)(2,1)S(1)} %slice.52), channel_id=1, source_target_pairs={{0,1},{1,0},{2,3},{3,2},{4,5},{5,4},{6,7},{7,6},{8,9},{9,8},{10,11... | collective-permute-start | bytes 884744 | tf_op jit(solution)/shard_map/ppermute | solution.py:464
  152.9 8.9 %rpn.1 = bf16[15,8,512]{2,1,0:T(8,128)(2,1)} custom-call(bf16[1,512,256]{2,1,0:T(8,128)(2,1)S(1)} %copy-done.13, bf16[8,512,256]{2,1,0:T(8,128)(2,1)S(1)} %bitcast.51, bf16[1,512,256]{2,1,0:T(8,128)(2,1)S(1)} %copy-done.11, bf16[3,3,256,256]{3,2,1,0:T(8,128)(2,1)S(1)} %copy-done.9, bf16[15,256]{1,0:T(8,128)(2,1)S(1)} %bitcast.53), custom_call_target="tpu_custom_call" | custom-call | flops 8999999488 | bytes 4000000 | tf_op jit(solution)/shard_map/rpn/pallas_call | solution.py:58
  162.6 5.7 %collective-permute-start.21 = (bf16[144,1024]{1,0:T(8,128)(2,1)S(1)}, bf16[144,1024]{1,0:T(8,128)(2,1)S(1)}, u32[]{:S(2)}, u32[]{:S(2)}) collective-permute-start(bf16[144,1024]{1,0:T(8,128)(2,1)S(1)} %slice.64), channel_id=1, source_target_pairs={{0,1},{1,0},{2,3},{3,2},{4,5},{5,4},{6,7},{7,6},{8,9},{9,8},{10,11... | collective-permute-start | bytes 884744 | tf_op jit(solution)/shard_map/ppermute | solution.py:464
  170.0 3.3 %assemble.1 = (f32[196,1024]{1,0:T(8,128)}, f32[1024,1024]{1,0:T(8,128)}, f32[81,1024]{1,0:T(8,128)}) custom-call(s32[3]{0:T(128)S(1)} %pad_add_fusion.place, bf16[192,1024]{1,0:T(8,128)(2,1)S(1)} %sum_parts.1.refs_0_, bf16[192,1024]{1,0:T(8,128)(2,1)S(1)} %collective-permute-done.18.refs_1_, bf16[192,1024]{1,0:T(8,128)(2,1)S(1)} %collective-permute-done.17.refs_2_, ...), custom_call_target="tpu_custom_call" | custom-call | tf_op jit(solution)/shard_map/assemble/pallas_call | solution.py:367
  (105 shorter events, 27.5 us)
Async XLA Ops:
  8.5 42.0 %all-to-all-start = ((bf16[64,32,256]{2,1,0:T(8,128)(2,1)}), bf16[64,32,256]{2,1,0:T(8,128)(2,1)S(1)}, u32[]{:S(2)}, u32[]{:S(2)}) async-start(bf16[64,32,256]{2,1,0:T(8,128)(2,1)} %collect.1), calls=%async_computation | async-start | bytes 2097152 | tf_op jit(solution)/shard_map/all_to_all | solution.py:405
  21.8 34.0 %collective-permute-start.2 = (bf16[196,1024]{1,0:T(8,128)(2,1)S(1)}, bf16[196,1024]{1,0:T(8,128)(2,1)S(1)}, u32[]{:S(2)}, u32[]{:S(2)}) collective-permute-start(bf16[196,1024]{1,0:T(8,128)(2,1)S(1)} %copy-done.1), channel_id=1, source_target_pairs={{0,48},{1,49},{2,50},{3,51},{4,52},{5,53},{6,54},{7,55},{8,56},{9,... | collective-permute-start | bytes 1204232 | tf_op jit(solution)/shard_map/ppermute | solution.py:159
  24.7 31.1 %collective-permute-start.1 = (bf16[196,1024]{1,0:T(8,128)(2,1)S(1)}, bf16[196,1024]{1,0:T(8,128)(2,1)S(1)}, u32[]{:S(2)}, u32[]{:S(2)}) collective-permute-start(bf16[196,1024]{1,0:T(8,128)(2,1)S(1)} %copy-done.1), channel_id=1, source_target_pairs={{0,32},{1,33},{2,34},{3,35},{4,36},{5,37},{6,38},{7,39},{8,40},{9,... | collective-permute-start | bytes 1204232 | tf_op jit(solution)/shard_map/ppermute | solution.py:159
  25.1 31.1 %collective-permute-start = (bf16[196,1024]{1,0:T(8,128)(2,1)S(1)}, bf16[196,1024]{1,0:T(8,128)(2,1)S(1)}, u32[]{:S(2)}, u32[]{:S(2)}) collective-permute-start(bf16[196,1024]{1,0:T(8,128)(2,1)S(1)} %copy-done.1), channel_id=1, source_target_pairs={{0,16},{1,17},{2,18},{3,19},{4,20},{5,21},{6,22},{7,23},{8,24},{9,... | collective-permute-start | bytes 1204232 | tf_op jit(solution)/shard_map/ppermute | solution.py:159
  25.8 5.2 %collective-permute-start.5 = (bf16[8,128]{1,0:T(8,128)(2,1)S(1)}, bf16[8,128]{1,0:T(8,128)(2,1)S(1)}, u32[]{:S(2)}, u32[]{:S(2)}) collective-permute-start(bf16[8,128]{1,0:T(8,128)(2,1)S(1)} %broadcast_in_dim.10), channel_id=1, source_target_pairs={{0,1},{1,0},{2,3},{3,2},{4,5},{5,4},{6,7},{7,6},{8,9},{9,8},{10,11... | collective-permute-start | bytes 6152 | tf_op jit(solution)/shard_map/ppermute | solution.py:412
  28.9 25.5 %collective-permute-start.4 = (bf16[1,512,256]{2,1,0:T(8,128)(2,1)}, bf16[1,512,256]{2,1,0:T(8,128)(2,1)S(1)}, u32[]{:S(2)}, u32[]{:S(2)}) collective-permute-start(bf16[1,512,256]{2,1,0:T(8,128)(2,1)} %get-tuple-element.70), channel_id=1, source_target_pairs={{1,0},{2,1},{3,2},{4,3},{5,4},{6,5},{7,6},{8,7},{9,8},{10,9},{11,1... | collective-permute-start | bytes 786440 | tf_op jit(solution)/shard_map/ppermute | solution.py:25
  31.1 24.0 %collective-permute-start.3 = (bf16[1,512,256]{2,1,0:T(8,128)(2,1)}, bf16[1,512,256]{2,1,0:T(8,128)(2,1)S(1)}, u32[]{:S(2)}, u32[]{:S(2)}) collective-permute-start(bf16[1,512,256]{2,1,0:T(8,128)(2,1)} %get-tuple-element.71), channel_id=1, source_target_pairs={{0,1},{1,2},{2,3},{3,4},{4,5},{5,6},{6,7},{7,8},{8,9},{9,10},{10,1... | collective-permute-start | bytes 786440 | tf_op jit(solution)/shard_map/ppermute | solution.py:24
  58.0 18.2 %all-to-all-start.1 = ((bf16[16,8,1024]{2,1,0:T(8,128)(2,1)}), bf16[16,8,1024]{2,1,0:T(8,128)(2,1)S(1)}, u32[]{:S(2)}, u32[]{:S(2)}) async-start(bf16[16,8,1024]{2,1,0:T(8,128)(2,1)} %reshape.49), calls=%async_computation.1 | async-start | bytes 524288 | tf_op jit(solution)/shard_map/all_to_all | solution.py:82
  113.2 5.3 %collective-permute-start.7 = (bf16[512,640]{1,0:T(8,128)(2,1)S(1)}, bf16[512,640]{1,0:T(8,128)(2,1)}, u32[]{:S(2)}, u32[]{:S(2)}) collective-permute-start(bf16[512,640]{1,0:T(8,128)(2,1)S(1)} %bitcast.44), channel_id=1, source_target_pairs={{0,1},{1,0},{2,3},{3,2},{4,5},{5,4},{6,7},{7,6},{8,9},{9,8},{10,11... | collective-permute-start | bytes 1966088 | tf_op jit(solution)/shard_map/ppermute | solution.py:445
  125.1 15.3 %collective-permute-start.11 = (bf16[128,1152]{1,0:T(8,128)(2,1)S(1)}, bf16[128,1152]{1,0:T(8,128)(2,1)S(1)}, u32[]{:S(2)}, u32[]{:S(2)}) collective-permute-start(bf16[128,1152]{1,0:T(8,128)(2,1)S(1)} %get-tuple-element.52), channel_id=1, source_target_pairs={{0,64},{64,128},{128,192},{192,0},{1,65},{65,129},{129,193},{193,1... | collective-permute-start | bytes 884744 | tf_op jit(solution)/shard_map/ppermute | solution.py:93
  126.3 14.0 %collective-permute-start.12 = (bf16[128,1152]{1,0:T(8,128)(2,1)S(1)}, bf16[128,1152]{1,0:T(8,128)(2,1)S(1)}, u32[]{:S(2)}, u32[]{:S(2)}) collective-permute-start(bf16[128,1152]{1,0:T(8,128)(2,1)S(1)} %get-tuple-element.53), channel_id=1, source_target_pairs={{0,192},{64,0},{128,64},{192,128},{1,193},{65,1},{129,65},{193,129... | collective-permute-start | bytes 884744 | tf_op jit(solution)/shard_map/ppermute | solution.py:93
  127.9 3.8 %collective-permute-start.10 = (bf16[128,256]{1,0:T(8,128)(2,1)S(1)}, bf16[128,256]{1,0:T(8,128)(2,1)S(1)}, u32[]{:S(2)}, u32[]{:S(2)}) collective-permute-start(bf16[128,256]{1,0:T(8,128)(2,1)S(1)} %get-tuple-element.72), channel_id=1, source_target_pairs={{0,48},{1,49},{2,50},{3,51},{4,52},{5,53},{6,54},{7,55},{8,56},{9,... | collective-permute-start | bytes 196616 | tf_op jit(solution)/shard_map/ppermute | solution.py:159
  129.1 14.4 %collective-permute-start.13 = (bf16[128,1152]{1,0:T(8,128)(2,1)S(1)}, bf16[128,1152]{1,0:T(8,128)(2,1)S(1)}, u32[]{:S(2)}, u32[]{:S(2)}) collective-permute-start(bf16[128,1152]{1,0:T(8,128)(2,1)S(1)} %get-tuple-element.55), channel_id=1, source_target_pairs={{0,128},{64,192},{128,0},{192,64},{1,129},{65,193},{129,1},{193,65... | collective-permute-start | bytes 884744 | tf_op jit(solution)/shard_map/ppermute | solution.py:93
  130.5 6.0 %collective-permute-start.9 = (bf16[128,256]{1,0:T(8,128)(2,1)S(1)}, bf16[128,256]{1,0:T(8,128)(2,1)S(1)}, u32[]{:S(2)}, u32[]{:S(2)}) collective-permute-start(bf16[128,256]{1,0:T(8,128)(2,1)S(1)} %get-tuple-element.73), channel_id=1, source_target_pairs={{0,32},{1,33},{2,34},{3,35},{4,36},{5,37},{6,38},{7,39},{8,40},{9,... | collective-permute-start | bytes 196616 | tf_op jit(solution)/shard_map/ppermute | solution.py:159
  131.7 4.8 %collective-permute-start.8 = (bf16[128,256]{1,0:T(8,128)(2,1)S(1)}, bf16[128,256]{1,0:T(8,128)(2,1)S(1)}, u32[]{:S(2)}, u32[]{:S(2)}) collective-permute-start(bf16[128,256]{1,0:T(8,128)(2,1)S(1)} %get-tuple-element.74), channel_id=1, source_target_pairs={{0,16},{1,17},{2,18},{3,19},{4,20},{5,21},{6,22},{7,23},{8,24},{9,... | collective-permute-start | bytes 196616 | tf_op jit(solution)/shard_map/ppermute | solution.py:159
  137.6 5.9 %collective-permute-start.14 = (bf16[196,256]{1,0:T(8,128)(2,1)S(1)}, bf16[196,256]{1,0:T(8,128)(2,1)S(1)}, u32[]{:S(2)}, u32[]{:S(2)}) collective-permute-start(bf16[196,256]{1,0:T(8,128)(2,1)S(1)} %get-tuple-element.58), channel_id=1, source_target_pairs={{0,64},{64,128},{128,192},{192,0},{1,65},{65,129},{129,193},{193,1... | collective-permute-start | bytes 301064 | tf_op jit(solution)/shard_map/ppermute | solution.py:93
  137.9 5.6 %collective-permute-start.16 = (bf16[196,256]{1,0:T(8,128)(2,1)S(1)}, bf16[196,256]{1,0:T(8,128)(2,1)S(1)}, u32[]{:S(2)}, u32[]{:S(2)}) collective-permute-start(bf16[196,256]{1,0:T(8,128)(2,1)S(1)} %get-tuple-element.60), channel_id=1, source_target_pairs={{0,192},{64,0},{128,64},{192,128},{1,193},{65,1},{129,65},{193,129... | collective-permute-start | bytes 301064 | tf_op jit(solution)/shard_map/ppermute | solution.py:93
  140.4 6.1 %collective-permute-start.15 = (bf16[196,256]{1,0:T(8,128)(2,1)S(1)}, bf16[196,256]{1,0:T(8,128)(2,1)S(1)}, u32[]{:S(2)}, u32[]{:S(2)}) collective-permute-start(bf16[196,256]{1,0:T(8,128)(2,1)S(1)} %get-tuple-element.59), channel_id=1, source_target_pairs={{0,128},{64,192},{128,0},{192,64},{1,129},{65,193},{129,1},{193,65... | collective-permute-start | bytes 301064 | tf_op jit(solution)/shard_map/ppermute | solution.py:93
  146.8 15.0 %collective-permute-start.19 = (bf16[192,1024]{1,0:T(8,128)(2,1)S(1)}, bf16[192,1024]{1,0:T(8,128)(2,1)S(1)}, u32[]{:S(2)}, u32[]{:S(2)}) collective-permute-start(bf16[192,1024]{1,0:T(8,128)(2,1)S(1)} %sum_parts.1.refs_0_), channel_id=1, source_target_pairs={{0,192},{64,0},{128,64},{192,128},{1,193},{65,1},{129,65},{193,129... | collective-permute-start | bytes 1179656 | tf_op jit(solution)/shard_map/ppermute | solution.py:93
  147.1 15.5 %collective-permute-start.18 = (bf16[192,1024]{1,0:T(8,128)(2,1)S(1)}, bf16[192,1024]{1,0:T(8,128)(2,1)S(1)}, u32[]{:S(2)}, u32[]{:S(2)}) collective-permute-start(bf16[192,1024]{1,0:T(8,128)(2,1)S(1)} %sum_parts.1.refs_0_), channel_id=1, source_target_pairs={{0,64},{64,128},{128,192},{192,0},{1,65},{65,129},{129,193},{193,1... | collective-permute-start | bytes 1179656 | tf_op jit(solution)/shard_map/ppermute | solution.py:93
  148.3 20.0 %collective-permute-start.17 = (bf16[192,1024]{1,0:T(8,128)(2,1)S(1)}, bf16[192,1024]{1,0:T(8,128)(2,1)S(1)}, u32[]{:S(2)}, u32[]{:S(2)}) collective-permute-start(bf16[192,1024]{1,0:T(8,128)(2,1)S(1)} %sum_parts.1.refs_0_), channel_id=1, source_target_pairs={{0,128},{64,192},{128,0},{192,64},{1,129},{65,193},{129,1},{193,65... | collective-permute-start | bytes 1179656 | tf_op jit(solution)/shard_map/ppermute | solution.py:93
  148.3 20.1 %collective-permute-start.20 = (bf16[144,1024]{1,0:T(8,128)(2,1)S(1)}, bf16[144,1024]{1,0:T(8,128)(2,1)S(1)}, u32[]{:S(2)}, u32[]{:S(2)}) collective-permute-start(bf16[144,1024]{1,0:T(8,128)(2,1)S(1)} %slice.52), channel_id=1, source_target_pairs={{0,1},{1,0},{2,3},{3,2},{4,5},{5,4},{6,7},{7,6},{8,9},{9,8},{10,11... | collective-permute-start | bytes 884744 | tf_op jit(solution)/shard_map/ppermute | solution.py:464
  161.8 6.6 %collective-permute-start.23 = (bf16[144,1024]{1,0:T(8,128)(2,1)S(1)}, bf16[144,1024]{1,0:T(8,128)(2,1)S(1)}, u32[]{:S(2)}, u32[]{:S(2)}) collective-permute-start(bf16[144,1024]{1,0:T(8,128)(2,1)S(1)} %slice.65), channel_id=1, source_target_pairs={{0,1},{1,0},{2,3},{3,2},{4,5},{5,4},{6,7},{7,6},{8,9},{9,8},{10,11... | collective-permute-start | bytes 884744 | tf_op jit(solution)/shard_map/ppermute | solution.py:464
  162.6 7.0 %collective-permute-start.21 = (bf16[144,1024]{1,0:T(8,128)(2,1)S(1)}, bf16[144,1024]{1,0:T(8,128)(2,1)S(1)}, u32[]{:S(2)}, u32[]{:S(2)}) collective-permute-start(bf16[144,1024]{1,0:T(8,128)(2,1)S(1)} %slice.64), channel_id=1, source_target_pairs={{0,1},{1,0},{2,3},{3,2},{4,5},{5,4},{6,7},{7,6},{8,9},{9,8},{10,11... | collective-permute-start | bytes 884744 | tf_op jit(solution)/shard_map/ppermute | solution.py:464
  (21 other events, 247.1 us)
